TPU v7x, 32 devices: a whole 2x2x4 slice. The times are simulated.
32 devices in a mesh: section: 4 (over y, core), wide: 8 (over z, x).
Axes of the slice: x: 2, y: 2, z: 4, core: 2. Of those that a mesh axis runs over, the one named last changes fastest.
Arguments:
- token_ids: int32 [8, 2, 64], P('wide'), may hold values from 0 to 2047
- targets: int32 [8, 2, 64], P('wide'), may hold values from 0 to 2047
- slot_ids: int32 [2048, 8], P(('section', 'wide')), may hold values from 0 to 1023
- group_ids: int32 [2048], P(('section', 'wide')), may hold values from 0 to 3
- group_offsets: int32 [4], replicated, may hold values from 0 to 3072
- piece_table: bfloat16 [4096, 512], replicated, may hold values from -6 to 6
- prenorm_gain: float32 [512], P(('section', 'wide')), may hold values from 0.25 to 1.75
- prenorm_bias: float32 [512], P(('section', 'wide')), may hold values from -2 to 2
- query_map: float32 [512, 512], P(('section', 'wide')), may hold values from -0.25 to 0.25
- key_map: float32 [512, 512], P(('section', 'wide')), may hold values from -0.25 to 0.25
- value_map: float32 [512, 512], P(('section', 'wide')), may hold values from -0.25 to 0.25
- output_map: float32 [512, 512], P(('section', 'wide')), may hold values from -0.5 to 0.5
- midnorm_gain: float32 [512], P(('section', 'wide')), may hold values from 0.25 to 1.75
- midnorm_bias: float32 [512], P(('section', 'wide')), may hold values from -2 to 2
- expand_map: float32 [512, 2048], P(('section', 'wide')), may hold values from -0.25 to 0.25
- reduce_map: float32 [2048, 512], P(('section', 'wide')), may hold values from -0.1875 to 0.1875
- embed_map: float32 [512, 2048], P(('section', 'wide')), may hold values from -0.0234375 to 0.0234375
- attention_gain: bfloat16 [2, 2048], P(None, 'wide'), may hold values from 0.25 to 1.75
- query_weight: bfloat16 [2, 2048, 2048], P(None, 'wide'), may hold values from -0.125 to 0.125
- key_weight: bfloat16 [2, 2048, 256], P(None, 'wide'), may hold values from -0.125 to 0.125
- value_weight: bfloat16 [2, 2048, 256], P(None, 'wide'), may hold values from -0.125 to 0.125
- output_weight: bfloat16 [2, 2048, 2048], P(None, 'wide'), may hold values from -0.375 to 0.375
- feed_gain: bfloat16 [2, 2048], P(None, 'wide'), may hold values from 0.25 to 1.75
- gate_weight: bfloat16 [2, 2048, 5632], P(None, 'wide'), may hold values from -0.125 to 0.125
- up_weight: bfloat16 [2, 2048, 5632], P(None, 'wide'), may hold values from -0.125 to 0.125
- down_weight: bfloat16 [2, 5632, 2048], P(None, 'wide'), may hold values from -0.109375 to 0.109375
- final_gain: bfloat16 [2048], replicated, may hold values from 0.25 to 1.75
Outputs:
- mean_loss: float32 [], replicated
- grad_prescale: float32 [512], P(('section', 'wide'))
- prenorm_bias_gradient: float32 [512], P(('section', 'wide'))
- grad_query: float32 [512, 512], P(('section', 'wide'))
- grad_key: float32 [512, 512], P(('section', 'wide'))
- grad_value: float32 [512, 512], P(('section', 'wide'))
- grad_output: float32 [512, 512], P(('section', 'wide'))
- grad_midscale: float32 [512], P(('section', 'wide'))
- grad_midshift: float32 [512], P(('section', 'wide'))
- grad_expand: float32 [512, 2048], P(('section', 'wide'))
- grad_reduce: float32 [2048, 512], P(('section', 'wide'))
- grad_embed: float32 [512, 2048], P(('section', 'wide'))
All inputs are finite; a program needn't handle non-finite values.
Results may differ from a plain program's by a relative error of at most 0.035.
The roundings to bfloat16 on the way count: a program that leaves them out, or rounds other values in their place, can miss the bound.
Values may be sent and summed in bfloat16 or wider, within the bound.
A program may use at most 448 MiB of HBM per device.

v0:
```python
import jax
import jax.numpy as jnp
from jax import lax
from jax.sharding import PartitionSpec as P

HEAD_DIM = 64
HYPER_HEAD_COUNT = 8
MB = 2
LEN = 64


norm_eps = 1e-05
inv_root_two = 0.7071067811865476
inv_root_tau = 0.3989422804014327


def passed_along(value, axis, steps):
    count = lax.axis_size(axis)
    leading, last = (max(0, -steps), min(count, count - steps))
    return lax.ppermute(value, axis, [(source, source + steps) for source in range(leading, last)])


def from_root(block, axis, holder):
    block = jnp.where(lax.axis_index(axis) == holder, block, jnp.zeros_like(block))
    return lax.psum(block, axis)


def combined_all(shard, axis, combine):
    everything = jax.tree.map(
        lambda part, kind: lax.all_gather(part.astype(kind), axis),
        shard,
        (jnp.bfloat16, jnp.bfloat16, jnp.bfloat16),
    )

    def take(k):
        return jax.tree.map(lambda part, own: part[k].astype(own.dtype), everything, shard)

    return lax.fori_loop(
        1, lax.axis_size(axis), lambda k, so_far: combine(so_far, take(k)), take(0)
    )


def matmul(former, latter):
    return jnp.dot(former, latter, preferred_element_type=jnp.float32)


def times_trans(former, latter):
    return lax.dot_general(
        former, latter, (((1,), (1,)), ((), ())), preferred_element_type=jnp.float32
    )


def trans_times(former, latter):
    return lax.dot_general(
        former, latter, (((0,), (0,)), ((), ())), preferred_element_type=jnp.float32
    )


def center_norm(values):
    center = values - jnp.mean(values, axis=-1, keepdims=True)
    inverse = lax.rsqrt(jnp.mean(center * center, axis=-1, keepdims=True) + norm_eps)
    return (center * inverse, inverse)


def center_back(normed, inverse, normed_grad):
    mean_grad = jnp.mean(normed_grad, axis=-1, keepdims=True)
    mean_mix = jnp.mean(normed_grad * normed, axis=-1, keepdims=True)
    return inverse * (normed_grad - mean_grad - normed * mean_mix)


def root_inverse(values):
    return lax.rsqrt(jnp.mean(values * values, axis=-1, keepdims=True) + norm_eps)


def reciprocal_root_backward(values, inverse, gain_vec, outer_grad):
    scaled = outer_grad * gain_vec
    mixing = jnp.mean(scaled * values, axis=-1, keepdims=True)
    return inverse * scaled - values * inverse * inverse * inverse * mixing


def rope_tables(positions, head_width):
    halfway = head_width // 2
    frequency = jnp.exp(
        -jnp.log(10000.0) * (2.0 * jnp.arange(halfway, dtype=jnp.float32) / head_width)
    )
    angles = jnp.arange(positions, dtype=jnp.float32)[:, None] * frequency[None, :]
    angles = jnp.concatenate([angles, angles], axis=1)
    return (jnp.cos(angles), jnp.sin(angles))


def apply_rotary(values, cosines, sines):
    halfway = values.shape[-1] // 2
    turned = jnp.concatenate([-values[..., halfway:], values[..., :halfway]], axis=-1)
    return values * cosines[None, :, None, :] + turned * sines[None, :, None, :]


def invert_rotary(gradient, cosines, sines):
    halfway = gradient.shape[-1] // 2
    scaled = gradient * sines[None, :, None, :]
    turned = jnp.concatenate([scaled[..., halfway:], -scaled[..., :halfway]], axis=-1)
    return gradient * cosines[None, :, None, :] + turned


def hyper_forward(pieces, params, head_count):
    (
        gain_one,
        bias_one,
        query_mat,
        key_mat,
        value_mat,
        out_mat,
        second_gain,
        bias_two,
        expand_mat,
        reduce_mat,
        embed_mat,
    ) = params
    entries, slot_count, model_width = pieces.shape
    head_width = model_width // head_count
    score_scale = head_width ** (-0.5)
    flat_in = pieces.reshape(entries * slot_count, model_width)
    normed_one, inverse_one = center_norm(flat_in)
    attn_in = (normed_one * gain_one.astype(jnp.float32) + bias_one.astype(jnp.float32)).astype(
        jnp.bfloat16
    )
    queries = (
        matmul(attn_in, query_mat)
        .astype(jnp.bfloat16)
        .reshape(entries, slot_count, head_count, head_width)
    )
    key_rows = (
        matmul(attn_in, key_mat)
        .astype(jnp.bfloat16)
        .reshape(entries, slot_count, head_count, head_width)
    )
    value_rows = (
        matmul(attn_in, value_mat)
        .astype(jnp.bfloat16)
        .reshape(entries, slot_count, head_count, head_width)
    )
    scores = (
        jnp.einsum("eshd,ethd->ehst", queries, key_rows, preferred_element_type=jnp.float32)
        * score_scale
    )
    weights_full = jax.nn.softmax(scores, axis=-1)
    weights_low = weights_full.astype(jnp.bfloat16)
    mixed = jnp.einsum(
        "ehst,ethd->eshd", weights_low, value_rows, preferred_element_type=jnp.float32
    )
    mixed = mixed.astype(jnp.bfloat16).reshape(entries * slot_count, model_width)
    middle = flat_in + matmul(mixed, out_mat)
    normed_two, inverse_two = center_norm(middle)
    ffn_in = (normed_two * second_gain.astype(jnp.float32) + bias_two.astype(jnp.float32)).astype(
        jnp.bfloat16
    )
    expanded = matmul(ffn_in, expand_mat)
    activated = jax.nn.gelu(expanded, approximate=False).astype(jnp.bfloat16)
    outcome = middle + matmul(activated, reduce_mat)
    pooled = jnp.mean(outcome.reshape(entries, slot_count, model_width), axis=1).astype(
        jnp.bfloat16
    )
    table_rows = matmul(pooled, embed_mat).astype(jnp.bfloat16)
    stored = (
        normed_one,
        inverse_one,
        attn_in,
        queries,
        key_rows,
        value_rows,
        weights_full,
        weights_low,
        mixed,
        normed_two,
        inverse_two,
        ffn_in,
        expanded,
        activated,
        pooled,
    )
    return (table_rows, stored)


def hyper_backward(params, stored, table_grad):
    (
        gain_one,
        bias_one,
        query_mat,
        key_mat,
        value_mat,
        out_mat,
        second_gain,
        bias_two,
        expand_mat,
        reduce_mat,
        embed_mat,
    ) = params
    (
        normed_one,
        inverse_one,
        attn_in,
        queries,
        key_rows,
        value_rows,
        weights_full,
        weights_low,
        mixed,
        normed_two,
        inverse_two,
        ffn_in,
        expanded,
        activated,
        pooled,
    ) = stored
    entries, slot_count, head_total, head_width = queries.shape
    model_width = head_total * head_width
    score_scale = head_width ** (-0.5)
    grad_low = table_grad.astype(jnp.bfloat16)
    grad_embed = trans_times(pooled, grad_low)
    pooled_grad = times_trans(grad_low, embed_mat) / slot_count
    outcome_grad = jnp.broadcast_to(pooled_grad[:, None, :], (entries, slot_count, model_width))
    outcome_grad = outcome_grad.reshape(entries * slot_count, model_width)
    outcome_low = outcome_grad.astype(jnp.bfloat16)
    grad_reduce = trans_times(activated, outcome_low)
    act_grad = times_trans(outcome_low, reduce_mat)
    slope = (
        0.5 * (1.0 + lax.erf(expanded * inv_root_two))
        + expanded * jnp.exp(-0.5 * expanded * expanded) * inv_root_tau
    )
    expanded_low = (act_grad * slope).astype(jnp.bfloat16)
    grad_expand = trans_times(ffn_in, expanded_low)
    ffn_grad = times_trans(expanded_low, expand_mat)
    grad_midscale = jnp.sum(ffn_grad * normed_two, axis=0)
    grad_midshift = jnp.sum(ffn_grad, axis=0)
    middle_grad = outcome_grad + center_back(
        normed_two, inverse_two, ffn_grad * second_gain.astype(jnp.float32)
    )
    middle_low = middle_grad.astype(jnp.bfloat16)
    grad_output = trans_times(mixed, middle_low)
    mixed_grad = times_trans(middle_low, out_mat).astype(jnp.bfloat16).reshape(queries.shape)
    weight_grad = jnp.einsum(
        "eshd,ethd->ehst", mixed_grad, value_rows, preferred_element_type=jnp.float32
    )
    value_grad = jnp.einsum(
        "ehst,eshd->ethd", weights_low, mixed_grad, preferred_element_type=jnp.float32
    )
    score_grad = weights_full * (
        weight_grad - jnp.sum(weights_full * weight_grad, axis=-1, keepdims=True)
    )
    score_grad = score_grad.astype(jnp.bfloat16)
    query_grad = (
        jnp.einsum("ehst,ethd->eshd", score_grad, key_rows, preferred_element_type=jnp.float32)
        * score_scale
    )
    key_grad = (
        jnp.einsum("ehst,eshd->ethd", score_grad, queries, preferred_element_type=jnp.float32)
        * score_scale
    )
    query_low = query_grad.astype(jnp.bfloat16).reshape(entries * slot_count, model_width)
    key_low = key_grad.astype(jnp.bfloat16).reshape(entries * slot_count, model_width)
    value_low = value_grad.astype(jnp.bfloat16).reshape(entries * slot_count, model_width)
    grad_query = trans_times(attn_in, query_low)
    grad_key = trans_times(attn_in, key_low)
    grad_value = trans_times(attn_in, value_low)
    attention_gradient = (
        times_trans(query_low, query_mat)
        + times_trans(key_low, key_mat)
        + times_trans(value_low, value_mat)
    )
    grad_prescale = jnp.sum(attention_gradient * normed_one, axis=0)
    prenorm_bias_gradient = jnp.sum(attention_gradient, axis=0)
    return (
        grad_prescale,
        prenorm_bias_gradient,
        grad_query,
        grad_key,
        grad_value,
        grad_output,
        grad_midscale,
        grad_midshift,
        grad_expand,
        grad_reduce,
        grad_embed,
    )


def decoder_forward(inputs, weights, cosines, sines):
    gain_attn, query_mat, key_mat, value_mat, out_mat, gain_ffn, gate_mat, up_mat, down_mat = (
        weights
    )
    sequences, positions, model_width = inputs.shape
    head_width = cosines.shape[1]
    head_count = query_mat.shape[1] // head_width
    key_heads = key_mat.shape[1] // head_width
    shared = head_count // key_heads
    score_scale = head_width ** (-0.5)
    flat_in = inputs.reshape(sequences * positions, model_width).astype(jnp.float32)
    inverse_one = root_inverse(flat_in)
    normed_one = (flat_in * inverse_one * gain_attn.astype(jnp.float32)).astype(jnp.bfloat16)
    query_pre = matmul(normed_one, query_mat).reshape(sequences, positions, head_count, head_width)
    key_pre = matmul(normed_one, key_mat).reshape(sequences, positions, key_heads, head_width)
    value_rows = (
        matmul(normed_one, value_mat)
        .astype(jnp.bfloat16)
        .reshape(sequences, positions, key_heads, head_width)
    )
    queries = apply_rotary(query_pre, cosines, sines).astype(jnp.bfloat16)
    queries = queries.reshape(sequences, positions, key_heads, shared, head_width)
    key_rows = apply_rotary(key_pre, cosines, sines).astype(jnp.bfloat16)
    causal = jnp.arange(positions)[:, None] >= jnp.arange(positions)[None, :]
    scores = (
        jnp.einsum("blkgd,bmkd->bkglm", queries, key_rows, preferred_element_type=jnp.float32)
        * score_scale
    )
    scores = jnp.where(causal, scores, -1e30)
    weights_full = jax.nn.softmax(scores, axis=-1)
    weights_low = weights_full.astype(jnp.bfloat16)
    mixed = jnp.einsum(
        "bkglm,bmkd->blkgd", weights_low, value_rows, preferred_element_type=jnp.float32
    )
    mixed = mixed.astype(jnp.bfloat16).reshape(sequences * positions, model_width)
    middle = flat_in + matmul(mixed, out_mat)
    inverse_two = root_inverse(middle)
    normed_two = (middle * inverse_two * gain_ffn.astype(jnp.float32)).astype(jnp.bfloat16)
    gate_pre = matmul(normed_two, gate_mat)
    up_pre = matmul(normed_two, up_mat)
    activated = (jax.nn.silu(gate_pre) * up_pre).astype(jnp.bfloat16)
    outcome = middle + matmul(activated, down_mat)
    stored = (
        flat_in,
        inverse_one,
        queries,
        key_rows,
        value_rows,
        weights_full,
        weights_low,
        middle,
        inverse_two,
        gate_pre,
        up_pre,
    )
    return (outcome.reshape(sequences, positions, model_width), stored)


def decoder_backward(inputs, weights, cosines, sines, outer_grad):
    gain_attn, query_mat, key_mat, value_mat, out_mat, gain_ffn, gate_mat, up_mat, down_mat = (
        weights
    )
    sequences, positions, model_width = inputs.shape
    outcome, stored = decoder_forward(inputs, weights, cosines, sines)
    (
        flat_in,
        inverse_one,
        queries,
        key_rows,
        value_rows,
        weights_full,
        weights_low,
        middle,
        inverse_two,
        gate_pre,
        up_pre,
    ) = stored
    head_width = cosines.shape[1]
    score_scale = head_width ** (-0.5)
    row_count = sequences * positions
    grad_low = outer_grad.reshape(row_count, model_width)
    activated_grad = times_trans(grad_low, down_mat)
    gate_sig = jax.nn.sigmoid(gate_pre)
    gate_silu = gate_pre * gate_sig
    gate_grad = (activated_grad * up_pre * gate_sig * (1.0 + gate_pre * (1.0 - gate_sig))).astype(
        jnp.bfloat16
    )
    up_grad = (activated_grad * gate_silu).astype(jnp.bfloat16)
    normed_two_grad = times_trans(gate_grad, gate_mat) + times_trans(up_grad, up_mat)
    middle_grad = grad_low.astype(jnp.float32) + reciprocal_root_backward(
        middle, inverse_two, gain_ffn.astype(jnp.float32), normed_two_grad
    )
    middle_low = middle_grad.astype(jnp.bfloat16)
    mixed_grad = times_trans(middle_low, out_mat).astype(jnp.bfloat16).reshape(queries.shape)
    weight_grad = jnp.einsum(
        "blkgd,bmkd->bkglm", mixed_grad, value_rows, preferred_element_type=jnp.float32
    )
    value_grad = jnp.einsum(
        "bkglm,blkgd->bmkd", weights_low, mixed_grad, preferred_element_type=jnp.float32
    )
    score_grad = weights_full * (
        weight_grad - jnp.sum(weights_full * weight_grad, axis=-1, keepdims=True)
    )
    score_grad = score_grad.astype(jnp.bfloat16)
    query_grad = (
        jnp.einsum("bkglm,bmkd->blkgd", score_grad, key_rows, preferred_element_type=jnp.float32)
        * score_scale
    )
    key_grad = (
        jnp.einsum("bkglm,blkgd->bmkd", score_grad, queries, preferred_element_type=jnp.float32)
        * score_scale
    )
    query_grad = query_grad.reshape(sequences, positions, -1, head_width)
    query_low = (
        invert_rotary(query_grad, cosines, sines).astype(jnp.bfloat16).reshape(row_count, -1)
    )
    key_low = invert_rotary(key_grad, cosines, sines).astype(jnp.bfloat16).reshape(row_count, -1)
    value_low = value_grad.astype(jnp.bfloat16).reshape(row_count, -1)
    normed_one_grad = (
        times_trans(query_low, query_mat)
        + times_trans(key_low, key_mat)
        + times_trans(value_low, value_mat)
    )
    input_grad = middle_grad + reciprocal_root_backward(
        flat_in, inverse_one, gain_attn.astype(jnp.float32), normed_one_grad
    )
    return input_grad.reshape(sequences, positions, model_width)


def shards(
    token_ids,
    targets,
    slot_ids,
    group_ids,
    group_offsets,
    piece_table,
    prenorm_gain,
    prenorm_bias,
    query_map,
    key_map,
    value_map,
    output_map,
    midnorm_gain,
    midnorm_bias,
    expand_map,
    reduce_map,
    embed_map,
    attention_gain,
    query_weight,
    key_weight,
    value_weight,
    output_weight,
    feed_gain,
    gate_weight,
    up_weight,
    down_weight,
    final_gain,
):
    gain_one = prenorm_gain.astype(jnp.bfloat16)
    bias_one = prenorm_bias.astype(jnp.bfloat16)
    query_low = query_map.astype(jnp.bfloat16)
    key_low = key_map.astype(jnp.bfloat16)
    value_low = value_map.astype(jnp.bfloat16)
    output_low = output_map.astype(jnp.bfloat16)
    second_gain = midnorm_gain.astype(jnp.bfloat16)
    bias_two = midnorm_bias.astype(jnp.bfloat16)
    expand_low = expand_map.astype(jnp.bfloat16)
    reduce_low = reduce_map.astype(jnp.bfloat16)
    embed_low = embed_map.astype(jnp.bfloat16)
    params = (
        lax.all_gather(gain_one, ("section", "wide"), axis=0, tiled=True),
        lax.all_gather(bias_one, ("section", "wide"), axis=0, tiled=True),
        lax.all_gather(query_low, ("section", "wide"), axis=0, tiled=True),
        lax.all_gather(key_low, ("section", "wide"), axis=0, tiled=True),
        lax.all_gather(value_low, ("section", "wide"), axis=0, tiled=True),
        lax.all_gather(output_low, ("section", "wide"), axis=0, tiled=True),
        lax.all_gather(second_gain, ("section", "wide"), axis=0, tiled=True),
        lax.all_gather(bias_two, ("section", "wide"), axis=0, tiled=True),
        lax.all_gather(expand_low, ("section", "wide"), axis=0, tiled=True),
        lax.all_gather(reduce_low, ("section", "wide"), axis=0, tiled=True),
        lax.all_gather(embed_low, ("section", "wide"), axis=0, tiled=True),
    )
    entries, slot_count = slot_ids.shape
    group_hits = (
        group_ids[:, None] == jnp.arange(group_offsets.shape[0], dtype=jnp.int32)[None, :]
    ).astype(jnp.int32)
    row_start = jnp.sum(group_hits * group_offsets[None, :], axis=1)
    piece_rows = (row_start[:, None] + slot_ids).reshape(-1)
    pieces = (
        jnp.take(piece_table, piece_rows, axis=0)
        .astype(jnp.float32)
        .reshape(entries, slot_count, piece_table.shape[1])
    )
    table_shard, hyper_stored = hyper_forward(pieces, params, HYPER_HEAD_COUNT)
    all_ids, all_targets = (
        lax.all_gather(token_ids, "wide", axis=0, tiled=True),
        lax.all_gather(targets, "wide", axis=0, tiled=True),
    )
    ids_flat = all_ids.reshape(-1)
    targets_flat = all_targets.reshape(-1)
    local_ids = token_ids.reshape(-1)
    local_targets = targets.reshape(-1)
    local_tokens = local_ids.shape[0]
    total_tokens = ids_flat.shape[0]
    model_width = table_shard.shape[1]
    section_index = lax.axis_index("section")
    wide_index = lax.axis_index("wide")
    owner_index = lax.axis_index(("section", "wide"))
    row_base = owner_index * entries
    own_rows = row_base + jnp.arange(entries, dtype=jnp.int32)
    layer_slot = jnp.clip(section_index - 1, 0, 1)

    def select(stack):
        return lax.dynamic_index_in_dim(stack, layer_slot, 0, keepdims=False)

    layer_weights = (
        lax.all_gather(select(attention_gain), "wide", axis=0, tiled=True),
        lax.all_gather(select(query_weight), "wide", axis=0, tiled=True),
        lax.all_gather(select(key_weight), "wide", axis=0, tiled=True),
        lax.all_gather(select(value_weight), "wide", axis=0, tiled=True),
        lax.all_gather(select(output_weight), "wide", axis=0, tiled=True),
        lax.all_gather(select(feed_gain), "wide", axis=0, tiled=True),
        lax.all_gather(select(gate_weight), "wide", axis=0, tiled=True),
        lax.all_gather(select(up_weight), "wide", axis=0, tiled=True),
        lax.all_gather(select(down_weight), "wide", axis=0, tiled=True),
    )
    block_rows = lax.all_gather(table_shard, ("section", "wide"), axis=0, tiled=True)

    def lookup_accumulate(current):
        matches = local_ids[:, None] == jnp.arange(block_rows.shape[0], dtype=jnp.int32)[None, :]
        return matmul(matches.astype(jnp.bfloat16), block_rows)

    embedded = lax.cond(
        section_index == 0,
        lookup_accumulate,
        lambda current: current,
        jnp.zeros((local_tokens, model_width), jnp.float32),
    )
    embedded = embedded.astype(jnp.bfloat16).reshape(MB, LEN, model_width)
    cosines, sines = rope_tables(LEN, HEAD_DIM)
    group_count = 1
    group_size = MB // group_count
    is_layer = (section_index == 1) | (section_index == 2)

    def run_layer(layer_input):
        return decoder_forward(layer_input, layer_weights, cosines, sines)[0].astype(jnp.bfloat16)

    outgoing = jnp.zeros((group_size, LEN, model_width), jnp.bfloat16)
    kept_inputs = jnp.zeros((MB, LEN, model_width), jnp.bfloat16)
    final_rows = jnp.zeros((MB, LEN, model_width), jnp.bfloat16)
    for moment in range(group_count + 3):
        incoming = jnp.zeros_like(outgoing)
        if moment > 0:
            incoming = passed_along(outgoing, "section", 1)
        slot_index = moment - section_index
        active = (slot_index >= 0) & (slot_index < group_count)
        layer_out = lax.cond(active & is_layer, run_layer, jnp.zeros_like, incoming)
        stored_rows = kept_inputs
        kept_inputs = jnp.where(active & is_layer, incoming, stored_rows)
        landed = final_rows
        final_rows = jnp.where(active & (section_index == 3), incoming, landed)
        if moment < group_count:
            source = embedded
        else:
            source = jnp.zeros_like(outgoing)
        outgoing = jnp.where(section_index == 0, source, layer_out)
    final_flat = final_rows.reshape(local_tokens, model_width).astype(jnp.float32)
    final_inverse = root_inverse(final_flat)
    final_scale = final_gain.astype(jnp.float32)
    final_normed = (final_flat * final_inverse * final_scale).astype(jnp.bfloat16)
    shared_normed = from_root(final_normed, "section", 3)
    logits = times_trans(lax.all_gather(shared_normed, "wide", axis=0, tiled=True), table_shard)
    row_peak = jnp.max(logits, axis=1)
    row_mass = jnp.sum(jnp.exp(logits - row_peak[:, None]), axis=1)
    chosen = jnp.sum(jnp.where(targets_flat[:, None] == own_rows[None, :], logits, 0.0), axis=1)
    maxima = row_peak
    totals = row_mass
    picked = chosen

    def combine(former, latter):
        largest = jnp.maximum(former[0], latter[0])
        summed = former[1] * jnp.exp(former[0] - largest) + latter[1] * jnp.exp(latter[0] - largest)
        return (largest, summed, former[2] + latter[2])

    maxima, totals, picked = combined_all((maxima, totals, picked), ("section", "wide"), combine)
    log_norm = maxima + jnp.log(totals)
    mean_loss = jnp.sum(log_norm - picked) / total_tokens
    local_norm = lax.dynamic_slice_in_dim(log_norm, wide_index * local_tokens, local_tokens)
    head_block_rows = lax.all_gather(table_shard, ("section", "wide"), axis=0, tiled=True)

    def head_accumulate(current):
        logits = times_trans(final_normed, head_block_rows)
        matches = (
            local_targets[:, None] == jnp.arange(head_block_rows.shape[0], dtype=jnp.int32)[None, :]
        )
        logit_grad = (
            (jnp.exp(logits - local_norm[:, None]) - matches.astype(jnp.float32)) / total_tokens
        ).astype(jnp.bfloat16)
        return matmul(logit_grad, head_block_rows)

    normed_grad = lax.cond(
        section_index == 3,
        head_accumulate,
        lambda current: current,
        jnp.zeros((local_tokens, model_width), jnp.float32),
    )
    final_grad = reciprocal_root_backward(final_flat, final_inverse, final_scale, normed_grad)
    final_grad = final_grad.astype(jnp.bfloat16).reshape(MB, LEN, model_width)

    def back_layer(couple):
        return decoder_backward(couple[0], layer_weights, cosines, sines, couple[1]).astype(
            jnp.bfloat16
        )

    def no_layer(couple):
        return jnp.zeros_like(couple[1])

    outgoing = jnp.zeros((group_size, LEN, model_width), jnp.bfloat16)
    inject_grad = jnp.zeros((MB, LEN, model_width), jnp.bfloat16)
    for moment in range(group_count + 3):
        incoming = jnp.zeros_like(outgoing)
        if moment > 0:
            incoming = passed_along(outgoing, "section", -1)
        slot_index = moment - (3 - section_index)
        active = (slot_index >= 0) & (slot_index < group_count)
        layer_input = kept_inputs
        layer_back = lax.cond(active & is_layer, back_layer, no_layer, (layer_input, incoming))
        landed = inject_grad
        inject_grad = jnp.where(active & (section_index == 0), incoming, landed)
        if moment < group_count:
            source = final_grad
        else:
            source = jnp.zeros_like(outgoing)
        outgoing = jnp.where(section_index == 3, source, layer_back)
    shared_grad = from_root(inject_grad.reshape(local_tokens, model_width), "section", 0)

    def table_rows(running, pieces_here, offset):
        normed_rows, grad_rows = pieces_here
        logits = times_trans(normed_rows, table_shard)
        hit_rows = (targets_flat[:, None] == own_rows[None, :]).astype(jnp.float32)
        logit_grad = ((jnp.exp(logits - log_norm[:, None]) - hit_rows) / total_tokens).astype(
            jnp.bfloat16
        )
        chosen = (ids_flat[:, None] == own_rows[None, :]).astype(jnp.bfloat16)
        return trans_times(logit_grad, normed_rows) + trans_times(chosen, grad_rows)

    table_grad = table_rows(
        jnp.zeros((entries, model_width), jnp.float32),
        (
            lax.all_gather(shared_normed, "wide", axis=0, tiled=True),
            lax.all_gather(shared_grad, "wide", axis=0, tiled=True),
        ),
        jnp.int32(0),
    )
    gradients = hyper_backward(params, hyper_stored, table_grad)
    (
        grad_prescale,
        prenorm_bias_gradient,
        grad_query,
        grad_key,
        grad_value,
        grad_output,
        grad_midscale,
        grad_midshift,
        grad_expand,
        grad_reduce,
        grad_embed,
    ) = gradients
    summed = (
        lax.psum_scatter(grad_prescale, ("section", "wide"), scatter_dimension=0, tiled=True),
        lax.psum_scatter(
            prenorm_bias_gradient, ("section", "wide"), scatter_dimension=0, tiled=True
        ),
        lax.psum_scatter(grad_query, ("section", "wide"), scatter_dimension=0, tiled=True),
        lax.psum_scatter(grad_key, ("section", "wide"), scatter_dimension=0, tiled=True),
        lax.psum_scatter(grad_value, ("section", "wide"), scatter_dimension=0, tiled=True),
        lax.psum_scatter(grad_output, ("section", "wide"), scatter_dimension=0, tiled=True),
        lax.psum_scatter(grad_midscale, ("section", "wide"), scatter_dimension=0, tiled=True),
        lax.psum_scatter(grad_midshift, ("section", "wide"), scatter_dimension=0, tiled=True),
        lax.psum_scatter(grad_expand, ("section", "wide"), scatter_dimension=0, tiled=True),
        lax.psum_scatter(grad_reduce, ("section", "wide"), scatter_dimension=0, tiled=True),
        lax.psum_scatter(grad_embed, ("section", "wide"), scatter_dimension=0, tiled=True),
    )
    return (
        mean_loss,
        summed[0],
        summed[1],
        summed[2],
        summed[3],
        summed[4],
        summed[5],
        summed[6],
        summed[7],
        summed[8],
        summed[9],
        summed[10],
    )


def solution(mesh):
    placed = (
        P("wide", None, None),
        P("wide", None, None),
        P(("section", "wide"), None),
        P(("section", "wide")),
        P(),
        P(),
        P(("section", "wide")),
        P(("section", "wide")),
        P(("section", "wide"), None),
        P(("section", "wide"), None),
        P(("section", "wide"), None),
        P(("section", "wide"), None),
        P(("section", "wide")),
        P(("section", "wide")),
        P(("section", "wide"), None),
        P(("section", "wide"), None),
        P(("section", "wide"), None),
        P(None, "wide"),
        P(None, "wide", None),
        P(None, "wide", None),
        P(None, "wide", None),
        P(None, "wide", None),
        P(None, "wide"),
        P(None, "wide", None),
        P(None, "wide", None),
        P(None, "wide", None),
        P(),
    )
    return jax.shard_map(
        shards,
        mesh=mesh,
        in_specs=placed,
        out_specs=(
            P(),
            P(("section", "wide")),
            P(("section", "wide")),
            P(("section", "wide"), None),
            P(("section", "wide"), None),
            P(("section", "wide"), None),
            P(("section", "wide"), None),
            P(("section", "wide")),
            P(("section", "wide")),
            P(("section", "wide"), None),
            P(("section", "wide"), None),
            P(("section", "wide"), None),
        ),
        check_vma=False,
    )
```

profile of v0, /device:TPU:0, one launch (start us, length us, event | category | flops | bytes accessed | tf_op | source)
XLA Modules:
  0.0 4008.7 jit_solution(12865758043879077949)
XLA Ops:
  17.4 42.1 %all-reduce.9 = (bf16[512]{0:T(512)(128)(2,1)S(1)}, bf16[512]{0:T(512)(128)(2,1)S(1)}, bf16[512]{0:T(512)(128)(2,1)S(1)}, bf16[512]{0:T(512)(128)(2,1)S(1)}) all-reduce(bf16[512]{0:T(512)(128)(2,1)S(1)} %dynamic-update-slice.1, bf16[512]{0:T(512)(128)(2,1)S(1)} %dynamic-update-slice, ...), channel_id=1, replica_groups=mesh['section'=4,'wide'=8] {'section','wide'}, use_global_device_ids=true, to_apply=%add.1 | all-reduce | flops 2048 | bytes 8192
  59.6 4.8 gather_fusion
  65.0 69.7 %all_gather.91 = bf16[512,512]{1,0:T(8,128)(2,1)S(1)} all-gather(bf16[16,512]{1,0:T(8,128)(2,1)S(1)} %convert_element_type.692), channel_id=1, replica_groups=mesh['section'=4,'wide'=8] {'section','wide'}, dimensions={0}, use_global_device_ids=true | all-gather | bytes 540672 | tf_op jit(solution)/shard_map/all_gather | solution.py:460
  139.2 67.5 %all_gather.93 = bf16[512,512]{1,0:T(8,128)(2,1)S(1)} all-gather(bf16[16,512]{1,0:T(8,128)(2,1)S(1)} %convert_element_type.696), channel_id=1, replica_groups=mesh['section'=4,'wide'=8] {'section','wide'}, dimensions={0}, use_global_device_ids=true | all-gather | bytes 540672 | tf_op jit(solution)/shard_map/all_gather | solution.py:459
  209.5 68.7 %all_gather.92 = bf16[512,512]{1,0:T(8,128)(2,1)S(1)} all-gather(bf16[16,512]{1,0:T(8,128)(2,1)S(1)} %convert_element_type.694), channel_id=1, replica_groups=mesh['section'=4,'wide'=8] {'section','wide'}, dimensions={0}, use_global_device_ids=true | all-gather | bytes 540672 | tf_op jit(solution)/shard_map/all_gather | solution.py:458
  281.9 4.5 fusion.416
  290.9 67.1 %all_gather.94 = bf16[512,512]{1,0:T(8,128)(2,1)S(1)} all-gather(bf16[16,512]{1,0:T(8,128)(2,1)S(1)} %convert_element_type.701), channel_id=1, replica_groups=mesh['section'=4,'wide'=8] {'section','wide'}, dimensions={0}, use_global_device_ids=true | all-gather | bytes 540672 | tf_op jit(solution)/shard_map/all_gather | solution.py:461
  360.9 13.2 fusion.307
  397.6 18.6 all-gather
  416.2 16.3 all-gather.5
  432.7 23.7 all-gather.32.cloned.1.call-done
  456.4 4.8 conditional.8
  456.5 4.7 convolution_convert_fusion
  461.2 36.5 all-gather.38.cloned.1.call-done
  497.7 40.8 %all-gather.40.cloned.1.call-done = bf16[1,2048,256]{1,2,0:T(8,128)(2,1)} async-done(((bf16[1,256,256]{1,2,0:T(8,128)(2,1)}), bf16[1,2048,256]{1,2,0:T(8,128)(2,1)}) %all-gather.40.cloned.1.call-update) | async-done | bytes 1048592 | tf_op jit(solution)/shard_map/all_gather | solution.py:504
  538.5 126.4 %all-gather.42.cloned.1.call-done = bf16[1,2048,2048]{1,2,0:T(8,128)(2,1)} async-done(((bf16[1,256,2048]{1,2,0:T(8,128)(2,1)}), bf16[1,2048,2048]{1,2,0:T(8,128)(2,1)}) %all-gather.42.cloned.1.call-update) | async-done | bytes 8388624 | tf_op jit(solution)/shard_map/all_gather | solution.py:503
  664.9 125.3 %all-gather.44.cloned.1.call-done = bf16[1,2048,2048]{2,1,0:T(8,128)(2,1)} async-done(((bf16[1,256,2048]{2,1,0:T(8,128)(2,1)}), bf16[1,2048,2048]{2,1,0:T(8,128)(2,1)}) %all-gather.44.cloned.1.call-update) | async-done | bytes 8388624 | tf_op jit(solution)/shard_map/all_gather | solution.py:506
  790.1 440.9 %all-gather.46.cloned.1.call-done = bf16[1,2048,5632]{2,1,0:T(8,128)(2,1)} async-done(((bf16[1,256,5632]{2,1,0:T(8,128)(2,1)}), bf16[1,2048,5632]{2,1,0:T(8,128)(2,1)}) %all-gather.46.cloned.1.call-update) | async-done | bytes 23068688 | tf_op jit(solution)/shard_map/all_gather | solution.py:508
  1231.0 442.5 %all-gather.48.cloned.1.call-done = bf16[1,2048,5632]{2,1,0:T(8,128)(2,1)} async-done(((bf16[1,256,5632]{2,1,0:T(8,128)(2,1)}), bf16[1,2048,5632]{2,1,0:T(8,128)(2,1)}) %all-gather.48.cloned.1.call-update) | async-done | bytes 23068688 | tf_op jit(solution)/shard_map/all_gather | solution.py:509
  1673.5 442.7 %all-gather.50.cloned.1.call-done = bf16[1,5632,2048]{2,1,0:T(8,128)(2,1)} async-done(((bf16[1,704,2048]{2,1,0:T(8,128)(2,1)}), bf16[1,5632,2048]{2,1,0:T(8,128)(2,1)}) %all-gather.50.cloned.1.call-update) | async-done | bytes 23068688 | tf_op jit(solution)/shard_map/all_gather | solution.py:510
  2116.2 8.2 conditional.9
  2128.7 8.5 conditional.10
  2137.3 54.6 %collective-permute-start.1 = (bf16[2,64,2048]{2,1,0:T(8,128)(2,1)S(1)}, bf16[2,64,2048]{2,1,0:T(8,128)(2,1)S(1)}, u32[]{:S(2)}, u32[]{:S(2)}) collective-permute-start(bf16[2,64,2048]{2,1,0:T(8,128)(2,1)S(1)} %broadcast_select_fusion.5), channel_id=1, source_target_pairs={{0,8},{8,16},{16,24},{1,9},{9,17},{17,25},{2,10},{10,18},{18,26},{... | collective-permute-start | bytes 1572872 | tf_op jit(solution)/shard_map/ppermute | solution.py:20
  2193.4 10.5 conditional.11
  2204.0 7.6 collective-permute-start.2
  2215.6 84.1 %all-reduce.13.cloned.1.call-done = bf16[128,2048]{1,0:T(8,128)(2,1)} async-done(((bf16[128,2048]{1,0:T(8,128)(2,1)}), bf16[128,2048]{1,0:T(8,128)(2,1)}) %all-reduce.13.cloned.1.call-update) | async-done | bytes 524304 | tf_op jit(solution)/shard_map/psum | solution.py:25
  2299.8 20.7 all_gather.113
  2321.8 5.7 conditional.13
  2328.3 46.9 %all-gather.34.cloned.1.call-done = bf16[1024,2048]{1,0:T(8,128)(2,1)} async-done(((bf16[128,2048]{1,0:T(8,128)(2,1)}), bf16[1024,2048]{1,0:T(8,128)(2,1)}) %all-gather.34.cloned.1.call-update) | async-done | bytes 4194320 | tf_op jit(solution)/shard_map/all_gather | solution.py:557
  2378.9 65.7 %all-gather.9 = bf16[32768]{0:T(1024)(128)(2,1)S(1)} all-gather(bf16[1024]{0:T(1024)(128)(2,1)S(1)} %convert_element_type.719), channel_id=11, replica_groups=mesh['section'=4,'wide'=8] {'section','wide'}, dimensions={0}, use_global_device_ids=true | all-gather | bytes 67584 | tf_op jit(solution)/shard_map/all_gather | solution.py:30
  2444.8 63.9 %all-gather.10 = bf16[32768]{0:T(1024)(128)(2,1)S(1)} all-gather(bf16[1024]{0:T(1024)(128)(2,1)S(1)} %get-tuple-element.569), channel_id=12, replica_groups=mesh['section'=4,'wide'=8] {'section','wide'}, dimensions={0}, use_global_device_ids=true | all-gather | bytes 67584 | tf_op jit(solution)/shard_map/all_gather | solution.py:30
  2508.7 65.7 %all-gather.11 = bf16[32768]{0:T(1024)(128)(2,1)S(1)} all-gather(bf16[1024]{0:T(1024)(128)(2,1)S(1)} %get-tuple-element.568), channel_id=13, replica_groups=mesh['section'=4,'wide'=8] {'section','wide'}, dimensions={0}, use_global_device_ids=true | all-gather | bytes 67584 | tf_op jit(solution)/shard_map/all_gather | solution.py:30
  2587.8 10.0 conditional.14
  2600.2 7.7 collective-permute-done.4
  2607.9 9.4 conditional.15
  2619.7 272.7 %collective-permute-done.5 = bf16[2,64,2048]{2,1,0:T(8,128)(2,1)S(1)} collective-permute-done((bf16[2,64,2048]{2,1,0:T(8,128)(2,1)S(1)}, bf16[2,64,2048]{2,1,0:T(8,128)(2,1)S(1)}, u32[]{:S(2)}, u32[]{:S(2)}) %collective-permute-start.5) | collective-permute-done | bytes 524320 | tf_op jit(solution)/shard_map/ppermute | solution.py:20
  2893.4 40.6 %all-reduce.15.cloned.1.call-done = bf16[128,2048]{1,0:T(8,128)(2,1)} async-done(((bf16[128,2048]{1,0:T(8,128)(2,1)}), bf16[128,2048]{1,0:T(8,128)(2,1)}) %all-reduce.15.cloned.1.call-update) | async-done | bytes 524304 | tf_op jit(solution)/shard_map/psum | solution.py:25
  2934.0 20.6 all_gather.115
  2954.7 54.6 %all-gather.36.cloned.1.call-done = bf16[1024,2048]{1,0:T(8,128)(2,1)} async-done(((bf16[128,2048]{1,0:T(8,128)(2,1)}), bf16[1024,2048]{1,0:T(8,128)(2,1)}) %all-gather.36.cloned.1.call-update) | async-done | bytes 4194320 | tf_op jit(solution)/shard_map/all_gather | solution.py:636
  3047.4 5.0 fusion.395
  3067.0 38.8 all-reduce.8
  3108.2 59.5 %reduce-scatter.8.cloned.1.call-done = f32[16,512]{1,0:T(8,128)} async-done(((f32[512,512]{1,0:T(8,128)}), f32[16,512]{1,0:T(8,128)}) %reduce-scatter.8.cloned.1.call-update) | async-done | bytes 32784 | tf_op jit(solution)/shard_map/reduce_scatter | solution.py:659
  3167.7 134.2 %reduce-scatter.10.cloned.1.call-done = f32[16,512]{1,0:T(8,128)} async-done(((f32[512,512]{1,0:T(8,128)}), f32[16,512]{1,0:T(8,128)}) %reduce-scatter.10.cloned.1.call-update) | async-done | bytes 32784 | tf_op jit(solution)/shard_map/reduce_scatter | solution.py:660
  3301.8 133.9 %reduce-scatter.12.cloned.1.call-done = f32[16,512]{1,0:T(8,128)} async-done(((f32[512,512]{1,0:T(8,128)}), f32[16,512]{1,0:T(8,128)}) %reduce-scatter.12.cloned.1.call-update) | async-done | bytes 32784 | tf_op jit(solution)/shard_map/reduce_scatter | solution.py:661
  3435.7 134.3 %reduce-scatter.14.cloned.1.call-done = f32[16,512]{1,0:T(8,128)} async-done(((f32[512,512]{1,0:T(8,128)}), f32[16,512]{1,0:T(8,128)}) %reduce-scatter.14.cloned.1.call-update) | async-done | bytes 32784 | tf_op jit(solution)/shard_map/reduce_scatter | solution.py:662
  3570.0 142.3 %reduce-scatter.16.cloned.1.call-done = f32[16,2048]{1,0:T(8,128)} async-done(((f32[512,2048]{1,0:T(8,128)}), f32[16,2048]{1,0:T(8,128)}) %reduce-scatter.16.cloned.1.call-update) | async-done | bytes 131088 | tf_op jit(solution)/shard_map/reduce_scatter | solution.py:665
  3712.4 143.9 %reduce-scatter.18.cloned.1.call-done = f32[64,512]{1,0:T(8,128)} async-done(((f32[2048,512]{1,0:T(8,128)}), f32[64,512]{1,0:T(8,128)}) %reduce-scatter.18.cloned.1.call-update) | async-done | bytes 131088 | tf_op jit(solution)/shard_map/reduce_scatter | solution.py:666
  3856.3 144.2 %reduce-scatter.20.cloned.1.call-done = f32[16,2048]{1,0:T(8,128)} async-done(((f32[512,2048]{1,0:T(8,128)}), f32[16,2048]{1,0:T(8,128)}) %reduce-scatter.20.cloned.1.call-update) | async-done | bytes 131088 | tf_op jit(solution)/shard_map/reduce_scatter | solution.py:667
  (488 shorter events, 148.3 us)
Async XLA Ops:
  7.2 375.2 %copy-start = (bf16[2,256,2048]{2,1,0:T(8,128)(2,1)S(1)}, bf16[2,256,2048]{2,1,0:T(8,128)(2,1)}, u32[]{:S(2)}) copy-start(bf16[2,256,2048]{2,1,0:T(8,128)(2,1)} %param.63) | copy-start | bytes 6291460
  7.2 353.7 %all-gather.26.cloned.1.call-start = ((), (), s32[]{:S(2)}) async-start(), calls=%async_computation.7 | async-start | bytes 2162688 | tf_op jit(solution)/shard_map/all_gather | solution.py:464
  8.9 365.1 %all-gather.28.cloned.1.call-start = ((), (), s32[]{:S(2)}) async-start(), calls=%async_computation.8 | async-start | bytes 2162688 | tf_op jit(solution)/shard_map/all_gather | solution.py:465
  10.6 367.3 %all-gather.30.cloned.1.call-start = ((), (), s32[]{:S(2)}) async-start(), calls=%async_computation.9 | async-start | bytes 2162688 | tf_op jit(solution)/shard_map/all_gather | solution.py:466
  12.2 444.2 %all-gather.32.cloned.1.call-start = ((), (), s32[]{:S(2)}) async-start(), calls=%async_computation.10 | async-start | bytes 8650752 | tf_op jit(solution)/shard_map/all_gather | solution.py:512
  59.5 298.5 %copy-start.115 = (pred[512]{0:T(512)(128)(4,1)}, pred[512]{0:T(512)(128)(4,1)S(1)}, u32[]{:S(2)}) copy-start(pred[512]{0:T(512)(128)(4,1)S(1)} %compare_and_fusion) | copy-start | bytes 1540
  64.3 74.9 %copy-start.14 = (bf16[512,512]{1,0:T(8,128)(2,1)}, bf16[512,512]{1,0:T(8,128)(2,1)S(1)}, u32[]{:S(2)}) copy-start(bf16[512,512]{1,0:T(8,128)(2,1)S(1)} %gather_fusion) | copy-start | bytes 1572868
  135.5 142.6 %copy-start.6 = (bf16[512,512]{1,0:T(8,128)(2,1)}, bf16[512,512]{1,0:T(8,128)(2,1)S(1)}, u32[]{:S(2)}) copy-start(bf16[512,512]{1,0:T(8,128)(2,1)S(1)} %fusion.334) | copy-start | bytes 1572868
  380.7 117.0 %all-gather.38.cloned.1.call-start = ((), (), s32[]{:S(2)}) async-start(), calls=%async_computation.22 | async-start | bytes 1179648 | tf_op jit(solution)/shard_map/all_gather | solution.py:505
  381.5 157.0 %all-gather.40.cloned.1.call-start = ((), (), s32[]{:S(2)}) async-start(), calls=%async_computation.23 | async-start | bytes 1179648 | tf_op jit(solution)/shard_map/all_gather | solution.py:504
  382.3 282.5 %all-gather.42.cloned.1.call-start = ((), (), s32[]{:S(2)}) async-start(), calls=%async_computation.24 | async-start | bytes 9437184 | tf_op jit(solution)/shard_map/all_gather | solution.py:503
  383.8 406.3 %all-gather.44.cloned.1.call-start = ((), (), s32[]{:S(2)}) async-start(), calls=%async_computation.25 | async-start | bytes 9437184 | tf_op jit(solution)/shard_map/all_gather | solution.py:506
  385.6 845.4 %all-gather.46.cloned.1.call-start = ((), (), s32[]{:S(2)}) async-start(), calls=%async_computation.26 | async-start | bytes 25952256 | tf_op jit(solution)/shard_map/all_gather | solution.py:508
  389.3 1284.2 %all-gather.48.cloned.1.call-start = ((), (), s32[]{:S(2)}) async-start(), calls=%async_computation.27 | async-start | bytes 25952256 | tf_op jit(solution)/shard_map/all_gather | solution.py:509
  393.0 1723.2 %all-gather.50.cloned.1.call-start = ((), (), s32[]{:S(2)}) async-start(), calls=%async_computation.28 | async-start | bytes 25952256 | tf_op jit(solution)/shard_map/all_gather | solution.py:510
  396.9 1902.8 %all-reduce.13.cloned.1.call-start = ((), (), s32[]{:S(2)}) async-start(), calls=%async_computation.11 | async-start | bytes 1048576 | tf_op jit(solution)/shard_map/psum | solution.py:25
  461.1 1655.0 %copy-start.66 = (bf16[2,64,2048]{2,1,0:T(8,128)(2,1)}, bf16[2,64,2048]{2,1,0:T(8,128)(2,1)S(1)}, u32[]{:S(2)}) copy-start(bf16[2,64,2048]{2,1,0:T(8,128)(2,1)S(1)} %get-tuple-element.788) | copy-start | bytes 1572868
  2125.5 3.3 collective-permute-start
  2137.3 56.1 %collective-permute-start.1 = (bf16[2,64,2048]{2,1,0:T(8,128)(2,1)S(1)}, bf16[2,64,2048]{2,1,0:T(8,128)(2,1)S(1)}, u32[]{:S(2)}, u32[]{:S(2)}) collective-permute-start(bf16[2,64,2048]{2,1,0:T(8,128)(2,1)S(1)} %broadcast_select_fusion.5), channel_id=1, source_target_pairs={{0,8},{8,16},{16,24},{1,9},{9,17},{17,25},{2,10},{10,18},{18,26},{... | collective-permute-start | bytes 1572872 | tf_op jit(solution)/shard_map/ppermute | solution.py:20
  2203.9 95.9 %copy-start.134 = (s32[1,2,64]{2,1,0:T(2,128)S(1)}, s32[1,2,64]{2,1,0:T(2,128)}, u32[]{:S(2)}) copy-start(s32[1,2,64]{2,1,0:T(2,128)} %param.46) | copy-start | bytes 1540
  2204.0 9.1 collective-permute-start.2
  2214.2 107.6 %copy-start.38 = (bf16[2,64,2048]{2,1,0:T(8,128)(2,1)}, bf16[2,64,2048]{2,1,0:T(8,128)(2,1)S(1)}, u32[]{:S(2)}) copy-start(bf16[2,64,2048]{2,1,0:T(8,128)(2,1)S(1)} %get-tuple-element.599) | copy-start | bytes 1572868
  2214.2 107.5 %copy-start.17 = (bf16[2,64,2048]{2,1,0:T(8,128)(2,1)S(1)}, bf16[2,64,2048]{2,1,0:T(8,128)(2,1)}, u32[]{:S(2)}) copy-start(bf16[2,64,2048]{2,1,0:T(8,128)(2,1)} %copy-done.16) | copy-start | bytes 1572868
  2214.2 107.6 %copy-start.2 = (bf16[1,2048,256]{2,1,0:T(8,128)(2,1)S(1)}, bf16[1,2048,256]{2,1,0:T(8,128)(2,1)}, u32[]{:S(2)}) copy-start(bf16[1,2048,256]{2,1,0:T(8,128)(2,1)} %all-gather.38.cloned.1.call-done) | copy-start | bytes 3145732
  2214.3 85.5 %copy-start.128 = (f32[128]{0:T(128)}, f32[128]{0:T(128)S(1)}, u32[]{:S(2)}) copy-start(f32[128]{0:T(128)S(1)} %rsqrt.142) | copy-start | bytes 1540
  2215.5 159.7 %all-gather.34.cloned.1.call-start = ((), (), s32[]{:S(2)}) async-start(), calls=%async_computation.12 | async-start | bytes 4718592 | tf_op jit(solution)/shard_map/all_gather | solution.py:557
  2299.7 634.2 %all-reduce.15.cloned.1.call-start = ((), (), s32[]{:S(2)}) async-start(), calls=%async_computation.13 | async-start | bytes 1048576 | tf_op jit(solution)/shard_map/psum | solution.py:25
  2328.3 116.3 %copy-start.101 = (s32[1024]{0:T(1024)S(1)}, s32[1024]{0:T(1024)}, u32[]{:S(2)}) copy-start(s32[1024]{0:T(1024)} %eq.71) | copy-start | bytes 12292
  2328.3 116.3 %copy-start.121 = (s32[64]{0:T(128)S(1)}, s32[64]{0:T(128)}, u32[]{:S(2)}) copy-start(s32[64]{0:T(128)} %iota_add_fusion) | copy-start | bytes 772
  2328.3 250.3 %copy-start.64 = (bf16[128,2048]{1,0:T(8,128)(2,1)S(1)}, bf16[128,2048]{1,0:T(8,128)(2,1)}, u32[]{:S(2)}) copy-start(bf16[128,2048]{1,0:T(8,128)(2,1)} %get-tuple-element.597) | copy-start | bytes 1572868
  2328.3 250.3 %copy-start.135 = (s32[1,2,64]{2,1,0:T(2,128)S(1)}, s32[1,2,64]{2,1,0:T(2,128)}, u32[]{:S(2)}) copy-start(s32[1,2,64]{2,1,0:T(2,128)} %param.46) | copy-start | bytes 1540
  2378.9 199.7 %copy-start.60 = (f32[1024,64]{0,1:T(8,128)}, f32[1024,64]{0,1:T(8,128)S(1)}, u32[]{:S(2)}) copy-start(f32[1024,64]{0,1:T(8,128)S(1)} %get-tuple-element.701) | copy-start | bytes 786436
  2583.8 4.0 collective-permute-start.3
  2598.9 9.0 collective-permute-start.4
  2617.2 316.8 %copy-start.137 = (s32[1,2,64]{2,1,0:T(2,128)S(1)}, s32[1,2,64]{2,1,0:T(2,128)}, u32[]{:S(2)}) copy-start(s32[1,2,64]{2,1,0:T(2,128)} %param.45) | copy-start | bytes 1540
  2617.3 392.1 %copy-start.122 = (s32[64]{0:T(128)S(1)}, s32[64]{0:T(128)}, u32[]{:S(2)}) copy-start(s32[64]{0:T(128)} %iota_add_fusion) | copy-start | bytes 772
  2618.4 274.0 %collective-permute-start.5 = (bf16[2,64,2048]{2,1,0:T(8,128)(2,1)S(1)}, bf16[2,64,2048]{2,1,0:T(8,128)(2,1)S(1)}, u32[]{:S(2)}, u32[]{:S(2)}) collective-permute-start(bf16[2,64,2048]{2,1,0:T(8,128)(2,1)S(1)} %broadcast_select_fusion.1), channel_id=1, source_target_pairs={{8,0},{16,8},{24,16},{9,1},{17,9},{25,17},{10,2},{18,10},{26,18},{... | collective-permute-start | bytes 1572872 | tf_op jit(solution)/shard_map/ppermute | solution.py:20
  2893.3 119.3 %copy-start.61 = (f32[1024,64]{0,1:T(8,128)S(1)}, f32[1024,64]{0,1:T(8,128)}, u32[]{:S(2)}) copy-start(f32[1024,64]{0,1:T(8,128)} %copy-done.60) | copy-start | bytes 786436
  2893.3 119.3 %copy-start.102 = (s32[1024]{0:T(1024)S(1)}, s32[1024]{0:T(1024)}, u32[]{:S(2)}) copy-start(s32[1024]{0:T(1024)} %eq.71) | copy-start | bytes 12292
  2893.3 116.0 %all-gather.36.cloned.1.call-start = ((), (), s32[]{:S(2)}) async-start(), calls=%async_computation.14 | async-start | bytes 4718592 | tf_op jit(solution)/shard_map/all_gather | solution.py:636
  2934.0 233.7 %reduce-scatter.8.cloned.1.call-start = ((), (), s32[]{:S(2)}) async-start(), calls=%async_computation.15 | async-start | bytes 1081344 | tf_op jit(solution)/shard_map/reduce_scatter | solution.py:659
  3034.2 267.7 %reduce-scatter.10.cloned.1.call-start = ((), (), s32[]{:S(2)}) async-start(), calls=%async_computation.16 | async-start | bytes 1081344 | tf_op jit(solution)/shard_map/reduce_scatter | solution.py:660
  3038.5 397.2 %reduce-scatter.12.cloned.1.call-start = ((), (), s32[]{:S(2)}) async-start(), calls=%async_computation.17 | async-start | bytes 1081344 | tf_op jit(solution)/shard_map/reduce_scatter | solution.py:661
  3045.8 524.2 %reduce-scatter.14.cloned.1.call-start = ((), (), s32[]{:S(2)}) async-start(), calls=%async_computation.18 | async-start | bytes 1081344 | tf_op jit(solution)/shard_map/reduce_scatter | solution.py:662
  3047.3 665.0 %reduce-scatter.16.cloned.1.call-start = ((), (), s32[]{:S(2)}) async-start(), calls=%async_computation.19 | async-start | bytes 4325376 | tf_op jit(solution)/shard_map/reduce_scatter | solution.py:665
  3052.4 803.8 %reduce-scatter.18.cloned.1.call-start = ((), (), s32[]{:S(2)}) async-start(), calls=%async_computation.20 | async-start | bytes 4325376 | tf_op jit(solution)/shard_map/reduce_scatter | solution.py:666
  3057.3 943.1 %reduce-scatter.20.cloned.1.call-start = ((), (), s32[]{:S(2)}) async-start(), calls=%async_computation.21 | async-start | bytes 4325376 | tf_op jit(solution)/shard_map/reduce_scatter | solution.py:667
  3061.8 938.7 %copy-start.1 = (bf16[2,256,2048]{2,1,0:T(8,128)(2,1)S(1)}, bf16[2,256,2048]{2,1,0:T(8,128)(2,1)}, u32[]{:S(2)}) copy-start(bf16[2,256,2048]{2,1,0:T(8,128)(2,1)} %param.63) | copy-start | bytes 6291460
  (65 other events, 685.3 us)
Sparse Core Ops, SparseCore 0:
  11.6 59.2 all-gather.25
  74.5 57.3 all-gather.27
  135.4 56.3 all-gather.29
  380.8 75.5 all-gather.31
  458.9 38.7 all-gather.37
  500.2 38.2 all-gather.39
  540.5 124.2 all-gather.41
  667.0 123.1 all-gather.43
  791.7 439.2 all-gather.45
  1232.4 441.0 all-gather.47
  1675.0 441.0 all-gather.49
  2215.7 84.0 all-reduce.12
  2301.8 73.3 all-gather.33
  2893.4 40.4 all-reduce.14
  2935.9 73.3 all-gather.35
  3034.3 133.3 reduce-scatter.7
  3170.4 131.3 reduce-scatter.9
  3304.5 131.1 reduce-scatter.11
  3438.6 131.3 reduce-scatter.13
  3572.7 139.5 reduce-scatter.15
  3715.2 141.0 reduce-scatter.17
  3859.1 141.3 reduce-scatter.19
where the time goes:
time: 4020 us; the launch traced here: 4010 us
  waiting for transfers between devices  3090 us (77%)
  blocking collectives  625 us (16%)
  matrix products  82.6 us (2%)
  starting transfers between devices  68.9 us (2%)
  local copies, waits for them, and re-layouts  54.9 us (1%)
  loops' own time  49.4 us (1%)
    all_gather x1, waiting for transfers between devices, shards(): lax.all_gather(select(down_weight), 'wide', axis=0, tiled=True)  443 us
    all_gather x1, waiting for transfers between devices, shards(): lax.all_gather(select(up_weight), 'wide', axis=0, tiled=True)  442 us
    all_gather x1, waiting for transfers between devices, shards(): lax.all_gather(select(gate_weight), 'wide', axis=0, tiled=True)  441 us
    ppermute x6, waiting for transfers between devices, passed_along(): lax.ppermute(value, axis, [(source, source + steps) for source in range(l...  287 us
    all_gather x3, blocking collectives, combined_all(): lax.all_gather(part.astype(kind), axis)  195 us
    reduce_scatter x1, waiting for transfers between devices, shards(): lax.psum_scatter(grad_embed, ('section', 'wide'), scatter_dimension=0, ti...  144 us
    reduce_scatter x1, waiting for transfers between devices, shards(): lax.psum_scatter(grad_reduce, ('section', 'wide'), scatter_dimension=0, t...  144 us
    reduce_scatter x1, waiting for transfers between devices, shards(): lax.psum_scatter(grad_expand, ('section', 'wide'), scatter_dimension=0, t...  142 us
  transfers between devices with their start and end apart: 28, of which 25 were waited for; matrix products, arithmetic and copies ran while one was open for 3% of the time, Pallas kernels for 0%

commit v1 on v0

v1 whole, which is shorter than its diff:
```python
import functools

import jax
import jax.numpy as jnp
from jax import lax
from jax.experimental import pallas as pl
from jax.experimental.pallas import tpu as pltpu
from jax.sharding import PartitionSpec as P

HEAD_DIM = 64
HYPER_HEAD_COUNT = 8
MB = 2
LEN = 64
TEAM = 8
SECTIONS = 4
ROWS = MB * LEN * TEAM // SECTIONS
OWN = ROWS // TEAM
LANES = 128
MESH_IDS = pl.DeviceIdType.MESH
ANYWHERE = pl.BlockSpec(memory_space=pl.ANY)
IN_VMEM = pl.BlockSpec(memory_space=pltpu.VMEM)
VMEM_LIMIT = 56 * 1024 * 1024

norm_eps = 1e-05
inv_root_two = 0.7071067811865476
inv_root_tau = 0.3989422804014327


def matmul(former, latter):
    return jnp.dot(former, latter, preferred_element_type=jnp.float32)


def times_trans(former, latter):
    return lax.dot_general(
        former, latter, (((1,), (1,)), ((), ())), preferred_element_type=jnp.float32
    )


def trans_times(former, latter):
    return lax.dot_general(
        former, latter, (((0,), (0,)), ((), ())), preferred_element_type=jnp.float32
    )


def center_norm(values):
    center = values - jnp.mean(values, axis=-1, keepdims=True)
    inverse = lax.rsqrt(jnp.mean(center * center, axis=-1, keepdims=True) + norm_eps)
    return (center * inverse, inverse)


def center_back(normed, inverse, normed_grad):
    mean_grad = jnp.mean(normed_grad, axis=-1, keepdims=True)
    mean_mix = jnp.mean(normed_grad * normed, axis=-1, keepdims=True)
    return inverse * (normed_grad - mean_grad - normed * mean_mix)


def root_inverse(values):
    return lax.rsqrt(jnp.mean(values * values, axis=-1, keepdims=True) + norm_eps)


def reciprocal_root_backward(values, inverse, gain_vec, outer_grad):
    scaled = outer_grad * gain_vec
    mixing = jnp.mean(scaled * values, axis=-1, keepdims=True)
    return inverse * scaled - values * inverse * inverse * inverse * mixing


def rope_tables(positions, head_width):
    halfway = head_width // 2
    frequency = jnp.exp(
        -jnp.log(10000.0) * (2.0 * jnp.arange(halfway, dtype=jnp.float32) / head_width)
    )
    angles = jnp.arange(positions, dtype=jnp.float32)[:, None] * frequency[None, :]
    angles = jnp.concatenate([angles, angles], axis=1)
    return (jnp.cos(angles), jnp.sin(angles))


def apply_rotary(values, cosines, sines):
    halfway = values.shape[-1] // 2
    turned = jnp.concatenate([-values[..., halfway:], values[..., :halfway]], axis=-1)
    return values * cosines[None, :, None, :] + turned * sines[None, :, None, :]


def invert_rotary(gradient, cosines, sines):
    halfway = gradient.shape[-1] // 2
    scaled = gradient * sines[None, :, None, :]
    turned = jnp.concatenate([scaled[..., halfway:], -scaled[..., :halfway]], axis=-1)
    return gradient * cosines[None, :, None, :] + turned


def hyper_forward(pieces, params, head_count):
    (
        gain_one,
        bias_one,
        query_mat,
        key_mat,
        value_mat,
        out_mat,
        second_gain,
        bias_two,
        expand_mat,
        reduce_mat,
        embed_mat,
    ) = params
    entries, slot_count, model_width = pieces.shape
    head_width = model_width // head_count
    score_scale = head_width ** (-0.5)
    flat_in = pieces.reshape(entries * slot_count, model_width)
    normed_one, inverse_one = center_norm(flat_in)
    attn_in = (normed_one * gain_one.astype(jnp.float32) + bias_one.astype(jnp.float32)).astype(
        jnp.bfloat16
    )
    queries = (
        matmul(attn_in, query_mat)
        .astype(jnp.bfloat16)
        .reshape(entries, slot_count, head_count, head_width)
    )
    key_rows = (
        matmul(attn_in, key_mat)
        .astype(jnp.bfloat16)
        .reshape(entries, slot_count, head_count, head_width)
    )
    value_rows = (
        matmul(attn_in, value_mat)
        .astype(jnp.bfloat16)
        .reshape(entries, slot_count, head_count, head_width)
    )
    scores = (
        jnp.einsum("eshd,ethd->ehst", queries, key_rows, preferred_element_type=jnp.float32)
        * score_scale
    )
    weights_full = jax.nn.softmax(scores, axis=-1)
    weights_low = weights_full.astype(jnp.bfloat16)
    mixed = jnp.einsum(
        "ehst,ethd->eshd", weights_low, value_rows, preferred_element_type=jnp.float32
    )
    mixed = mixed.astype(jnp.bfloat16).reshape(entries * slot_count, model_width)
    middle = flat_in + matmul(mixed, out_mat)
    normed_two, inverse_two = center_norm(middle)
    ffn_in = (normed_two * second_gain.astype(jnp.float32) + bias_two.astype(jnp.float32)).astype(
        jnp.bfloat16
    )
    expanded = matmul(ffn_in, expand_mat)
    activated = jax.nn.gelu(expanded, approximate=False).astype(jnp.bfloat16)
    outcome = middle + matmul(activated, reduce_mat)
    pooled = jnp.mean(outcome.reshape(entries, slot_count, model_width), axis=1).astype(
        jnp.bfloat16
    )
    table_rows = matmul(pooled, embed_mat).astype(jnp.bfloat16)
    stored = (
        normed_one,
        inverse_one,
        attn_in,
        queries,
        key_rows,
        value_rows,
        weights_full,
        weights_low,
        mixed,
        normed_two,
        inverse_two,
        ffn_in,
        expanded,
        activated,
        pooled,
    )
    return (table_rows, stored)


def hyper_backward(params, stored, table_grad):
    (
        gain_one,
        bias_one,
        query_mat,
        key_mat,
        value_mat,
        out_mat,
        second_gain,
        bias_two,
        expand_mat,
        reduce_mat,
        embed_mat,
    ) = params
    (
        normed_one,
        inverse_one,
        attn_in,
        queries,
        key_rows,
        value_rows,
        weights_full,
        weights_low,
        mixed,
        normed_two,
        inverse_two,
        ffn_in,
        expanded,
        activated,
        pooled,
    ) = stored
    entries, slot_count, head_total, head_width = queries.shape
    model_width = head_total * head_width
    score_scale = head_width ** (-0.5)
    grad_low = table_grad.astype(jnp.bfloat16)
    grad_embed = trans_times(pooled, grad_low)
    pooled_grad = times_trans(grad_low, embed_mat) / slot_count
    outcome_grad = jnp.broadcast_to(pooled_grad[:, None, :], (entries, slot_count, model_width))
    outcome_grad = outcome_grad.reshape(entries * slot_count, model_width)
    outcome_low = outcome_grad.astype(jnp.bfloat16)
    grad_reduce = trans_times(activated, outcome_low)
    act_grad = times_trans(outcome_low, reduce_mat)
    slope = (
        0.5 * (1.0 + lax.erf(expanded * inv_root_two))
        + expanded * jnp.exp(-0.5 * expanded * expanded) * inv_root_tau
    )
    expanded_low = (act_grad * slope).astype(jnp.bfloat16)
    grad_expand = trans_times(ffn_in, expanded_low)
    ffn_grad = times_trans(expanded_low, expand_mat)
    grad_midscale = jnp.sum(ffn_grad * normed_two, axis=0)
    grad_midshift = jnp.sum(ffn_grad, axis=0)
    middle_grad = outcome_grad + center_back(
        normed_two, inverse_two, ffn_grad * second_gain.astype(jnp.float32)
    )
    middle_low = middle_grad.astype(jnp.bfloat16)
    grad_output = trans_times(mixed, middle_low)
    mixed_grad = times_trans(middle_low, out_mat).astype(jnp.bfloat16).reshape(queries.shape)
    weight_grad = jnp.einsum(
        "eshd,ethd->ehst", mixed_grad, value_rows, preferred_element_type=jnp.float32
    )
    value_grad = jnp.einsum(
        "ehst,eshd->ethd", weights_low, mixed_grad, preferred_element_type=jnp.float32
    )
    score_grad = weights_full * (
        weight_grad - jnp.sum(weights_full * weight_grad, axis=-1, keepdims=True)
    )
    score_grad = score_grad.astype(jnp.bfloat16)
    query_grad = (
        jnp.einsum("ehst,ethd->eshd", score_grad, key_rows, preferred_element_type=jnp.float32)
        * score_scale
    )
    key_grad = (
        jnp.einsum("ehst,eshd->ethd", score_grad, queries, preferred_element_type=jnp.float32)
        * score_scale
    )
    query_low = query_grad.astype(jnp.bfloat16).reshape(entries * slot_count, model_width)
    key_low = key_grad.astype(jnp.bfloat16).reshape(entries * slot_count, model_width)
    value_low = value_grad.astype(jnp.bfloat16).reshape(entries * slot_count, model_width)
    grad_query = trans_times(attn_in, query_low)
    grad_key = trans_times(attn_in, key_low)
    grad_value = trans_times(attn_in, value_low)
    attention_gradient = (
        times_trans(query_low, query_mat)
        + times_trans(key_low, key_mat)
        + times_trans(value_low, value_mat)
    )
    grad_prescale = jnp.sum(attention_gradient * normed_one, axis=0)
    prenorm_bias_gradient = jnp.sum(attention_gradient, axis=0)
    return (
        grad_prescale,
        prenorm_bias_gradient,
        grad_query,
        grad_key,
        grad_value,
        grad_output,
        grad_midscale,
        grad_midshift,
        grad_expand,
        grad_reduce,
        grad_embed,
    )


def greet(peers):
    barrier = pltpu.get_barrier_semaphore()
    for peer in peers:
        pl.semaphore_signal(barrier, inc=1, device_id=peer, device_id_type=MESH_IDS)
    pl.semaphore_wait(barrier, len(peers))


def remote(source, target, send, recv, peer):
    return pltpu.make_async_remote_copy(
        src_ref=source,
        dst_ref=target,
        send_sem=send,
        recv_sem=recv,
        device_id=peer,
        device_id_type=MESH_IDS,
    )


def settings(collective_id):
    return pltpu.CompilerParams(
        collective_id=collective_id, has_side_effects=True, vmem_limit_bytes=VMEM_LIMIT
    )


def dma_sems(*shape):
    return pltpu.SemaphoreType.DMA(shape)


def fold_kernel(finish, outer, n_in, n_out, *refs):
    partial, extras = refs[0], refs[1:n_in]
    gathered, outs = refs[n_in], refs[n_in + 1 : n_in + n_out]
    (
        own,
        side,
        pair,
        far,
        ready,
        load_sem,
        keep_sem,
        side_send,
        side_recv,
        far_send,
        far_recv,
        out_send,
        out_recv,
        over_send,
        over_recv,
    ) = refs[n_in + n_out :]
    wide = lax.axis_index("wide")
    rank, team = wide // outer, wide % outer
    line, column = rank // 2, rank % 2
    lines = TEAM // 2

    def at(some_line, some_column):
        return (some_line % lines) * 2 + some_column

    def member(some_line, some_column):
        return {"wide": at(some_line, some_column) * outer + team}

    beside = member(line, 1 - column)
    greet([beside] + [member(line + j, column) for j in range(1, lines)])
    order = (2, 1, 3, 0)
    loads = [
        pltpu.make_async_copy(partial.at[at(line + j, column)], own.at[j], load_sem.at[j])
        for j in range(lines)
    ]
    sides = [
        remote(
            partial.at[at(line + j, 1 - column)],
            side.at[j],
            side_send.at[j],
            side_recv.at[j],
            beside,
        )
        for j in range(lines)
    ]
    fars = [None] + [
        remote(pair.at[j], far.at[j], far_send.at[j], far_recv.at[j], member(line + j, column))
        for j in range(1, lines)
    ]
    for j in order:
        sides[j].start()
        loads[j].start()
    for j in order[:3]:
        loads[j].wait()
        sides[j].wait_recv()
        pair[j] = (own[j].astype(jnp.float32) + side[j].astype(jnp.float32)).astype(jnp.bfloat16)
        fars[j].start()
    loads[0].wait()
    sides[0].wait_recv()
    total = own[0].astype(jnp.float32) + side[0].astype(jnp.float32)
    for j in (1, 3, 2):
        fars[j].wait_recv()
        total = total + far[j].astype(jnp.float32)
    ready[...] = finish(total, extras, outs)
    mine = at(line, column)
    keep = pltpu.make_async_copy(ready, gathered.at[mine], keep_sem)
    pushes = [None] + [
        remote(ready, gathered.at[mine], out_send.at[j], out_recv.at[j], member(line + j, column))
        for j in range(1, lines)
    ]
    overs = [
        remote(
            ready if j == 0 else gathered.at[at(line - j, column)],
            gathered.at[at(line - j, column)],
            over_send.at[j],
            over_recv.at[j],
            beside,
        )
        for j in range(lines)
    ]
    for j in (2, 1, 3):
        pushes[j].start()
    overs[0].start()
    keep.start()
    for j in (1, 3, 2):
        pushes[j].wait_recv()
        overs[j].start()
    for j in range(lines):
        overs[j].wait()
        sides[j].wait_send()
        if j:
            fars[j].wait_send()
            pushes[j].wait_send()
    keep.wait()


def fold(finish, outer, collective_id, partial, extras, outs):
    width = partial.shape[-1]
    lines = TEAM // 2
    slots = pltpu.VMEM((lines, OWN, width), jnp.bfloat16)
    return pl.pallas_call(
        functools.partial(fold_kernel, finish, outer, 1 + len(extras), 1 + len(outs)),
        out_shape=(jax.ShapeDtypeStruct((TEAM, OWN, width), jnp.bfloat16),)
        + tuple(jax.ShapeDtypeStruct((OWN, width), kind) for kind in outs),
        in_specs=[ANYWHERE] + [IN_VMEM] * len(extras),
        out_specs=(ANYWHERE,) + (IN_VMEM,) * len(outs),
        scratch_shapes=[slots, slots, slots, slots, pltpu.VMEM((OWN, width), jnp.bfloat16)]
        + [dma_sems(lines), pltpu.SemaphoreType.DMA]
        + [dma_sems(lines)] * 8,
        compiler_params=settings(collective_id),
        name=finish.__name__,
    )(partial.reshape(TEAM, OWN, width), *extras)


def inject(total, extras, outs):
    (gain,) = extras
    hidden = total.astype(jnp.bfloat16)
    outs[0][...] = hidden
    wide = hidden.astype(jnp.float32)
    return (wide * root_inverse(wide) * gain[...]).astype(jnp.bfloat16)


def enter_feed(total, extras, outs):
    hidden, gain = extras
    middle = hidden[...].astype(jnp.float32) + total
    outs[0][...] = middle
    return (middle * root_inverse(middle) * gain[...]).astype(jnp.bfloat16)


def leave_layer(total, extras, outs):
    middle, gain = extras
    hidden = (middle[...] + total).astype(jnp.bfloat16)
    outs[0][...] = hidden
    wide = hidden.astype(jnp.float32)
    return (wide * root_inverse(wide) * gain[...]).astype(jnp.bfloat16)


def head_back(total, extras, outs):
    hidden, gain = extras
    wide = hidden[...].astype(jnp.float32)
    grad = reciprocal_root_backward(wide, root_inverse(wide), gain[...], total)
    grad = grad.astype(jnp.bfloat16)
    outs[0][...] = grad
    return grad


def feed_back(total, extras, outs):
    outer_grad, middle, gain = extras
    wide = middle[...]
    grad = outer_grad[...].astype(jnp.float32) + reciprocal_root_backward(
        wide, root_inverse(wide), gain[...], total
    )
    outs[0][...] = grad
    return grad.astype(jnp.bfloat16)


def layer_back(total, extras, outs):
    middle_grad, hidden, gain = extras
    wide = hidden[...].astype(jnp.float32)
    grad = middle_grad[...] + reciprocal_root_backward(wide, root_inverse(wide), gain[...], total)
    grad = grad.astype(jnp.bfloat16)
    outs[0][...] = grad
    return grad


def team_kernel(outer, block, gathered, send, recv):
    wide = lax.axis_index("wide")
    rank, team = wide // outer, wide % outer
    peers = [{"wide": ((rank + k) % TEAM) * outer + team} for k in range(1, TEAM)]
    greet(peers)
    copies = [
        remote(block, gathered.at[rank], send.at[k], recv.at[k], peer)
        for k, peer in enumerate(peers)
    ]
    for copy in copies:
        copy.start()
    gathered[rank] = block[...]
    for copy in copies:
        copy.wait()


def team_gather(outer, collective_id, block):
    return pl.pallas_call(
        functools.partial(team_kernel, outer),
        out_shape=jax.ShapeDtypeStruct((TEAM,) + block.shape, block.dtype),
        in_specs=[IN_VMEM],
        out_specs=IN_VMEM,
        scratch_shapes=[dma_sems(TEAM - 1), dma_sems(TEAM - 1)],
        compiler_params=settings(collective_id),
        name="team_gather",
    )(block)


def section_places():
    section = lax.axis_index("section")
    core = section % 2
    partner = section + 1 - 2 * core
    across = (section + 2) % SECTIONS
    return section, partner, across


def section_gather_kernel(block, gathered, keep_sem, send, recv):
    section, partner, across = section_places()
    greet([{"section": partner}, {"section": across}])
    keep = pltpu.make_async_copy(block, gathered.at[section], keep_sem)
    near = remote(block, gathered.at[section], send.at[0], recv.at[0], {"section": partner})
    far = remote(block, gathered.at[section], send.at[1], recv.at[1], {"section": across})
    on = remote(
        gathered.at[across], gathered.at[across], send.at[2], recv.at[2], {"section": partner}
    )
    far.start()
    near.start()
    keep.start()
    far.wait_recv()
    on.start()
    near.wait()
    on.wait()
    far.wait_send()
    keep.wait()


def section_gather(collective_id, block):
    return pl.pallas_call(
        section_gather_kernel,
        out_shape=jax.ShapeDtypeStruct((SECTIONS,) + block.shape, block.dtype),
        in_specs=[ANYWHERE],
        out_specs=ANYWHERE,
        scratch_shapes=[pltpu.SemaphoreType.DMA, dma_sems(3), dma_sems(3)],
        compiler_params=settings(collective_id),
        name="section_gather",
    )(block)


def section_sum_kernel(partial, loss, summed, loss_sum, own, near, pair, far, loss_near, loss_pair, loss_far, load_sem, send, recv):
    section, partner, across = section_places()
    beyond = (partner + 2) % SECTIONS
    greet([{"section": partner}, {"section": across}])
    loads = [
        pltpu.make_async_copy(partial.at[section], own.at[0], load_sem.at[0]),
        pltpu.make_async_copy(partial.at[across], own.at[1], load_sem.at[1]),
    ]
    nears = [
        remote(partial.at[partner], near.at[0], send.at[0], recv.at[0], {"section": partner}),
        remote(partial.at[beyond], near.at[1], send.at[1], recv.at[1], {"section": partner}),
        remote(loss, loss_near, send.at[2], recv.at[2], {"section": partner}),
    ]
    fars = [
        remote(pair, far, send.at[3], recv.at[3], {"section": across}),
        remote(loss_pair, loss_far, send.at[4], recv.at[4], {"section": across}),
    ]
    for j in (1, 2, 0):
        nears[j].start()
    loads[1].start()
    loads[0].start()
    loads[1].wait()
    nears[1].wait_recv()
    pair[...] = (own[1].astype(jnp.float32) + near[1].astype(jnp.float32)).astype(jnp.bfloat16)
    fars[0].start()
    nears[2].wait_recv()
    loss_pair[...] = loss[...] + loss_near[...]
    fars[1].start()
    loads[0].wait()
    nears[0].wait_recv()
    total = own[0].astype(jnp.float32) + near[0].astype(jnp.float32)
    fars[0].wait_recv()
    summed[...] = total + far[...].astype(jnp.float32)
    fars[1].wait_recv()
    loss_sum[...] = loss_pair[...] + loss_far[...]
    for copy in nears + fars:
        copy.wait_send()


def section_sum(collective_id, partial, loss):
    shape = partial.shape[1:]
    low, low_two = pltpu.VMEM(shape, jnp.bfloat16), pltpu.VMEM((2,) + shape, jnp.bfloat16)
    number = pltpu.VMEM(loss.shape, jnp.float32)
    return pl.pallas_call(
        section_sum_kernel,
        out_shape=(
            jax.ShapeDtypeStruct(shape, jnp.float32),
            jax.ShapeDtypeStruct(loss.shape, jnp.float32),
        ),
        in_specs=[ANYWHERE, IN_VMEM],
        out_specs=(IN_VMEM, IN_VMEM),
        scratch_shapes=[low_two, low_two, low, low, number, number, number]
        + [dma_sems(2), dma_sems(5), dma_sems(5)],
        compiler_params=settings(collective_id),
        name="section_sum",
    )(partial, loss)


def all_places(halves):
    section, partner, across = section_places()
    wide = lax.axis_index("wide")
    line, column = wide // 2, wide % 2

    def wide_at(j):
        return ((line + j) % halves) * 2 + column

    return section, partner, across, wide, wide_at


def steps_of(x_first, section, partner, across, wide):
    column_flip = wide + 1 - 2 * (wide % 2)
    x_step = ({"wide": column_flip}, False, True)
    y_step = ({"section": across}, True, False)
    return (x_step, y_step) if x_first else (y_step, x_step)


def owner_of(home, flips_y, flips_x, wide_block):
    section = (home + 2) % SECTIONS if flips_y else home
    return section, (wide_block + 1 - 2 * (wide_block % 2) if flips_x else wide_block)


def spread_kernel(count, halves, *refs):
    blocks, gathereds = refs[:count], refs[count : 2 * count]
    keep_sem, z_send, a_send, b_send, c_send, z_recv, a_recv, b_recv, c_recv = refs[2 * count :]
    section, partner, across, wide, wide_at = all_places(halves)
    beside = wide + 1 - 2 * (wide % 2)
    barrier = pltpu.get_barrier_semaphore()
    for peer in ({"section": partner}, {"section": across}, {"wide": beside}):
        pl.semaphore_signal(barrier, inc=1, device_id=peer, device_id_type=MESH_IDS)

    def hello(j, carry):
        peer = {"wide": wide_at(j)}
        pl.semaphore_signal(barrier, inc=1, device_id=peer, device_id_type=MESH_IDS)
        return carry

    lax.fori_loop(1, halves, hello, 0)
    pl.semaphore_wait(barrier, 3 + halves - 1)

    keeps = [
        pltpu.make_async_copy(blocks[n], gathereds[n].at[section, wide], keep_sem.at[n])
        for n in range(count)
    ]

    def z_copy(n, j):
        return remote(
            blocks[n],
            gathereds[n].at[section, wide],
            z_send.at[n, j],
            z_recv.at[n, j],
            {"wide": wide_at(j)},
        )

    def a_copy(n, j):
        (peer, _, _), _ = steps_of(n == 0, section, partner, across, wide)
        block = gathereds[n].at[section, wide_at(-j)]
        return remote(block, block, a_send.at[n, j], a_recv.at[n, j], peer)

    def b_copy(n, flip, j):
        (_, y_a, x_a), (peer, _, _) = steps_of(n == 0, section, partner, across, wide)
        place = owner_of(section, y_a and flip, x_a and flip, wide_at(-j))
        block = gathereds[n].at[place[0], place[1]]
        slot = j + (halves if flip else 0)
        return remote(block, block, b_send.at[n, slot], b_recv.at[n, slot], peer)

    def c_copy(n, which):
        home = (section + 2) % SECTIONS if which else section
        block = gathereds[n].at[home]
        return remote(
            block, block, c_send.at[n, which], c_recv.at[n, which], {"section": partner}
        )

    for keep in keeps:
        keep.start()

    def start_z(j, carry):
        for n in range(count):
            z_copy(n, j).start()
        return carry

    lax.fori_loop(1, halves, start_z, 0)
    for n in range(count):
        keeps[n].wait()
        a_copy(n, 0).start()
        b_copy(n, False, 0).start()

    def pass_z(j, carry):
        for n in range(count):
            z_copy(n, j).wait_recv()
            a_copy(n, j).start()
            b_copy(n, False, j).start()
        return carry

    lax.fori_loop(1, halves, pass_z, 0)

    def pass_a(j, carry):
        for n in range(count):
            a_copy(n, j).wait_recv()
            b_copy(n, True, j).start()
        return carry

    lax.fori_loop(0, halves, pass_a, 0)

    def settle_b(j, carry):
        for n in range(count):
            for flip in (False, True):
                b_copy(n, flip, j).wait_recv()
        return carry

    c_copy(0, 0).start()
    lax.fori_loop(0, halves, settle_b, 0)
    c_copy(0, 1).start()
    for n in range(1, count):
        c_copy(n, 0).start()
        c_copy(n, 1).start()
    for n in range(count):
        c_copy(n, 0).wait()
        c_copy(n, 1).wait()

    def drain(j, carry):
        for n in range(count):
            a_copy(n, j).wait_send()
            b_copy(n, False, j).wait_send()
            b_copy(n, True, j).wait_send()
        return carry

    lax.fori_loop(0, halves, drain, 0)

    def drain_z(j, carry):
        for n in range(count):
            z_copy(n, j).wait_send()
        return carry

    lax.fori_loop(1, halves, drain_z, 0)


def spread(collective_id, wides, blocks):
    count, halves = len(blocks), wides // 2
    return pl.pallas_call(
        functools.partial(spread_kernel, count, halves),
        out_shape=tuple(
            jax.ShapeDtypeStruct((SECTIONS, wides) + block.shape, block.dtype) for block in blocks
        ),
        in_specs=[ANYWHERE] * count,
        out_specs=(ANYWHERE,) * count,
        scratch_shapes=[dma_sems(count)]
        + [
            dma_sems(count, halves),
            dma_sems(count, halves),
            dma_sems(count, 2 * halves),
            dma_sems(count, 2),
        ]
        * 2,
        compiler_params=settings(collective_id),
        name="spread",
    )(*blocks)


def collect_kernel(count, halves, *refs):
    partials, sums = refs[:count], refs[count : 2 * count]
    keeps, c_in, b_in, a_in, z_in = (refs[(2 + k) * count : (3 + k) * count] for k in range(5))
    load_sem, c_send, b_send, a_send, z_send, c_recv, b_recv, a_recv, z_recv = refs[7 * count :]
    section, partner, across, wide, wide_at = all_places(halves)
    beside = wide + 1 - 2 * (wide % 2)
    barrier = pltpu.get_barrier_semaphore()
    for peer in ({"section": partner}, {"section": across}, {"wide": beside}):
        pl.semaphore_signal(barrier, inc=1, device_id=peer, device_id_type=MESH_IDS)

    def hello(j, carry):
        peer = {"wide": wide_at(j)}
        pl.semaphore_signal(barrier, inc=1, device_id=peer, device_id_type=MESH_IDS)
        return carry

    lax.fori_loop(1, halves, hello, 0)
    pl.semaphore_wait(barrier, 3 + halves - 1)

    def place(n, home, flip_b, flip_a, j):
        (_, y_a, x_a), (_, y_b, x_b) = steps_of(n == 0, section, partner, across, wide)
        flips_y = (y_a and flip_a) or (y_b and flip_b)
        flips_x = (x_a and flip_a) or (x_b and flip_b)
        return owner_of(home, flips_y, flips_x, wide_at(j))

    def load(n, fb, fa, j):
        owner = place(n, section, fb, fa, j)
        slot = (fb * 2 + fa) * halves + j
        return pltpu.make_async_copy(
            partials[n].at[owner[0], owner[1]], keeps[n].at[slot], load_sem.at[n, slot]
        )

    def c_copy(n, fb, fa, j):
        owner = place(n, partner, fb, fa, j)
        slot = (fb * 2 + fa) * halves + j
        return remote(
            partials[n].at[owner[0], owner[1]],
            c_in[n].at[slot],
            c_send.at[n, slot],
            c_recv.at[n, slot],
            {"section": partner},
        )

    def b_copy(n, fa, j):
        _, (peer, _, _) = steps_of(n == 0, section, partner, across, wide)
        slot = fa * halves + j
        return remote(
            keeps[n].at[2 * halves + slot],
            b_in[n].at[slot],
            b_send.at[n, slot],
            b_recv.at[n, slot],
            peer,
        )

    def a_copy(n, j):
        (peer, _, _), _ = steps_of(n == 0, section, partner, across, wide)
        return remote(
            keeps[n].at[halves + j], a_in[n].at[j], a_send.at[n, j], a_recv.at[n, j], peer
        )

    def z_copy(n, j):
        return remote(
            keeps[n].at[j],
            z_in[n].at[j],
            z_send.at[n, j],
            z_recv.at[n, j],
            {"wide": wide_at(j)},
        )

    def add(n, slot, more):
        keeps[n][slot] = (
            keeps[n][slot].astype(jnp.float32) + more.astype(jnp.float32)
        ).astype(jnp.bfloat16)

    groups = ((1, 1), (1, 0), (0, 1), (0, 0))
    for fb, fa in groups:

        def start_c(j, carry):
            for n in range(count):
                c_copy(n, fb, fa, j).start()
                load(n, fb, fa, j).start()
            return carry

        lax.fori_loop(0, halves, start_c, 0)

    for fb, fa in groups:

        def sum_c(j, carry):
            for n in range(count):
                slot = (fb * 2 + fa) * halves + j
                load(n, fb, fa, j).wait()
                c_copy(n, fb, fa, j).wait_recv()
                add(n, slot, c_in[n][slot])
                if fb:
                    b_copy(n, fa, j).start()
            return carry

        lax.fori_loop(0, halves, sum_c, 0)

    for fa in (1, 0):

        def sum_b(j, carry):
            for n in range(count):
                slot = fa * halves + j
                b_copy(n, fa, j).wait_recv()
                add(n, slot, b_in[n][slot])
                if fa:
                    a_copy(n, j).start()
            return carry

        lax.fori_loop(0, halves, sum_b, 0)

    def sum_a(j, carry):
        for n in range(count):
            a_copy(n, j).wait_recv()
            add(n, j, a_in[n][j])
            z_copy(n, j).start()
        return carry

    lax.fori_loop(1, halves, sum_a, 0)
    for n in range(count):
        a_copy(n, 0).wait_recv()
        sums[n][...] = keeps[n][0].astype(jnp.float32) + a_in[n][0].astype(jnp.float32)

    def sum_z(j, carry):
        for n in range(count):
            z_copy(n, j).wait_recv()
            sums[n][...] += z_in[n][j].astype(jnp.float32)
        return carry

    lax.fori_loop(1, halves, sum_z, 0)

    def drain(j, carry):
        for n in range(count):
            for fb, fa in groups:
                c_copy(n, fb, fa, j).wait_send()
            b_copy(n, 0, j).wait_send()
            b_copy(n, 1, j).wait_send()
            a_copy(n, j).wait_send()
        return carry

    lax.fori_loop(0, halves, drain, 0)

    def drain_z(j, carry):
        for n in range(count):
            z_copy(n, j).wait_send()
        return carry

    lax.fori_loop(1, halves, drain_z, 0)


def collect(collective_id, partials):
    count, halves = len(partials), partials[0].shape[1] // 2
    shapes = [partial.shape[2:] for partial in partials]

    def slots(number):
        return [pltpu.VMEM((number,) + shape, jnp.bfloat16) for shape in shapes]

    return pl.pallas_call(
        functools.partial(collect_kernel, count, halves),
        out_shape=tuple(jax.ShapeDtypeStruct(shape, jnp.float32) for shape in shapes),
        in_specs=[ANYWHERE] * count,
        out_specs=(IN_VMEM,) * count,
        scratch_shapes=slots(4 * halves)
        + slots(4 * halves)
        + slots(2 * halves)
        + slots(halves)
        + slots(halves)
        + [dma_sems(count, 4 * halves)]
        + [
            dma_sems(count, 4 * halves),
            dma_sems(count, 2 * halves),
            dma_sems(count, halves),
            dma_sems(count, halves),
        ]
        * 2,
        compiler_params=settings(collective_id),
        name="collect",
    )(*partials)


def column_starts(rank, feed_width):
    share = feed_width // TEAM
    return (rank * share) // LANES * LANES, (rank // 4) * LANES


def reshard_kernel(
    outer,
    span,
    query,
    key,
    value,
    gate,
    up,
    small,
    notes,
    heads_out,
    feed_out,
    small_out,
    notes_out,
    keep_sem,
    push_send,
    push_recv,
    y_send,
    y_recv,
    core_send,
    core_recv,
    small_send,
    small_recv,
    notes_send,
    notes_recv,
):
    section, partner, across = section_places()
    wide = lax.axis_index("wide")
    rank, team = wide // outer, wide % outer
    depth, rows = query.shape[0], query.shape[1]
    half = rows // 2
    mine = pl.ds(pl.multiple_of((section // 2) * half, half), half)
    q_width = query.shape[2] // TEAM

    def member(k):
        return {"wide": ((rank + k) % TEAM) * outer + team}

    greet([{"section": partner}, {"section": across}] + [member(k) for k in range(1, TEAM)])

    def pieces(core, target_rank):
        feed_start, head_start = column_starts(target_rank, gate.shape[2])
        feed_start = pl.multiple_of(feed_start, LANES)
        head_start = pl.multiple_of(head_start, LANES)
        if core == 0:
            return [
                (gate, pl.ds(feed_start, span), feed_out, pl.ds(0, span)),
                (
                    query,
                    pl.ds(pl.multiple_of(target_rank * q_width, LANES), q_width),
                    heads_out,
                    pl.ds(0, q_width),
                ),
            ]
        return [
            (up, pl.ds(feed_start, span), feed_out, pl.ds(span, span)),
            (key, pl.ds(head_start, LANES), heads_out, pl.ds(q_width, LANES)),
            (value, pl.ds(head_start, LANES), heads_out, pl.ds(q_width + LANES, LANES)),
        ]

    for k in range(1, TEAM):
        remote(
            small, small_out.at[rank], small_send.at[k], small_recv.at[k], member(k)
        ).start()
        remote(
            notes, notes_out.at[rank], notes_send.at[k], notes_recv.at[k], member(k)
        ).start()
    small_keep = pltpu.make_async_copy(small, small_out.at[rank], keep_sem.at[2])
    notes_keep = pltpu.make_async_copy(notes, notes_out.at[rank], keep_sem.at[3])
    small_keep.start()
    notes_keep.start()

    total = span + q_width

    def layer_bytes(layer, semaphores):
        block = feed_out.at[layer, :, :, pl.ds(0, total)]
        return pltpu.make_async_copy(block, block, semaphores.at[layer])

    def all_moves(core):
        def keep(layer):
            return [
                pltpu.make_async_copy(
                    source.at[layer, mine, columns],
                    target.at[layer, rank, mine, to],
                    keep_sem.at[layer],
                )
                for source, columns, target, to in pieces(core, rank)
            ]

        def push(layer, k):
            return [
                remote(
                    source.at[layer, mine, columns],
                    target.at[layer, rank, mine, to],
                    push_send.at[layer, k],
                    push_recv.at[layer, k],
                    member(k),
                )
                for source, columns, target, to in pieces(core, (rank + k) % TEAM)
            ]

        def over(layer, k):
            origin = (rank + TEAM - k) % TEAM
            return [
                remote(
                    target.at[layer, origin, mine, to],
                    target.at[layer, origin, mine, to],
                    y_send.at[layer, k],
                    y_recv.at[layer, k],
                    {"section": across},
                )
                for _, _, target, to in pieces(core, rank)
            ]

        def on(layer):
            return [
                remote(
                    target.at[layer, :, :, to],
                    target.at[layer, :, :, to],
                    core_send.at[layer],
                    core_recv.at[layer],
                    {"section": partner},
                )
                for _, _, target, to in pieces(core, rank)
            ]

        def bytes_of(semaphore):
            block = gate.at[0, mine, pl.ds(0, total)]
            return pltpu.make_async_copy(block, block, semaphore)

        order = (4, 3, 5, 2, 6, 1, 7)
        for layer in range(depth):
            for copy in keep(layer):
                copy.start()
            for k in order:
                for copy in push(layer, k):
                    copy.start()
        for layer in range(depth):
            bytes_of(keep_sem.at[layer]).wait()
            for copy in over(layer, 0):
                copy.start()
            for k in order[::-1]:
                bytes_of(push_recv.at[layer, k]).wait()
                for copy in over(layer, k):
                    copy.start()
        for layer in range(depth):
            for k in range(TEAM):
                bytes_of(y_recv.at[layer, k]).wait()
            for copy in on(layer):
                copy.start()
        for layer in range(depth):
            layer_bytes(layer, core_send).wait()
            for k in range(TEAM):
                bytes_of(y_send.at[layer, k]).wait()
                if k:
                    bytes_of(push_send.at[layer, k]).wait()

    core = section % 2

    @pl.when(core == 0)
    def _():
        all_moves(0)

    @pl.when(core == 1)
    def _():
        all_moves(1)

    for layer in range(depth):
        layer_bytes(layer, core_recv).wait()
    small_keep.wait()
    notes_keep.wait()
    for k in range(1, TEAM):
        remote(small, small_out.at[rank], small_send.at[k], small_recv.at[k], member(k)).wait()
        remote(notes, notes_out.at[rank], notes_send.at[k], notes_recv.at[k], member(k)).wait()


def reshard(outer, collective_id, query, key, value, gate, up, small, notes):
    depth, rows = query.shape[:2]
    share = gate.shape[2] // TEAM
    span = -(-(share + LANES // 2) // LANES) * LANES
    heads_width = query.shape[2] // TEAM + 2 * LANES
    return pl.pallas_call(
        functools.partial(reshard_kernel, outer, span),
        out_shape=(
            jax.ShapeDtypeStruct((depth, TEAM, rows, heads_width), jnp.bfloat16),
            jax.ShapeDtypeStruct((depth, TEAM, rows, 2 * span), jnp.bfloat16),
            jax.ShapeDtypeStruct((TEAM,) + small.shape, small.dtype),
            jax.ShapeDtypeStruct((TEAM,) + notes.shape, notes.dtype),
        ),
        in_specs=[ANYWHERE] * 7,
        out_specs=(ANYWHERE,) * 4,
        scratch_shapes=[dma_sems(4)]
        + [dma_sems(depth, TEAM)] * 4
        + [dma_sems(depth)] * 2
        + [dma_sems(TEAM)] * 4,
        compiler_params=settings(collective_id),
        name="reshard",
    )(query, key, value, gate, up, small, notes)
def team_groups(wides, outer):
    return [[rank * outer + team for team in range(outer)] for rank in range(wides // outer)]


def turn(values, cosines, sines):
    halfway = values.shape[-1] // 2
    turned = jnp.concatenate([-values[..., halfway:], values[..., :halfway]], axis=-1)
    return values * cosines[None, :, None, :] + turned * sines[None, :, None, :]


def attention_forward(normed, heads_weight, out_weight, offset, cosines, sines):
    width = HEAD_DIM
    rows = normed.shape[0] // LEN
    q_width = out_weight.shape[0]
    shared = q_width // width
    projected = matmul(normed, heads_weight)
    query_pre = projected[:, :q_width].reshape(rows, LEN, shared, width)
    key_pre = lax.dynamic_slice_in_dim(projected[:, q_width : q_width + LANES], offset, width, 1)
    value_rows = lax.dynamic_slice_in_dim(projected[:, q_width + LANES :], offset, width, 1)
    queries = turn(query_pre, cosines, sines).astype(jnp.bfloat16)
    key_rows = turn(key_pre.reshape(rows, LEN, 1, width), cosines, sines)[:, :, 0]
    key_rows = key_rows.astype(jnp.bfloat16)
    value_rows = value_rows.astype(jnp.bfloat16).reshape(rows, LEN, width)
    causal = jnp.arange(LEN)[:, None] >= jnp.arange(LEN)[None, :]
    scores = jnp.einsum(
        "blgd,bmd->bglm", queries, key_rows, preferred_element_type=jnp.float32
    ) * width ** (-0.5)
    scores = jnp.where(causal, scores, -1e30)
    weights_full = jax.nn.softmax(scores, axis=-1)
    weights_low = weights_full.astype(jnp.bfloat16)
    mixed = jnp.einsum("bglm,bmd->blgd", weights_low, value_rows, preferred_element_type=jnp.float32)
    mixed = mixed.astype(jnp.bfloat16).reshape(rows * LEN, q_width)
    partial = matmul(mixed, out_weight).astype(jnp.bfloat16)
    return partial, (queries, key_rows, value_rows, weights_full, weights_low)


def attention_backward(grad, stored, heads_weight, out_weight, offset, cosines, sines):
    queries, key_rows, value_rows, weights_full, weights_low = stored
    rows, _, shared, width = queries.shape
    count = rows * LEN
    scale = width ** (-0.5)
    mixed_grad = times_trans(grad, out_weight).astype(jnp.bfloat16).reshape(queries.shape)
    weight_grad = jnp.einsum(
        "blgd,bmd->bglm", mixed_grad, value_rows, preferred_element_type=jnp.float32
    )
    value_grad = jnp.einsum(
        "bglm,blgd->bmd", weights_low, mixed_grad, preferred_element_type=jnp.float32
    )
    score_grad = weights_full * (
        weight_grad - jnp.sum(weights_full * weight_grad, axis=-1, keepdims=True)
    )
    score_grad = score_grad.astype(jnp.bfloat16)
    query_grad = (
        jnp.einsum("bglm,bmd->blgd", score_grad, key_rows, preferred_element_type=jnp.float32)
        * scale
    )
    key_grad = (
        jnp.einsum("bglm,blgd->bmd", score_grad, queries, preferred_element_type=jnp.float32)
        * scale
    )
    query_low = turn(query_grad, cosines, -sines).astype(jnp.bfloat16).reshape(count, -1)
    key_low = turn(key_grad[:, :, None], cosines, -sines).astype(jnp.bfloat16)
    blank = jnp.zeros((count, LANES), jnp.bfloat16)
    key_low = lax.dynamic_update_slice_in_dim(blank, key_low.reshape(count, width), offset, 1)
    value_low = value_grad.astype(jnp.bfloat16).reshape(count, width)
    value_low = lax.dynamic_update_slice_in_dim(blank, value_low, offset, 1)
    all_low = jnp.concatenate([query_low, key_low, value_low], axis=1)
    return times_trans(all_low, heads_weight).astype(jnp.bfloat16)


def feed_forward(normed, feed_weight, down_weight, offset):
    span = feed_weight.shape[1] // 2
    share = down_weight.shape[0]
    both = matmul(normed, feed_weight)
    gate_pre = lax.dynamic_slice_in_dim(both[:, :span], offset, share, 1)
    up_pre = lax.dynamic_slice_in_dim(both[:, span:], offset, share, 1)
    activated = (jax.nn.silu(gate_pre) * up_pre).astype(jnp.bfloat16)
    return matmul(activated, down_weight).astype(jnp.bfloat16), (gate_pre, up_pre)


def feed_backward(grad, stored, feed_weight, down_weight, offset):
    gate_pre, up_pre = stored
    span = feed_weight.shape[1] // 2
    activated_grad = times_trans(grad, down_weight)
    gate_sig = jax.nn.sigmoid(gate_pre)
    gate_grad = activated_grad * up_pre * gate_sig * (1.0 + gate_pre * (1.0 - gate_sig))
    up_grad = activated_grad * gate_pre * gate_sig
    blank = jnp.zeros((grad.shape[0], 2 * span), jnp.bfloat16)
    both = lax.dynamic_update_slice_in_dim(blank, gate_grad.astype(jnp.bfloat16), offset, 1)
    both = lax.dynamic_update_slice_in_dim(both, up_grad.astype(jnp.bfloat16), span + offset, 1)
    return times_trans(both, feed_weight).astype(jnp.bfloat16)


def shards(
    token_ids,
    targets,
    slot_ids,
    group_ids,
    group_offsets,
    piece_table,
    prenorm_gain,
    prenorm_bias,
    query_map,
    key_map,
    value_map,
    output_map,
    midnorm_gain,
    midnorm_bias,
    expand_map,
    reduce_map,
    embed_map,
    attention_gain,
    query_weight,
    key_weight,
    value_weight,
    output_weight,
    feed_gain,
    gate_weight,
    up_weight,
    down_weight,
    final_gain,
):
    wides = lax.axis_size("wide")
    outer = wides // TEAM
    groups = team_groups(wides, outer)
    section_index = lax.axis_index("section")
    wide_index = lax.axis_index("wide")
    rank = wide_index // outer
    hyper_width, hyper_feed = piece_table.shape[1], expand_map.shape[1]
    model_width = embed_map.shape[1]
    total_tokens = wides * MB * LEN

    owned = query_map.shape[0]
    vectors = jnp.stack([prenorm_gain, prenorm_bias, midnorm_gain, midnorm_bias], axis=1)
    vectors = jnp.pad(vectors, ((0, 0), (0, LANES - 4)))
    first = jnp.concatenate([query_map, key_map, value_map, output_map, expand_map], axis=1)
    second = jnp.concatenate([embed_map, vectors], axis=1)
    first, second, third = spread(
        1,
        wides,
        (first.astype(jnp.bfloat16), second.astype(jnp.bfloat16), reduce_map.astype(jnp.bfloat16)),
    )
    first = first.reshape(hyper_width, -1)
    second = second.reshape(hyper_width, -1)
    reduce_low = third.reshape(hyper_feed, hyper_width)
    query_low, key_low, value_low, output_low = (
        first[:, n * hyper_width : (n + 1) * hyper_width] for n in range(4)
    )
    expand_low = first[:, 4 * hyper_width :]
    embed_low = second[:, :model_width]
    gain_one, bias_one, second_gain, bias_two = (second[:, model_width + n] for n in range(4))
    params = (
        gain_one,
        bias_one,
        query_low,
        key_low,
        value_low,
        output_low,
        second_gain,
        bias_two,
        expand_low,
        reduce_low,
        embed_low,
    )

    gains = jnp.concatenate([attention_gain, feed_gain], axis=0)
    gains = jnp.pad(gains, ((0, 16 - gains.shape[0]), (0, 0)))
    notes = jnp.concatenate([token_ids.reshape(1, -1), targets.reshape(1, -1)], axis=0)
    notes = jnp.pad(notes, ((0, 6), (0, 0)))
    heads_all, feed_all, gains, notes = reshard(
        outer,
        2,
        query_weight,
        key_weight,
        value_weight,
        gate_weight,
        up_weight,
        gains,
        notes,
    )
    if outer > 1:
        heads_all, feed_all = (
            lax.all_gather(item, "wide", axis=2, axis_index_groups=groups)
            for item in (heads_all, feed_all)
        )
        gains = lax.all_gather(gains, "wide", axis=1, axis_index_groups=groups)
        gains = gains.reshape(-1, gains.shape[2], gains.shape[3])
        output_weight, down_weight = (
            lax.all_gather(item, "wide", axis=1, axis_index_groups=groups, tiled=True)
            for item in (output_weight, down_weight)
        )
    heads_all = heads_all.reshape(2, model_width, -1)
    feed_all = feed_all.reshape(2, model_width, -1)
    gains = gains.astype(jnp.float32).transpose(1, 0, 2).reshape(-1, 1, model_width)
    attention_gains, feed_gains = gains[:2], gains[2:4]
    final_scale = final_gain.astype(jnp.float32).reshape(1, model_width)
    notes = lax.dynamic_slice_in_dim(notes, section_index * 2, 2, 0)
    ids, wanted = notes[:, 0].reshape(-1), notes[:, 1].reshape(-1)
    share = down_weight.shape[1]
    feed_offset = rank * share % LANES
    head_offset = rank // 2 % 2 * HEAD_DIM
    cosines, sines = rope_tables(LEN, HEAD_DIM)

    entries, slot_count = slot_ids.shape
    group_hits = (
        group_ids[:, None] == jnp.arange(group_offsets.shape[0], dtype=jnp.int32)[None, :]
    ).astype(jnp.int32)
    row_start = jnp.sum(group_hits * group_offsets[None, :], axis=1)
    piece_rows = (row_start[:, None] + slot_ids).reshape(-1)
    pieces = (
        jnp.take(piece_table, piece_rows, axis=0)
        .astype(jnp.float32)
        .reshape(entries, slot_count, hyper_width)
    )
    table_shard, hyper_stored = hyper_forward(pieces, params, HYPER_HEAD_COUNT)

    table_rows = section_gather(3, table_shard)
    if outer > 1:
        table_rows = lax.all_gather(table_rows, "wide", axis=1, axis_index_groups=groups)
    table_rows = table_rows.reshape(-1, model_width)
    wide_rows = rank * outer + jnp.arange(outer, dtype=jnp.int32)
    row_starts = (
        jnp.arange(SECTIONS, dtype=jnp.int32)[:, None] * wides + wide_rows[None, :]
    ) * entries
    own_rows = row_starts[:, :, None] + jnp.arange(entries, dtype=jnp.int32)[None, None, :]
    own_rows = own_rows.reshape(-1)
    hits = (ids[:, None] == own_rows[None, :]).astype(jnp.bfloat16)
    injected = matmul(hits, table_rows).astype(jnp.bfloat16)
    normed, hidden = fold(inject, outer, 4, injected, (attention_gains[0],), (jnp.bfloat16,))

    kept = []
    for layer in range(2):
        heads_weight, feed_weight = heads_all[layer], feed_all[layer]
        partial, attended = attention_forward(
            normed.reshape(ROWS, model_width),
            heads_weight,
            output_weight[layer],
            head_offset,
            cosines,
            sines,
        )
        normed, middle = fold(
            enter_feed, outer, 5, partial, (hidden, feed_gains[layer]), (jnp.float32,)
        )
        partial, fed = feed_forward(
            normed.reshape(ROWS, model_width), feed_weight, down_weight[layer], feed_offset
        )
        kept.append((hidden, attended, middle, fed))
        next_gain = attention_gains[1] if layer == 0 else final_scale
        normed, hidden = fold(
            leave_layer, outer, 6, partial, (middle, next_gain), (jnp.bfloat16,)
        )

    final_normed = normed.reshape(ROWS, model_width)
    logits = times_trans(final_normed, table_rows)
    row_peak = jnp.max(logits, axis=1)
    row_mass = jnp.sum(jnp.exp(logits - row_peak[:, None]), axis=1)
    wanted_hits = wanted[:, None] == own_rows[None, :]
    chosen = jnp.sum(jnp.where(wanted_hits, logits, 0.0), axis=1)
    blank = jnp.zeros_like(chosen)
    stats = jnp.stack([row_peak, row_mass, chosen] + [blank] * 5, axis=0)
    stats = team_gather(outer, 7, stats)
    peak = jnp.max(stats[:, 0], axis=0)
    mass = jnp.sum(stats[:, 1] * jnp.exp(stats[:, 0] - peak[None, :]), axis=0)
    log_norm = peak + jnp.log(mass)
    loss_part = jnp.sum(log_norm - jnp.sum(stats[:, 2], axis=0)) / total_tokens
    logit_grad = (
        (jnp.exp(logits - log_norm[:, None]) - wanted_hits.astype(jnp.float32)) / total_tokens
    ).astype(jnp.bfloat16)
    partial = matmul(logit_grad, table_rows).astype(jnp.bfloat16)
    grads, outer_grad = fold(
        head_back, outer, 8, partial, (hidden, final_scale), (jnp.bfloat16,)
    )

    for layer in (1, 0):
        heads_weight, feed_weight = heads_all[layer], feed_all[layer]
        hidden, attended, middle, fed = kept[layer]
        partial = feed_backward(
            grads.reshape(ROWS, model_width), fed, feed_weight, down_weight[layer], feed_offset
        )
        grads, middle_grad = fold(
            feed_back, outer, 9, partial, (outer_grad, middle, feed_gains[layer]), (jnp.float32,)
        )
        partial = attention_backward(
            grads.reshape(ROWS, model_width),
            attended,
            heads_weight,
            output_weight[layer],
            head_offset,
            cosines,
            sines,
        )
        grads, outer_grad = fold(
            layer_back,
            outer,
            10,
            partial,
            (middle_grad, hidden, attention_gains[layer]),
            (jnp.bfloat16,),
        )

    table_part = trans_times(logit_grad, final_normed) + trans_times(
        hits, grads.reshape(ROWS, model_width)
    )
    table_part = table_part.astype(jnp.bfloat16).reshape(SECTIONS, outer, entries, model_width)
    loss_block = jnp.full((8, LANES), loss_part, jnp.float32)
    if outer > 1:
        table_part = lax.psum_scatter(
            table_part.astype(jnp.float32),
            "wide",
            scatter_dimension=1,
            axis_index_groups=groups,
        ).astype(jnp.bfloat16)
        loss_block = lax.psum(loss_block, "wide", axis_index_groups=groups)
    table_grad, loss_block = section_sum(
        11, table_part.reshape(SECTIONS, entries, model_width), loss_block
    )
    mean_loss = loss_block[0, 0]
    (
        grad_prescale,
        prenorm_bias_gradient,
        grad_query,
        grad_key,
        grad_value,
        grad_output,
        grad_midscale,
        grad_midshift,
        grad_expand,
        grad_reduce,
        grad_embed,
    ) = hyper_backward(params, hyper_stored, table_grad)
    vectors = jnp.stack(
        [grad_prescale, prenorm_bias_gradient, grad_midscale, grad_midshift], axis=1
    )
    vectors = jnp.pad(vectors, ((0, 0), (0, LANES - 4)))
    first = jnp.concatenate([grad_query, grad_key, grad_value, grad_output, grad_expand], axis=1)
    second = jnp.concatenate([grad_embed, vectors], axis=1)
    first, second, third = (
        item.astype(jnp.bfloat16).reshape(SECTIONS, wides, -1, item.shape[1])
        for item in (first, second, grad_reduce)
    )
    first, second, third = collect(12, (first, second, third))
    grad_query, grad_key, grad_value, grad_output = (
        first[:, n * hyper_width : (n + 1) * hyper_width] for n in range(4)
    )
    return (
        mean_loss,
        second[:, model_width],
        second[:, model_width + 1],
        grad_query,
        grad_key,
        grad_value,
        grad_output,
        second[:, model_width + 2],
        second[:, model_width + 3],
        first[:, 4 * hyper_width :],
        third,
        second[:, :model_width],
    )


def solution(mesh):
    placed = (
        P("wide", None, None),
        P("wide", None, None),
        P(("section", "wide"), None),
        P(("section", "wide")),
        P(),
        P(),
        P(("section", "wide")),
        P(("section", "wide")),
        P(("section", "wide"), None),
        P(("section", "wide"), None),
        P(("section", "wide"), None),
        P(("section", "wide"), None),
        P(("section", "wide")),
        P(("section", "wide")),
        P(("section", "wide"), None),
        P(("section", "wide"), None),
        P(("section", "wide"), None),
        P(None, "wide"),
        P(None, "wide", None),
        P(None, "wide", None),
        P(None, "wide", None),
        P(None, "wide", None),
        P(None, "wide"),
        P(None, "wide", None),
        P(None, "wide", None),
        P(None, "wide", None),
        P(),
    )
    return jax.shard_map(
        shards,
        mesh=mesh,
        in_specs=placed,
        out_specs=(
            P(),
            P(("section", "wide")),
            P(("section", "wide")),
            P(("section", "wide"), None),
            P(("section", "wide"), None),
            P(("section", "wide"), None),
            P(("section", "wide"), None),
            P(("section", "wide")),
            P(("section", "wide")),
            P(("section", "wide"), None),
            P(("section", "wide"), None),
            P(("section", "wide"), None),
        ),
        check_vma=False,
    )
```

time: 4020 us -> 941 us (0.23)
  waiting for transfers between devices: 3090 us -> 0 us
  Pallas kernels: 0 us -> 669 us
  blocking collectives: 625 us -> 0 us
  starting transfers between devices: 68.9 us -> 0 us
  matrix products: 82.6 us -> 144 us
  loops' own time: 49.4 us -> 0 us
    all_gather x13 -> x0, waiting for transfers between devices: 1780 us -> none  [the longest x1 443 us: shards(): lax.all_gather(select(down_weight), 'wide', axis=0, tiled=True)]
    reduce_scatter x7 -> x0, waiting for transfers between devices: 892 us -> none  [the longest x1 144 us: shards(): lax.psum_scatter(grad_embed, ('section', 'wide'), scatter_dimension=0, ti...]
    pallas_call x0 -> x16, Pallas kernels: none -> 669 us  [the longest x10 390 us: fold(): pl.pallas_call(functools.partial(fold_kernel, finish, outer, 1 + len(extr...]
    all_gather x11 -> x0, blocking collectives: 544 us -> none  [the longest x3 195 us: combined_all(): lax.all_gather(part.astype(kind), axis)]
    ppermute x6 -> x0, waiting for transfers between devices: 287 us -> none  [passed_along(): lax.ppermute(value, axis, [(source, source + steps) for source in range(l...]
    psum x2 -> x0, waiting for transfers between devices: 125 us -> none  [from_root(): return lax.psum(block, axis)]
    unnamed x2 -> x0, blocking collectives: 80.9 us -> none
    ppermute x6 -> x0, starting transfers between devices: 67.8 us -> none  [passed_along(): lax.ppermute(value, axis, [(source, source + steps) for source in range(l...]
  transfers between devices with their start and end apart: 28 -> 0, of which waited for: 25 -> 0; matrix products, arithmetic and copies ran while one was open for 3% -> 0% of each run, Pallas kernels for 0% -> 0%
where the time goes in v1:
time: 941 us; the launch traced here: 927 us
  Pallas kernels  669 us (71%)
  matrix products  144 us (15%)
  local copies, waits for them, and re-layouts  92.8 us (10%)
  other arithmetic  17.9 us (2%)
    pallas_call x10, Pallas kernels, fold(): pl.pallas_call(functools.partial(fold_kernel, finish, outer, 1 + len(extr...  390 us
    pallas_call x1, Pallas kernels, reshard(): pl.pallas_call(functools.partial(reshard_kernel, outer, span), out_shape=...  136 us
    pallas_call x1, Pallas kernels, collect(): pl.pallas_call(functools.partial(collect_kernel, count, halves), out_shap...  58.3 us
    pallas_call x1, Pallas kernels, spread(): pl.pallas_call(functools.partial(spread_kernel, count, halves), out_shape...  53.5 us
    dot_general x16, matrix products, times_trans(): lax.dot_general(former, latter, (((1,), (1,)), ((), ())), preferred_eleme...  49.7 us
    dot_general x17, matrix products, matmul(): return jnp.dot(former, latter, preferred_element_type=jnp.float32)  49.1 us

profile of v1, /device:TPU:0, one launch (start us, length us, event | category | flops | bytes accessed | tf_op | source)
XLA Modules:
  0.0 927.3 jit_solution(9200889145492810039)
XLA Ops:
  2.5 4.7 gather_fusion
  9.7 53.5 %spread.1 = (bf16[4,8,16,4096]{3,2,1,0:T(8,128)(2,1)}, bf16[4,8,16,2176]{3,2,1,0:T(8,128)(2,1)}, bf16[4,8,64,512]{3,2,1,0:T(8,128)(2,1)}) custom-call(bf16[16,4096]{1,0:T(8,128)(2,1)} %copy-done.41, bf16[16,2176]{1,0:T(8,128)(2,1)} %fusion.166.refs_1_, bf16[64,512]{1,0:T(8,128)(2,1)} %convert_element_type.272.refs_2_), custom_call_target="tpu_custom_call" | custom-call | tf_op jit(solution)/shard_map/spread/pallas_call | solution.py:733
  70.5 3.6 fusion.245
  77.3 2.4 fusion.46
  84.0 12.8 %fusion.5 = (bf16[512,2048]{1,0:T(8,128)(2,1)S(1)}, f32[512,2048]{1,0:T(8,128)}) fusion(bf16[512,4096]{1,0:T(8,128)(2,1)} %bitcast.376, f32[512,512]{1,0:T(8,128)S(1)} %get-tuple-element.141, f32[512]{0:T(512)S(1)} %bitcast.415, f32[512]{0:T(512)S(1)} %bitcast.408, f32[512]{0:T(512)S(1)} %add_rsqrt_fusion, f32[512]{0:T(512)S(1)} %broadcast_multiply_fusion.5), kind=kOutput, calls=%fused_computation.8 | convolution fusion | flops 1143209984 | bytes 9445376 | tf_op jit(solution)/shard_map/dot_general | solution.py:30
  100.3 10.6 %section_gather.1 = bf16[4,64,2048]{2,1,0:T(8,128)(2,1)} custom-call(bf16[64,2048]{1,0:T(8,128)(2,1)} %convolution_convert_fusion.11.block), custom_call_target="tpu_custom_call" | custom-call | tf_op jit(solution)/shard_map/section_gather/pallas_call | solution.py:525
  112.4 136.0 %reshard.1 = (bf16[2,8,256,512]{3,2,1,0:T(8,128)(2,1)}, bf16[2,8,256,1536]{3,2,1,0:T(8,128)(2,1)}, bf16[8,16,256]{2,1,0:T(8,128)(2,1)}, s32[8,8,128]{2,1,0:T(8,128)}) custom-call(bf16[2,256,2048]{2,1,0:T(8,128)(2,1)} %query.1, bf16[2,256,256]{2,1,0:T(8,128)(2,1)} %key.1, bf16[2,256,256]{2,1,0:T(8,128)(2,1)} %value.1, bf16[2,256,5632]{2,1,0:T(8,128)(2,1)} %gate.1, ...), custom_call_target="tpu_custom_call" | custom-call | tf_op jit(solution)/shard_map/reshard/pallas_call | solution.py:1118
  252.4 73.3 %inject.1 = (bf16[8,32,2048]{2,1,0:T(8,128)(2,1)}, bf16[32,2048]{1,0:T(8,128)(2,1)}) custom-call(bf16[8,32,2048]{2,1,0:T(8,128)(2,1)} %bitcast.337, f32[1,2048]{1,0:T(1,128)} %bitcast.384), custom_call_target="tpu_custom_call" | custom-call | tf_op jit(solution)/shard_map/inject/pallas_call | solution.py:403
  325.7 3.9 fusion.240
  342.8 2.7 convolution_convert_fusion.9
  345.5 40.5 %enter_feed.2 = (bf16[8,32,2048]{2,1,0:T(8,128)(2,1)}, f32[32,2048]{1,0:T(8,128)}) custom-call(bf16[8,32,2048]{2,1,0:T(8,128)(2,1)} %bitcast.341, bf16[32,2048]{1,0:T(8,128)(2,1)} %get-tuple-element.50.refs_1_.refs_2_, f32[1,2048]{1,0:T(1,128)} %bitcast.386), custom_call_target="tpu_custom_call" | custom-call | tf_op jit(solution)/shard_map/enter_feed/pallas_call | solution.py:403
  386.0 8.5 fusion.239
  398.5 4.6 fusion.28
  403.1 36.6 %leave_layer.2 = (bf16[8,32,2048]{2,1,0:T(8,128)(2,1)}, bf16[32,2048]{1,0:T(8,128)(2,1)}) custom-call(bf16[8,32,2048]{2,1,0:T(8,128)(2,1)} %bitcast.355, f32[32,2048]{1,0:T(8,128)} %get-tuple-element.53.refs_1_.refs_2_, f32[1,2048]{1,0:T(1,128)} %bitcast.388), custom_call_target="tpu_custom_call" | custom-call | tf_op jit(solution)/shard_map/leave_layer/pallas_call | solution.py:403
  453.3 2.6 convolution_convert_fusion.8
  455.9 37.5 %enter_feed.3 = (bf16[8,32,2048]{2,1,0:T(8,128)(2,1)}, f32[32,2048]{1,0:T(8,128)}) custom-call(bf16[8,32,2048]{2,1,0:T(8,128)(2,1)} %bitcast.340, bf16[32,2048]{1,0:T(8,128)(2,1)} %get-tuple-element.55.refs_1_.refs_2_, f32[1,2048]{1,0:T(1,128)} %bitcast.390), custom_call_target="tpu_custom_call" | custom-call | tf_op jit(solution)/shard_map/enter_feed/pallas_call | solution.py:403
  493.4 4.9 fusion.262
  498.5 4.7 fusion.31
  503.8 36.6 %leave_layer.3 = (bf16[8,32,2048]{2,1,0:T(8,128)(2,1)}, bf16[32,2048]{1,0:T(8,128)(2,1)}) custom-call(bf16[8,32,2048]{2,1,0:T(8,128)(2,1)} %bitcast.354, f32[32,2048]{1,0:T(8,128)} %get-tuple-element.57.refs_1_.refs_2_, f32[1,2048]{1,0:T(1,128)} %bitcast.382), custom_call_target="tpu_custom_call" | custom-call | tf_op jit(solution)/shard_map/leave_layer/pallas_call | solution.py:403
  542.9 9.0 team_gather.1
  555.1 33.0 %head_back.1 = (bf16[8,32,2048]{2,1,0:T(8,128)(2,1)}, bf16[32,2048]{1,0:T(8,128)(2,1)}) custom-call(bf16[8,32,2048]{2,1,0:T(8,128)(2,1)} %bitcast.336, bf16[32,2048]{1,0:T(8,128)(2,1)} %get-tuple-element.59.refs_1_, f32[1,2048]{1,0:T(1,128)} %bitcast.383), custom_call_target="tpu_custom_call" | custom-call | tf_op jit(solution)/shard_map/head_back/pallas_call | solution.py:403
  588.1 4.6 multiply_convert_fusion.5
  592.8 5.4 dynamic_update_slice.24
  598.3 4.7 dynamic_update_slice.25
  603.0 5.8 convolution_convert_fusion.6
  608.8 33.8 %feed_back.2 = (bf16[8,32,2048]{2,1,0:T(8,128)(2,1)}, f32[32,2048]{1,0:T(8,128)}) custom-call(bf16[8,32,2048]{2,1,0:T(8,128)(2,1)} %bitcast.358, bf16[32,2048]{1,0:T(8,128)(2,1)} %get-tuple-element.61.refs_1_, f32[32,2048]{1,0:T(8,128)} %get-tuple-element.57.refs_1_.refs_2_, f32[1,2048]{1,0:T(1,128)} %bitcast.391), custom_call_target="tpu_custom_call" | custom-call | tf_op jit(solution)/shard_map/feed_back/pallas_call | solution.py:403
  651.6 3.6 convolution_convert_fusion.4
  655.1 33.4 %layer_back.2 = (bf16[8,32,2048]{2,1,0:T(8,128)(2,1)}, bf16[32,2048]{1,0:T(8,128)(2,1)}) custom-call(bf16[8,32,2048]{2,1,0:T(8,128)(2,1)} %bitcast.356, f32[32,2048]{1,0:T(8,128)} %get-tuple-element.63.refs_1_, bf16[32,2048]{1,0:T(8,128)(2,1)} %get-tuple-element.55.refs_1_.refs_2_, f32[1,2048]{1,0:T(1,128)} %bitcast.389), custom_call_target="tpu_custom_call" | custom-call | tf_op jit(solution)/shard_map/layer_back/pallas_call | solution.py:403
  688.5 4.1 multiply_convert_fusion.3
  692.7 5.0 dynamic_update_slice.28
  697.7 4.9 dynamic_update_slice.29
  702.6 5.7 convolution_convert_fusion.5
  708.4 33.1 %feed_back.3 = (bf16[8,32,2048]{2,1,0:T(8,128)(2,1)}, f32[32,2048]{1,0:T(8,128)}) custom-call(bf16[8,32,2048]{2,1,0:T(8,128)(2,1)} %bitcast.359, bf16[32,2048]{1,0:T(8,128)(2,1)} %get-tuple-element.65.refs_1_, f32[32,2048]{1,0:T(8,128)} %get-tuple-element.53.refs_1_.refs_2_, f32[1,2048]{1,0:T(1,128)} %bitcast.387), custom_call_target="tpu_custom_call" | custom-call | tf_op jit(solution)/shard_map/feed_back/pallas_call | solution.py:403
  749.5 3.4 convolution_convert_fusion.3
  752.8 31.9 %layer_back.3 = (bf16[8,32,2048]{2,1,0:T(8,128)(2,1)}, bf16[32,2048]{1,0:T(8,128)(2,1)}) custom-call(bf16[8,32,2048]{2,1,0:T(8,128)(2,1)} %bitcast.357, f32[32,2048]{1,0:T(8,128)} %get-tuple-element.67.refs_1_, bf16[32,2048]{1,0:T(8,128)(2,1)} %get-tuple-element.50.refs_1_.refs_2_, f32[1,2048]{1,0:T(1,128)} %bitcast.385), custom_call_target="tpu_custom_call" | custom-call | tf_op jit(solution)/shard_map/layer_back/pallas_call | solution.py:403
  785.3 2.7 fusion.27
  789.2 11.8 %section_sum.1 = (f32[64,2048]{1,0:T(8,128)}, f32[8,128]{1,0:T(8,128)}) custom-call(bf16[4,64,2048]{2,1,0:T(8,128)(2,1)} %bitcast.342, f32[8,128]{1,0:T(8,128)} %broadcast_in_dim.42.loss), custom_call_target="tpu_custom_call" | custom-call | tf_op jit(solution)/shard_map/section_sum/pallas_call | solution.py:579
  801.0 2.5 fusion.258
  803.6 4.8 fusion.11
  812.8 3.0 multiply_reduce_fusion
  818.7 2.5 fusion.119
  824.0 2.8 convolution_add_fusion.2
  826.9 2.6 fusion.47
  830.8 2.8 reshape.518
  838.4 3.6 convolution_convert_fusion.2
  853.6 3.2 constant_dynamic-update-slice_fusion.4.refs_0_
  856.8 2.7 convolution_convert_fusion
  859.5 58.3 %collect.1 = (f32[16,4096]{1,0:T(8,128)}, f32[16,2176]{1,0:T(8,128)}, f32[64,512]{1,0:T(8,128)}) custom-call(bf16[4,8,16,4096]{3,2,1,0:T(8,128)(2,1)} %constant_dynamic-update-slice_fusion.4.refs_0_, bf16[4,8,16,2176]{3,2,1,0:T(8,128)(2,1)} %pad_maximum_fusion.refs_1_, bf16[4,8,64,512]{3,2,1,0:T(8,128)(2,1)} %bitcast.353), custom_call_target="tpu_custom_call" | custom-call | tf_op jit(solution)/shard_map/collect/pallas_call | solution.py:910
  (375 shorter events, 118.5 us)
Async XLA Ops:
  0.6 7.4 copy-start.79
  0.7 7.4 copy-start.78
  0.7 7.4 copy-start.81
  0.7 7.4 copy-start.80
  0.7 7.5 copy-start.42
  0.7 8.2 copy-start.49
  0.7 8.2 copy-start.50
  0.7 8.2 copy-start.51
  0.7 8.2 copy-start.52
  0.7 8.2 copy-start.43
  0.7 8.2 copy-start.44
  7.4 826.2 %copy-start.59 = (pred[512]{0:T(512)(128)(4,1)}, pred[512]{0:T(512)(128)(4,1)S(1)}, u32[]{:S(2)}) copy-start(pred[512]{0:T(512)(128)(4,1)S(1)} %compare_and_fusion) | copy-start | bytes 1540
  7.6 58.2 %copy-start.47 = (f32[512]{0:T(512)}, f32[512]{0:T(512)S(1)}, u32[]{:S(2)}) copy-start(f32[512]{0:T(512)S(1)} %broadcast_multiply_fusion.6) | copy-start | bytes 6148
  8.0 57.8 %copy-start.57 = (f32[512]{0:T(512)}, f32[512]{0:T(512)S(1)}, u32[]{:S(2)}) copy-start(f32[512]{0:T(512)S(1)} %add_rsqrt_fusion.1) | copy-start | bytes 6148
  80.6 16.1 %copy-start.9 = (bf16[512,512]{1,0:T(8,128)(2,1)}, bf16[512,512]{1,0:T(8,128)(2,1)S(1)}, u32[]{:S(2)}) copy-start(bf16[512,512]{1,0:T(8,128)(2,1)S(1)} %reshape.470) | copy-start | bytes 1572868
  82.4 728.1 %copy-start.6 = (f32[512,512]{1,0:T(8,128)}, f32[512,512]{1,0:T(8,128)S(1)}, u32[]{:S(2)}) copy-start(f32[512,512]{1,0:T(8,128)S(1)} %get-tuple-element.141) | copy-start | bytes 3145732
  82.7 14.1 %copy-start.67 = (f32[512]{0:T(512)}, f32[512]{0:T(512)S(1)}, u32[]{:S(2)}) copy-start(f32[512]{0:T(512)S(1)} %add_rsqrt_fusion) | copy-start | bytes 6148
  83.8 12.9 %copy-start.65 = (f32[512,1]{0,1:T(1,128)}, f32[512,1]{0,1:T(1,128)S(1)}, u32[]{:S(2)}) copy-start(f32[512,1]{0,1:T(1,128)S(1)} %copy.411) | copy-start | bytes 6148
  84.0 12.8 %copy-start.73 = (f32[512,1]{0,1:T(1,128)}, f32[512,1]{0,1:T(1,128)S(1)}, u32[]{:S(2)}) copy-start(f32[512,1]{0,1:T(1,128)S(1)} %copy.412) | copy-start | bytes 6148
  84.0 12.8 %copy-start.82 = (bf16[4,8,64,512]{3,2,1,0:T(8,128)(2,1)S(1)}, bf16[4,8,64,512]{3,2,1,0:T(8,128)(2,1)}, u32[]{:S(2)}) copy-start(bf16[4,8,64,512]{3,2,1,0:T(8,128)(2,1)} %get-tuple-element.46) | copy-start | bytes 6291460
  96.8 14.2 %copy-start.74 = (bf16[2,256]{1,0:T(2,128)(2,1)S(1)}, bf16[2,256]{1,0:T(2,128)(2,1)}, u32[]{:S(2)}) copy-start(bf16[2,256]{1,0:T(2,128)(2,1)} %param.49) | copy-start | bytes 3076
  96.8 14.2 %copy-start.75 = (bf16[2,256]{1,0:T(2,128)(2,1)S(1)}, bf16[2,256]{1,0:T(2,128)(2,1)}, u32[]{:S(2)}) copy-start(bf16[2,256]{1,0:T(2,128)(2,1)} %param.44) | copy-start | bytes 3076
  96.8 14.8 %copy-start.85 = (s32[1,2,64]{2,1,0:T(2,128)S(1)}, s32[1,2,64]{2,1,0:T(2,128)}, u32[]{:S(2)}) copy-start(s32[1,2,64]{2,1,0:T(2,128)} %param.27) | copy-start | bytes 1540
  96.8 14.9 %copy-start.86 = (s32[1,2,64]{2,1,0:T(2,128)S(1)}, s32[1,2,64]{2,1,0:T(2,128)}, u32[]{:S(2)}) copy-start(s32[1,2,64]{2,1,0:T(2,128)} %param.28) | copy-start | bytes 1540
  99.1 12.6 %copy-start.30 = (f32[64,512]{1,0:T(8,128)}, f32[64,512]{1,0:T(8,128)S(1)}, u32[]{:S(2)}) copy-start(f32[64,512]{1,0:T(8,128)S(1)} %fusion.57) | copy-start | bytes 393220
  112.4 137.0 %copy-start = (bf16[4,64,2048]{2,1,0:T(8,128)(2,1)S(1)}, bf16[4,64,2048]{2,1,0:T(8,128)(2,1)}, u32[]{:S(2)}) copy-start(bf16[4,64,2048]{2,1,0:T(8,128)(2,1)} %section_gather.1) | copy-start | bytes 3145732
  249.2 80.4 %copy-start.63 = (s32[2,1,128]{2,1,0:T(1,128)}, s32[2,1,128]{2,1,0:T(1,128)S(1)}, u32[]{:S(2)}) copy-start(s32[2,1,128]{2,1,0:T(1,128)S(1)} %get-tuple-element.133) | copy-start | bytes 3076
  386.0 8.6 copy-start.83
  398.5 41.2 %copy-start.15 = (bf16[1,8,256,512]{3,2,1,0:T(8,128)(2,1)S(1)}, bf16[1,8,256,512]{3,2,1,0:T(8,128)(2,1)}, u32[]{:S(2)}) copy-start(bf16[1,8,256,512]{3,2,1,0:T(8,128)(2,1)} %get-tuple-element.92) | copy-start | bytes 6291460
  449.8 48.6 %copy-start.71 = (f32[4,4,64]{2,1,0:T(4,128)}, f32[4,4,64]{2,1,0:T(4,128)S(1)}, u32[]{:S(2)}) copy-start(f32[4,4,64]{2,1,0:T(4,128)S(1)} %get-tuple-element.146) | copy-start | bytes 12292
  553.5 39.2 %copy-start.61 = (f32[256]{0:T(256)}, f32[256]{0:T(256)S(1)}, u32[]{:S(2)}) copy-start(f32[256]{0:T(256)S(1)} %get-tuple-element.89) | copy-start | bytes 3076
  603.0 39.6 %copy-start.11 = (bf16[2,256,2048]{2,1,0:T(8,128)(2,1)S(1)}, bf16[2,256,2048]{2,1,0:T(8,128)(2,1)}, u32[]{:S(2)}) copy-start(bf16[2,256,2048]{2,1,0:T(8,128)(2,1)} %param.48) | copy-start | bytes 6291460
  608.8 35.7 %copy-start.27 = (f32[4,4,64,64]{2,3,1,0:T(8,128)S(1)}, f32[4,4,64,64]{2,3,1,0:T(8,128)}, u32[]{:S(2)}) copy-start(f32[4,4,64,64]{2,3,1,0:T(8,128)} %get-tuple-element.147) | copy-start | bytes 786436
  608.8 37.8 %copy-start.40 = (bf16[4,64,64,1]{1,0,2,3:T(4,128)(2,1)S(1)}, bf16[4,64,64,1]{1,0,2,3:T(4,128)(2,1)}, u32[]{:S(2)}) copy-start(bf16[4,64,64,1]{1,0,2,3:T(4,128)(2,1)} %fusion.169) | copy-start | bytes 98308
  649.3 39.1 %copy-start.20 = (f32[256,768]{1,0:T(8,128)S(1)}, f32[256,768]{1,0:T(8,128)}, u32[]{:S(2)}) copy-start(f32[256,768]{1,0:T(8,128)} %get-tuple-element.104) | copy-start | bytes 2359300
  651.5 36.9 %copy-start.21 = (f32[256,768]{1,0:T(8,128)S(1)}, f32[256,768]{1,0:T(8,128)}, u32[]{:S(2)}) copy-start(f32[256,768]{1,0:T(8,128)} %get-tuple-element.105) | copy-start | bytes 2359300
  702.6 38.8 %copy-start.12 = (bf16[2,256,2048]{2,1,0:T(8,128)(2,1)S(1)}, bf16[2,256,2048]{2,1,0:T(8,128)(2,1)}, u32[]{:S(2)}) copy-start(bf16[2,256,2048]{2,1,0:T(8,128)(2,1)} %param.48) | copy-start | bytes 6291460
  708.3 35.0 %copy-start.26 = (f32[4,4,64,64]{2,3,1,0:T(8,128)S(1)}, f32[4,4,64,64]{2,3,1,0:T(8,128)}, u32[]{:S(2)}) copy-start(f32[4,4,64,64]{2,3,1,0:T(8,128)} %get-tuple-element.145) | copy-start | bytes 786436
  708.4 37.1 %copy-start.39 = (bf16[4,64,64,1]{1,0,2,3:T(4,128)(2,1)S(1)}, bf16[4,64,64,1]{1,0,2,3:T(4,128)(2,1)}, u32[]{:S(2)}) copy-start(bf16[4,64,64,1]{1,0,2,3:T(4,128)(2,1)} %fusion.170) | copy-start | bytes 98308
  747.2 37.5 %copy-start.8 = (bf16[8,32,2048]{2,1,0:T(8,128)(2,1)S(1)}, bf16[8,32,2048]{2,1,0:T(8,128)(2,1)}, u32[]{:S(2)}) copy-start(bf16[8,32,2048]{2,1,0:T(8,128)(2,1)} %get-tuple-element.58) | copy-start | bytes 3145732
  747.2 37.5 %copy-start.62 = (f32[256]{0:T(256)S(1)}, f32[256]{0:T(256)}, u32[]{:S(2)}) copy-start(f32[256]{0:T(256)} %copy-done.61) | copy-start | bytes 3076
  749.2 36.1 %copy-start.64 = (s32[2,1,128]{2,1,0:T(1,128)S(1)}, s32[2,1,128]{2,1,0:T(1,128)}, u32[]{:S(2)}) copy-start(s32[2,1,128]{2,1,0:T(1,128)} %copy-done.63) | copy-start | bytes 3076
  826.9 6.7 copy-start.48
  826.9 6.7 copy-start.58
  838.4 8.3 copy-start.54
  838.4 8.3 copy-start.56
  838.4 8.3 copy-start.60
  845.3 6.8 copy-start.10
  (43 other events, 130.3 us)

commit v2 on v1

--- a/solution.py
+++ b/solution.py
@@ -72,201 +72,6 @@
     angles = jnp.arange(positions, dtype=jnp.float32)[:, None] * frequency[None, :]
     angles = jnp.concatenate([angles, angles], axis=1)
     return (jnp.cos(angles), jnp.sin(angles))
-
-
-def apply_rotary(values, cosines, sines):
-    halfway = values.shape[-1] // 2
-    turned = jnp.concatenate([-values[..., halfway:], values[..., :halfway]], axis=-1)
-    return values * cosines[None, :, None, :] + turned * sines[None, :, None, :]
-
-
-def invert_rotary(gradient, cosines, sines):
-    halfway = gradient.shape[-1] // 2
-    scaled = gradient * sines[None, :, None, :]
-    turned = jnp.concatenate([scaled[..., halfway:], -scaled[..., :halfway]], axis=-1)
-    return gradient * cosines[None, :, None, :] + turned
-
-
-def hyper_forward(pieces, params, head_count):
-    (
-        gain_one,
-        bias_one,
-        query_mat,
-        key_mat,
-        value_mat,
-        out_mat,
-        second_gain,
-        bias_two,
-        expand_mat,
-        reduce_mat,
-        embed_mat,
-    ) = params
-    entries, slot_count, model_width = pieces.shape
-    head_width = model_width // head_count
-    score_scale = head_width ** (-0.5)
-    flat_in = pieces.reshape(entries * slot_count, model_width)
-    normed_one, inverse_one = center_norm(flat_in)
-    attn_in = (normed_one * gain_one.astype(jnp.float32) + bias_one.astype(jnp.float32)).astype(
-        jnp.bfloat16
-    )
-    queries = (
-        matmul(attn_in, query_mat)
-        .astype(jnp.bfloat16)
-        .reshape(entries, slot_count, head_count, head_width)
-    )
-    key_rows = (
-        matmul(attn_in, key_mat)
-        .astype(jnp.bfloat16)
-        .reshape(entries, slot_count, head_count, head_width)
-    )
-    value_rows = (
-        matmul(attn_in, value_mat)
-        .astype(jnp.bfloat16)
-        .reshape(entries, slot_count, head_count, head_width)
-    )
-    scores = (
-        jnp.einsum("eshd,ethd->ehst", queries, key_rows, preferred_element_type=jnp.float32)
-        * score_scale
-    )
-    weights_full = jax.nn.softmax(scores, axis=-1)
-    weights_low = weights_full.astype(jnp.bfloat16)
-    mixed = jnp.einsum(
-        "ehst,ethd->eshd", weights_low, value_rows, preferred_element_type=jnp.float32
-    )
-    mixed = mixed.astype(jnp.bfloat16).reshape(entries * slot_count, model_width)
-    middle = flat_in + matmul(mixed, out_mat)
-    normed_two, inverse_two = center_norm(middle)
-    ffn_in = (normed_two * second_gain.astype(jnp.float32) + bias_two.astype(jnp.float32)).astype(
-        jnp.bfloat16
-    )
-    expanded = matmul(ffn_in, expand_mat)
-    activated = jax.nn.gelu(expanded, approximate=False).astype(jnp.bfloat16)
-    outcome = middle + matmul(activated, reduce_mat)
-    pooled = jnp.mean(outcome.reshape(entries, slot_count, model_width), axis=1).astype(
-        jnp.bfloat16
-    )
-    table_rows = matmul(pooled, embed_mat).astype(jnp.bfloat16)
-    stored = (
-        normed_one,
-        inverse_one,
-        attn_in,
-        queries,
-        key_rows,
-        value_rows,
-        weights_full,
-        weights_low,
-        mixed,
-        normed_two,
-        inverse_two,
-        ffn_in,
-        expanded,
-        activated,
-        pooled,
-    )
-    return (table_rows, stored)
-
-
-def hyper_backward(params, stored, table_grad):
-    (
-        gain_one,
-        bias_one,
-        query_mat,
-        key_mat,
-        value_mat,
-        out_mat,
-        second_gain,
-        bias_two,
-        expand_mat,
-        reduce_mat,
-        embed_mat,
-    ) = params
-    (
-        normed_one,
-        inverse_one,
-        attn_in,
-        queries,
-        key_rows,
-        value_rows,
-        weights_full,
-        weights_low,
-        mixed,
-        normed_two,
-        inverse_two,
-        ffn_in,
-        expanded,
-        activated,
-        pooled,
-    ) = stored
-    entries, slot_count, head_total, head_width = queries.shape
-    model_width = head_total * head_width
-    score_scale = head_width ** (-0.5)
-    grad_low = table_grad.astype(jnp.bfloat16)
-    grad_embed = trans_times(pooled, grad_low)
-    pooled_grad = times_trans(grad_low, embed_mat) / slot_count
-    outcome_grad = jnp.broadcast_to(pooled_grad[:, None, :], (entries, slot_count, model_width))
-    outcome_grad = outcome_grad.reshape(entries * slot_count, model_width)
-    outcome_low = outcome_grad.astype(jnp.bfloat16)
-    grad_reduce = trans_times(activated, outcome_low)
-    act_grad = times_trans(outcome_low, reduce_mat)
-    slope = (
-        0.5 * (1.0 + lax.erf(expanded * inv_root_two))
-        + expanded * jnp.exp(-0.5 * expanded * expanded) * inv_root_tau
-    )
-    expanded_low = (act_grad * slope).astype(jnp.bfloat16)
-    grad_expand = trans_times(ffn_in, expanded_low)
-    ffn_grad = times_trans(expanded_low, expand_mat)
-    grad_midscale = jnp.sum(ffn_grad * normed_two, axis=0)
-    grad_midshift = jnp.sum(ffn_grad, axis=0)
-    middle_grad = outcome_grad + center_back(
-        normed_two, inverse_two, ffn_grad * second_gain.astype(jnp.float32)
-    )
-    middle_low = middle_grad.astype(jnp.bfloat16)
-    grad_output = trans_times(mixed, middle_low)
-    mixed_grad = times_trans(middle_low, out_mat).astype(jnp.bfloat16).reshape(queries.shape)
-    weight_grad = jnp.einsum(
-        "eshd,ethd->ehst", mixed_grad, value_rows, preferred_element_type=jnp.float32
-    )
-    value_grad = jnp.einsum(
-        "ehst,eshd->ethd", weights_low, mixed_grad, preferred_element_type=jnp.float32
-    )
-    score_grad = weights_full * (
-        weight_grad - jnp.sum(weights_full * weight_grad, axis=-1, keepdims=True)
-    )
-    score_grad = score_grad.astype(jnp.bfloat16)
-    query_grad = (
-        jnp.einsum("ehst,ethd->eshd", score_grad, key_rows, preferred_element_type=jnp.float32)
-        * score_scale
-    )
-    key_grad = (
-        jnp.einsum("ehst,eshd->ethd", score_grad, queries, preferred_element_type=jnp.float32)
-        * score_scale
-    )
-    query_low = query_grad.astype(jnp.bfloat16).reshape(entries * slot_count, model_width)
-    key_low = key_grad.astype(jnp.bfloat16).reshape(entries * slot_count, model_width)
-    value_low = value_grad.astype(jnp.bfloat16).reshape(entries * slot_count, model_width)
-    grad_query = trans_times(attn_in, query_low)
-    grad_key = trans_times(attn_in, key_low)
-    grad_value = trans_times(attn_in, value_low)
-    attention_gradient = (
-        times_trans(query_low, query_mat)
-        + times_trans(key_low, key_mat)
-        + times_trans(value_low, value_mat)
-    )
-    grad_prescale = jnp.sum(attention_gradient * normed_one, axis=0)
-    prenorm_bias_gradient = jnp.sum(attention_gradient, axis=0)
-    return (
-        grad_prescale,
-        prenorm_bias_gradient,
-        grad_query,
-        grad_key,
-        grad_value,
-        grad_output,
-        grad_midscale,
-        grad_midshift,
-        grad_expand,
-        grad_reduce,
-        grad_embed,
-    )
 
 
 def greet(peers):
@@ -614,10 +419,26 @@
     return section, (wide_block + 1 - 2 * (wide_block % 2) if flips_x else wide_block)
 
 
-def spread_kernel(count, halves, *refs):
-    blocks, gathereds = refs[:count], refs[count : 2 * count]
-    keep_sem, z_send, a_send, b_send, c_send, z_recv, a_recv, b_recv, c_recv = refs[2 * count :]
+def spread_kernel(count, halves, outer, *refs):
+    blocks, notes = refs[:count], refs[count : count + 2]
+    gathereds, notes_out = refs[count + 2 : 2 * count + 2], refs[2 * count + 2 : 2 * count + 4]
+    (
+        keep_sem,
+        note_keep,
+        note_send,
+        note_recv,
+        z_send,
+        a_send,
+        b_send,
+        c_send,
+        z_recv,
+        a_recv,
+        b_recv,
+        c_recv,
+    ) = refs[2 * count + 4 :]
     section, partner, across, wide, wide_at = all_places(halves)
+    rank, team = wide // outer, wide % outer
+    members = [None] + [{"wide": (rank + k) % TEAM * outer + team} for k in range(1, TEAM)]
     beside = wide + 1 - 2 * (wide % 2)
     barrier = pltpu.get_barrier_semaphore()
     for peer in ({"section": partner}, {"section": across}, {"wide": beside}):
@@ -629,7 +450,19 @@
         return carry
 
     lax.fori_loop(1, halves, hello, 0)
-    pl.semaphore_wait(barrier, 3 + halves - 1)
+    for peer in members[1:]:
+        pl.semaphore_signal(barrier, inc=1, device_id=peer, device_id_type=MESH_IDS)
+    pl.semaphore_wait(barrier, 3 + halves - 1 + TEAM - 1)
+    note_keeps = [
+        pltpu.make_async_copy(notes[m], notes_out[m].at[rank], note_keep.at[m]) for m in range(2)
+    ]
+    note_copies = [
+        remote(notes[m], notes_out[m].at[rank], note_send.at[m, k], note_recv.at[m, k], members[k])
+        for m in range(2)
+        for k in range(1, TEAM)
+    ]
+    for copy in note_keeps + note_copies:
+        copy.start()
 
     keeps = [
         pltpu.make_async_copy(blocks[n], gathereds[n].at[section, wide], keep_sem.at[n])
@@ -726,18 +559,21 @@
         return carry
 
     lax.fori_loop(1, halves, drain_z, 0)
-
-
-def spread(collective_id, wides, blocks):
+    for copy in note_keeps + note_copies:
+        copy.wait()
+
+
+def spread(collective_id, wides, outer, blocks, notes):
     count, halves = len(blocks), wides // 2
     return pl.pallas_call(
-        functools.partial(spread_kernel, count, halves),
+        functools.partial(spread_kernel, count, halves, outer),
         out_shape=tuple(
             jax.ShapeDtypeStruct((SECTIONS, wides) + block.shape, block.dtype) for block in blocks
-        ),
-        in_specs=[ANYWHERE] * count,
-        out_specs=(ANYWHERE,) * count,
-        scratch_shapes=[dma_sems(count)]
+        )
+        + tuple(jax.ShapeDtypeStruct((TEAM,) + note.shape, note.dtype) for note in notes),
+        in_specs=[ANYWHERE] * (count + 2),
+        out_specs=(ANYWHERE,) * (count + 2),
+        scratch_shapes=[dma_sems(count), dma_sems(2), dma_sems(2, TEAM), dma_sems(2, TEAM)]
         + [
             dma_sems(count, halves),
             dma_sems(count, halves),
@@ -747,7 +583,7 @@
         * 2,
         compiler_params=settings(collective_id),
         name="spread",
-    )(*blocks)
+    )(*blocks, *notes)
 
 
 def collect_kernel(count, halves, *refs):
@@ -930,299 +766,630 @@
     )(*partials)
 
 
-def column_starts(rank, feed_width):
-    share = feed_width // TEAM
-    return (rank * share) // LANES * LANES, (rank // 4) * LANES
-
-
-def reshard_kernel(
-    outer,
-    span,
-    query,
-    key,
-    value,
-    gate,
-    up,
-    small,
-    notes,
+TILE = 256
+
+
+def causal_blocks(count, length):
+    row = lax.broadcasted_iota(jnp.int32, (count, count), 0)
+    column = lax.broadcasted_iota(jnp.int32, (count, count), 1)
+    return (row // length == column // length) & (column <= row)
+
+
+def turn(values, tables):
+    cosines, upper, lower = tables
+    parts = []
+    for start in range(0, values.shape[1], LANES):
+        part = values[:, start : start + LANES]
+        ahead = pltpu.roll(part, LANES - HEAD_DIM // 2, 1)
+        behind = pltpu.roll(part, HEAD_DIM // 2, 1)
+        parts.append(part * cosines + ahead * upper + behind * lower)
+    return parts[0] if len(parts) == 1 else jnp.concatenate(parts, axis=1)
+
+
+def turn_tables(back):
+    cosines, sines = rope_tables(LEN, HEAD_DIM)
+    sines = -sines if back else sines
+    first = jnp.arange(HEAD_DIM) < HEAD_DIM // 2
+    upper, lower = jnp.where(first, -sines, 0.0), jnp.where(first, 0.0, sines)
+    blank = jnp.zeros_like(cosines)
+    pairs = [(cosines, cosines), (upper, upper), (lower, lower)]
+    pairs += [(cosines, blank + 1.0), (upper, blank), (lower, blank)]
+    tables = jnp.stack([jnp.concatenate(pair, axis=1) for pair in pairs])
+    return jnp.tile(tables, (1, ROWS // LEN, 1))
+
+
+def load_weight(pieces, columns, scratch, sem):
+    section = lax.axis_index("section")
+    partner = section + 1 - 2 * (section % 2)
+    places = (section, (section + 2) % SECTIONS, partner, (partner + 2) % SECTIONS)
+    copies = [
+        pltpu.make_async_copy(source.at[:, :, columns], scratch.at[:, place], sem.at[n])
+        for n, (source, place) in enumerate(zip(pieces, places))
+    ]
+    for copy in copies:
+        copy.start()
+    return copies
+
+
+def attend(queries, key, mask, scale):
+    scores = times_trans(queries, key) * scale
+    scores = jnp.where(mask, scores, -1e30)
+    peak = jnp.max(scores, axis=1, keepdims=True)
+    mass = jnp.exp(scores - peak)
+    return mass / jnp.sum(mass, axis=1, keepdims=True)
+
+
+def attention_kernel(
+    normed, out_weight, tables, own, other_y, other_core, beyond, partial, queries_out, pairs_out, weight, sem
+):
+    heads_width = weight.shape[-1]
+    q_width = heads_width - LANES
+    copies = load_weight((own, other_y, other_core, beyond), pl.ds(0, heads_width), weight, sem)
+    for copy in copies:
+        copy.wait()
+    rows = normed[...]
+    projected = matmul(rows, weight[...].reshape(-1, heads_width))
+    queries = turn(projected[:, :q_width], [tables[n] for n in range(3)]).astype(jnp.bfloat16)
+    pairs = turn(projected[:, q_width:], [tables[n] for n in range(3, 6)]).astype(jnp.bfloat16)
+    queries_out[...] = queries
+    pairs_out[...] = pairs
+    key, value = pairs[:, :HEAD_DIM], pairs[:, HEAD_DIM:]
+    mask = causal_blocks(ROWS, LEN)
+    mixed = []
+    for start in range(0, q_width, HEAD_DIM):
+        weights = attend(queries[:, start : start + HEAD_DIM], key, mask, HEAD_DIM ** (-0.5))
+        mixed.append(matmul(weights.astype(jnp.bfloat16), value))
+    mixed = jnp.concatenate(mixed, axis=1).astype(jnp.bfloat16)
+
+    @pl.loop(0, partial.shape[1] // TILE)
+    def _(n):
+        columns = pl.ds(pl.multiple_of(n * TILE, TILE), TILE)
+        partial[:, columns] = matmul(mixed, out_weight[:, columns]).astype(jnp.bfloat16)
+
+
+def attention_back_kernel(
+    grad, queries, pairs, out_weight, tables, own, other_y, other_core, beyond, partial, weight, sem
+):
+    heads_width = weight.shape[-1]
+    q_width = heads_width - LANES
+    scale = HEAD_DIM ** (-0.5)
+    copies = load_weight((own, other_y, other_core, beyond), pl.ds(0, heads_width), weight, sem)
+    mixed_grad = times_trans(grad[...], out_weight[...]).astype(jnp.bfloat16)
+    key, value = pairs[:, :HEAD_DIM], pairs[:, HEAD_DIM:]
+    mask = causal_blocks(ROWS, LEN)
+    query_grads, key_grad, value_grad = [], 0.0, 0.0
+    for start in range(0, q_width, HEAD_DIM):
+        query = queries[:, start : start + HEAD_DIM]
+        outer = mixed_grad[:, start : start + HEAD_DIM]
+        weights = attend(query, key, mask, scale)
+        weight_grad = times_trans(outer, value)
+        score_grad = weights * (
+            weight_grad - jnp.sum(weights * weight_grad, axis=1, keepdims=True)
+        )
+        score_grad = score_grad.astype(jnp.bfloat16)
+        query_grads.append(matmul(score_grad, key) * scale)
+        key_grad = key_grad + trans_times(score_grad, query) * scale
+        value_grad = value_grad + trans_times(weights.astype(jnp.bfloat16), outer)
+    query_grad = turn(jnp.concatenate(query_grads, axis=1), [tables[n] for n in range(3)])
+    pair_grad = jnp.concatenate([key_grad, value_grad], axis=1)
+    pair_grad = turn(pair_grad, [tables[n] for n in range(3, 6)])
+    both = jnp.concatenate([query_grad, pair_grad], axis=1).astype(jnp.bfloat16)
+    for copy in copies:
+        copy.wait()
+    tiles = partial.shape[1] // TILE
+    each = weight.shape[0] // tiles
+
+    @pl.loop(0, tiles)
+    def _(n):
+        columns = pl.ds(pl.multiple_of(n * TILE, TILE), TILE)
+        block = weight[pl.ds(n * each, each)].reshape(TILE, heads_width)
+        partial[:, columns] = times_trans(both, block).astype(jnp.bfloat16)
+
+
+def feed_kernel(normed, down, own, other_y, other_core, beyond, partial, kept, weight, active, sem):
+    width = weight.shape[-1]
+    share = down.shape[0]
+    edge = share // LANES * LANES
+    tail = share - edge
+    copies = load_weight(
+        (own, other_y, other_core, beyond), pl.ds(own.shape[-1] - width, width), weight, sem
+    )
+    for copy in copies:
+        copy.wait()
+    depth = partial.shape[1]
+
+    @pl.loop(0, width // LANES)
+    def _(n):
+        columns = pl.ds(pl.multiple_of(n * LANES, LANES), LANES)
+        kept[:, columns] = matmul(normed[...], weight[:, :, :, columns].reshape(depth, LANES))
+
+    def activate(gate, up):
+        return (jax.nn.silu(gate) * up).astype(jnp.bfloat16)
+
+    active[:, :edge] = activate(kept[:, :edge], kept[:, edge : 2 * edge])
+    if tail:
+        last = kept[:, 2 * edge :]
+        active[:, edge:] = activate(last[:, :tail], last[:, tail:])
+
+    @pl.loop(0, depth // TILE)
+    def _(n):
+        columns = pl.ds(pl.multiple_of(n * TILE, TILE), TILE)
+        partial[:, columns] = matmul(active[...], down[:, columns]).astype(jnp.bfloat16)
+
+
+def feed_back_kernel(grad, kept, down, own, other_y, other_core, beyond, partial, weight, both, sem):
+    width = weight.shape[-1]
+    share = down.shape[0]
+    edge = share // LANES * LANES
+    tail = share - edge
+    copies = load_weight(
+        (own, other_y, other_core, beyond), pl.ds(own.shape[-1] - width, width), weight, sem
+    )
+    active_grad = times_trans(grad[...], down[...])
+
+    def back(outer, gate, up):
+        sigmoid = jax.nn.sigmoid(gate)
+        gate_grad = outer * up * sigmoid * (1.0 + gate * (1.0 - sigmoid))
+        return gate_grad.astype(jnp.bfloat16), (outer * gate * sigmoid).astype(jnp.bfloat16)
+
+    gate_grad, up_grad = back(active_grad[:, :edge], kept[:, :edge], kept[:, edge : 2 * edge])
+    both[:, :edge] = gate_grad
+    both[:, edge : 2 * edge] = up_grad
+    if tail:
+        last = kept[:, 2 * edge :]
+        gate_grad, up_grad = back(active_grad[:, edge:], last[:, :tail], last[:, tail:])
+        both[:, 2 * edge :] = jnp.concatenate([gate_grad, up_grad], axis=1)
+    for copy in copies:
+        copy.wait()
+    tiles = partial.shape[1] // TILE
+    each = weight.shape[0] // tiles
+
+    @pl.loop(0, tiles)
+    def _(n):
+        columns = pl.ds(pl.multiple_of(n * TILE, TILE), TILE)
+        block = weight[pl.ds(n * each, each)].reshape(TILE, width)
+        partial[:, columns] = times_trans(both[...], block).astype(jnp.bfloat16)
+
+
+class Layer:
+    def __init__(self, stack, index):
+        self.stack, self.index, self.shape = stack, index, stack.shape[1:]
+
+    def spec(self):
+        return pl.BlockSpec(
+            (None,) + self.shape, lambda step: (self.index, 0, 0), memory_space=pltpu.VMEM
+        )
+
+
+def local(kernel, operands, weights, outs, scratch, name):
+    specs = [item.spec() if isinstance(item, Layer) else IN_VMEM for item in operands]
+    operands = [item.stack if isinstance(item, Layer) else item for item in operands]
+    return pl.pallas_call(
+        kernel,
+        grid=(1,),
+        out_shape=tuple(jax.ShapeDtypeStruct(shape, kind) for shape, kind in outs),
+        in_specs=specs + [ANYWHERE] * len(weights),
+        out_specs=(IN_VMEM,) * len(outs),
+        scratch_shapes=list(scratch),
+        compiler_params=pltpu.CompilerParams(vmem_limit_bytes=VMEM_LIMIT),
+        name=name,
+    )(*operands, *weights)
+
+
+def weight_scratch(pieces, width):
+    groups, rows = pieces[0].shape[:2]
+    return pltpu.VMEM((groups, SECTIONS, rows, width), jnp.bfloat16)
+
+
+def attention_forward(normed, pieces, out_weight, tables):
+    q_width, depth = out_weight.shape
+    partial, queries, pairs = local(
+        attention_kernel,
+        (normed, out_weight, tables),
+        pieces,
+        [
+            ((ROWS, depth), jnp.bfloat16),
+            ((ROWS, q_width), jnp.bfloat16),
+            ((ROWS, LANES), jnp.bfloat16),
+        ],
+        [weight_scratch(pieces, q_width + LANES), dma_sems(4)],
+        "attention",
+    )
+    return partial, (queries, pairs)
+
+
+def attention_backward(grad, stored, pieces, out_weight, tables):
+    q_width, depth = out_weight.shape
+    (partial,) = local(
+        attention_back_kernel,
+        (grad, *stored, out_weight, tables),
+        pieces,
+        [((ROWS, depth), jnp.bfloat16)],
+        [weight_scratch(pieces, q_width + LANES), dma_sems(4)],
+        "attention_grad",
+    )
+    return partial
+
+
+def feed_forward(normed, pieces, down):
+    share, depth = down.shape
+    partial, kept = local(
+        feed_kernel,
+        (normed, down),
+        pieces,
+        [((ROWS, depth), jnp.bfloat16), ((ROWS, 2 * share), jnp.float32)],
+        [
+            weight_scratch(pieces, 2 * share),
+            pltpu.VMEM((ROWS, share), jnp.bfloat16),
+            dma_sems(4),
+        ],
+        "feed",
+    )
+    return partial, kept
+
+
+def feed_backward(grad, kept, pieces, down):
+    share, depth = down.shape
+    (partial,) = local(
+        feed_back_kernel,
+        (grad, kept, down),
+        pieces,
+        [((ROWS, depth), jnp.bfloat16)],
+        [
+            weight_scratch(pieces, 2 * share),
+            pltpu.VMEM((ROWS, 2 * share), jnp.bfloat16),
+            dma_sems(4),
+        ],
+        "feed_grad",
+    )
+    return partial
+
+
+CHUNK = 128
+
+
+def same_entry(count, slots):
+    row = lax.broadcasted_iota(jnp.int32, (count, count), 0)
+    column = lax.broadcasted_iota(jnp.int32, (count, count), 1)
+    return row // slots == column // slots
+
+
+def gelu(values):
+    return 0.5 * values * (1.0 + lax.erf(values * inv_root_two))
+
+
+def hyper_kernel(
+    slots,
+    pieces,
+    first,
+    second,
+    third,
+    vectors,
+    table,
     heads_out,
-    feed_out,
-    small_out,
-    notes_out,
-    keep_sem,
-    push_send,
-    push_recv,
-    y_send,
-    y_recv,
-    core_send,
-    core_recv,
-    small_send,
-    small_recv,
-    notes_send,
-    notes_recv,
+    mixed_out,
+    middle_out,
+    expanded_out,
+    pooled_out,
+    entered,
+    outcome,
 ):
-    section, partner, across = section_places()
-    wide = lax.axis_index("wide")
-    rank, team = wide // outer, wide % outer
-    depth, rows = query.shape[0], query.shape[1]
-    half = rows // 2
-    mine = pl.ds(pl.multiple_of((section // 2) * half, half), half)
-    q_width = query.shape[2] // TEAM
-
-    def member(k):
-        return {"wide": ((rank + k) % TEAM) * outer + team}
-
-    greet([{"section": partner}, {"section": across}] + [member(k) for k in range(1, TEAM)])
-
-    def pieces(core, target_rank):
-        feed_start, head_start = column_starts(target_rank, gate.shape[2])
-        feed_start = pl.multiple_of(feed_start, LANES)
-        head_start = pl.multiple_of(head_start, LANES)
-        if core == 0:
-            return [
-                (gate, pl.ds(feed_start, span), feed_out, pl.ds(0, span)),
-                (
-                    query,
-                    pl.ds(pl.multiple_of(target_rank * q_width, LANES), q_width),
-                    heads_out,
-                    pl.ds(0, q_width),
-                ),
+    width = pieces.shape[1]
+    count, feed = pieces.shape[0], third.shape[0]
+    head = width // HYPER_HEAD_COUNT
+    flat = pieces[...].astype(jnp.float32)
+    normed, _ = center_norm(flat)
+    entered[...] = (normed * vectors[0:1] + vectors[1:2]).astype(jnp.bfloat16)
+
+    @pl.loop(0, 3 * width // TILE)
+    def _(n):
+        columns = pl.ds(pl.multiple_of(n * TILE, TILE), TILE)
+        heads_out[:, columns] = matmul(entered[...], first[:, columns]).astype(jnp.bfloat16)
+
+    mask = same_entry(CHUNK, slots)
+
+    @pl.loop(0, count // CHUNK)
+    def _(n):
+        rows = pl.ds(pl.multiple_of(n * CHUNK, CHUNK), CHUNK)
+        block = heads_out[rows, :]
+        mixed = []
+        for start in range(0, width, head):
+            query, key, value = (
+                block[:, part * width + start : part * width + start + head] for part in range(3)
+            )
+            weights = attend(query, key, mask, head ** (-0.5))
+            mixed.append(matmul(weights.astype(jnp.bfloat16), value))
+        mixed_out[rows, :] = jnp.concatenate(mixed, axis=1).astype(jnp.bfloat16)
+
+    for start in range(0, width, TILE):
+        columns = pl.ds(start, TILE)
+        middle_out[:, columns] = pieces[:, columns].astype(jnp.float32) + matmul(
+            mixed_out[...], first[:, pl.ds(3 * width + start, TILE)]
+        )
+    normed, _ = center_norm(middle_out[...])
+    entered[...] = (normed * vectors[2:3] + vectors[3:4]).astype(jnp.bfloat16)
+    outcome[...] = middle_out[...]
+
+    @pl.loop(0, feed // TILE)
+    def _(n):
+        start = pl.multiple_of(n * TILE, TILE)
+        columns = pl.ds(pl.multiple_of(4 * width + start, TILE), TILE)
+        expanded = matmul(entered[...], first[:, columns])
+        expanded_out[:, pl.ds(start, TILE)] = expanded
+        outcome[...] += matmul(gelu(expanded).astype(jnp.bfloat16), third[pl.ds(start, TILE), :])
+
+    pooled = jnp.mean(outcome[...].reshape(count // slots, slots, width), axis=1)
+    pooled_out[...] = pooled.astype(jnp.bfloat16)
+
+    @pl.loop(0, table.shape[1] // TILE)
+    def _(n):
+        columns = pl.ds(pl.multiple_of(n * TILE, TILE), TILE)
+        table[:, columns] = matmul(pooled_out[...], second[:, columns]).astype(jnp.bfloat16)
+
+
+def hyper_forward(pieces, slots, params):
+    count, width = pieces.shape
+    first, second, third, vectors = params
+    feed = third.shape[0]
+    depth = second.shape[1] - LANES
+    entries = count // slots
+    table, *stored = local(
+        functools.partial(hyper_kernel, slots),
+        (pieces, *params),
+        (),
+        [
+            ((entries, depth), jnp.bfloat16),
+            ((count, 3 * width), jnp.bfloat16),
+            ((count, width), jnp.bfloat16),
+            ((count, width), jnp.float32),
+            ((count, feed), jnp.float32),
+            ((entries, width), jnp.bfloat16),
+        ],
+        [pltpu.VMEM((count, width), jnp.bfloat16), pltpu.VMEM((count, width), jnp.float32)],
+        "hyper",
+    )
+    return table, stored
+
+
+def hyper_back_kernel(
+    slots,
+    table_grad,
+    pieces,
+    first,
+    second,
+    third,
+    vectors,
+    heads,
+    mixed,
+    middle,
+    expanded,
+    pooled,
+    first_grad,
+    second_grad,
+    third_grad,
+    entered,
+    outcome_low,
+    feed_grad,
+    heads_grad,
+    mixed_grad,
+):
+    width = pieces.shape[1]
+    count, feed = pieces.shape[0], third.shape[0]
+    depth = table_grad.shape[1]
+    head = width // HYPER_HEAD_COUNT
+    scale = head ** (-0.5)
+    grad_low = table_grad[...].astype(jnp.bfloat16)
+    pooled_turned = jnp.transpose(pooled[...].astype(jnp.float32)).astype(jnp.bfloat16)
+
+    for start in range(0, depth, TILE):
+        columns = pl.ds(start, TILE)
+        second_grad[:, columns] = matmul(
+            pooled_turned, grad_low[:, start : start + TILE]
+        ).astype(jnp.bfloat16)
+    pooled_grad = times_trans(grad_low, second[:, pl.ds(0, depth)]) / slots
+    outcome_grad = jnp.broadcast_to(pooled_grad[:, None, :], (count // slots, slots, width))
+    outcome_grad = outcome_grad.reshape(count, width)
+    outcome_low[...] = outcome_grad.astype(jnp.bfloat16)
+    normed, inverse = center_norm(middle[...])
+    entered[...] = jnp.transpose(normed * vectors[2:3] + vectors[3:4]).astype(jnp.bfloat16)
+    feed_grad[...] = jnp.zeros_like(feed_grad)
+
+    @pl.loop(0, feed // TILE)
+    def _(n):
+        start = pl.multiple_of(n * TILE, TILE)
+        tile = pl.ds(start, TILE)
+        columns = pl.ds(pl.multiple_of(4 * width + start, TILE), TILE)
+        values = expanded[:, tile]
+        erf = 0.5 * (1.0 + lax.erf(values * inv_root_two))
+        active = (values * erf).astype(jnp.bfloat16)
+        third_grad[tile, :] = trans_times(active, outcome_low[...]).astype(jnp.bfloat16)
+        active_grad = times_trans(outcome_low[...], third[tile, :])
+        slope = erf + values * jnp.exp(-0.5 * values * values) * inv_root_tau
+        low = (active_grad * slope).astype(jnp.bfloat16)
+        first_grad[:, columns] = matmul(entered[...], low).astype(jnp.bfloat16)
+        feed_grad[...] += times_trans(low, first[:, columns])
+
+    grad = feed_grad[...]
+    scale_two = jnp.sum(grad * normed, axis=0, keepdims=True)
+    shift_two = jnp.sum(grad, axis=0, keepdims=True)
+    middle_grad = outcome_grad + center_back(normed, inverse, grad * vectors[2:3])
+    middle_low = middle_grad.astype(jnp.bfloat16)
+    out_columns = pl.ds(3 * width, width)
+    first_grad[:, out_columns] = trans_times(mixed[...], middle_low).astype(jnp.bfloat16)
+    mixed_grad[...] = times_trans(middle_low, first[:, out_columns]).astype(jnp.bfloat16)
+    mask = same_entry(CHUNK, slots)
+
+    @pl.loop(0, count // CHUNK)
+    def _(n):
+        rows = pl.ds(pl.multiple_of(n * CHUNK, CHUNK), CHUNK)
+        block = heads[rows, :]
+        outer_block = mixed_grad[rows, :]
+        grads = [[], [], []]
+        for start in range(0, width, head):
+            query, key, value = (
+                block[:, part * width + start : part * width + start + head] for part in range(3)
+            )
+            outer = outer_block[:, start : start + head]
+            weights = attend(query, key, mask, scale)
+            weight_grad = times_trans(outer, value)
+            score_grad = weights * (
+                weight_grad - jnp.sum(weights * weight_grad, axis=1, keepdims=True)
+            )
+            score_grad = score_grad.astype(jnp.bfloat16)
+            grads[0].append(matmul(score_grad, key) * scale)
+            grads[1].append(trans_times(score_grad, query) * scale)
+            grads[2].append(trans_times(weights.astype(jnp.bfloat16), outer))
+        for part in range(3):
+            heads_grad[rows, pl.ds(part * width, width)] = jnp.concatenate(
+                grads[part], axis=1
+            ).astype(jnp.bfloat16)
+
+    normed, _ = center_norm(pieces[...].astype(jnp.float32))
+    entered[...] = jnp.transpose(normed * vectors[0:1] + vectors[1:2]).astype(jnp.bfloat16)
+    feed_grad[...] = jnp.zeros_like(feed_grad)
+
+    @pl.loop(0, 3 * width // TILE)
+    def _(n):
+        columns = pl.ds(pl.multiple_of(n * TILE, TILE), TILE)
+        low = heads_grad[:, columns]
+        first_grad[:, columns] = matmul(entered[...], low).astype(jnp.bfloat16)
+        feed_grad[...] += times_trans(low, first[:, columns])
+
+    grad = feed_grad[...]
+    scale_one = jnp.sum(grad * normed, axis=0, keepdims=True)
+    shift_one = jnp.sum(grad, axis=0, keepdims=True)
+    row = lax.broadcasted_iota(jnp.int32, (LANES, width), 0)
+    summed = jnp.zeros((LANES, width), jnp.float32)
+    for n, item in enumerate((scale_one, shift_one, scale_two, shift_two)):
+        summed = jnp.where(row == n, item, summed)
+    second_grad[:, pl.ds(depth, LANES)] = jnp.transpose(summed).astype(jnp.bfloat16)
+
+
+def hyper_backward(pieces, slots, params, stored, table_grad):
+    count, width = pieces.shape
+    first, second, third, _ = params
+    return local(
+        functools.partial(hyper_back_kernel, slots),
+        (table_grad, pieces, *params, *stored),
+        (),
+        [(item.shape, jnp.bfloat16) for item in (first, second, third)],
+        [
+            pltpu.VMEM((width, count), jnp.bfloat16),
+            pltpu.VMEM((count, width), jnp.bfloat16),
+            pltpu.VMEM((count, width), jnp.float32),
+            pltpu.VMEM((count, 3 * width), jnp.bfloat16),
+            pltpu.VMEM((count, width), jnp.bfloat16),
+        ],
+        "hyper_back",
+    )
+
+
+def column_plan(q_columns, kv_columns, ff_columns):
+    share = ff_columns // TEAM
+    edge = share // LANES * LANES
+    tail = share - edge
+    heads = kv_columns // HEAD_DIM
+    q_share = q_columns // TEAM
+    plan = []
+    for rank in range(TEAM):
+        kv = rank * heads // TEAM * HEAD_DIM
+        widths = [
+            (0, rank * q_share, q_share),
+            (1, kv, HEAD_DIM),
+            (2, kv, HEAD_DIM),
+            (3, rank * share, edge),
+            (4, rank * share, edge),
+            (3, rank * share + edge, tail),
+            (4, rank * share + edge, tail),
+        ]
+        moves, start = [], 0
+        for item, source, size in widths:
+            moves.append((item, source, start, size))
+            start += size
+        plan.append(moves)
+    return plan, start
+
+
+def pack_kernel(plan, rows, *refs):
+    sources, targets = refs[:5], refs[5:7]
+    blocks, sem = refs[7:12], refs[12]
+    section = lax.axis_index("section")
+    mine = pl.ds(pl.multiple_of(section * rows, rows), rows)
+    copies = [
+        [
+            pltpu.make_async_copy(source.at[layer, mine], block.at[layer], sem.at[layer, n])
+            for n, (source, block) in enumerate(zip(sources, blocks))
+        ]
+        for layer in range(2)
+    ]
+    for layer in range(2):
+        for copy in copies[layer]:
+            copy.start()
+    for layer in range(2):
+        for copy in copies[layer]:
+            copy.wait()
+        for rank, moves in enumerate(plan):
+            parts = [
+                blocks[item][layer, :, source : source + size] for item, source, _, size in moves
             ]
-        return [
-            (up, pl.ds(feed_start, span), feed_out, pl.ds(span, span)),
-            (key, pl.ds(head_start, LANES), heads_out, pl.ds(q_width, LANES)),
-            (value, pl.ds(head_start, LANES), heads_out, pl.ds(q_width + LANES, LANES)),
-        ]
-
-    for k in range(1, TEAM):
-        remote(
-            small, small_out.at[rank], small_send.at[k], small_recv.at[k], member(k)
-        ).start()
-        remote(
-            notes, notes_out.at[rank], notes_send.at[k], notes_recv.at[k], member(k)
-        ).start()
-    small_keep = pltpu.make_async_copy(small, small_out.at[rank], keep_sem.at[2])
-    notes_keep = pltpu.make_async_copy(notes, notes_out.at[rank], keep_sem.at[3])
-    small_keep.start()
-    notes_keep.start()
-
-    total = span + q_width
-
-    def layer_bytes(layer, semaphores):
-        block = feed_out.at[layer, :, :, pl.ds(0, total)]
-        return pltpu.make_async_copy(block, block, semaphores.at[layer])
-
-    def all_moves(core):
-        def keep(layer):
-            return [
-                pltpu.make_async_copy(
-                    source.at[layer, mine, columns],
-                    target.at[layer, rank, mine, to],
-                    keep_sem.at[layer],
-                )
-                for source, columns, target, to in pieces(core, rank)
-            ]
-
-        def push(layer, k):
-            return [
-                remote(
-                    source.at[layer, mine, columns],
-                    target.at[layer, rank, mine, to],
-                    push_send.at[layer, k],
-                    push_recv.at[layer, k],
-                    member(k),
-                )
-                for source, columns, target, to in pieces(core, (rank + k) % TEAM)
-            ]
-
-        def over(layer, k):
-            origin = (rank + TEAM - k) % TEAM
-            return [
-                remote(
-                    target.at[layer, origin, mine, to],
-                    target.at[layer, origin, mine, to],
-                    y_send.at[layer, k],
-                    y_recv.at[layer, k],
-                    {"section": across},
-                )
-                for _, _, target, to in pieces(core, rank)
-            ]
-
-        def on(layer):
-            return [
-                remote(
-                    target.at[layer, :, :, to],
-                    target.at[layer, :, :, to],
-                    core_send.at[layer],
-                    core_recv.at[layer],
-                    {"section": partner},
-                )
-                for _, _, target, to in pieces(core, rank)
-            ]
-
-        def bytes_of(semaphore):
-            block = gate.at[0, mine, pl.ds(0, total)]
-            return pltpu.make_async_copy(block, block, semaphore)
-
-        order = (4, 3, 5, 2, 6, 1, 7)
-        for layer in range(depth):
-            for copy in keep(layer):
-                copy.start()
-            for k in order:
-                for copy in push(layer, k):
-                    copy.start()
-        for layer in range(depth):
-            bytes_of(keep_sem.at[layer]).wait()
-            for copy in over(layer, 0):
-                copy.start()
-            for k in order[::-1]:
-                bytes_of(push_recv.at[layer, k]).wait()
-                for copy in over(layer, k):
-                    copy.start()
-        for layer in range(depth):
-            for k in range(TEAM):
-                bytes_of(y_recv.at[layer, k]).wait()
-            for copy in on(layer):
-                copy.start()
-        for layer in range(depth):
-            layer_bytes(layer, core_send).wait()
-            for k in range(TEAM):
-                bytes_of(y_send.at[layer, k]).wait()
-                if k:
-                    bytes_of(push_send.at[layer, k]).wait()
-
-    core = section % 2
-
-    @pl.when(core == 0)
-    def _():
-        all_moves(0)
-
-    @pl.when(core == 1)
-    def _():
-        all_moves(1)
-
-    for layer in range(depth):
-        layer_bytes(layer, core_recv).wait()
-    small_keep.wait()
-    notes_keep.wait()
-    for k in range(1, TEAM):
-        remote(small, small_out.at[rank], small_send.at[k], small_recv.at[k], member(k)).wait()
-        remote(notes, notes_out.at[rank], notes_send.at[k], notes_recv.at[k], member(k)).wait()
-
-
-def reshard(outer, collective_id, query, key, value, gate, up, small, notes):
-    depth, rows = query.shape[:2]
-    share = gate.shape[2] // TEAM
-    span = -(-(share + LANES // 2) // LANES) * LANES
-    heads_width = query.shape[2] // TEAM + 2 * LANES
+            heads = jnp.concatenate(parts[1:3], axis=1)
+            ends = jnp.concatenate(parts[5:7], axis=1)
+            for part, start in zip(
+                (parts[0], heads, parts[3], parts[4], ends),
+                (moves[0][2], moves[1][2], moves[3][2], moves[4][2], moves[5][2]),
+            ):
+                if part.shape[1]:
+                    targets[layer][rank, :, start : start + part.shape[1]] = part
+
+
+def pack(weights):
+    rows = weights[0].shape[1] // SECTIONS
+    plan, width = column_plan(weights[0].shape[2], weights[1].shape[2], weights[3].shape[2])
+    if rows % 16:
+        section = lax.axis_index("section")
+        mine = [lax.dynamic_slice_in_dim(item, section * rows, rows, 1) for item in weights]
+        return tuple(
+            jnp.stack(
+                [
+                    jnp.concatenate(
+                        [mine[item][layer, :, at : at + size] for item, at, _, size in moves], axis=1
+                    )
+                    for moves in plan
+                ]
+            )
+            for layer in range(2)
+        )
     return pl.pallas_call(
-        functools.partial(reshard_kernel, outer, span),
-        out_shape=(
-            jax.ShapeDtypeStruct((depth, TEAM, rows, heads_width), jnp.bfloat16),
-            jax.ShapeDtypeStruct((depth, TEAM, rows, 2 * span), jnp.bfloat16),
-            jax.ShapeDtypeStruct((TEAM,) + small.shape, small.dtype),
-            jax.ShapeDtypeStruct((TEAM,) + notes.shape, notes.dtype),
-        ),
-        in_specs=[ANYWHERE] * 7,
-        out_specs=(ANYWHERE,) * 4,
-        scratch_shapes=[dma_sems(4)]
-        + [dma_sems(depth, TEAM)] * 4
-        + [dma_sems(depth)] * 2
-        + [dma_sems(TEAM)] * 4,
-        compiler_params=settings(collective_id),
-        name="reshard",
-    )(query, key, value, gate, up, small, notes)
+        functools.partial(pack_kernel, plan, rows),
+        out_shape=(jax.ShapeDtypeStruct((TEAM, rows, width), jnp.bfloat16),) * 2,
+        in_specs=[ANYWHERE] * 5,
+        out_specs=(IN_VMEM,) * 2,
+        scratch_shapes=[pltpu.VMEM((2, rows, item.shape[2]), jnp.bfloat16) for item in weights]
+        + [dma_sems(2, 5)],
+        compiler_params=pltpu.CompilerParams(vmem_limit_bytes=VMEM_LIMIT),
+        name="pack",
+    )(*weights)
+
+
 def team_groups(wides, outer):
     return [[rank * outer + team for team in range(outer)] for rank in range(wides // outer)]
 
 
-def turn(values, cosines, sines):
-    halfway = values.shape[-1] // 2
-    turned = jnp.concatenate([-values[..., halfway:], values[..., :halfway]], axis=-1)
-    return values * cosines[None, :, None, :] + turned * sines[None, :, None, :]
-
-
-def attention_forward(normed, heads_weight, out_weight, offset, cosines, sines):
-    width = HEAD_DIM
-    rows = normed.shape[0] // LEN
-    q_width = out_weight.shape[0]
-    shared = q_width // width
-    projected = matmul(normed, heads_weight)
-    query_pre = projected[:, :q_width].reshape(rows, LEN, shared, width)
-    key_pre = lax.dynamic_slice_in_dim(projected[:, q_width : q_width + LANES], offset, width, 1)
-    value_rows = lax.dynamic_slice_in_dim(projected[:, q_width + LANES :], offset, width, 1)
-    queries = turn(query_pre, cosines, sines).astype(jnp.bfloat16)
-    key_rows = turn(key_pre.reshape(rows, LEN, 1, width), cosines, sines)[:, :, 0]
-    key_rows = key_rows.astype(jnp.bfloat16)
-    value_rows = value_rows.astype(jnp.bfloat16).reshape(rows, LEN, width)
-    causal = jnp.arange(LEN)[:, None] >= jnp.arange(LEN)[None, :]
-    scores = jnp.einsum(
-        "blgd,bmd->bglm", queries, key_rows, preferred_element_type=jnp.float32
-    ) * width ** (-0.5)
-    scores = jnp.where(causal, scores, -1e30)
-    weights_full = jax.nn.softmax(scores, axis=-1)
-    weights_low = weights_full.astype(jnp.bfloat16)
-    mixed = jnp.einsum("bglm,bmd->blgd", weights_low, value_rows, preferred_element_type=jnp.float32)
-    mixed = mixed.astype(jnp.bfloat16).reshape(rows * LEN, q_width)
-    partial = matmul(mixed, out_weight).astype(jnp.bfloat16)
-    return partial, (queries, key_rows, value_rows, weights_full, weights_low)
-
-
-def attention_backward(grad, stored, heads_weight, out_weight, offset, cosines, sines):
-    queries, key_rows, value_rows, weights_full, weights_low = stored
-    rows, _, shared, width = queries.shape
-    count = rows * LEN
-    scale = width ** (-0.5)
-    mixed_grad = times_trans(grad, out_weight).astype(jnp.bfloat16).reshape(queries.shape)
-    weight_grad = jnp.einsum(
-        "blgd,bmd->bglm", mixed_grad, value_rows, preferred_element_type=jnp.float32
-    )
-    value_grad = jnp.einsum(
-        "bglm,blgd->bmd", weights_low, mixed_grad, preferred_element_type=jnp.float32
-    )
-    score_grad = weights_full * (
-        weight_grad - jnp.sum(weights_full * weight_grad, axis=-1, keepdims=True)
-    )
-    score_grad = score_grad.astype(jnp.bfloat16)
-    query_grad = (
-        jnp.einsum("bglm,bmd->blgd", score_grad, key_rows, preferred_element_type=jnp.float32)
-        * scale
-    )
-    key_grad = (
-        jnp.einsum("bglm,blgd->bmd", score_grad, queries, preferred_element_type=jnp.float32)
-        * scale
-    )
-    query_low = turn(query_grad, cosines, -sines).astype(jnp.bfloat16).reshape(count, -1)
-    key_low = turn(key_grad[:, :, None], cosines, -sines).astype(jnp.bfloat16)
-    blank = jnp.zeros((count, LANES), jnp.bfloat16)
-    key_low = lax.dynamic_update_slice_in_dim(blank, key_low.reshape(count, width), offset, 1)
-    value_low = value_grad.astype(jnp.bfloat16).reshape(count, width)
-    value_low = lax.dynamic_update_slice_in_dim(blank, value_low, offset, 1)
-    all_low = jnp.concatenate([query_low, key_low, value_low], axis=1)
-    return times_trans(all_low, heads_weight).astype(jnp.bfloat16)
-
-
-def feed_forward(normed, feed_weight, down_weight, offset):
-    span = feed_weight.shape[1] // 2
-    share = down_weight.shape[0]
-    both = matmul(normed, feed_weight)
-    gate_pre = lax.dynamic_slice_in_dim(both[:, :span], offset, share, 1)
-    up_pre = lax.dynamic_slice_in_dim(both[:, span:], offset, share, 1)
-    activated = (jax.nn.silu(gate_pre) * up_pre).astype(jnp.bfloat16)
-    return matmul(activated, down_weight).astype(jnp.bfloat16), (gate_pre, up_pre)
-
-
-def feed_backward(grad, stored, feed_weight, down_weight, offset):
-    gate_pre, up_pre = stored
-    span = feed_weight.shape[1] // 2
-    activated_grad = times_trans(grad, down_weight)
-    gate_sig = jax.nn.sigmoid(gate_pre)
-    gate_grad = activated_grad * up_pre * gate_sig * (1.0 + gate_pre * (1.0 - gate_sig))
-    up_grad = activated_grad * gate_pre * gate_sig
-    blank = jnp.zeros((grad.shape[0], 2 * span), jnp.bfloat16)
-    both = lax.dynamic_update_slice_in_dim(blank, gate_grad.astype(jnp.bfloat16), offset, 1)
-    both = lax.dynamic_update_slice_in_dim(both, up_grad.astype(jnp.bfloat16), span + offset, 1)
-    return times_trans(both, feed_weight).astype(jnp.bfloat16)
+SWAP_Y = [(source, (source + 2) % SECTIONS) for source in range(SECTIONS)]
+SWAP_CORE = [(source, source + 1 - 2 * (source % 2)) for source in range(SECTIONS)]
+
+
+def together(*items):
+    return lax.optimization_barrier(items)
+
+
+def all_teams(pieces, outer, groups):
+    if outer == 1:
+        return pieces
+    pieces = [
+        lax.all_gather(piece, "wide", axis=1, axis_index_groups=groups) for piece in pieces
+    ]
+    return [piece.reshape((-1,) + piece.shape[2:]) for piece in pieces]
 
 
 def shards(
@@ -1264,76 +1431,53 @@
     model_width = embed_map.shape[1]
     total_tokens = wides * MB * LEN
 
-    owned = query_map.shape[0]
+    rank_groups = [[rank * outer + team for rank in range(TEAM)] for team in range(outer)]
+
+    def to_ranks(block):
+        return lax.all_to_all(
+            block, "wide", 0, 0, axis_index_groups=rank_groups if outer > 1 else None, tiled=True
+        )
+
+    blocks = pack((query_weight, key_weight, value_weight, gate_weight, up_weight))
+    own_one = to_ranks(blocks[0])
+
     vectors = jnp.stack([prenorm_gain, prenorm_bias, midnorm_gain, midnorm_bias], axis=1)
     vectors = jnp.pad(vectors, ((0, 0), (0, LANES - 4)))
     first = jnp.concatenate([query_map, key_map, value_map, output_map, expand_map], axis=1)
     second = jnp.concatenate([embed_map, vectors], axis=1)
-    first, second, third = spread(
-        1,
-        wides,
-        (first.astype(jnp.bfloat16), second.astype(jnp.bfloat16), reduce_map.astype(jnp.bfloat16)),
-    )
-    first = first.reshape(hyper_width, -1)
-    second = second.reshape(hyper_width, -1)
-    reduce_low = third.reshape(hyper_feed, hyper_width)
-    query_low, key_low, value_low, output_low = (
-        first[:, n * hyper_width : (n + 1) * hyper_width] for n in range(4)
-    )
-    expand_low = first[:, 4 * hyper_width :]
-    embed_low = second[:, :model_width]
-    gain_one, bias_one, second_gain, bias_two = (second[:, model_width + n] for n in range(4))
-    params = (
-        gain_one,
-        bias_one,
-        query_low,
-        key_low,
-        value_low,
-        output_low,
-        second_gain,
-        bias_two,
-        expand_low,
-        reduce_low,
-        embed_low,
-    )
-
     gains = jnp.concatenate([attention_gain, feed_gain], axis=0)
     gains = jnp.pad(gains, ((0, 16 - gains.shape[0]), (0, 0)))
     notes = jnp.concatenate([token_ids.reshape(1, -1), targets.reshape(1, -1)], axis=0)
     notes = jnp.pad(notes, ((0, 6), (0, 0)))
-    heads_all, feed_all, gains, notes = reshard(
+    first, second, third, gains, notes = spread(
+        1,
+        wides,
         outer,
-        2,
-        query_weight,
-        key_weight,
-        value_weight,
-        gate_weight,
-        up_weight,
-        gains,
-        notes,
-    )
+        (first.astype(jnp.bfloat16), second.astype(jnp.bfloat16), reduce_map.astype(jnp.bfloat16)),
+        (gains, notes),
+    )
+    first, own_one, block = together(first, own_one, blocks[1])
+    own_two = to_ranks(block)
+    y_one = lax.ppermute(own_one, "section", SWAP_Y)
+    core_one = lax.ppermute(own_one, "section", SWAP_CORE)
+    first = first.reshape(hyper_width, -1)
+    second = second.reshape(hyper_width, -1)
+    third = third.reshape(hyper_feed, hyper_width)
+    vectors = second[:, model_width : model_width + 8].astype(jnp.float32).T
+    params = (first, second, third, vectors)
     if outer > 1:
-        heads_all, feed_all = (
-            lax.all_gather(item, "wide", axis=2, axis_index_groups=groups)
-            for item in (heads_all, feed_all)
-        )
         gains = lax.all_gather(gains, "wide", axis=1, axis_index_groups=groups)
         gains = gains.reshape(-1, gains.shape[2], gains.shape[3])
         output_weight, down_weight = (
             lax.all_gather(item, "wide", axis=1, axis_index_groups=groups, tiled=True)
             for item in (output_weight, down_weight)
         )
-    heads_all = heads_all.reshape(2, model_width, -1)
-    feed_all = feed_all.reshape(2, model_width, -1)
     gains = gains.astype(jnp.float32).transpose(1, 0, 2).reshape(-1, 1, model_width)
     attention_gains, feed_gains = gains[:2], gains[2:4]
     final_scale = final_gain.astype(jnp.float32).reshape(1, model_width)
     notes = lax.dynamic_slice_in_dim(notes, section_index * 2, 2, 0)
     ids, wanted = notes[:, 0].reshape(-1), notes[:, 1].reshape(-1)
-    share = down_weight.shape[1]
-    feed_offset = rank * share % LANES
-    head_offset = rank // 2 % 2 * HEAD_DIM
-    cosines, sines = rope_tables(LEN, HEAD_DIM)
+    tables, back_tables = turn_tables(False), turn_tables(True)
 
     entries, slot_count = slot_ids.shape
     group_hits = (
@@ -1341,14 +1485,14 @@
     ).astype(jnp.int32)
     row_start = jnp.sum(group_hits * group_offsets[None, :], axis=1)
     piece_rows = (row_start[:, None] + slot_ids).reshape(-1)
-    pieces = (
-        jnp.take(piece_table, piece_rows, axis=0)
-        .astype(jnp.float32)
-        .reshape(entries, slot_count, hyper_width)
-    )
-    table_shard, hyper_stored = hyper_forward(pieces, params, HYPER_HEAD_COUNT)
-
+    pieces = jnp.take(piece_table, piece_rows, axis=0)
+    table_shard, hyper_stored = hyper_forward(pieces, slot_count, params)
+    table_shard, y_one = together(table_shard, y_one)
+    beyond_one = lax.ppermute(y_one, "section", SWAP_CORE)
     table_rows = section_gather(3, table_shard)
+    table_rows, own_two = together(table_rows, own_two)
+    y_two = lax.ppermute(own_two, "section", SWAP_Y)
+    core_two = lax.ppermute(own_two, "section", SWAP_CORE)
     if outer > 1:
         table_rows = lax.all_gather(table_rows, "wide", axis=1, axis_index_groups=groups)
     table_rows = table_rows.reshape(-1, model_width)
@@ -1362,23 +1506,22 @@
     injected = matmul(hits, table_rows).astype(jnp.bfloat16)
     normed, hidden = fold(inject, outer, 4, injected, (attention_gains[0],), (jnp.bfloat16,))
 
+    weights = [all_teams((own_one, y_one, core_one, beyond_one), outer, groups)]
     kept = []
     for layer in range(2):
-        heads_weight, feed_weight = heads_all[layer], feed_all[layer]
         partial, attended = attention_forward(
-            normed.reshape(ROWS, model_width),
-            heads_weight,
-            output_weight[layer],
-            head_offset,
-            cosines,
-            sines,
+            normed.reshape(ROWS, model_width), weights[layer], Layer(output_weight, layer), tables
         )
         normed, middle = fold(
             enter_feed, outer, 5, partial, (hidden, feed_gains[layer]), (jnp.float32,)
         )
         partial, fed = feed_forward(
-            normed.reshape(ROWS, model_width), feed_weight, down_weight[layer], feed_offset
-        )
+            normed.reshape(ROWS, model_width), weights[layer], Layer(down_weight, layer)
+        )
+        if layer == 0:
+            partial, y_two = together(partial, y_two)
+            beyond_two = lax.ppermute(y_two, "section", SWAP_CORE)
+            weights.append(all_teams((own_two, y_two, core_two, beyond_two), outer, groups))
         kept.append((hidden, attended, middle, fed))
         next_gain = attention_gains[1] if layer == 0 else final_scale
         normed, hidden = fold(
@@ -1407,10 +1550,9 @@
     )
 
     for layer in (1, 0):
-        heads_weight, feed_weight = heads_all[layer], feed_all[layer]
         hidden, attended, middle, fed = kept[layer]
         partial = feed_backward(
-            grads.reshape(ROWS, model_width), fed, feed_weight, down_weight[layer], feed_offset
+            grads.reshape(ROWS, model_width), fed, weights[layer], Layer(down_weight, layer)
         )
         grads, middle_grad = fold(
             feed_back, outer, 9, partial, (outer_grad, middle, feed_gains[layer]), (jnp.float32,)
@@ -1418,11 +1560,9 @@
         partial = attention_backward(
             grads.reshape(ROWS, model_width),
             attended,
-            heads_weight,
-            output_weight[layer],
-            head_offset,
-            cosines,
-            sines,
+            weights[layer],
+            Layer(output_weight, layer),
+            back_tables,
         )
         grads, outer_grad = fold(
             layer_back,
@@ -1450,28 +1590,9 @@
         11, table_part.reshape(SECTIONS, entries, model_width), loss_block
     )
     mean_loss = loss_block[0, 0]
-    (
-        grad_prescale,
-        prenorm_bias_gradient,
-        grad_query,
-        grad_key,
-        grad_value,
-        grad_output,
-        grad_midscale,
-        grad_midshift,
-        grad_expand,
-        grad_reduce,
-        grad_embed,
-    ) = hyper_backward(params, hyper_stored, table_grad)
-    vectors = jnp.stack(
-        [grad_prescale, prenorm_bias_gradient, grad_midscale, grad_midshift], axis=1
-    )
-    vectors = jnp.pad(vectors, ((0, 0), (0, LANES - 4)))
-    first = jnp.concatenate([grad_query, grad_key, grad_value, grad_output, grad_expand], axis=1)
-    second = jnp.concatenate([grad_embed, vectors], axis=1)
+    grads = hyper_backward(pieces, slot_count, params, hyper_stored, table_grad)
     first, second, third = (
-        item.astype(jnp.bfloat16).reshape(SECTIONS, wides, -1, item.shape[1])
-        for item in (first, second, grad_reduce)
+        item.reshape(SECTIONS, wides, -1, item.shape[1]) for item in grads
     )
     first, second, third = collect(12, (first, second, third))
     grad_query, grad_key, grad_value, grad_output = (

time: 941 us -> 771 us (0.82)
  matrix products: 144 us -> 9.23 us
  local copies, waits for them, and re-layouts: 92.8 us -> 23 us
  Pallas kernels: 669 us -> 699 us
  starting transfers between devices: 0 us -> 19.8 us
  other arithmetic: 17.9 us -> 6.73 us
    dot_general x16 -> x1, matrix products: 49.7 us -> 1.8 us  [times_trans(): lax.dot_general(former, latter, (((1,), (1,)), ((), ())), preferred_eleme...]
    pallas_call x2 -> x12, Pallas kernels: 190 us -> 236 us  [the longest x10 145 us: local(): pl.pallas_call(kernel, grid=(1,), out_shape=tuple((jax.ShapeDtypeStruct(s...]
    dot_general x17 -> x2, matrix products: 49.1 us -> 4.27 us  [matmul(): return jnp.dot(former, latter, preferred_element_type=jnp.float32)]
    dynamic_update_slice x8 -> x0, local copies, waits for them, and re-layouts: 21.1 us -> none  [the longest x2 10.5 us: feed_backward(): lax.dynamic_update_slice_in_dim(blank, gate_grad.astype(jnp.bfloat16), of...]
    dot_general x15 -> x0, matrix products: 21 us -> none  [the longest x1 3.03 us: hyper_backward(): jnp.einsum('eshd,ethd->ehst', mixed_grad, value_rows, preferred_element_t...]
    reshape x25 -> x0, local copies, waits for them, and re-layouts: 18.9 us -> none  [the longest x2 4.66 us: hyper_backward(): value_grad.astype(jnp.bfloat16).reshape(entries * slot_count, model_width)]
    pallas_call x10, Pallas kernels: 390 us -> 371 us  [fold(): pl.pallas_call(functools.partial(fold_kernel, finish, outer, 1 + len(extr...]
    all_to_all x0 -> x2, starting transfers between devices: none -> 17.3 us  [to_ranks(): lax.all_to_all(block, 'wide', 0, 0, axis_index_groups=rank_groups if oute...]
  transfers between devices with their start and end apart: 0 -> 8, of which waited for: 0 -> 1; matrix products, arithmetic and copies ran while one was open for 0% -> 2% of each run, Pallas kernels for 0% -> 35%
where the time goes in v2:
time: 771 us; the launch traced here: 764 us
  Pallas kernels  699 us (91%)
  local copies, waits for them, and re-layouts  23 us (3%)
  starting transfers between devices  19.8 us (3%)
  matrix products  9.23 us (1%)
    pallas_call x10, Pallas kernels, fold(): pl.pallas_call(functools.partial(fold_kernel, finish, outer, 1 + len(extr...  371 us
    pallas_call x10, Pallas kernels, local(): pl.pallas_call(kernel, grid=(1,), out_shape=tuple((jax.ShapeDtypeStruct(s...  145 us
    pallas_call x1, Pallas kernels, spread(): pl.pallas_call(functools.partial(spread_kernel, count, halves, outer), ou...  87.8 us
    pallas_call x1, Pallas kernels, collect(): pl.pallas_call(functools.partial(collect_kernel, count, halves), out_shap...  58.7 us
    all_to_all x2, starting transfers between devices, to_ranks(): lax.all_to_all(block, 'wide', 0, 0, axis_index_groups=rank_groups if oute...  17.3 us
  transfers between devices with their start and end apart: 8, of which 1 were waited for; matrix products, arithmetic and copies ran while one was open for 2% of the time, Pallas kernels for 35%

profile of v2, /device:TPU:0, one launch (start us, length us, event | category | flops | bytes accessed | tf_op | source)
XLA Modules:
  0.0 764.0 jit_solution(5694890403388380499)
XLA Ops:
  0.6 4.0 pack.1
  4.8 7.4 all-to-all-start
  15.9 87.8 %spread.1 = (bf16[4,8,16,4096]{3,2,1,0:T(8,128)(2,1)}, bf16[4,8,16,2176]{3,2,1,0:T(8,128)(2,1)}, bf16[4,8,64,512]{3,2,1,0:T(8,128)(2,1)}, bf16[8,16,256]{2,1,0:T(8,128)(2,1)}, s32[8,8,128]{2,1,0:T(8,128)}) custom-call(bf16[16,4096]{1,0:T(8,128)(2,1)} %copy-done.5, bf16[16,2176]{1,0:T(8,128)(2,1)} %fusion.12.refs_1_, ...), custom_call_target="tpu_custom_call" | custom-call | tf_op jit(solution)/shard_map/spread/pallas_call | solution.py:568
  103.7 9.9 %all-to-all-start.1 = ((bf16[8,64,1792]{2,1,0:T(8,128)(2,1)}), bf16[8,64,1792]{2,1,0:T(8,128)(2,1)}, u32[]{:S(2)}, u32[]{:S(2)}) async-start(bf16[8,64,1792]{2,1,0:T(8,128)(2,1)} %get-tuple-element.81), calls=%async_computation.1 | async-start | bytes 3670016 | tf_op jit(solution)/shard_map/all_to_all | solution.py:1437
  113.7 1.6 collective-permute-start
  115.6 0.9 slice.103
  116.8 4.7 gather_fusion
  122.4 1.0 broadcast_select_fusion.pieces
  123.4 28.4 %hyper.1 = (bf16[64,2048]{1,0:T(8,128)(2,1)}, bf16[512,1536]{1,0:T(8,128)(2,1)}, bf16[512,512]{1,0:T(8,128)(2,1)}, f32[512,512]{1,0:T(8,128)}, f32[512,2048]{1,0:T(8,128)}, /*index=5*/bf16[64,512]{1,0:T(8,128)(2,1)}) custom-call(bf16[512,512]{1,0:T(8,128)(2,1)} %broadcast_select_fusion.pieces, bf16[512,4096]{1,0:T(8,128)(2,1)} %bitcast.105, ...), custom_call_target="tpu_custom_call" | custom-call | tf_op jit(solution)/shard_map/hyper/pallas_call | solution.py:967
  151.8 4.1 collective-permute-done.other_y
  155.9 10.6 %section_gather.1 = bf16[4,64,2048]{2,1,0:T(8,128)(2,1)} custom-call(bf16[64,2048]{1,0:T(8,128)(2,1)} %get-tuple-element.80.block), custom_call_target="tpu_custom_call" | custom-call | tf_op jit(solution)/shard_map/section_gather/pallas_call | solution.py:330
  167.4 0.8 constant_dynamic-slice_fusion.1
  169.3 2.8 convolution_convert_fusion.1
  172.0 39.8 %inject.1 = (bf16[8,32,2048]{2,1,0:T(8,128)(2,1)}, bf16[32,2048]{1,0:T(8,128)(2,1)}) custom-call(bf16[8,32,2048]{2,1,0:T(8,128)(2,1)} %bitcast.124, f32[1,2048]{1,0:T(1,128)} %bitcast.146), custom_call_target="tpu_custom_call" | custom-call | tf_op jit(solution)/shard_map/inject/pallas_call | solution.py:208
  211.9 1.0 tile.8
  212.8 7.4 attention.2
  220.2 40.5 %enter_feed.2 = (bf16[8,32,2048]{2,1,0:T(8,128)(2,1)}, f32[32,2048]{1,0:T(8,128)}) custom-call(bf16[8,32,2048]{2,1,0:T(8,128)(2,1)} %bitcast.140, bf16[32,2048]{1,0:T(8,128)(2,1)} %get-tuple-element.87.refs_1_.refs_2_, f32[1,2048]{1,0:T(1,128)} %bitcast.148), custom_call_target="tpu_custom_call" | custom-call | tf_op jit(solution)/shard_map/enter_feed/pallas_call | solution.py:208
  260.8 13.3 %feed.2 = (bf16[256,2048]{1,0:T(8,128)(2,1)}, f32[256,1408]{1,0:T(8,128)}) custom-call(bf16[256,2048]{1,0:T(8,128)(2,1)} %bitcast.135, bf16[2,704,2048]{2,1,0:T(8,128)(2,1)} %down.7, bf16[8,64,1792]{2,1,0:T(8,128)(2,1)} %copy-done, bf16[8,64,1792]{2,1,0:T(8,128)(2,1)} %collective-permute-done.other_y, ...), custom_call_target="tpu_custom_call" | custom-call | tf_op jit(solution)/shard_map/feed/pallas_call | solution.py:967
  274.7 42.3 %leave_layer.2 = (bf16[8,32,2048]{2,1,0:T(8,128)(2,1)}, bf16[32,2048]{1,0:T(8,128)(2,1)}) custom-call(bf16[8,32,2048]{2,1,0:T(8,128)(2,1)} %bitcast.137, f32[32,2048]{1,0:T(8,128)} %get-tuple-element.92.refs_1_.refs_2_, f32[1,2048]{1,0:T(1,128)} %bitcast.150), custom_call_target="tpu_custom_call" | custom-call | tf_op jit(solution)/shard_map/leave_layer/pallas_call | solution.py:208
  317.1 1.2 copy-done.1
  318.8 7.4 attention.3
  326.3 39.2 %enter_feed.3 = (bf16[8,32,2048]{2,1,0:T(8,128)(2,1)}, f32[32,2048]{1,0:T(8,128)}) custom-call(bf16[8,32,2048]{2,1,0:T(8,128)(2,1)} %bitcast.139, bf16[32,2048]{1,0:T(8,128)(2,1)} %get-tuple-element.96.refs_1_.refs_2_, f32[1,2048]{1,0:T(1,128)} %bitcast.152), custom_call_target="tpu_custom_call" | custom-call | tf_op jit(solution)/shard_map/enter_feed/pallas_call | solution.py:208
  365.5 13.3 %feed.3 = (bf16[256,2048]{1,0:T(8,128)(2,1)}, f32[256,1408]{1,0:T(8,128)}) custom-call(bf16[256,2048]{1,0:T(8,128)(2,1)} %bitcast.136, bf16[2,704,2048]{2,1,0:T(8,128)(2,1)} %down.7, bf16[8,64,1792]{2,1,0:T(8,128)(2,1)} %all-to-all-done.1.own, bf16[8,64,1792]{2,1,0:T(8,128)(2,1)} %collective-permute-done.3.other_y, bf16[8,64,1792]{2,1,0:T(8,128)(2,1)} %copy-done.1, ...), custom_call_target="tpu_custom_call" | custom-call | tf_op jit(solution)/shard_map/feed/pallas_call | solution.py:967
  378.8 37.8 %leave_layer.3 = (bf16[8,32,2048]{2,1,0:T(8,128)(2,1)}, bf16[32,2048]{1,0:T(8,128)(2,1)}) custom-call(bf16[8,32,2048]{2,1,0:T(8,128)(2,1)} %bitcast.138, f32[32,2048]{1,0:T(8,128)} %get-tuple-element.99.refs_1_.refs_2_, f32[1,2048]{1,0:T(1,128)} %bitcast.144), custom_call_target="tpu_custom_call" | custom-call | tf_op jit(solution)/shard_map/leave_layer/pallas_call | solution.py:208
  416.6 1.8 fusion.27
  419.2 9.6 %team_gather.1 = f32[8,8,256]{2,1,0:T(8,128)} custom-call(f32[8,256]{1,0:T(8,128)} %stack.89.block), custom_call_target="tpu_custom_call" | custom-call | tf_op jit(solution)/shard_map/team_gather/pallas_call | solution.py:290
  428.8 1.0 slice_reduce_fusion.4
  430.4 1.5 convolution_convert_fusion
  432.4 34.5 %head_back.1 = (bf16[8,32,2048]{2,1,0:T(8,128)(2,1)}, bf16[32,2048]{1,0:T(8,128)(2,1)}) custom-call(bf16[8,32,2048]{2,1,0:T(8,128)(2,1)} %bitcast.121, bf16[32,2048]{1,0:T(8,128)(2,1)} %get-tuple-element.101.refs_1_, f32[1,2048]{1,0:T(1,128)} %bitcast.145), custom_call_target="tpu_custom_call" | custom-call | tf_op jit(solution)/shard_map/head_back/pallas_call | solution.py:208
  466.9 9.5 %feed_grad.2 = bf16[256,2048]{1,0:T(8,128)(2,1)} custom-call(bf16[256,2048]{1,0:T(8,128)(2,1)} %bitcast.134, f32[256,1408]{1,0:T(8,128)} %get-tuple-element.103.kept, bf16[2,704,2048]{2,1,0:T(8,128)(2,1)} %down.7, bf16[8,64,1792]{2,1,0:T(8,128)(2,1)} %all-to-all-done.1.own, bf16[8,64,1792]{2,1,0:T(8,128)(2,1)} %collective-permute-done.3.other_y, ...), custom_call_target="tpu_custom_call" | custom-call | tf_op jit(solution)/shard_map/feed_grad/pallas_call | solution.py:967
  476.4 35.3 %feed_back.2 = (bf16[8,32,2048]{2,1,0:T(8,128)(2,1)}, f32[32,2048]{1,0:T(8,128)}) custom-call(bf16[8,32,2048]{2,1,0:T(8,128)(2,1)} %bitcast.122, bf16[32,2048]{1,0:T(8,128)(2,1)} %get-tuple-element.104.refs_1_, f32[32,2048]{1,0:T(8,128)} %get-tuple-element.99.refs_1_.refs_2_, f32[1,2048]{1,0:T(1,128)} %bitcast.153), custom_call_target="tpu_custom_call" | custom-call | tf_op jit(solution)/shard_map/feed_back/pallas_call | solution.py:208
  511.8 1.0 tile.20
  512.8 8.3 %attention_grad.2 = bf16[256,2048]{1,0:T(8,128)(2,1)} custom-call(bf16[256,2048]{1,0:T(8,128)(2,1)} %bitcast.131, bf16[256,256]{1,0:T(8,128)(2,1)} %get-tuple-element.106.queries, bf16[256,128]{1,0:T(8,128)(2,1)} %get-tuple-element.107.pairs, bf16[2,256,2048]{2,1,0:T(8,128)(2,1)} %out_weight.7, f32[6,256,128]{2,1,0:T(8,128)} %bitcast.115, ...), custom_call_target="tpu_custom_call" | custom-call | tf_op jit(solution)/shard_map/attention_grad/pallas_call | solution.py:967
  521.1 34.5 %layer_back.2 = (bf16[8,32,2048]{2,1,0:T(8,128)(2,1)}, bf16[32,2048]{1,0:T(8,128)(2,1)}) custom-call(bf16[8,32,2048]{2,1,0:T(8,128)(2,1)} %bitcast.120, f32[32,2048]{1,0:T(8,128)} %get-tuple-element.108.refs_1_, bf16[32,2048]{1,0:T(8,128)(2,1)} %get-tuple-element.96.refs_1_.refs_2_, f32[1,2048]{1,0:T(1,128)} %bitcast.151), custom_call_target="tpu_custom_call" | custom-call | tf_op jit(solution)/shard_map/layer_back/pallas_call | solution.py:208
  555.6 9.6 %feed_grad.3 = bf16[256,2048]{1,0:T(8,128)(2,1)} custom-call(bf16[256,2048]{1,0:T(8,128)(2,1)} %bitcast.133, f32[256,1408]{1,0:T(8,128)} %get-tuple-element.110.kept, bf16[2,704,2048]{2,1,0:T(8,128)(2,1)} %down.7, bf16[8,64,1792]{2,1,0:T(8,128)(2,1)} %copy-done, bf16[8,64,1792]{2,1,0:T(8,128)(2,1)} %collective-permute-done.other_y, ...), custom_call_target="tpu_custom_call" | custom-call | tf_op jit(solution)/shard_map/feed_grad/pallas_call | solution.py:967
  565.2 34.1 %feed_back.3 = (bf16[8,32,2048]{2,1,0:T(8,128)(2,1)}, f32[32,2048]{1,0:T(8,128)}) custom-call(bf16[8,32,2048]{2,1,0:T(8,128)(2,1)} %bitcast.123, bf16[32,2048]{1,0:T(8,128)(2,1)} %get-tuple-element.111.refs_1_, f32[32,2048]{1,0:T(8,128)} %get-tuple-element.92.refs_1_.refs_2_, f32[1,2048]{1,0:T(1,128)} %bitcast.149), custom_call_target="tpu_custom_call" | custom-call | tf_op jit(solution)/shard_map/feed_back/pallas_call | solution.py:208
  599.3 8.2 %attention_grad.3 = bf16[256,2048]{1,0:T(8,128)(2,1)} custom-call(bf16[256,2048]{1,0:T(8,128)(2,1)} %bitcast.132, bf16[256,256]{1,0:T(8,128)(2,1)} %get-tuple-element.113.queries, bf16[256,128]{1,0:T(8,128)(2,1)} %get-tuple-element.114.pairs, bf16[2,256,2048]{2,1,0:T(8,128)(2,1)} %out_weight.7, f32[6,256,128]{2,1,0:T(8,128)} %bitcast.116, ...), custom_call_target="tpu_custom_call" | custom-call | tf_op jit(solution)/shard_map/attention_grad/pallas_call | solution.py:967
  607.5 33.1 %layer_back.3 = (bf16[8,32,2048]{2,1,0:T(8,128)(2,1)}, bf16[32,2048]{1,0:T(8,128)(2,1)}) custom-call(bf16[8,32,2048]{2,1,0:T(8,128)(2,1)} %bitcast.119, f32[32,2048]{1,0:T(8,128)} %get-tuple-element.115.refs_1_, bf16[32,2048]{1,0:T(8,128)(2,1)} %get-tuple-element.87.refs_1_.refs_2_, f32[1,2048]{1,0:T(1,128)} %bitcast.147), custom_call_target="tpu_custom_call" | custom-call | tf_op jit(solution)/shard_map/layer_back/pallas_call | solution.py:208
  640.7 2.7 fusion
  644.6 12.0 %section_sum.1 = (f32[64,2048]{1,0:T(8,128)}, f32[8,128]{1,0:T(8,128)}) custom-call(bf16[4,64,2048]{2,1,0:T(8,128)(2,1)} %bitcast.128, f32[8,128]{1,0:T(8,128)} %broadcast_in_dim.58.loss), custom_call_target="tpu_custom_call" | custom-call | tf_op jit(solution)/shard_map/section_sum/pallas_call | solution.py:384
  656.7 39.2 %hyper_back.1 = (bf16[512,4096]{1,0:T(8,128)(2,1)}, bf16[512,2176]{1,0:T(8,128)(2,1)}, bf16[2048,512]{1,0:T(8,128)(2,1)}) custom-call(f32[64,2048]{1,0:T(8,128)} %get-tuple-element.118.table_grad, bf16[512,512]{1,0:T(8,128)(2,1)} %broadcast_select_fusion.pieces, bf16[512,4096]{1,0:T(8,128)(2,1)} %bitcast.106, bf16[512,2176]{1,0:T(8,128)(2,1)} %bitcast.112, ...), custom_call_target="tpu_custom_call" | custom-call | tf_op jit(solution)/shard_map/hyper_back/pallas_call | solution.py:967
  695.9 58.7 %collect.1 = (f32[16,4096]{1,0:T(8,128)}, f32[16,2176]{1,0:T(8,128)}, f32[64,512]{1,0:T(8,128)}) custom-call(bf16[4,8,16,4096]{3,2,1,0:T(8,128)(2,1)} %bitcast.125, bf16[4,8,16,2176]{3,2,1,0:T(8,128)(2,1)} %bitcast.129, bf16[4,8,64,512]{3,2,1,0:T(8,128)(2,1)} %bitcast.130), custom_call_target="tpu_custom_call" | custom-call | tf_op jit(solution)/shard_map/collect/pallas_call | solution.py:746
  754.6 1.5 fusion.25
  756.1 1.6 slice.99
  757.6 1.6 slice.100
  759.2 1.6 slice_reduce_fusion
  760.8 1.2 slice.90
  762.0 1.6 copy.94
  (118 shorter events, 10.7 us)
Async XLA Ops:
  4.7 7.6 copy-start.18
  4.7 7.6 copy-start.19
  4.7 7.6 copy-start.20
  4.7 7.6 copy-start.21
  4.7 7.7 %copy-start.6 = (f32[16,2048]{1,0:T(8,128)S(1)}, f32[16,2048]{1,0:T(8,128)}, u32[]{:S(2)}) copy-start(f32[16,2048]{1,0:T(8,128)} %param.43) | copy-start | bytes 393220
  4.7 7.7 %copy-start.7 = (f32[64,512]{1,0:T(8,128)S(1)}, f32[64,512]{1,0:T(8,128)}, u32[]{:S(2)}) copy-start(f32[64,512]{1,0:T(8,128)} %param.42) | copy-start | bytes 393220
  4.7 8.4 %copy-start.22 = (s32[1,2,64]{2,1,0:T(2,128)S(1)}, s32[1,2,64]{2,1,0:T(2,128)}, u32[]{:S(2)}) copy-start(s32[1,2,64]{2,1,0:T(2,128)} %param.27) | copy-start | bytes 1540
  4.7 8.4 %copy-start.23 = (s32[1,2,64]{2,1,0:T(2,128)S(1)}, s32[1,2,64]{2,1,0:T(2,128)}, u32[]{:S(2)}) copy-start(s32[1,2,64]{2,1,0:T(2,128)} %param.28) | copy-start | bytes 1540
  4.8 9.1 %copy-start.16 = (bf16[2,256]{1,0:T(2,128)(2,1)S(1)}, bf16[2,256]{1,0:T(2,128)(2,1)}, u32[]{:S(2)}) copy-start(bf16[2,256]{1,0:T(2,128)(2,1)} %param.49) | copy-start | bytes 3076
  4.8 9.1 %copy-start.17 = (bf16[2,256]{1,0:T(2,128)(2,1)S(1)}, bf16[2,256]{1,0:T(2,128)(2,1)}, u32[]{:S(2)}) copy-start(bf16[2,256]{1,0:T(2,128)(2,1)} %param.44) | copy-start | bytes 3076
  4.8 9.7 %copy-start.10 = (f32[16,512]{1,0:T(8,128)S(1)}, f32[16,512]{1,0:T(8,128)}, u32[]{:S(2)}) copy-start(f32[16,512]{1,0:T(8,128)} %param.35) | copy-start | bytes 98308
  4.8 9.7 %copy-start.11 = (f32[16,512]{1,0:T(8,128)S(1)}, f32[16,512]{1,0:T(8,128)}, u32[]{:S(2)}) copy-start(f32[16,512]{1,0:T(8,128)} %param.36) | copy-start | bytes 98308
  4.8 9.7 %copy-start.12 = (f32[16,512]{1,0:T(8,128)S(1)}, f32[16,512]{1,0:T(8,128)}, u32[]{:S(2)}) copy-start(f32[16,512]{1,0:T(8,128)} %param.37) | copy-start | bytes 98308
  4.8 9.7 %copy-start.13 = (f32[16,512]{1,0:T(8,128)S(1)}, f32[16,512]{1,0:T(8,128)}, u32[]{:S(2)}) copy-start(f32[16,512]{1,0:T(8,128)} %param.38) | copy-start | bytes 98308
  4.8 10.4 %copy-start.8 = (f32[16,2048]{1,0:T(8,128)S(1)}, f32[16,2048]{1,0:T(8,128)}, u32[]{:S(2)}) copy-start(f32[16,2048]{1,0:T(8,128)} %param.41) | copy-start | bytes 393220
  4.8 98.8 %all-to-all-start = ((bf16[8,64,1792]{2,1,0:T(8,128)(2,1)}), bf16[8,64,1792]{2,1,0:T(8,128)(2,1)S(1)}, u32[]{:S(2)}, u32[]{:S(2)}) async-start(bf16[8,64,1792]{2,1,0:T(8,128)(2,1)} %get-tuple-element.73), calls=%async_computation | async-start | bytes 3670016 | tf_op jit(solution)/shard_map/all_to_all | solution.py:1437
  15.2 98.4 %copy-start.24 = (s32[4]{0:T(128)S(1)}, s32[4]{0:T(128)}, u32[]{:S(2)}) copy-start(s32[4]{0:T(128)} %param.31) | copy-start | bytes 52
  15.2 98.4 %copy-start.25 = (s32[64]{0:T(128)S(1)}, s32[64]{0:T(128)}, u32[]{:S(2)}) copy-start(s32[64]{0:T(128)} %param.30) | copy-start | bytes 772
  15.2 98.5 %copy-start.15 = (s32[64,8]{0,1:T(8,128)S(1)}, s32[64,8]{0,1:T(8,128)}, u32[]{:S(2)}) copy-start(s32[64,8]{0,1:T(8,128)} %param.29) | copy-start | bytes 6148
  15.2 0.7 copy-start.5
  103.7 19.7 %copy-start = (bf16[8,64,1792]{2,1,0:T(8,128)(2,1)}, bf16[8,64,1792]{2,1,0:T(8,128)(2,1)S(1)}, u32[]{:S(2)}) copy-start(bf16[8,64,1792]{2,1,0:T(8,128)(2,1)S(1)} %all-to-all-done.own) | copy-start | bytes 5505028
  103.7 63.1 %all-to-all-start.1 = ((bf16[8,64,1792]{2,1,0:T(8,128)(2,1)}), bf16[8,64,1792]{2,1,0:T(8,128)(2,1)}, u32[]{:S(2)}, u32[]{:S(2)}) async-start(bf16[8,64,1792]{2,1,0:T(8,128)(2,1)} %get-tuple-element.81), calls=%async_computation.1 | async-start | bytes 3670016 | tf_op jit(solution)/shard_map/all_to_all | solution.py:1437
  113.7 42.2 %collective-permute-start = (bf16[8,64,1792]{2,1,0:T(8,128)(2,1)S(1)}, bf16[8,64,1792]{2,1,0:T(8,128)(2,1)}, u32[]{:S(2)}, u32[]{:S(2)}) collective-permute-start(bf16[8,64,1792]{2,1,0:T(8,128)(2,1)S(1)} %all-to-all-done.own), channel_id=1, source_target_pairs={{0,16},{8,24},{16,0},{24,8},{1,17},{9,25},{17,1},{25,9},{2,18},{10... | collective-permute-start | bytes 5505032 | tf_op jit(solution)/shard_map/ppermute | solution.py:1461
  123.4 88.5 %collective-permute-start.1 = (bf16[8,64,1792]{2,1,0:T(8,128)(2,1)S(1)}, bf16[8,64,1792]{2,1,0:T(8,128)(2,1)}, u32[]{:S(2)}, u32[]{:S(2)}) collective-permute-start(bf16[8,64,1792]{2,1,0:T(8,128)(2,1)S(1)} %all-to-all-done.own), channel_id=1, source_target_pairs={{0,8},{8,0},{16,24},{24,16},{1,9},{9,1},{17,25},{25,17},{2,10},{10... | collective-permute-start | bytes 5505032 | tf_op jit(solution)/shard_map/ppermute | solution.py:1462
  151.8 16.7 %copy-start.9 = (bf16[8,16,256]{2,1,0:T(8,128)(2,1)S(1)}, bf16[8,16,256]{2,1,0:T(8,128)(2,1)}, u32[]{:S(2)}) copy-start(bf16[8,16,256]{2,1,0:T(8,128)(2,1)} %get-tuple-element.83) | copy-start | bytes 196612
  166.5 45.3 %collective-permute-start.2 = (bf16[8,64,1792]{2,1,0:T(8,128)(2,1)}, bf16[8,64,1792]{2,1,0:T(8,128)(2,1)}, u32[]{:S(2)}, u32[]{:S(2)}) collective-permute-start(bf16[8,64,1792]{2,1,0:T(8,128)(2,1)} %collective-permute-done.other_y), channel_id=1, source_target_pairs={{0,8},{8,0},{16,24},{24,16},{1,9},{9,1},{17,25},{25,17},{2,10},{10... | collective-permute-start | bytes 5505032 | tf_op jit(solution)/shard_map/ppermute | solution.py:1491
  166.7 107.3 %collective-permute-start.3 = (bf16[8,64,1792]{2,1,0:T(8,128)(2,1)}, bf16[8,64,1792]{2,1,0:T(8,128)(2,1)}, u32[]{:S(2)}, u32[]{:S(2)}) collective-permute-start(bf16[8,64,1792]{2,1,0:T(8,128)(2,1)} %all-to-all-done.1.own), channel_id=1, source_target_pairs={{0,16},{8,24},{16,0},{24,8},{1,17},{9,25},{17,1},{25,9},{2,18},{10... | collective-permute-start | bytes 5505032 | tf_op jit(solution)/shard_map/ppermute | solution.py:1494
  169.2 147.9 %collective-permute-start.4 = (bf16[8,64,1792]{2,1,0:T(8,128)(2,1)}, bf16[8,64,1792]{2,1,0:T(8,128)(2,1)S(1)}, u32[]{:S(2)}, u32[]{:S(2)}) collective-permute-start(bf16[8,64,1792]{2,1,0:T(8,128)(2,1)} %all-to-all-done.1.own), channel_id=1, source_target_pairs={{0,8},{8,0},{16,24},{24,16},{1,9},{9,1},{17,25},{25,17},{2,10},{10... | collective-permute-start | bytes 5505032 | tf_op jit(solution)/shard_map/ppermute | solution.py:1495
  260.7 13.4 %copy-start.14 = (bf16[2048]{0:T(1024)(128)(2,1)S(1)}, bf16[2048]{0:T(1024)(128)(2,1)}, u32[]{:S(2)}) copy-start(bf16[2048]{0:T(1024)(128)(2,1)} %param.53) | copy-start | bytes 12292
  274.0 43.0 %collective-permute-start.5 = (bf16[8,64,1792]{2,1,0:T(8,128)(2,1)}, bf16[8,64,1792]{2,1,0:T(8,128)(2,1)S(1)}, u32[]{:S(2)}, u32[]{:S(2)}) collective-permute-start(bf16[8,64,1792]{2,1,0:T(8,128)(2,1)} %collective-permute-done.3.other_y), channel_id=1, source_target_pairs={{0,8},{8,0},{16,24},{24,16},{1,9},{9,1},{17,25},{25,17},{2,10},{10... | collective-permute-start | bytes 5505032 | tf_op jit(solution)/shard_map/ppermute | solution.py:1523
  317.1 1.2 copy-start.1
  317.1 1.8 copy-start.2
  365.5 51.1 %copy-start.3 = (bf16[4,64,2048]{2,1,0:T(8,128)(2,1)S(1)}, bf16[4,64,2048]{2,1,0:T(8,128)(2,1)}, u32[]{:S(2)}) copy-start(bf16[4,64,2048]{2,1,0:T(8,128)(2,1)} %section_gather.1) | copy-start | bytes 3145732
  416.6 15.3 %copy-start.4 = (bf16[8,32,2048]{2,1,0:T(8,128)(2,1)S(1)}, bf16[8,32,2048]{2,1,0:T(8,128)(2,1)}, u32[]{:S(2)}) copy-start(bf16[8,32,2048]{2,1,0:T(8,128)(2,1)} %get-tuple-element.100) | copy-start | bytes 3145732

commit v3 on v2

--- a/solution.py
+++ b/solution.py
@@ -14,7 +14,10 @@
 TEAM = 8
 SECTIONS = 4
 ROWS = MB * LEN * TEAM // SECTIONS
-OWN = ROWS // TEAM
+HALF = ROWS // 2
+EACH = HALF // TEAM
+LINES = TEAM // 2
+FIRST, SECOND = 0, 1
 LANES = 128
 MESH_IDS = pl.DeviceIdType.MESH
 ANYWHERE = pl.BlockSpec(memory_space=pl.ANY)
@@ -100,202 +103,6 @@
 
 def dma_sems(*shape):
     return pltpu.SemaphoreType.DMA(shape)
-
-
-def fold_kernel(finish, outer, n_in, n_out, *refs):
-    partial, extras = refs[0], refs[1:n_in]
-    gathered, outs = refs[n_in], refs[n_in + 1 : n_in + n_out]
-    (
-        own,
-        side,
-        pair,
-        far,
-        ready,
-        load_sem,
-        keep_sem,
-        side_send,
-        side_recv,
-        far_send,
-        far_recv,
-        out_send,
-        out_recv,
-        over_send,
-        over_recv,
-    ) = refs[n_in + n_out :]
-    wide = lax.axis_index("wide")
-    rank, team = wide // outer, wide % outer
-    line, column = rank // 2, rank % 2
-    lines = TEAM // 2
-
-    def at(some_line, some_column):
-        return (some_line % lines) * 2 + some_column
-
-    def member(some_line, some_column):
-        return {"wide": at(some_line, some_column) * outer + team}
-
-    beside = member(line, 1 - column)
-    greet([beside] + [member(line + j, column) for j in range(1, lines)])
-    order = (2, 1, 3, 0)
-    loads = [
-        pltpu.make_async_copy(partial.at[at(line + j, column)], own.at[j], load_sem.at[j])
-        for j in range(lines)
-    ]
-    sides = [
-        remote(
-            partial.at[at(line + j, 1 - column)],
-            side.at[j],
-            side_send.at[j],
-            side_recv.at[j],
-            beside,
-        )
-        for j in range(lines)
-    ]
-    fars = [None] + [
-        remote(pair.at[j], far.at[j], far_send.at[j], far_recv.at[j], member(line + j, column))
-        for j in range(1, lines)
-    ]
-    for j in order:
-        sides[j].start()
-        loads[j].start()
-    for j in order[:3]:
-        loads[j].wait()
-        sides[j].wait_recv()
-        pair[j] = (own[j].astype(jnp.float32) + side[j].astype(jnp.float32)).astype(jnp.bfloat16)
-        fars[j].start()
-    loads[0].wait()
-    sides[0].wait_recv()
-    total = own[0].astype(jnp.float32) + side[0].astype(jnp.float32)
-    for j in (1, 3, 2):
-        fars[j].wait_recv()
-        total = total + far[j].astype(jnp.float32)
-    ready[...] = finish(total, extras, outs)
-    mine = at(line, column)
-    keep = pltpu.make_async_copy(ready, gathered.at[mine], keep_sem)
-    pushes = [None] + [
-        remote(ready, gathered.at[mine], out_send.at[j], out_recv.at[j], member(line + j, column))
-        for j in range(1, lines)
-    ]
-    overs = [
-        remote(
-            ready if j == 0 else gathered.at[at(line - j, column)],
-            gathered.at[at(line - j, column)],
-            over_send.at[j],
-            over_recv.at[j],
-            beside,
-        )
-        for j in range(lines)
-    ]
-    for j in (2, 1, 3):
-        pushes[j].start()
-    overs[0].start()
-    keep.start()
-    for j in (1, 3, 2):
-        pushes[j].wait_recv()
-        overs[j].start()
-    for j in range(lines):
-        overs[j].wait()
-        sides[j].wait_send()
-        if j:
-            fars[j].wait_send()
-            pushes[j].wait_send()
-    keep.wait()
-
-
-def fold(finish, outer, collective_id, partial, extras, outs):
-    width = partial.shape[-1]
-    lines = TEAM // 2
-    slots = pltpu.VMEM((lines, OWN, width), jnp.bfloat16)
-    return pl.pallas_call(
-        functools.partial(fold_kernel, finish, outer, 1 + len(extras), 1 + len(outs)),
-        out_shape=(jax.ShapeDtypeStruct((TEAM, OWN, width), jnp.bfloat16),)
-        + tuple(jax.ShapeDtypeStruct((OWN, width), kind) for kind in outs),
-        in_specs=[ANYWHERE] + [IN_VMEM] * len(extras),
-        out_specs=(ANYWHERE,) + (IN_VMEM,) * len(outs),
-        scratch_shapes=[slots, slots, slots, slots, pltpu.VMEM((OWN, width), jnp.bfloat16)]
-        + [dma_sems(lines), pltpu.SemaphoreType.DMA]
-        + [dma_sems(lines)] * 8,
-        compiler_params=settings(collective_id),
-        name=finish.__name__,
-    )(partial.reshape(TEAM, OWN, width), *extras)
-
-
-def inject(total, extras, outs):
-    (gain,) = extras
-    hidden = total.astype(jnp.bfloat16)
-    outs[0][...] = hidden
-    wide = hidden.astype(jnp.float32)
-    return (wide * root_inverse(wide) * gain[...]).astype(jnp.bfloat16)
-
-
-def enter_feed(total, extras, outs):
-    hidden, gain = extras
-    middle = hidden[...].astype(jnp.float32) + total
-    outs[0][...] = middle
-    return (middle * root_inverse(middle) * gain[...]).astype(jnp.bfloat16)
-
-
-def leave_layer(total, extras, outs):
-    middle, gain = extras
-    hidden = (middle[...] + total).astype(jnp.bfloat16)
-    outs[0][...] = hidden
-    wide = hidden.astype(jnp.float32)
-    return (wide * root_inverse(wide) * gain[...]).astype(jnp.bfloat16)
-
-
-def head_back(total, extras, outs):
-    hidden, gain = extras
-    wide = hidden[...].astype(jnp.float32)
-    grad = reciprocal_root_backward(wide, root_inverse(wide), gain[...], total)
-    grad = grad.astype(jnp.bfloat16)
-    outs[0][...] = grad
-    return grad
-
-
-def feed_back(total, extras, outs):
-    outer_grad, middle, gain = extras
-    wide = middle[...]
-    grad = outer_grad[...].astype(jnp.float32) + reciprocal_root_backward(
-        wide, root_inverse(wide), gain[...], total
-    )
-    outs[0][...] = grad
-    return grad.astype(jnp.bfloat16)
-
-
-def layer_back(total, extras, outs):
-    middle_grad, hidden, gain = extras
-    wide = hidden[...].astype(jnp.float32)
-    grad = middle_grad[...] + reciprocal_root_backward(wide, root_inverse(wide), gain[...], total)
-    grad = grad.astype(jnp.bfloat16)
-    outs[0][...] = grad
-    return grad
-
-
-def team_kernel(outer, block, gathered, send, recv):
-    wide = lax.axis_index("wide")
-    rank, team = wide // outer, wide % outer
-    peers = [{"wide": ((rank + k) % TEAM) * outer + team} for k in range(1, TEAM)]
-    greet(peers)
-    copies = [
-        remote(block, gathered.at[rank], send.at[k], recv.at[k], peer)
-        for k, peer in enumerate(peers)
-    ]
-    for copy in copies:
-        copy.start()
-    gathered[rank] = block[...]
-    for copy in copies:
-        copy.wait()
-
-
-def team_gather(outer, collective_id, block):
-    return pl.pallas_call(
-        functools.partial(team_kernel, outer),
-        out_shape=jax.ShapeDtypeStruct((TEAM,) + block.shape, block.dtype),
-        in_specs=[IN_VMEM],
-        out_specs=IN_VMEM,
-        scratch_shapes=[dma_sems(TEAM - 1), dma_sems(TEAM - 1)],
-        compiler_params=settings(collective_id),
-        name="team_gather",
-    )(block)
 
 
 def section_places():
@@ -795,20 +602,7 @@
     pairs = [(cosines, cosines), (upper, upper), (lower, lower)]
     pairs += [(cosines, blank + 1.0), (upper, blank), (lower, blank)]
     tables = jnp.stack([jnp.concatenate(pair, axis=1) for pair in pairs])
-    return jnp.tile(tables, (1, ROWS // LEN, 1))
-
-
-def load_weight(pieces, columns, scratch, sem):
-    section = lax.axis_index("section")
-    partner = section + 1 - 2 * (section % 2)
-    places = (section, (section + 2) % SECTIONS, partner, (partner + 2) % SECTIONS)
-    copies = [
-        pltpu.make_async_copy(source.at[:, :, columns], scratch.at[:, place], sem.at[n])
-        for n, (source, place) in enumerate(zip(pieces, places))
-    ]
-    for copy in copies:
-        copy.start()
-    return copies
+    return jnp.tile(tables, (1, HALF // LEN, 1))
 
 
 def attend(queries, key, mask, scale):
@@ -819,230 +613,16 @@
     return mass / jnp.sum(mass, axis=1, keepdims=True)
 
 
-def attention_kernel(
-    normed, out_weight, tables, own, other_y, other_core, beyond, partial, queries_out, pairs_out, weight, sem
-):
-    heads_width = weight.shape[-1]
-    q_width = heads_width - LANES
-    copies = load_weight((own, other_y, other_core, beyond), pl.ds(0, heads_width), weight, sem)
-    for copy in copies:
-        copy.wait()
-    rows = normed[...]
-    projected = matmul(rows, weight[...].reshape(-1, heads_width))
-    queries = turn(projected[:, :q_width], [tables[n] for n in range(3)]).astype(jnp.bfloat16)
-    pairs = turn(projected[:, q_width:], [tables[n] for n in range(3, 6)]).astype(jnp.bfloat16)
-    queries_out[...] = queries
-    pairs_out[...] = pairs
-    key, value = pairs[:, :HEAD_DIM], pairs[:, HEAD_DIM:]
-    mask = causal_blocks(ROWS, LEN)
-    mixed = []
-    for start in range(0, q_width, HEAD_DIM):
-        weights = attend(queries[:, start : start + HEAD_DIM], key, mask, HEAD_DIM ** (-0.5))
-        mixed.append(matmul(weights.astype(jnp.bfloat16), value))
-    mixed = jnp.concatenate(mixed, axis=1).astype(jnp.bfloat16)
-
-    @pl.loop(0, partial.shape[1] // TILE)
-    def _(n):
-        columns = pl.ds(pl.multiple_of(n * TILE, TILE), TILE)
-        partial[:, columns] = matmul(mixed, out_weight[:, columns]).astype(jnp.bfloat16)
-
-
-def attention_back_kernel(
-    grad, queries, pairs, out_weight, tables, own, other_y, other_core, beyond, partial, weight, sem
-):
-    heads_width = weight.shape[-1]
-    q_width = heads_width - LANES
-    scale = HEAD_DIM ** (-0.5)
-    copies = load_weight((own, other_y, other_core, beyond), pl.ds(0, heads_width), weight, sem)
-    mixed_grad = times_trans(grad[...], out_weight[...]).astype(jnp.bfloat16)
-    key, value = pairs[:, :HEAD_DIM], pairs[:, HEAD_DIM:]
-    mask = causal_blocks(ROWS, LEN)
-    query_grads, key_grad, value_grad = [], 0.0, 0.0
-    for start in range(0, q_width, HEAD_DIM):
-        query = queries[:, start : start + HEAD_DIM]
-        outer = mixed_grad[:, start : start + HEAD_DIM]
-        weights = attend(query, key, mask, scale)
-        weight_grad = times_trans(outer, value)
-        score_grad = weights * (
-            weight_grad - jnp.sum(weights * weight_grad, axis=1, keepdims=True)
-        )
-        score_grad = score_grad.astype(jnp.bfloat16)
-        query_grads.append(matmul(score_grad, key) * scale)
-        key_grad = key_grad + trans_times(score_grad, query) * scale
-        value_grad = value_grad + trans_times(weights.astype(jnp.bfloat16), outer)
-    query_grad = turn(jnp.concatenate(query_grads, axis=1), [tables[n] for n in range(3)])
-    pair_grad = jnp.concatenate([key_grad, value_grad], axis=1)
-    pair_grad = turn(pair_grad, [tables[n] for n in range(3, 6)])
-    both = jnp.concatenate([query_grad, pair_grad], axis=1).astype(jnp.bfloat16)
-    for copy in copies:
-        copy.wait()
-    tiles = partial.shape[1] // TILE
-    each = weight.shape[0] // tiles
-
-    @pl.loop(0, tiles)
-    def _(n):
-        columns = pl.ds(pl.multiple_of(n * TILE, TILE), TILE)
-        block = weight[pl.ds(n * each, each)].reshape(TILE, heads_width)
-        partial[:, columns] = times_trans(both, block).astype(jnp.bfloat16)
-
-
-def feed_kernel(normed, down, own, other_y, other_core, beyond, partial, kept, weight, active, sem):
-    width = weight.shape[-1]
-    share = down.shape[0]
-    edge = share // LANES * LANES
-    tail = share - edge
-    copies = load_weight(
-        (own, other_y, other_core, beyond), pl.ds(own.shape[-1] - width, width), weight, sem
-    )
-    for copy in copies:
-        copy.wait()
-    depth = partial.shape[1]
-
-    @pl.loop(0, width // LANES)
-    def _(n):
-        columns = pl.ds(pl.multiple_of(n * LANES, LANES), LANES)
-        kept[:, columns] = matmul(normed[...], weight[:, :, :, columns].reshape(depth, LANES))
-
-    def activate(gate, up):
-        return (jax.nn.silu(gate) * up).astype(jnp.bfloat16)
-
-    active[:, :edge] = activate(kept[:, :edge], kept[:, edge : 2 * edge])
-    if tail:
-        last = kept[:, 2 * edge :]
-        active[:, edge:] = activate(last[:, :tail], last[:, tail:])
-
-    @pl.loop(0, depth // TILE)
-    def _(n):
-        columns = pl.ds(pl.multiple_of(n * TILE, TILE), TILE)
-        partial[:, columns] = matmul(active[...], down[:, columns]).astype(jnp.bfloat16)
-
-
-def feed_back_kernel(grad, kept, down, own, other_y, other_core, beyond, partial, weight, both, sem):
-    width = weight.shape[-1]
-    share = down.shape[0]
-    edge = share // LANES * LANES
-    tail = share - edge
-    copies = load_weight(
-        (own, other_y, other_core, beyond), pl.ds(own.shape[-1] - width, width), weight, sem
-    )
-    active_grad = times_trans(grad[...], down[...])
-
-    def back(outer, gate, up):
-        sigmoid = jax.nn.sigmoid(gate)
-        gate_grad = outer * up * sigmoid * (1.0 + gate * (1.0 - sigmoid))
-        return gate_grad.astype(jnp.bfloat16), (outer * gate * sigmoid).astype(jnp.bfloat16)
-
-    gate_grad, up_grad = back(active_grad[:, :edge], kept[:, :edge], kept[:, edge : 2 * edge])
-    both[:, :edge] = gate_grad
-    both[:, edge : 2 * edge] = up_grad
-    if tail:
-        last = kept[:, 2 * edge :]
-        gate_grad, up_grad = back(active_grad[:, edge:], last[:, :tail], last[:, tail:])
-        both[:, 2 * edge :] = jnp.concatenate([gate_grad, up_grad], axis=1)
-    for copy in copies:
-        copy.wait()
-    tiles = partial.shape[1] // TILE
-    each = weight.shape[0] // tiles
-
-    @pl.loop(0, tiles)
-    def _(n):
-        columns = pl.ds(pl.multiple_of(n * TILE, TILE), TILE)
-        block = weight[pl.ds(n * each, each)].reshape(TILE, width)
-        partial[:, columns] = times_trans(both[...], block).astype(jnp.bfloat16)
-
-
-class Layer:
-    def __init__(self, stack, index):
-        self.stack, self.index, self.shape = stack, index, stack.shape[1:]
-
-    def spec(self):
-        return pl.BlockSpec(
-            (None,) + self.shape, lambda step: (self.index, 0, 0), memory_space=pltpu.VMEM
-        )
-
-
-def local(kernel, operands, weights, outs, scratch, name):
-    specs = [item.spec() if isinstance(item, Layer) else IN_VMEM for item in operands]
-    operands = [item.stack if isinstance(item, Layer) else item for item in operands]
+def local(kernel, operands, outs, scratch, name):
     return pl.pallas_call(
         kernel,
-        grid=(1,),
         out_shape=tuple(jax.ShapeDtypeStruct(shape, kind) for shape, kind in outs),
-        in_specs=specs + [ANYWHERE] * len(weights),
+        in_specs=[IN_VMEM] * len(operands),
         out_specs=(IN_VMEM,) * len(outs),
         scratch_shapes=list(scratch),
         compiler_params=pltpu.CompilerParams(vmem_limit_bytes=VMEM_LIMIT),
         name=name,
-    )(*operands, *weights)
-
-
-def weight_scratch(pieces, width):
-    groups, rows = pieces[0].shape[:2]
-    return pltpu.VMEM((groups, SECTIONS, rows, width), jnp.bfloat16)
-
-
-def attention_forward(normed, pieces, out_weight, tables):
-    q_width, depth = out_weight.shape
-    partial, queries, pairs = local(
-        attention_kernel,
-        (normed, out_weight, tables),
-        pieces,
-        [
-            ((ROWS, depth), jnp.bfloat16),
-            ((ROWS, q_width), jnp.bfloat16),
-            ((ROWS, LANES), jnp.bfloat16),
-        ],
-        [weight_scratch(pieces, q_width + LANES), dma_sems(4)],
-        "attention",
-    )
-    return partial, (queries, pairs)
-
-
-def attention_backward(grad, stored, pieces, out_weight, tables):
-    q_width, depth = out_weight.shape
-    (partial,) = local(
-        attention_back_kernel,
-        (grad, *stored, out_weight, tables),
-        pieces,
-        [((ROWS, depth), jnp.bfloat16)],
-        [weight_scratch(pieces, q_width + LANES), dma_sems(4)],
-        "attention_grad",
-    )
-    return partial
-
-
-def feed_forward(normed, pieces, down):
-    share, depth = down.shape
-    partial, kept = local(
-        feed_kernel,
-        (normed, down),
-        pieces,
-        [((ROWS, depth), jnp.bfloat16), ((ROWS, 2 * share), jnp.float32)],
-        [
-            weight_scratch(pieces, 2 * share),
-            pltpu.VMEM((ROWS, share), jnp.bfloat16),
-            dma_sems(4),
-        ],
-        "feed",
-    )
-    return partial, kept
-
-
-def feed_backward(grad, kept, pieces, down):
-    share, depth = down.shape
-    (partial,) = local(
-        feed_back_kernel,
-        (grad, kept, down),
-        pieces,
-        [((ROWS, depth), jnp.bfloat16)],
-        [
-            weight_scratch(pieces, 2 * share),
-            pltpu.VMEM((ROWS, 2 * share), jnp.bfloat16),
-            dma_sems(4),
-        ],
-        "feed_grad",
-    )
-    return partial
+    )(*operands)
 
 
 CHUNK = 128
@@ -1136,7 +716,6 @@
     table, *stored = local(
         functools.partial(hyper_kernel, slots),
         (pieces, *params),
-        (),
         [
             ((entries, depth), jnp.bfloat16),
             ((count, 3 * width), jnp.bfloat16),
@@ -1271,7 +850,6 @@
     return local(
         functools.partial(hyper_back_kernel, slots),
         (table_grad, pieces, *params, *stored),
-        (),
         [(item.shape, jnp.bfloat16) for item in (first, second, third)],
         [
             pltpu.VMEM((width, count), jnp.bfloat16),
@@ -1369,6 +947,581 @@
         compiler_params=pltpu.CompilerParams(vmem_limit_bytes=VMEM_LIMIT),
         name="pack",
     )(*weights)
+
+
+def run(main, beside, most):
+    for count, _ in enumerate(main):
+        if beside is not None and count < most:
+            next(beside, None)
+
+
+def finish(*steps):
+    steps = list(steps)
+    while steps:
+        steps = [step for step in steps if next(step, steps) is not steps]
+
+
+class Decoder:
+    def __init__(self, shape, refs):
+        self.outer, self.tokens, self.share, self.q_width, self.depth = shape
+        for name, ref in refs.items():
+            setattr(self, name, ref)
+        self.section, self.partner, self.across = section_places()
+        self.beyond = (self.partner + 2) % SECTIONS
+        wide = lax.axis_index("wide")
+        self.rank, self.team = wide // self.outer, wide % self.outer
+        self.line, self.column = self.rank // 2, self.rank % 2
+        self.mine = self.rank
+        self.beside = self.member(self.line, 1 - self.column)
+        self.edge = self.share // LANES * LANES
+        self.tail = self.share - self.edge
+
+    def at(self, line, column):
+        return (line % LINES) * 2 + column
+
+    def member(self, line, column):
+        return {"wide": self.at(line, column) * self.outer + self.team}
+
+    def ranked(self, step):
+        return {"wide": (self.rank + step) % TEAM * self.outer + self.team}
+
+    def greet(self):
+        sections = [{"section": place} for place in (self.partner, self.across, self.beyond)]
+        greet(sections + [self.ranked(k) for k in range(1, TEAM)])
+
+    def weight_copies(self):
+        heads, feed = pl.ds(0, self.q_width + LANES), pl.ds(self.q_width + LANES, 2 * self.share)
+        places = (self.section, self.across, self.partner, self.beyond)
+        self.head_loads = [[], []]
+        self.feed_loads = [[], []]
+        for n, (piece, place) in enumerate(zip(self.pieces, places)):
+            self.head_loads[0].append(
+                pltpu.make_async_copy(
+                    piece.at[:, :, heads], self.head_weight.at[0, :, place], self.load_sem.at[0, n]
+                )
+            )
+            self.feed_loads[0].append(
+                pltpu.make_async_copy(
+                    piece.at[:, :, feed], self.feed_weight.at[0, :, place], self.load_sem.at[1, n]
+                )
+            )
+        self.head_loads[1].append(
+            pltpu.make_async_copy(
+                self.own_two.at[:, :, heads],
+                self.head_weight.at[1, :, self.section],
+                self.load_sem.at[2, 0],
+            )
+        )
+        self.feed_loads[1].append(
+            pltpu.make_async_copy(
+                self.own_two.at[:, :, feed],
+                self.feed_weight.at[1, :, self.section],
+                self.load_sem.at[3, 0],
+            )
+        )
+        for n, place in enumerate((self.across, self.beyond, self.partner)):
+            peer = {"section": place}
+            self.head_loads[1].append(
+                remote(
+                    self.own_two.at[:, :, heads],
+                    self.head_weight.at[1, :, self.section],
+                    self.share_send.at[0, n],
+                    self.share_recv.at[0, n],
+                    peer,
+                )
+            )
+            self.feed_loads[1].append(
+                remote(
+                    self.own_two.at[:, :, feed],
+                    self.feed_weight.at[1, :, self.section],
+                    self.share_send.at[1, n],
+                    self.share_recv.at[1, n],
+                    peer,
+                )
+            )
+        for layer in range(2):
+            self.head_loads[layer].append(
+                pltpu.make_async_copy(
+                    self.out_source.at[layer], self.out_weight.at[layer], self.load_sem.at[4, layer]
+                )
+            )
+            self.feed_loads[layer].append(
+                pltpu.make_async_copy(
+                    self.down_source.at[layer],
+                    self.down_weight.at[layer],
+                    self.load_sem.at[5, layer],
+                )
+            )
+        for layer in range(2):
+            for copy in self.head_loads[layer] + self.feed_loads[layer]:
+                copy.start()
+
+    def send(self, half):
+        self.sides = getattr(self, "sides", {})
+        self.sides[half] = [
+            remote(
+                self.partial.at[half, self.at(self.line + j, 1 - self.column)],
+                self.side.at[half, j],
+                self.side_send.at[half, j],
+                self.side_recv.at[half, j],
+                self.beside,
+            )
+            for j in range(LINES)
+        ]
+        for j in (2, 1, 3, 0):
+            self.sides[half][j].start()
+
+    def reduce(self, half, close):
+        sides = self.sides[half]
+        fars = [None] + [
+            remote(
+                self.pair.at[half, j],
+                self.far.at[half, j],
+                self.far_send.at[half, j],
+                self.far_recv.at[half, j],
+                self.member(self.line + j, self.column),
+            )
+            for j in range(1, LINES)
+        ]
+
+        def pair_sum(j):
+            sides[j].wait_recv()
+            own = self.partial[half, self.at(self.line + j, self.column)]
+            return own.astype(jnp.float32) + self.side[half, j].astype(jnp.float32)
+
+        for j in (2, 1, 3):
+            self.pair[half, j] = pair_sum(j).astype(jnp.bfloat16)
+            fars[j].start()
+            yield
+        total = pair_sum(0)
+        for j in (1, 3, 2):
+            fars[j].wait_recv()
+            total = total + self.far[half, j].astype(jnp.float32)
+        self.gathered[half, self.mine] = close(half, total)
+        for j in range(LINES):
+            sides[j].wait_send()
+            if j:
+                fars[j].wait_send()
+        pushes = [None] + [
+            remote(
+                self.gathered.at[half, self.mine],
+                self.gathered.at[half, self.mine],
+                self.out_send.at[half, j],
+                self.out_recv.at[half, j],
+                self.member(self.line + j, self.column),
+            )
+            for j in range(1, LINES)
+        ]
+        overs = []
+        for j in range(LINES):
+            block = self.gathered.at[half, self.at(self.line - j, self.column)]
+            overs.append(
+                remote(
+                    block, block, self.over_send.at[half, j], self.over_recv.at[half, j], self.beside
+                )
+            )
+        for j in (2, 1, 3):
+            pushes[j].start()
+        overs[0].start()
+        self.moving[half] = (pushes, overs)
+        yield
+
+    def gather(self, half):
+        pushes, overs = self.moving[half]
+        for j in (1, 3, 2):
+            pushes[j].wait_recv()
+            overs[j].start()
+            yield
+        for j in range(LINES):
+            overs[j].wait()
+            if j:
+                pushes[j].wait_send()
+        yield
+
+    def rows(self, half):
+        return self.gathered[half].reshape(HALF, self.depth)
+
+    def store_partial(self, half, columns, values):
+        self.partial[half, :, :, columns] = values.astype(jnp.bfloat16).reshape(
+            TEAM, EACH, values.shape[1]
+        )
+
+    def tiles(self, count, parts):
+        bounds = [count * n // parts for n in range(parts + 1)]
+        return [(low, high) for low, high in zip(bounds[:-1], bounds[1:]) if high > low]
+
+    def inject(self, half):
+        hits = self.own_rows[...] == self.ids[half : half + 1, :]
+        hits = jnp.where(hits, 1.0, 0.0).astype(jnp.bfloat16)
+
+        @pl.loop(0, self.depth // TILE)
+        def _(n):
+            columns = pl.ds(pl.multiple_of(n * TILE, TILE), TILE)
+            self.store_partial(half, columns, trans_times(hits, self.table[:, columns]))
+
+        yield
+
+    def attention(self, layer, half):
+        if half == FIRST:
+            for copy in self.head_loads[layer]:
+                copy.wait()
+        own = pl.ds(half * HALF, HALF)
+        width = self.q_width + LANES
+        projected = matmul(self.rows(half), self.head_weight[layer].reshape(self.depth, width))
+        yield
+        queries = turn(projected[:, : self.q_width], [self.tables[n] for n in range(3)])
+        pairs = turn(projected[:, self.q_width :], [self.tables[n] for n in range(3, 6)])
+        queries, pairs = queries.astype(jnp.bfloat16), pairs.astype(jnp.bfloat16)
+        self.queries[layer, own, :] = queries
+        self.pairs[layer, own, :] = pairs
+        key, value = pairs[:, :HEAD_DIM], pairs[:, HEAD_DIM:]
+        mask = causal_blocks(HALF, LEN)
+        mixed = []
+        for start in range(0, self.q_width, HEAD_DIM):
+            weights = attend(queries[:, start : start + HEAD_DIM], key, mask, HEAD_DIM ** (-0.5))
+            mixed.append(matmul(weights.astype(jnp.bfloat16), value))
+        mixed = jnp.concatenate(mixed, axis=1).astype(jnp.bfloat16)
+        yield
+
+        @pl.loop(0, self.depth // TILE)
+        def _(n):
+            columns = pl.ds(pl.multiple_of(n * TILE, TILE), TILE)
+            self.store_partial(half, columns, matmul(mixed, self.out_weight[layer, :, columns]))
+
+        yield
+
+    def feed(self, layer, half):
+        if half == FIRST:
+            for copy in self.feed_loads[layer]:
+                copy.wait()
+        own = pl.ds(half * HALF, HALF)
+        edge, tail = self.edge, self.tail
+        for low, high in self.tiles(2 * self.share // LANES, 3):
+
+            @pl.loop(low, high)
+            def _(n):
+                columns = pl.ds(pl.multiple_of(n * LANES, LANES), LANES)
+                block = self.feed_weight[layer, :, :, :, columns].reshape(self.depth, LANES)
+                self.kept[layer, own, columns] = matmul(self.rows(half), block)
+
+            yield
+
+        def activate(gate, up):
+            return (jax.nn.silu(gate) * up).astype(jnp.bfloat16)
+
+        self.active[:, :edge] = activate(
+            self.kept[layer, own, :edge], self.kept[layer, own, edge : 2 * edge]
+        )
+        if tail:
+            last = self.kept[layer, own, 2 * edge :]
+            self.active[:, edge:] = activate(last[:, :tail], last[:, tail:])
+        for low, high in self.tiles(self.depth // TILE, 2):
+
+            @pl.loop(low, high)
+            def _(n):
+                columns = pl.ds(pl.multiple_of(n * TILE, TILE), TILE)
+                block = self.down_weight[layer, :, columns]
+                self.store_partial(half, columns, matmul(self.active[...], block))
+
+            yield
+
+    def head(self, half):
+        keep = pltpu.make_async_copy(
+            self.gathered.at[half], self.normed_out.at[half], self.keep_sem.at[half]
+        )
+        keep.start()
+        logits = times_trans(self.table[...], self.rows(half))
+        peak = jnp.max(logits, axis=0, keepdims=True)
+        mass = jnp.sum(jnp.exp(logits - peak), axis=0, keepdims=True)
+        wanted = self.own_rows[...] == self.wanted[half : half + 1, :]
+        chosen = jnp.sum(jnp.where(wanted, logits, 0.0), axis=0, keepdims=True)
+        row = lax.broadcasted_iota(jnp.int32, (8, HALF), 0)
+        stats = jnp.where(row == 0, peak, jnp.where(row == 1, mass, chosen))
+        self.stats[half, self.rank] = stats
+        copies = [
+            remote(
+                self.stats.at[half, self.rank],
+                self.stats.at[half, self.rank],
+                self.stats_send.at[half, k],
+                self.stats_recv.at[half, k],
+                self.ranked(k),
+            )
+            for k in range(1, TEAM)
+        ]
+        for copy in copies:
+            copy.start()
+        yield
+        yield
+        for copy in copies:
+            copy.wait()
+        peaks = [self.stats[half, n, 0:1, :] for n in range(TEAM)]
+        top = functools.reduce(jnp.maximum, peaks)
+        mass = sum(self.stats[half, n, 1:2, :] * jnp.exp(peaks[n] - top) for n in range(TEAM))
+        chosen = sum(self.stats[half, n, 2:3, :] for n in range(TEAM))
+        log_norm = top + jnp.log(mass)
+        loss = jnp.sum(log_norm - chosen, axis=1, keepdims=True) / self.tokens
+        loss = jnp.broadcast_to(loss, self.loss_out.shape)
+        if half == FIRST:
+            self.loss_out[...] = loss
+        else:
+            self.loss_out[...] += loss
+        grad = (jnp.exp(logits - log_norm) - jnp.where(wanted, 1.0, 0.0)) / self.tokens
+        grad = grad.astype(jnp.bfloat16)
+        self.logit_grad[:, pl.ds(half * HALF, HALF)] = grad
+        yield
+
+        @pl.loop(0, self.depth // TILE)
+        def _(n):
+            columns = pl.ds(pl.multiple_of(n * TILE, TILE), TILE)
+            self.store_partial(half, columns, trans_times(grad, self.table[:, columns]))
+
+        keep.wait()
+        yield
+
+    def feed_back(self, layer, half):
+        own = pl.ds(half * HALF, HALF)
+        edge, tail = self.edge, self.tail
+        active_grad = times_trans(self.rows(half), self.down_weight[layer])
+        yield
+
+        def back(outer, gate, up):
+            sigmoid = jax.nn.sigmoid(gate)
+            gate_grad = outer * up * sigmoid * (1.0 + gate * (1.0 - sigmoid))
+            return gate_grad.astype(jnp.bfloat16), (outer * gate * sigmoid).astype(jnp.bfloat16)
+
+        gate_grad, up_grad = back(
+            active_grad[:, :edge],
+            self.kept[layer, own, :edge],
+            self.kept[layer, own, edge : 2 * edge],
+        )
+        self.both[:, :edge] = gate_grad
+        self.both[:, edge : 2 * edge] = up_grad
+        if tail:
+            last = self.kept[layer, own, 2 * edge :]
+            gate_grad, up_grad = back(active_grad[:, edge:], last[:, :tail], last[:, tail:])
+            self.both[:, 2 * edge :] = jnp.concatenate([gate_grad, up_grad], axis=1)
+        yield
+        tiles = self.depth // TILE
+        each = self.feed_weight.shape[1] // tiles
+        for low, high in self.tiles(tiles, 3):
+
+            @pl.loop(low, high)
+            def _(n):
+                columns = pl.ds(pl.multiple_of(n * TILE, TILE), TILE)
+                block = self.feed_weight[layer, pl.ds(n * each, each)].reshape(TILE, -1)
+                self.store_partial(half, columns, times_trans(self.both[...], block))
+
+            yield
+
+    def attention_back(self, layer, half):
+        own = pl.ds(half * HALF, HALF)
+        scale = HEAD_DIM ** (-0.5)
+        mixed_grad = times_trans(self.rows(half), self.out_weight[layer]).astype(jnp.bfloat16)
+        yield
+        queries, pairs = self.queries[layer, own, :], self.pairs[layer, own, :]
+        key, value = pairs[:, :HEAD_DIM], pairs[:, HEAD_DIM:]
+        mask = causal_blocks(HALF, LEN)
+        query_grads, key_grad, value_grad = [], 0.0, 0.0
+        for start in range(0, self.q_width, HEAD_DIM):
+            query = queries[:, start : start + HEAD_DIM]
+            outer = mixed_grad[:, start : start + HEAD_DIM]
+            weights = attend(query, key, mask, scale)
+            weight_grad = times_trans(outer, value)
+            score_grad = weights * (
+                weight_grad - jnp.sum(weights * weight_grad, axis=1, keepdims=True)
+            )
+            score_grad = score_grad.astype(jnp.bfloat16)
+            query_grads.append(matmul(score_grad, key) * scale)
+            key_grad = key_grad + trans_times(score_grad, query) * scale
+            value_grad = value_grad + trans_times(weights.astype(jnp.bfloat16), outer)
+        query_grad = jnp.concatenate(query_grads, axis=1)
+        query_grad = turn(query_grad, [self.back_tables[n] for n in range(3)])
+        pair_grad = jnp.concatenate([key_grad, value_grad], axis=1)
+        pair_grad = turn(pair_grad, [self.back_tables[n] for n in range(3, 6)])
+        both = jnp.concatenate([query_grad, pair_grad], axis=1).astype(jnp.bfloat16)
+        yield
+        tiles = self.depth // TILE
+        each = self.head_weight.shape[1] // tiles
+
+        @pl.loop(0, tiles)
+        def _(n):
+            columns = pl.ds(pl.multiple_of(n * TILE, TILE), TILE)
+            block = self.head_weight[layer, pl.ds(n * each, each)].reshape(TILE, -1)
+            self.store_partial(half, columns, times_trans(both, block))
+
+        yield
+
+    def normed(self, values, gain):
+        return (values * root_inverse(values) * gain[...]).astype(jnp.bfloat16)
+
+    def close_inject(self, half, total):
+        hidden = total.astype(jnp.bfloat16)
+        self.hidden[0, half] = hidden
+        return self.normed(hidden.astype(jnp.float32), self.gains[0])
+
+    def close_attention(self, layer):
+        def close(half, total):
+            middle = self.hidden[layer, half].astype(jnp.float32) + total
+            self.middle[layer, half] = middle
+            return self.normed(middle, self.gains[2 + layer])
+
+        return close
+
+    def close_feed(self, layer):
+        def close(half, total):
+            hidden = (self.middle[layer, half] + total).astype(jnp.bfloat16)
+            self.hidden[layer + 1, half] = hidden
+            gain = self.gains[4] if layer else self.gains[1]
+            return self.normed(hidden.astype(jnp.float32), gain)
+
+        return close
+
+    def close_head(self, half, total):
+        hidden = self.hidden[2, half].astype(jnp.float32)
+        grad = reciprocal_root_backward(hidden, root_inverse(hidden), self.gains[4][...], total)
+        grad = grad.astype(jnp.bfloat16)
+        self.grad[half] = grad.astype(jnp.float32)
+        return grad
+
+    def close_feed_back(self, layer):
+        def close(half, total):
+            middle = self.middle[layer, half]
+            grad = self.grad[half] + reciprocal_root_backward(
+                middle, root_inverse(middle), self.gains[2 + layer][...], total
+            )
+            self.grad[half] = grad
+            return grad.astype(jnp.bfloat16)
+
+        return close
+
+    def close_attention_back(self, layer):
+        def close(half, total):
+            hidden = self.hidden[layer, half].astype(jnp.float32)
+            grad = self.grad[half] + reciprocal_root_backward(
+                hidden, root_inverse(hidden), self.gains[layer][...], total
+            )
+            grad = grad.astype(jnp.bfloat16)
+            self.grad[half] = grad.astype(jnp.float32)
+            return grad
+
+        return close
+
+
+def decode_kernel(shape, names, *refs):
+    refs = dict(zip(names, refs))
+    refs["pieces"] = [refs.pop(name) for name in ("own_one", "y_one", "core_one", "beyond_one")]
+    refs["gains"] = [refs["gain_rows"].at[pl.ds(n, 1)] for n in range(5)]
+    this = Decoder(shape, refs)
+    this.greet()
+    this.moving = {}
+    this.weight_copies()
+    phases = [(this.inject, this.close_inject)]
+    for layer in range(2):
+        phases.append((functools.partial(this.attention, layer), this.close_attention(layer)))
+        phases.append((functools.partial(this.feed, layer), this.close_feed(layer)))
+    phases.append((this.head, this.close_head))
+    for layer in (1, 0):
+        phases.append((functools.partial(this.feed_back, layer), this.close_feed_back(layer)))
+        phases.append(
+            (functools.partial(this.attention_back, layer), this.close_attention_back(layer))
+        )
+    reduces, gathers = {}, {}
+
+    def settle(half, *beside):
+        if half in reduces:
+            finish(*beside, reduces.pop(half))
+            gathers[half] = this.gather(half)
+        else:
+            finish(*beside)
+
+    for work, close in phases:
+        for half in (FIRST, SECOND):
+            other = 1 - half
+            settle(other, gathers.pop(half, iter(())))
+            run(work(half), gathers.get(other), LINES - 1)
+            this.send(half)
+            reduces[half] = this.reduce(half, close)
+    settle(SECOND, gathers.pop(FIRST))
+    finish(gathers.pop(SECOND))
+    outs = [
+        pltpu.make_async_copy(
+            this.gathered.at[half], this.grad_out.at[half], this.keep_sem.at[half]
+        )
+        for half in (FIRST, SECOND)
+    ]
+    for copy in outs:
+        copy.start()
+    for copy in outs:
+        copy.wait()
+
+
+def decode(outer, collective_id, tokens, weights, out_source, down_source, gains, tables, table, own_rows, ids, wanted):
+    q_width, depth = out_source.shape[1:]
+    share = down_source.shape[1]
+    groups, quarter = weights[0].shape[:2]
+    entries = table.shape[0]
+    low, full = jnp.bfloat16, jnp.float32
+    block = (2, TEAM, EACH, depth)
+    slots = pltpu.VMEM((2, LINES, EACH, depth), low)
+    inputs = dict(
+        own_rows=own_rows,
+        ids=ids,
+        wanted=wanted,
+        table=table,
+        gain_rows=gains,
+        tables=tables[0],
+        back_tables=tables[1],
+    )
+    far_inputs = dict(
+        zip(("own_one", "y_one", "core_one", "beyond_one", "own_two"), weights),
+        out_source=out_source,
+        down_source=down_source,
+    )
+    outputs = dict(
+        normed_out=(jax.ShapeDtypeStruct(block, low), ANYWHERE),
+        grad_out=(jax.ShapeDtypeStruct(block, low), ANYWHERE),
+        logit_grad=(jax.ShapeDtypeStruct((entries, ROWS), low), IN_VMEM),
+        loss_out=(jax.ShapeDtypeStruct((8, LANES), full), IN_VMEM),
+    )
+    scratch = dict(
+        head_weight=pltpu.VMEM((2, groups, SECTIONS, quarter, q_width + LANES), low),
+        feed_weight=pltpu.VMEM((2, groups, SECTIONS, quarter, 2 * share), low),
+        out_weight=pltpu.VMEM((2, q_width, depth), low),
+        down_weight=pltpu.VMEM((2, share, depth), low),
+        gathered=pltpu.VMEM(block, low),
+        partial=pltpu.VMEM(block, low),
+        side=slots,
+        pair=slots,
+        far=slots,
+        kept=pltpu.VMEM((2, ROWS, 2 * share), full),
+        queries=pltpu.VMEM((2, ROWS, q_width), low),
+        pairs=pltpu.VMEM((2, ROWS, LANES), low),
+        active=pltpu.VMEM((HALF, share), low),
+        both=pltpu.VMEM((HALF, 2 * share), low),
+        hidden=pltpu.VMEM((3, 2, EACH, depth), low),
+        middle=pltpu.VMEM((2, 2, EACH, depth), full),
+        grad=pltpu.VMEM((2, EACH, depth), full),
+        stats=pltpu.VMEM((2, TEAM, 8, HALF), full),
+        load_sem=dma_sems(6, 4),
+        share_send=dma_sems(2, 3),
+        share_recv=dma_sems(2, 3),
+        stats_send=dma_sems(2, TEAM),
+        stats_recv=dma_sems(2, TEAM),
+        keep_sem=dma_sems(2),
+    )
+    for name in ("side", "far", "out", "over"):
+        scratch[name + "_send"] = dma_sems(2, LINES)
+        scratch[name + "_recv"] = dma_sems(2, LINES)
+    names = (*inputs, *far_inputs, *outputs, *scratch)
+    return pl.pallas_call(
+        functools.partial(decode_kernel, (outer, tokens, share, q_width, depth), names),
+        out_shape=tuple(shape for shape, _ in outputs.values()),
+        in_specs=[IN_VMEM] * len(inputs) + [ANYWHERE] * len(far_inputs),
+        out_specs=tuple(spec for _, spec in outputs.values()),
+        scratch_shapes=list(scratch.values()),
+        compiler_params=settings(collective_id),
+        name="decode",
+    )(*inputs.values(), *far_inputs.values())
 
 
 def team_groups(wides, outer):
@@ -1472,12 +1625,11 @@
             lax.all_gather(item, "wide", axis=1, axis_index_groups=groups, tiled=True)
             for item in (output_weight, down_weight)
         )
-    gains = gains.astype(jnp.float32).transpose(1, 0, 2).reshape(-1, 1, model_width)
-    attention_gains, feed_gains = gains[:2], gains[2:4]
+    gains = gains.astype(jnp.float32).transpose(1, 0, 2).reshape(-1, model_width)
     final_scale = final_gain.astype(jnp.float32).reshape(1, model_width)
+    gains = jnp.concatenate([gains[:4], final_scale, gains[:3]], axis=0)
     notes = lax.dynamic_slice_in_dim(notes, section_index * 2, 2, 0)
     ids, wanted = notes[:, 0].reshape(-1), notes[:, 1].reshape(-1)
-    tables, back_tables = turn_tables(False), turn_tables(True)
 
     entries, slot_count = slot_ids.shape
     group_hits = (
@@ -1490,9 +1642,6 @@
     table_shard, y_one = together(table_shard, y_one)
     beyond_one = lax.ppermute(y_one, "section", SWAP_CORE)
     table_rows = section_gather(3, table_shard)
-    table_rows, own_two = together(table_rows, own_two)
-    y_two = lax.ppermute(own_two, "section", SWAP_Y)
-    core_two = lax.ppermute(own_two, "section", SWAP_CORE)
     if outer > 1:
         table_rows = lax.all_gather(table_rows, "wide", axis=1, axis_index_groups=groups)
     table_rows = table_rows.reshape(-1, model_width)
@@ -1502,82 +1651,31 @@
     ) * entries
     own_rows = row_starts[:, :, None] + jnp.arange(entries, dtype=jnp.int32)[None, None, :]
     own_rows = own_rows.reshape(-1)
-    hits = (ids[:, None] == own_rows[None, :]).astype(jnp.bfloat16)
-    injected = matmul(hits, table_rows).astype(jnp.bfloat16)
-    normed, hidden = fold(inject, outer, 4, injected, (attention_gains[0],), (jnp.bfloat16,))
-
-    weights = [all_teams((own_one, y_one, core_one, beyond_one), outer, groups)]
-    kept = []
-    for layer in range(2):
-        partial, attended = attention_forward(
-            normed.reshape(ROWS, model_width), weights[layer], Layer(output_weight, layer), tables
-        )
-        normed, middle = fold(
-            enter_feed, outer, 5, partial, (hidden, feed_gains[layer]), (jnp.float32,)
-        )
-        partial, fed = feed_forward(
-            normed.reshape(ROWS, model_width), weights[layer], Layer(down_weight, layer)
-        )
-        if layer == 0:
-            partial, y_two = together(partial, y_two)
-            beyond_two = lax.ppermute(y_two, "section", SWAP_CORE)
-            weights.append(all_teams((own_two, y_two, core_two, beyond_two), outer, groups))
-        kept.append((hidden, attended, middle, fed))
-        next_gain = attention_gains[1] if layer == 0 else final_scale
-        normed, hidden = fold(
-            leave_layer, outer, 6, partial, (middle, next_gain), (jnp.bfloat16,)
-        )
-
-    final_normed = normed.reshape(ROWS, model_width)
-    logits = times_trans(final_normed, table_rows)
-    row_peak = jnp.max(logits, axis=1)
-    row_mass = jnp.sum(jnp.exp(logits - row_peak[:, None]), axis=1)
-    wanted_hits = wanted[:, None] == own_rows[None, :]
-    chosen = jnp.sum(jnp.where(wanted_hits, logits, 0.0), axis=1)
-    blank = jnp.zeros_like(chosen)
-    stats = jnp.stack([row_peak, row_mass, chosen] + [blank] * 5, axis=0)
-    stats = team_gather(outer, 7, stats)
-    peak = jnp.max(stats[:, 0], axis=0)
-    mass = jnp.sum(stats[:, 1] * jnp.exp(stats[:, 0] - peak[None, :]), axis=0)
-    log_norm = peak + jnp.log(mass)
-    loss_part = jnp.sum(log_norm - jnp.sum(stats[:, 2], axis=0)) / total_tokens
-    logit_grad = (
-        (jnp.exp(logits - log_norm[:, None]) - wanted_hits.astype(jnp.float32)) / total_tokens
-    ).astype(jnp.bfloat16)
-    partial = matmul(logit_grad, table_rows).astype(jnp.bfloat16)
-    grads, outer_grad = fold(
-        head_back, outer, 8, partial, (hidden, final_scale), (jnp.bfloat16,)
-    )
-
-    for layer in (1, 0):
-        hidden, attended, middle, fed = kept[layer]
-        partial = feed_backward(
-            grads.reshape(ROWS, model_width), fed, weights[layer], Layer(down_weight, layer)
-        )
-        grads, middle_grad = fold(
-            feed_back, outer, 9, partial, (outer_grad, middle, feed_gains[layer]), (jnp.float32,)
-        )
-        partial = attention_backward(
-            grads.reshape(ROWS, model_width),
-            attended,
-            weights[layer],
-            Layer(output_weight, layer),
-            back_tables,
-        )
-        grads, outer_grad = fold(
-            layer_back,
-            outer,
-            10,
-            partial,
-            (middle_grad, hidden, attention_gains[layer]),
-            (jnp.bfloat16,),
-        )
-
-    table_part = trans_times(logit_grad, final_normed) + trans_times(
+    own_rows = own_rows.reshape(-1, 1)
+
+    def by_halves(numbers):
+        return jnp.pad(numbers.reshape(2, -1), ((0, 6), (0, 0)))
+
+    normed, grads, logit_grad, loss_block = decode(
+        outer,
+        4,
+        total_tokens,
+        all_teams((own_one, y_one, core_one, beyond_one, own_two), outer, groups),
+        output_weight,
+        down_weight,
+        gains,
+        (turn_tables(False), turn_tables(True)),
+        table_rows,
+        own_rows,
+        by_halves(ids),
+        by_halves(wanted),
+    )
+
+    hits = (own_rows == ids[None, :]).astype(jnp.bfloat16)
+    table_part = matmul(logit_grad, normed.reshape(ROWS, model_width)) + matmul(
         hits, grads.reshape(ROWS, model_width)
     )
     table_part = table_part.astype(jnp.bfloat16).reshape(SECTIONS, outer, entries, model_width)
-    loss_block = jnp.full((8, LANES), loss_part, jnp.float32)
     if outer > 1:
         table_part = lax.psum_scatter(
             table_part.astype(jnp.float32),

time: 771 us -> 705 us (0.914)
  Pallas kernels: 699 us -> 647 us
    pallas_call x21 -> x3, Pallas kernels: 525 us -> 477 us  [the longest x1 409 us: decode(): pl.pallas_call(functools.partial(decode_kernel, (outer, tokens, share, q_...]
  transfers between devices with their start and end apart: 8 -> 5, of which waited for: 1 -> 0; matrix products, arithmetic and copies ran while one was open for 2% -> 2% of each run, Pallas kernels for 35% -> 18%
where the time goes in v3:
time: 705 us; the launch traced here: 696 us
  Pallas kernels  647 us (92%)
  local copies, waits for them, and re-layouts  20.3 us (3%)
  starting transfers between devices  19.4 us (3%)
    pallas_call x1, Pallas kernels, decode(): pl.pallas_call(functools.partial(decode_kernel, (outer, tokens, share, q_...  409 us
    pallas_call x1, Pallas kernels, spread(): pl.pallas_call(functools.partial(spread_kernel, count, halves, outer), ou...  87.8 us
    pallas_call x2, Pallas kernels, local(): pl.pallas_call(kernel, out_shape=tuple((jax.ShapeDtypeStruct(shape, kind)...  67.9 us
    pallas_call x1, Pallas kernels, collect(): pl.pallas_call(functools.partial(collect_kernel, count, halves), out_shap...  56.1 us
    all_to_all x2, starting transfers between devices, to_ranks(): lax.all_to_all(block, 'wide', 0, 0, axis_index_groups=rank_groups if oute...  17.3 us
  transfers between devices with their start and end apart: 5, of which 0 were waited for; matrix products, arithmetic and copies ran while one was open for 2% of the time, Pallas kernels for 18%

profile of v3, /device:TPU:0, one launch (start us, length us, event | category | flops | bytes accessed | tf_op | source)
XLA Modules:
  0.0 696.3 jit_solution(2557873453266693787)
XLA Ops:
  0.6 3.9 pack.1
  4.8 7.4 %all-to-all-start = ((bf16[8,64,1792]{2,1,0:T(8,128)(2,1)}), bf16[8,64,1792]{2,1,0:T(8,128)(2,1)S(1)}, u32[]{:S(2)}, u32[]{:S(2)}) async-start(bf16[8,64,1792]{2,1,0:T(8,128)(2,1)} %get-tuple-element.44), calls=%async_computation | async-start | bytes 3670016 | tf_op jit(solution)/shard_map/all_to_all | solution.py:1590
  12.2 0.1 reshape.166
  12.3 0.1 reshape.167
  12.5 0.1 copy.62
  12.5 0.6 convert_element_type.8.refs_2_
  13.2 0.6 pad.26.refs_4_
  13.8 0.6 fusion.11.refs_3_
  14.5 0.6 fusion.6.refs_1_
  15.2 0.6 copy-done.2
  15.8 87.8 %spread.1 = (bf16[4,8,16,4096]{3,2,1,0:T(8,128)(2,1)}, bf16[4,8,16,2176]{3,2,1,0:T(8,128)(2,1)}, bf16[4,8,64,512]{3,2,1,0:T(8,128)(2,1)}, bf16[8,16,256]{2,1,0:T(8,128)(2,1)}, s32[8,8,128]{2,1,0:T(8,128)}) custom-call(bf16[16,4096]{1,0:T(8,128)(2,1)} %copy-done.2, bf16[16,2176]{1,0:T(8,128)(2,1)} %fusion.6.refs_1_, ...), custom_call_target="tpu_custom_call" | custom-call | tf_op jit(solution)/shard_map/spread/pallas_call | solution.py:375
  103.7 0.1 select_reduce_fusion
  103.7 1.6 collective-permute-start
  105.4 0.1 copy.64
  105.4 0.1 reshape.169
  105.6 9.9 %all-to-all-start.1 = ((bf16[8,64,1792]{2,1,0:T(8,128)(2,1)}), bf16[8,64,1792]{2,1,0:T(8,128)(2,1)}, u32[]{:S(2)}, u32[]{:S(2)}) async-start(bf16[8,64,1792]{2,1,0:T(8,128)(2,1)} %get-tuple-element.54), calls=%async_computation.1 | async-start | bytes 3670016 | tf_op jit(solution)/shard_map/all_to_all | solution.py:1590
  115.5 0.1 reshape.168
  115.6 0.9 slice.74
  116.6 4.8 gather_fusion
  121.4 0.6 convert_bitcast_fusion.1.vectors
  122.1 1.0 broadcast_select_fusion.pieces
  123.1 28.4 %hyper.1 = (bf16[64,2048]{1,0:T(8,128)(2,1)}, bf16[512,1536]{1,0:T(8,128)(2,1)}, bf16[512,512]{1,0:T(8,128)(2,1)}, f32[512,512]{1,0:T(8,128)}, f32[512,2048]{1,0:T(8,128)}, /*index=5*/bf16[64,512]{1,0:T(8,128)(2,1)}) custom-call(bf16[512,512]{1,0:T(8,128)(2,1)} %broadcast_select_fusion.pieces, bf16[512,4096]{1,0:T(8,128)(2,1)} %bitcast.75, ...), custom_call_target="tpu_custom_call" | custom-call | tf_op jit(solution)/shard_map/hyper/pallas_call | solution.py:617
  151.5 0.5 collective-permute-start.2
  152.0 0.1 add.112
  152.1 0.8 add.114.refs_0_
  153.0 0.2 negate_select_fusion
  153.2 0.1 constant_dynamic-update-slice_fusion.9
  153.3 0.6 pad.27.refs_1_
  153.9 0.6 pad.28.refs_2_
  154.5 0.1 constant_dynamic-update-slice_fusion.14
  154.7 0.1 constant_dynamic-update-slice_fusion.13
  154.7 0.1 constant_dynamic-update-slice_fusion.7
  154.9 0.7 pad_maximum_fusion.refs_4_
  155.6 10.1 %section_gather.1 = bf16[4,64,2048]{2,1,0:T(8,128)(2,1)} custom-call(bf16[64,2048]{1,0:T(8,128)(2,1)} %get-tuple-element.51.block), custom_call_target="tpu_custom_call" | custom-call | tf_op jit(solution)/shard_map/section_gather/pallas_call | solution.py:137
  165.7 0.8 tile.8
  166.5 0.8 tile.20
  167.3 409.3 %decode.1 = (bf16[2,8,16,2048]{3,2,1,0:T(8,128)(2,1)}, bf16[2,8,16,2048]{3,2,1,0:T(8,128)(2,1)}, bf16[256,256]{1,0:T(8,128)(2,1)}, f32[8,128]{1,0:T(8,128)}) custom-call(s32[256,1]{1,0:T(8,128)} %add.114.refs_0_, s32[8,128]{1,0:T(8,128)} %pad.27.refs_1_, s32[8,128]{1,0:T(8,128)} %pad.28.refs_2_, bf16[256,2048]{1,0:T(8,128)(2,1)} %bitcast.82, ...), custom_call_target="tpu_custom_call" | custom-call | tf_op jit(solution)/shard_map/decode/pallas_call | solution.py:1516
  576.6 1.8 fusion.1
  578.4 1.5 fusion
  579.9 11.8 %section_sum.1 = (f32[64,2048]{1,0:T(8,128)}, f32[8,128]{1,0:T(8,128)}) custom-call(bf16[4,64,2048]{2,1,0:T(8,128)(2,1)} %bitcast.84, f32[8,128]{1,0:T(8,128)} %get-tuple-element.58.loss), custom_call_target="tpu_custom_call" | custom-call | tf_op jit(solution)/shard_map/section_sum/pallas_call | solution.py:191
  591.7 39.4 %hyper_back.1 = (bf16[512,4096]{1,0:T(8,128)(2,1)}, bf16[512,2176]{1,0:T(8,128)(2,1)}, bf16[2048,512]{1,0:T(8,128)(2,1)}) custom-call(f32[64,2048]{1,0:T(8,128)} %get-tuple-element.60.table_grad, bf16[512,512]{1,0:T(8,128)(2,1)} %broadcast_select_fusion.pieces, bf16[512,4096]{1,0:T(8,128)(2,1)} %bitcast.76, bf16[512,2176]{1,0:T(8,128)(2,1)} %bitcast.79, ...), custom_call_target="tpu_custom_call" | custom-call | tf_op jit(solution)/shard_map/hyper_back/pallas_call | solution.py:617
  631.1 56.1 %collect.1 = (f32[16,4096]{1,0:T(8,128)}, f32[16,2176]{1,0:T(8,128)}, f32[64,512]{1,0:T(8,128)}) custom-call(bf16[4,8,16,4096]{3,2,1,0:T(8,128)(2,1)} %bitcast.83, bf16[4,8,16,2176]{3,2,1,0:T(8,128)(2,1)} %bitcast.85, bf16[4,8,64,512]{3,2,1,0:T(8,128)(2,1)} %bitcast.86), custom_call_target="tpu_custom_call" | custom-call | tf_op jit(solution)/shard_map/collect/pallas_call | solution.py:553
  687.2 1.6 slice_reduce_fusion
  688.8 1.6 slice.71
  690.3 1.6 slice.70
  691.9 1.5 fusion.12
  693.4 1.2 slice.61
  694.6 1.6 copy.84
  (87 shorter events, 0.6 us)
Async XLA Ops:
  4.6 7.6 %copy-start.21 = (s32[1,2,64]{2,1,0:T(2,128)S(1)}, s32[1,2,64]{2,1,0:T(2,128)}, u32[]{:S(2)}) copy-start(s32[1,2,64]{2,1,0:T(2,128)} %param.27) | copy-start | bytes 1540
  4.6 7.7 %copy-start.22 = (s32[1,2,64]{2,1,0:T(2,128)S(1)}, s32[1,2,64]{2,1,0:T(2,128)}, u32[]{:S(2)}) copy-start(s32[1,2,64]{2,1,0:T(2,128)} %param.28) | copy-start | bytes 1540
  4.6 7.8 %copy-start.17 = (f32[16]{0:T(128)S(1)}, f32[16]{0:T(128)}, u32[]{:S(2)}) copy-start(f32[16]{0:T(128)} %param.34) | copy-start | bytes 196
  4.6 7.8 %copy-start.18 = (f32[16]{0:T(128)S(1)}, f32[16]{0:T(128)}, u32[]{:S(2)}) copy-start(f32[16]{0:T(128)} %param.33) | copy-start | bytes 196
  4.6 7.8 %copy-start.19 = (f32[16]{0:T(128)S(1)}, f32[16]{0:T(128)}, u32[]{:S(2)}) copy-start(f32[16]{0:T(128)} %param.40) | copy-start | bytes 196
  4.7 7.8 %copy-start.20 = (f32[16]{0:T(128)S(1)}, f32[16]{0:T(128)}, u32[]{:S(2)}) copy-start(f32[16]{0:T(128)} %param.39) | copy-start | bytes 196
  4.7 7.9 %copy-start.4 = (f32[64,512]{1,0:T(8,128)S(1)}, f32[64,512]{1,0:T(8,128)}, u32[]{:S(2)}) copy-start(f32[64,512]{1,0:T(8,128)} %param.42) | copy-start | bytes 393220
  4.7 8.5 %copy-start.5 = (f32[16,2048]{1,0:T(8,128)S(1)}, f32[16,2048]{1,0:T(8,128)}, u32[]{:S(2)}) copy-start(f32[16,2048]{1,0:T(8,128)} %param.43) | copy-start | bytes 393220
  4.7 9.1 %copy-start.15 = (bf16[2,256]{1,0:T(2,128)(2,1)S(1)}, bf16[2,256]{1,0:T(2,128)(2,1)}, u32[]{:S(2)}) copy-start(bf16[2,256]{1,0:T(2,128)(2,1)} %param.49) | copy-start | bytes 3076
  4.7 9.1 %copy-start.16 = (bf16[2,256]{1,0:T(2,128)(2,1)S(1)}, bf16[2,256]{1,0:T(2,128)(2,1)}, u32[]{:S(2)}) copy-start(bf16[2,256]{1,0:T(2,128)(2,1)} %param.44) | copy-start | bytes 3076
  4.7 9.7 %copy-start.8 = (f32[16,512]{1,0:T(8,128)S(1)}, f32[16,512]{1,0:T(8,128)}, u32[]{:S(2)}) copy-start(f32[16,512]{1,0:T(8,128)} %param.35) | copy-start | bytes 98308
  4.7 9.7 %copy-start.9 = (f32[16,512]{1,0:T(8,128)S(1)}, f32[16,512]{1,0:T(8,128)}, u32[]{:S(2)}) copy-start(f32[16,512]{1,0:T(8,128)} %param.36) | copy-start | bytes 98308
  4.7 9.7 %copy-start.10 = (f32[16,512]{1,0:T(8,128)S(1)}, f32[16,512]{1,0:T(8,128)}, u32[]{:S(2)}) copy-start(f32[16,512]{1,0:T(8,128)} %param.37) | copy-start | bytes 98308
  4.8 9.7 %copy-start.11 = (f32[16,512]{1,0:T(8,128)S(1)}, f32[16,512]{1,0:T(8,128)}, u32[]{:S(2)}) copy-start(f32[16,512]{1,0:T(8,128)} %param.38) | copy-start | bytes 98308
  4.8 10.4 %copy-start.6 = (f32[16,2048]{1,0:T(8,128)S(1)}, f32[16,2048]{1,0:T(8,128)}, u32[]{:S(2)}) copy-start(f32[16,2048]{1,0:T(8,128)} %param.41) | copy-start | bytes 393220
  4.8 98.9 %copy-start.23 = (s32[4]{0:T(128)S(1)}, s32[4]{0:T(128)}, u32[]{:S(2)}) copy-start(s32[4]{0:T(128)} %param.31) | copy-start | bytes 52
  4.8 98.9 %copy-start.24 = (s32[64]{0:T(128)S(1)}, s32[64]{0:T(128)}, u32[]{:S(2)}) copy-start(s32[64]{0:T(128)} %param.30) | copy-start | bytes 772
  4.8 100.5 %copy-start.14 = (s32[64,8]{0,1:T(8,128)S(1)}, s32[64,8]{0,1:T(8,128)}, u32[]{:S(2)}) copy-start(s32[64,8]{0,1:T(8,128)} %param.29) | copy-start | bytes 6148
  4.8 98.9 %all-to-all-start = ((bf16[8,64,1792]{2,1,0:T(8,128)(2,1)}), bf16[8,64,1792]{2,1,0:T(8,128)(2,1)S(1)}, u32[]{:S(2)}, u32[]{:S(2)}) async-start(bf16[8,64,1792]{2,1,0:T(8,128)(2,1)} %get-tuple-element.44), calls=%async_computation | async-start | bytes 3670016 | tf_op jit(solution)/shard_map/all_to_all | solution.py:1590
  15.2 0.7 copy-start.2
  103.7 19.3 %copy-start = (bf16[8,64,1792]{2,1,0:T(8,128)(2,1)}, bf16[8,64,1792]{2,1,0:T(8,128)(2,1)S(1)}, u32[]{:S(2)}) copy-start(bf16[8,64,1792]{2,1,0:T(8,128)(2,1)S(1)} %all-to-all-done.refs_7_) | copy-start | bytes 5505028
  103.7 47.8 %collective-permute-start = (bf16[8,64,1792]{2,1,0:T(8,128)(2,1)S(1)}, bf16[8,64,1792]{2,1,0:T(8,128)(2,1)}, u32[]{:S(2)}, u32[]{:S(2)}) collective-permute-start(bf16[8,64,1792]{2,1,0:T(8,128)(2,1)S(1)} %all-to-all-done.refs_7_), channel_id=1, source_target_pairs={{0,16},{8,24},{16,0},{24,8},{1,17},{9,25},{17,1},{25,9},{2,18},{10... | collective-permute-start | bytes 5505032 | tf_op jit(solution)/shard_map/ppermute | solution.py:1614
  105.6 60.1 %all-to-all-start.1 = ((bf16[8,64,1792]{2,1,0:T(8,128)(2,1)}), bf16[8,64,1792]{2,1,0:T(8,128)(2,1)}, u32[]{:S(2)}, u32[]{:S(2)}) async-start(bf16[8,64,1792]{2,1,0:T(8,128)(2,1)} %get-tuple-element.54), calls=%async_computation.1 | async-start | bytes 3670016 | tf_op jit(solution)/shard_map/all_to_all | solution.py:1590
  116.6 5.5 copy-start.7
  123.1 42.6 %collective-permute-start.1 = (bf16[8,64,1792]{2,1,0:T(8,128)(2,1)S(1)}, bf16[8,64,1792]{2,1,0:T(8,128)(2,1)}, u32[]{:S(2)}, u32[]{:S(2)}) collective-permute-start(bf16[8,64,1792]{2,1,0:T(8,128)(2,1)S(1)} %all-to-all-done.refs_7_), channel_id=1, source_target_pairs={{0,8},{8,0},{16,24},{24,16},{1,9},{9,1},{17,25},{25,17},{2,10},{10... | collective-permute-start | bytes 5505032 | tf_op jit(solution)/shard_map/ppermute | solution.py:1615
  123.1 29.9 %copy-start.13 = (bf16[2048]{0:T(1024)(128)(2,1)S(1)}, bf16[2048]{0:T(1024)(128)(2,1)}, u32[]{:S(2)}) copy-start(bf16[2048]{0:T(1024)(128)(2,1)} %param.53) | copy-start | bytes 12292
  123.1 30.2 %copy-start.12 = (s32[8,8,128]{2,1,0:T(8,128)S(1)}, s32[8,8,128]{2,1,0:T(8,128)}, u32[]{:S(2)}) copy-start(s32[8,8,128]{2,1,0:T(8,128)} %get-tuple-element.42) | copy-start | bytes 98308
  151.5 14.2 %collective-permute-start.2 = (bf16[8,64,1792]{2,1,0:T(8,128)(2,1)}, bf16[8,64,1792]{2,1,0:T(8,128)(2,1)}, u32[]{:S(2)}, u32[]{:S(2)}) collective-permute-start(bf16[8,64,1792]{2,1,0:T(8,128)(2,1)} %collective-permute-done.refs_8_), channel_id=1, source_target_pairs={{0,8},{8,0},{16,24},{24,16},{1,9},{9,1},{17,25},{25,17},{2,10},{10... | collective-permute-start | bytes 5505032 | tf_op jit(solution)/shard_map/ppermute | solution.py:1643
  576.6 1.8 copy-start.1
  576.6 1.8 copy-start.3

commit v4 on v3

--- a/solution.py
+++ b/solution.py
@@ -949,10 +949,7 @@
     )(*weights)
 
 
-def run(main, beside, most):
-    for count, _ in enumerate(main):
-        if beside is not None and count < most:
-            next(beside, None)
+ORDER = "grgrrgg"
 
 
 def finish(*steps):
@@ -1415,34 +1412,34 @@
     this.greet()
     this.moving = {}
     this.weight_copies()
-    phases = [(this.inject, this.close_inject)]
+    phases = [(this.inject, this.close_inject, 1)]
     for layer in range(2):
-        phases.append((functools.partial(this.attention, layer), this.close_attention(layer)))
-        phases.append((functools.partial(this.feed, layer), this.close_feed(layer)))
-    phases.append((this.head, this.close_head))
+        phases.append((functools.partial(this.attention, layer), this.close_attention(layer), 1))
+        phases.append((functools.partial(this.feed, layer), this.close_feed(layer), 2))
+    phases.append((this.head, this.close_head, 2))
     for layer in (1, 0):
-        phases.append((functools.partial(this.feed_back, layer), this.close_feed_back(layer)))
+        phases.append((functools.partial(this.feed_back, layer), this.close_feed_back(layer), 2))
         phases.append(
-            (functools.partial(this.attention_back, layer), this.close_attention_back(layer))
-        )
-    reduces, gathers = {}, {}
-
-    def settle(half, *beside):
-        if half in reduces:
-            finish(*beside, reduces.pop(half))
-            gathers[half] = this.gather(half)
-        else:
-            finish(*beside)
-
-    for work, close in phases:
+            (functools.partial(this.attention_back, layer), this.close_attention_back(layer), 1)
+        )
+    gathers = {}
+    sent = None
+    for work, close, parts in phases:
         for half in (FIRST, SECOND):
-            other = 1 - half
-            settle(other, gathers.pop(half, iter(())))
-            run(work(half), gathers.get(other), LINES - 1)
+            gather = gathers.pop(half, iter(()))
+            reduce = sent or iter(())
+            for kind in ORDER:
+                next(gather if kind == "g" else reduce, None)
+            for count, _ in enumerate(work(half)):
+                if count + 1 == parts:
+                    finish(reduce)
+            finish(reduce)
+            if sent is not None:
+                gathers[1 - half] = this.gather(1 - half)
             this.send(half)
-            reduces[half] = this.reduce(half, close)
-    settle(SECOND, gathers.pop(FIRST))
-    finish(gathers.pop(SECOND))
+            sent = this.reduce(half, close)
+    finish(gathers.pop(FIRST), sent)
+    finish(this.gather(SECOND))
     outs = [
         pltpu.make_async_copy(
             this.gathered.at[half], this.grad_out.at[half], this.keep_sem.at[half]
@@ -1524,6 +1521,337 @@
     )(*inputs.values(), *far_inputs.values())
 
 
+class Collector:
+    def __init__(self, halves, refs):
+        for name, ref in refs.items():
+            setattr(self, name, ref)
+        self.halves = halves
+        self.section, self.partner, self.across, self.wide, self.wide_at = all_places(halves)
+        self.groups = ((1, 1), (1, 0), (0, 1), (0, 0))
+
+    def greet(self):
+        beside = self.wide + 1 - 2 * (self.wide % 2)
+        peers = [{"section": self.partner}, {"section": self.across}, {"wide": beside}]
+        greet(peers + [{"wide": self.wide_at(j)} for j in range(1, self.halves)])
+
+    def steps(self, n):
+        return steps_of(n % 2 == 0, self.section, self.partner, self.across, self.wide)
+
+    def block(self, n, home, flip_b, flip_a, j):
+        (_, y_a, x_a), (_, y_b, x_b) = self.steps(n)
+        flips_y = (y_a and flip_a) or (y_b and flip_b)
+        flips_x = (x_a and flip_a) or (x_b and flip_b)
+        section, wide = owner_of(home, flips_y, flips_x, self.wide_at(j))
+        return self.partials[n].at[section * (2 * self.halves) + wide]
+
+    def core_copy(self, n, fb, fa, j):
+        slot = (fb * 2 + fa) * self.halves + j
+        return remote(
+            self.block(n, self.partner, fb, fa, j),
+            self.core_in[n].at[slot],
+            self.core_send.at[n, slot],
+            self.core_recv.at[n, slot],
+            {"section": self.partner},
+        )
+
+    def b_copy(self, n, fa, j):
+        _, (peer, _, _) = self.steps(n)
+        slot = fa * self.halves + j
+        return remote(
+            self.block(n, self.section, 1, fa, j),
+            self.b_in[n].at[slot],
+            self.b_send.at[n, slot],
+            self.b_recv.at[n, slot],
+            peer,
+        )
+
+    def a_copy(self, n, j):
+        (peer, _, _), _ = self.steps(n)
+        return remote(
+            self.block(n, self.section, 0, 1, j),
+            self.a_in[n].at[j],
+            self.a_send.at[n, j],
+            self.a_recv.at[n, j],
+            peer,
+        )
+
+    def z_copy(self, n, j):
+        return remote(
+            self.block(n, self.section, 0, 0, j),
+            self.z_in[n].at[j],
+            self.z_send.at[n, j],
+            self.z_recv.at[n, j],
+            {"wide": self.wide_at(j)},
+        )
+
+    def add(self, block, more):
+        block[...] = (block[...].astype(jnp.float32) + more.astype(jnp.float32)).astype(jnp.bfloat16)
+
+    def over(self, first, body):
+        def step(j, carry):
+            body(j)
+            return carry
+
+        lax.fori_loop(first, self.halves, step, 0)
+
+    def start(self, n):
+        for fb, fa in self.groups:
+            self.over(0, lambda j: self.core_copy(n, fb, fa, j).start())
+
+    def sum_core(self, n):
+        for fb, fa in self.groups:
+
+            def body(j):
+                slot = (fb * 2 + fa) * self.halves + j
+                self.core_copy(n, fb, fa, j).wait_recv()
+                self.add(self.block(n, self.section, fb, fa, j), self.core_in[n][slot])
+                if fb:
+                    self.b_copy(n, fa, j).start()
+
+            self.over(0, body)
+
+    def sum_b(self, n):
+        for fa in (1, 0):
+
+            def body(j):
+                self.b_copy(n, fa, j).wait_recv()
+                block = self.block(n, self.section, 0, fa, j)
+                self.add(block, self.b_in[n][fa * self.halves + j])
+                if fa:
+                    self.a_copy(n, j).start()
+
+            self.over(0, body)
+
+    def sum_a(self, n):
+        def body(j):
+            self.a_copy(n, j).wait_recv()
+            self.add(self.block(n, self.section, 0, 0, j), self.a_in[n][j])
+            self.z_copy(n, j).start()
+
+        self.over(1, body)
+        self.a_copy(n, 0).wait_recv()
+        own = self.block(n, self.section, 0, 0, 0)[...]
+        self.sums[n][...] = own.astype(jnp.float32) + self.a_in[n][0].astype(jnp.float32)
+
+    def sum_lines(self, n):
+        def body(j):
+            self.z_copy(n, j).wait_recv()
+            self.sums[n][...] += self.z_in[n][j].astype(jnp.float32)
+
+        self.over(1, body)
+
+    def drain(self, n):
+        def body(j):
+            for fb, fa in self.groups:
+                self.core_copy(n, fb, fa, j).wait_send()
+            self.b_copy(n, 0, j).wait_send()
+            self.b_copy(n, 1, j).wait_send()
+            self.a_copy(n, j).wait_send()
+
+        self.over(0, body)
+        self.over(1, lambda j: self.z_copy(n, j).wait_send())
+
+
+EMBED, EXPAND, REDUCE, FRONT, REAR = range(5)
+
+
+def hyper_collect_kernel(slots, halves, names, *refs):
+    refs = dict(zip(names, refs))
+    for name in ("sums", "partials", "core_in", "b_in", "a_in", "z_in"):
+        refs[name] = [refs.pop(f"{name}{n}") for n in range(5)]
+    this = Collector(halves, refs)
+    first, second, third, vectors = this.first, this.second, this.third, this.vectors
+    entered, outcome_low, feed_grad = this.entered, this.outcome_low, this.feed_grad
+    width = this.pieces.shape[1]
+    count, feed = this.pieces.shape[0], third.shape[0]
+    depth = this.table_grad.shape[1]
+    head = width // HYPER_HEAD_COUNT
+    scale = head ** (-0.5)
+    this.greet()
+
+    def store(n, columns, values):
+        block = this.partials[n]
+        block[:, :, columns] = values.astype(jnp.bfloat16).reshape(
+            block.shape[0], block.shape[1], values.shape[1]
+        )
+
+    grad_low = this.table_grad[...].astype(jnp.bfloat16)
+    pooled_turned = jnp.transpose(this.pooled[...].astype(jnp.float32)).astype(jnp.bfloat16)
+    for start in range(0, depth, TILE):
+        store(EMBED, pl.ds(start, TILE), matmul(pooled_turned, grad_low[:, start : start + TILE]))
+    this.start(EMBED)
+    pooled_grad = times_trans(grad_low, second[:, pl.ds(0, depth)]) / slots
+    outcome_grad = jnp.broadcast_to(pooled_grad[:, None, :], (count // slots, slots, width))
+    outcome_grad = outcome_grad.reshape(count, width)
+    outcome_low[...] = outcome_grad.astype(jnp.bfloat16)
+    normed, inverse = center_norm(this.middle[...])
+    entered[...] = jnp.transpose(normed * vectors[2:3] + vectors[3:4]).astype(jnp.bfloat16)
+    feed_grad[...] = jnp.zeros_like(feed_grad)
+    this.sum_core(EMBED)
+
+    def feed_tiles(low, high):
+        @pl.loop(low, high)
+        def _(n):
+            start = pl.multiple_of(n * TILE, TILE)
+            tile = pl.ds(start, TILE)
+            columns = pl.ds(pl.multiple_of(4 * width + start, TILE), TILE)
+            values = this.expanded[:, tile]
+            erf = 0.5 * (1.0 + lax.erf(values * inv_root_two))
+            active = (values * erf).astype(jnp.bfloat16)
+            block = this.partials[REDUCE]
+            owners = TILE // block.shape[1]
+            turned = trans_times(active, outcome_low[...]).astype(jnp.bfloat16)
+            block[pl.ds(n * owners, owners)] = turned.reshape(owners, block.shape[1], width)
+            active_grad = times_trans(outcome_low[...], third[tile, :])
+            slope = erf + values * jnp.exp(-0.5 * values * values) * inv_root_tau
+            low_grad = (active_grad * slope).astype(jnp.bfloat16)
+            store(EXPAND, tile, matmul(entered[...], low_grad))
+            feed_grad[...] += times_trans(low_grad, first[:, columns])
+
+    tiles = feed // TILE
+    feed_tiles(0, tiles // 2)
+    this.sum_b(EMBED)
+    feed_tiles(tiles // 2, tiles)
+    this.start(EXPAND)
+    this.start(REDUCE)
+    this.sum_a(EMBED)
+
+    grad = feed_grad[...]
+    scale_two = jnp.sum(grad * normed, axis=0, keepdims=True)
+    shift_two = jnp.sum(grad, axis=0, keepdims=True)
+    middle_grad = outcome_grad + center_back(normed, inverse, grad * vectors[2:3])
+    middle_low = middle_grad.astype(jnp.bfloat16)
+    out_columns = pl.ds(3 * width, width)
+    store(REAR, pl.ds(width, width), trans_times(this.mixed[...], middle_low))
+    this.mixed_grad[...] = times_trans(middle_low, first[:, out_columns]).astype(jnp.bfloat16)
+    mask = same_entry(CHUNK, slots)
+    this.sum_core(EXPAND)
+
+    def attention_chunks(low, high):
+        @pl.loop(low, high)
+        def _(n):
+            rows = pl.ds(pl.multiple_of(n * CHUNK, CHUNK), CHUNK)
+            block = this.heads[rows, :]
+            outer_block = this.mixed_grad[rows, :]
+            grads = [[], [], []]
+            for start in range(0, width, head):
+                query, key, value = (
+                    block[:, part * width + start : part * width + start + head]
+                    for part in range(3)
+                )
+                outer = outer_block[:, start : start + head]
+                weights = attend(query, key, mask, scale)
+                weight_grad = times_trans(outer, value)
+                score_grad = weights * (
+                    weight_grad - jnp.sum(weights * weight_grad, axis=1, keepdims=True)
+                )
+                score_grad = score_grad.astype(jnp.bfloat16)
+                grads[0].append(matmul(score_grad, key) * scale)
+                grads[1].append(trans_times(score_grad, query) * scale)
+                grads[2].append(trans_times(weights.astype(jnp.bfloat16), outer))
+            for part in range(3):
+                this.heads_grad[rows, pl.ds(part * width, width)] = jnp.concatenate(
+                    grads[part], axis=1
+                ).astype(jnp.bfloat16)
+
+    chunks = count // CHUNK
+    attention_chunks(0, chunks // 2)
+    this.sum_core(REDUCE)
+    this.sum_b(EXPAND)
+    attention_chunks(chunks // 2, chunks)
+    this.sum_b(REDUCE)
+
+    normed, _ = center_norm(this.pieces[...].astype(jnp.float32))
+    entered[...] = jnp.transpose(normed * vectors[0:1] + vectors[1:2]).astype(jnp.bfloat16)
+    feed_grad[...] = jnp.zeros_like(feed_grad)
+    for start in range(0, 3 * width, TILE):
+        columns = pl.ds(start, TILE)
+        low_grad = this.heads_grad[:, columns]
+        target = (FRONT, start) if start < 2 * width else (REAR, start - 2 * width)
+        store(target[0], pl.ds(target[1], TILE), matmul(entered[...], low_grad))
+        feed_grad[...] += times_trans(low_grad, first[:, columns])
+        if start + TILE == 2 * width:
+            this.start(FRONT)
+            this.sum_a(EXPAND)
+            this.sum_a(REDUCE)
+
+    grad = feed_grad[...]
+    scale_one = jnp.sum(grad * normed, axis=0, keepdims=True)
+    shift_one = jnp.sum(grad, axis=0, keepdims=True)
+    row = lax.broadcasted_iota(jnp.int32, (LANES, width), 0)
+    summed = jnp.zeros((LANES, width), jnp.float32)
+    for n, item in enumerate((scale_one, shift_one, scale_two, shift_two)):
+        summed = jnp.where(row == n, item, summed)
+    store(REAR, pl.ds(2 * width, LANES), jnp.transpose(summed))
+    this.start(REAR)
+    this.sum_core(FRONT)
+    this.sum_core(REAR)
+    for n in (EMBED, EXPAND, REDUCE):
+        this.sum_lines(n)
+    this.sum_b(FRONT)
+    this.sum_b(REAR)
+    this.sum_a(FRONT)
+    this.sum_a(REAR)
+    this.sum_lines(FRONT)
+    this.sum_lines(REAR)
+    for n in range(5):
+        this.drain(n)
+
+
+def hyper_collect(collective_id, wides, pieces, slots, params, stored, table_grad):
+    count, width = pieces.shape
+    first, second, third, vectors = params
+    depth, feed = table_grad.shape[1], third.shape[0]
+    devices, halves = SECTIONS * wides, wides // 2
+    low, full = jnp.bfloat16, jnp.float32
+    rows = width // devices
+    shapes = [
+        (rows, depth),
+        (rows, feed),
+        (feed // devices, width),
+        (rows, 2 * width),
+        (rows, 2 * width + LANES),
+    ]
+    inputs = dict(
+        table_grad=table_grad,
+        pieces=pieces,
+        first=first,
+        second=second,
+        third=third,
+        vectors=vectors,
+    )
+    inputs.update(zip(("heads", "mixed", "middle", "expanded", "pooled"), stored))
+    outputs = {f"sums{n}": jax.ShapeDtypeStruct(shape, full) for n, shape in enumerate(shapes)}
+    scratch = dict(
+        entered=pltpu.VMEM((width, count), low),
+        outcome_low=pltpu.VMEM((count, width), low),
+        feed_grad=pltpu.VMEM((count, width), full),
+        heads_grad=pltpu.VMEM((count, 3 * width), low),
+        mixed_grad=pltpu.VMEM((count, width), low),
+    )
+    for name, number in (
+        ("partials", devices),
+        ("core_in", 4 * halves),
+        ("b_in", 2 * halves),
+        ("a_in", halves),
+        ("z_in", halves),
+    ):
+        for n, shape in enumerate(shapes):
+            scratch[f"{name}{n}"] = pltpu.VMEM((number,) + shape, low)
+    for name, number in (("core", 4), ("b", 2), ("a", 1), ("z", 1)):
+        scratch[name + "_send"] = dma_sems(5, number * halves)
+        scratch[name + "_recv"] = dma_sems(5, number * halves)
+    return pl.pallas_call(
+        functools.partial(hyper_collect_kernel, slots, halves, (*inputs, *outputs, *scratch)),
+        out_shape=tuple(outputs.values()),
+        in_specs=[IN_VMEM] * len(inputs),
+        out_specs=(IN_VMEM,) * len(outputs),
+        scratch_shapes=list(scratch.values()),
+        compiler_params=settings(collective_id),
+        name="hyper_collect",
+    )(*inputs.values())
+
+
 def team_groups(wides, outer):
     return [[rank * outer + team for team in range(outer)] for rank in range(wides // outer)]
 
@@ -1688,27 +2016,33 @@
         11, table_part.reshape(SECTIONS, entries, model_width), loss_block
     )
     mean_loss = loss_block[0, 0]
-    grads = hyper_backward(pieces, slot_count, params, hyper_stored, table_grad)
-    first, second, third = (
-        item.reshape(SECTIONS, wides, -1, item.shape[1]) for item in grads
-    )
-    first, second, third = collect(12, (first, second, third))
-    grad_query, grad_key, grad_value, grad_output = (
-        first[:, n * hyper_width : (n + 1) * hyper_width] for n in range(4)
-    )
+    if hyper_width // (SECTIONS * wides) % 16 == 0:
+        grad_embed, grad_expand, grad_reduce, front, rear = hyper_collect(
+            12, wides, pieces, slot_count, params, hyper_stored, table_grad
+        )
+    else:
+        grads = hyper_backward(pieces, slot_count, params, hyper_stored, table_grad)
+        grads = [item.reshape(SECTIONS, wides, -1, item.shape[1]) for item in grads]
+        first, second, grad_reduce = collect(12, grads)
+        grad_embed, grad_expand = second[:, :model_width], first[:, 4 * hyper_width :]
+        front = first[:, : 2 * hyper_width]
+        rear = jnp.concatenate(
+            [first[:, 2 * hyper_width : 4 * hyper_width], second[:, model_width:]], axis=1
+        )
+    vectors = rear[:, 2 * hyper_width : 2 * hyper_width + 4]
     return (
         mean_loss,
-        second[:, model_width],
-        second[:, model_width + 1],
-        grad_query,
-        grad_key,
-        grad_value,
-        grad_output,
-        second[:, model_width + 2],
-        second[:, model_width + 3],
-        first[:, 4 * hyper_width :],
-        third,
-        second[:, :model_width],
+        vectors[:, 0],
+        vectors[:, 1],
+        front[:, :hyper_width],
+        front[:, hyper_width:],
+        rear[:, :hyper_width],
+        rear[:, hyper_width : 2 * hyper_width],
+        vectors[:, 2],
+        vectors[:, 3],
+        grad_expand,
+        grad_reduce,
+        grad_embed,
     )
 
 

time: 705 us -> 595 us (0.84)
  Pallas kernels: 647 us -> 540 us
    pallas_call x1, Pallas kernels: 409 us -> 318 us  [decode(): pl.pallas_call(functools.partial(decode_kernel, (outer, tokens, share, q_...]
    pallas_call x2 -> x1, Pallas kernels: 67.9 us -> 28.4 us  [local(): pl.pallas_call(kernel, out_shape=tuple((jax.ShapeDtypeStruct(shape, kind)...]
    pallas_call x1, Pallas kernels: 56.1 us -> 80.2 us  [hyper_collect(): pl.pallas_call(functools.partial(hyper_collect_kernel, slots, halves, (*i...]
  transfers between devices with their start and end apart: 5 -> 5, of which waited for: 0 -> 0; matrix products, arithmetic and copies ran while one was open for 2% -> 2% of each run, Pallas kernels for 18% -> 21%
where the time goes in v4:
time: 595 us; the launch traced here: 591 us
  Pallas kernels  540 us (91%)
  local copies, waits for them, and re-layouts  21.7 us (4%)
  starting transfers between devices  19.4 us (3%)
    pallas_call x1, Pallas kernels, decode(): pl.pallas_call(functools.partial(decode_kernel, (outer, tokens, share, q_...  318 us
    pallas_call x1, Pallas kernels, spread(): pl.pallas_call(functools.partial(spread_kernel, count, halves, outer), ou...  87.8 us
    pallas_call x1, Pallas kernels, hyper_collect(): pl.pallas_call(functools.partial(hyper_collect_kernel, slots, halves, (*i...  80.2 us
    pallas_call x1, Pallas kernels, local(): pl.pallas_call(kernel, out_shape=tuple((jax.ShapeDtypeStruct(shape, kind)...  28.4 us
    all_to_all x2, starting transfers between devices, to_ranks(): lax.all_to_all(block, 'wide', 0, 0, axis_index_groups=rank_groups if oute...  17.3 us
  transfers between devices with their start and end apart: 5, of which 0 were waited for; matrix products, arithmetic and copies ran while one was open for 2% of the time, Pallas kernels for 21%

profile of v4, /device:TPU:0, one launch (start us, length us, event | category | flops | bytes accessed | tf_op | source)
XLA Modules:
  0.0 591.1 jit_solution(9894680566164637853)
XLA Ops:
  0.6 3.9 pack.1
  4.7 7.4 %all-to-all-start = ((bf16[8,64,1792]{2,1,0:T(8,128)(2,1)}), bf16[8,64,1792]{2,1,0:T(8,128)(2,1)S(1)}, u32[]{:S(2)}, u32[]{:S(2)}) async-start(bf16[8,64,1792]{2,1,0:T(8,128)(2,1)} %get-tuple-element.43), calls=%async_computation | async-start | bytes 3670016 | tf_op jit(solution)/shard_map/all_to_all | solution.py:1918
  12.1 0.1 reshape.157
  12.2 0.1 reshape.158
  12.4 0.1 copy.62
  12.5 0.6 convert_element_type.8.refs_2_
  13.1 0.6 pad.26.refs_4_
  13.8 0.6 fusion.11.refs_3_
  14.4 0.6 fusion.6.refs_1_
  15.1 0.6 copy-done.2
  15.7 87.8 %spread.1 = (bf16[4,8,16,4096]{3,2,1,0:T(8,128)(2,1)}, bf16[4,8,16,2176]{3,2,1,0:T(8,128)(2,1)}, bf16[4,8,64,512]{3,2,1,0:T(8,128)(2,1)}, bf16[8,16,256]{2,1,0:T(8,128)(2,1)}, s32[8,8,128]{2,1,0:T(8,128)}) custom-call(bf16[16,4096]{1,0:T(8,128)(2,1)} %copy-done.2, bf16[16,2176]{1,0:T(8,128)(2,1)} %fusion.6.refs_1_, ...), custom_call_target="tpu_custom_call" | custom-call | tf_op jit(solution)/shard_map/spread/pallas_call | solution.py:375
  103.6 0.1 select_reduce_fusion
  103.7 1.6 collective-permute-start
  105.3 0.1 copy.64
  105.4 0.1 reshape.160
  105.5 9.9 %all-to-all-start.1 = ((bf16[8,64,1792]{2,1,0:T(8,128)(2,1)}), bf16[8,64,1792]{2,1,0:T(8,128)(2,1)}, u32[]{:S(2)}, u32[]{:S(2)}) async-start(bf16[8,64,1792]{2,1,0:T(8,128)(2,1)} %get-tuple-element.53), calls=%async_computation.1 | async-start | bytes 3670016 | tf_op jit(solution)/shard_map/all_to_all | solution.py:1918
  115.4 0.1 reshape.159
  115.5 0.9 slice.71
  116.5 4.8 gather_fusion
  121.4 0.6 convert_bitcast_fusion.1.vectors.refs_5_
  122.0 0.9 broadcast_select_fusion.pieces.refs_1_
  123.0 28.4 %hyper.1 = (bf16[64,2048]{1,0:T(8,128)(2,1)}, bf16[512,1536]{1,0:T(8,128)(2,1)}, bf16[512,512]{1,0:T(8,128)(2,1)}, f32[512,512]{1,0:T(8,128)}, f32[512,2048]{1,0:T(8,128)}, /*index=5*/bf16[64,512]{1,0:T(8,128)(2,1)}) custom-call(bf16[512,512]{1,0:T(8,128)(2,1)} %broadcast_select_fusion.pieces.refs_1_, bf16[512,4096]{1,0:T(8,128)(2,1)} %bitcast.72, ...), custom_call_target="tpu_custom_call" | custom-call | tf_op jit(solution)/shard_map/hyper/pallas_call | solution.py:617
  151.4 0.5 collective-permute-start.2
  151.9 0.1 add.112
  152.0 0.8 add.114.refs_0_
  152.8 0.2 negate_select_fusion
  153.1 0.1 constant_dynamic-update-slice_fusion.9
  153.2 0.6 pad.27.refs_1_
  153.8 0.6 pad.28.refs_2_
  154.5 0.1 constant_dynamic-update-slice_fusion.8
  154.6 0.1 constant_dynamic-update-slice_fusion.13
  154.6 0.1 constant_dynamic-update-slice_fusion.7
  154.8 0.7 pad_maximum_fusion.refs_4_
  155.4 10.1 %section_gather.1 = bf16[4,64,2048]{2,1,0:T(8,128)(2,1)} custom-call(bf16[64,2048]{1,0:T(8,128)(2,1)} %get-tuple-element.50.block), custom_call_target="tpu_custom_call" | custom-call | tf_op jit(solution)/shard_map/section_gather/pallas_call | solution.py:137
  165.6 0.8 tile.8
  166.4 0.8 tile.20
  167.2 318.2 %decode.1 = (bf16[2,8,16,2048]{3,2,1,0:T(8,128)(2,1)}, bf16[2,8,16,2048]{3,2,1,0:T(8,128)(2,1)}, bf16[256,256]{1,0:T(8,128)(2,1)}, f32[8,128]{1,0:T(8,128)}) custom-call(s32[256,1]{1,0:T(8,128)} %add.114.refs_0_, s32[8,128]{1,0:T(8,128)} %pad.27.refs_1_, s32[8,128]{1,0:T(8,128)} %pad.28.refs_2_, bf16[256,2048]{1,0:T(8,128)(2,1)} %bitcast.79, ...), custom_call_target="tpu_custom_call" | custom-call | tf_op jit(solution)/shard_map/decode/pallas_call | solution.py:1513
  485.4 1.8 fusion.1
  487.2 1.4 fusion
  488.7 11.7 %section_sum.1 = (f32[64,2048]{1,0:T(8,128)}, f32[8,128]{1,0:T(8,128)}) custom-call(bf16[4,64,2048]{2,1,0:T(8,128)(2,1)} %bitcast.80, f32[8,128]{1,0:T(8,128)} %get-tuple-element.57.loss), custom_call_target="tpu_custom_call" | custom-call | tf_op jit(solution)/shard_map/section_sum/pallas_call | solution.py:191
  500.4 80.2 %hyper_collect.1 = (f32[16,2048]{1,0:T(8,128)}, f32[16,2048]{1,0:T(8,128)}, f32[64,512]{1,0:T(8,128)}, f32[16,1024]{1,0:T(8,128)}, f32[16,1152]{1,0:T(8,128)}) custom-call(f32[64,2048]{1,0:T(8,128)} %get-tuple-element.59.refs_0_, bf16[512,512]{1,0:T(8,128)(2,1)} %broadcast_select_fusion.pieces.refs_1_, bf16[512,4096]{1,0:T(8,128)(2,1)} %bitcast.73, ...), custom_call_target="tpu_custom_call" | custom-call | tf_op jit(solution)/shard_map/hyper_collect/pallas_call | solution.py:1844
  580.7 1.6 slice_reduce_fusion
  582.2 1.4 fusion.12
  583.6 1.2 slice.60
  584.8 1.4 fusion.13
  586.2 1.6 copy.86
  587.8 1.6 copy.87
  589.4 1.6 copy.88
  (87 shorter events, 0.6 us)
Async XLA Ops:
  4.5 7.6 %copy-start.21 = (s32[1,2,64]{2,1,0:T(2,128)S(1)}, s32[1,2,64]{2,1,0:T(2,128)}, u32[]{:S(2)}) copy-start(s32[1,2,64]{2,1,0:T(2,128)} %param.27) | copy-start | bytes 1540
  4.5 7.7 %copy-start.22 = (s32[1,2,64]{2,1,0:T(2,128)S(1)}, s32[1,2,64]{2,1,0:T(2,128)}, u32[]{:S(2)}) copy-start(s32[1,2,64]{2,1,0:T(2,128)} %param.28) | copy-start | bytes 1540
  4.5 7.8 %copy-start.17 = (f32[16]{0:T(128)S(1)}, f32[16]{0:T(128)}, u32[]{:S(2)}) copy-start(f32[16]{0:T(128)} %param.34) | copy-start | bytes 196
  4.6 7.8 %copy-start.18 = (f32[16]{0:T(128)S(1)}, f32[16]{0:T(128)}, u32[]{:S(2)}) copy-start(f32[16]{0:T(128)} %param.33) | copy-start | bytes 196
  4.6 7.8 %copy-start.19 = (f32[16]{0:T(128)S(1)}, f32[16]{0:T(128)}, u32[]{:S(2)}) copy-start(f32[16]{0:T(128)} %param.40) | copy-start | bytes 196
  4.6 7.8 %copy-start.20 = (f32[16]{0:T(128)S(1)}, f32[16]{0:T(128)}, u32[]{:S(2)}) copy-start(f32[16]{0:T(128)} %param.39) | copy-start | bytes 196
  4.6 7.9 %copy-start.4 = (f32[64,512]{1,0:T(8,128)S(1)}, f32[64,512]{1,0:T(8,128)}, u32[]{:S(2)}) copy-start(f32[64,512]{1,0:T(8,128)} %param.42) | copy-start | bytes 393220
  4.6 8.5 %copy-start.5 = (f32[16,2048]{1,0:T(8,128)S(1)}, f32[16,2048]{1,0:T(8,128)}, u32[]{:S(2)}) copy-start(f32[16,2048]{1,0:T(8,128)} %param.43) | copy-start | bytes 393220
  4.6 9.1 %copy-start.15 = (bf16[2,256]{1,0:T(2,128)(2,1)S(1)}, bf16[2,256]{1,0:T(2,128)(2,1)}, u32[]{:S(2)}) copy-start(bf16[2,256]{1,0:T(2,128)(2,1)} %param.49) | copy-start | bytes 3076
  4.6 9.1 %copy-start.16 = (bf16[2,256]{1,0:T(2,128)(2,1)S(1)}, bf16[2,256]{1,0:T(2,128)(2,1)}, u32[]{:S(2)}) copy-start(bf16[2,256]{1,0:T(2,128)(2,1)} %param.44) | copy-start | bytes 3076
  4.6 9.7 %copy-start.8 = (f32[16,512]{1,0:T(8,128)S(1)}, f32[16,512]{1,0:T(8,128)}, u32[]{:S(2)}) copy-start(f32[16,512]{1,0:T(8,128)} %param.35) | copy-start | bytes 98308
  4.7 9.7 %copy-start.9 = (f32[16,512]{1,0:T(8,128)S(1)}, f32[16,512]{1,0:T(8,128)}, u32[]{:S(2)}) copy-start(f32[16,512]{1,0:T(8,128)} %param.36) | copy-start | bytes 98308
  4.7 9.7 %copy-start.10 = (f32[16,512]{1,0:T(8,128)S(1)}, f32[16,512]{1,0:T(8,128)}, u32[]{:S(2)}) copy-start(f32[16,512]{1,0:T(8,128)} %param.37) | copy-start | bytes 98308
  4.7 9.7 %copy-start.11 = (f32[16,512]{1,0:T(8,128)S(1)}, f32[16,512]{1,0:T(8,128)}, u32[]{:S(2)}) copy-start(f32[16,512]{1,0:T(8,128)} %param.38) | copy-start | bytes 98308
  4.7 10.4 %copy-start.6 = (f32[16,2048]{1,0:T(8,128)S(1)}, f32[16,2048]{1,0:T(8,128)}, u32[]{:S(2)}) copy-start(f32[16,2048]{1,0:T(8,128)} %param.41) | copy-start | bytes 393220
  4.7 98.9 %copy-start.23 = (s32[4]{0:T(128)S(1)}, s32[4]{0:T(128)}, u32[]{:S(2)}) copy-start(s32[4]{0:T(128)} %param.31) | copy-start | bytes 52
  4.7 98.9 %copy-start.24 = (s32[64]{0:T(128)S(1)}, s32[64]{0:T(128)}, u32[]{:S(2)}) copy-start(s32[64]{0:T(128)} %param.30) | copy-start | bytes 772
  4.7 100.5 %copy-start.14 = (s32[64,8]{0,1:T(8,128)S(1)}, s32[64,8]{0,1:T(8,128)}, u32[]{:S(2)}) copy-start(s32[64,8]{0,1:T(8,128)} %param.29) | copy-start | bytes 6148
  4.7 98.9 %all-to-all-start = ((bf16[8,64,1792]{2,1,0:T(8,128)(2,1)}), bf16[8,64,1792]{2,1,0:T(8,128)(2,1)S(1)}, u32[]{:S(2)}, u32[]{:S(2)}) async-start(bf16[8,64,1792]{2,1,0:T(8,128)(2,1)} %get-tuple-element.43), calls=%async_computation | async-start | bytes 3670016 | tf_op jit(solution)/shard_map/all_to_all | solution.py:1918
  15.1 0.7 copy-start.2
  103.7 19.3 %copy-start = (bf16[8,64,1792]{2,1,0:T(8,128)(2,1)}, bf16[8,64,1792]{2,1,0:T(8,128)(2,1)S(1)}, u32[]{:S(2)}) copy-start(bf16[8,64,1792]{2,1,0:T(8,128)(2,1)S(1)} %all-to-all-done.refs_7_) | copy-start | bytes 5505028
  103.7 47.7 %collective-permute-start = (bf16[8,64,1792]{2,1,0:T(8,128)(2,1)S(1)}, bf16[8,64,1792]{2,1,0:T(8,128)(2,1)}, u32[]{:S(2)}, u32[]{:S(2)}) collective-permute-start(bf16[8,64,1792]{2,1,0:T(8,128)(2,1)S(1)} %all-to-all-done.refs_7_), channel_id=1, source_target_pairs={{0,16},{8,24},{16,0},{24,8},{1,17},{9,25},{17,1},{25,9},{2,18},{10... | collective-permute-start | bytes 5505032 | tf_op jit(solution)/shard_map/ppermute | solution.py:1942
  105.5 60.1 %all-to-all-start.1 = ((bf16[8,64,1792]{2,1,0:T(8,128)(2,1)}), bf16[8,64,1792]{2,1,0:T(8,128)(2,1)}, u32[]{:S(2)}, u32[]{:S(2)}) async-start(bf16[8,64,1792]{2,1,0:T(8,128)(2,1)} %get-tuple-element.53), calls=%async_computation.1 | async-start | bytes 3670016 | tf_op jit(solution)/shard_map/all_to_all | solution.py:1918
  116.5 5.5 copy-start.7
  122.9 42.6 %collective-permute-start.1 = (bf16[8,64,1792]{2,1,0:T(8,128)(2,1)S(1)}, bf16[8,64,1792]{2,1,0:T(8,128)(2,1)}, u32[]{:S(2)}, u32[]{:S(2)}) collective-permute-start(bf16[8,64,1792]{2,1,0:T(8,128)(2,1)S(1)} %all-to-all-done.refs_7_), channel_id=1, source_target_pairs={{0,8},{8,0},{16,24},{24,16},{1,9},{9,1},{17,25},{25,17},{2,10},{10... | collective-permute-start | bytes 5505032 | tf_op jit(solution)/shard_map/ppermute | solution.py:1943
  122.9 29.9 %copy-start.13 = (bf16[2048]{0:T(1024)(128)(2,1)S(1)}, bf16[2048]{0:T(1024)(128)(2,1)}, u32[]{:S(2)}) copy-start(bf16[2048]{0:T(1024)(128)(2,1)} %param.53) | copy-start | bytes 12292
  122.9 30.2 %copy-start.12 = (s32[8,8,128]{2,1,0:T(8,128)S(1)}, s32[8,8,128]{2,1,0:T(8,128)}, u32[]{:S(2)}) copy-start(s32[8,8,128]{2,1,0:T(8,128)} %get-tuple-element.41) | copy-start | bytes 98308
  151.4 14.2 %collective-permute-start.2 = (bf16[8,64,1792]{2,1,0:T(8,128)(2,1)}, bf16[8,64,1792]{2,1,0:T(8,128)(2,1)}, u32[]{:S(2)}, u32[]{:S(2)}) collective-permute-start(bf16[8,64,1792]{2,1,0:T(8,128)(2,1)} %collective-permute-done.refs_8_), channel_id=1, source_target_pairs={{0,8},{8,0},{16,24},{24,16},{1,9},{9,1},{17,25},{25,17},{2,10},{10... | collective-permute-start | bytes 5505032 | tf_op jit(solution)/shard_map/ppermute | solution.py:1971
  485.4 1.8 copy-start.1
  485.4 1.8 copy-start.3

commit v5 on v4

--- a/solution.py
+++ b/solution.py
@@ -226,9 +226,13 @@
     return section, (wide_block + 1 - 2 * (wide_block % 2) if flips_x else wide_block)
 
 
-def spread_kernel(count, halves, outer, *refs):
-    blocks, notes = refs[:count], refs[count : count + 2]
-    gathereds, notes_out = refs[count + 2 : 2 * count + 2], refs[2 * count + 2 : 2 * count + 4]
+def spread_kernel(count, halves, outer, work, *refs):
+    blocks, notes, columns = refs[:count], refs[count : count + 2], refs[count + 2 : count + 4]
+    refs = refs[count + 4 :]
+    extra, refs = refs[: work.inputs], refs[work.inputs :]
+    gathereds, notes_out, columns_out = refs[:count], refs[count : count + 2], refs[count + 2 : count + 4]
+    refs = refs[count + 4 :]
+    extra, refs = extra + refs[: work.outputs], refs[work.outputs :]
     (
         keep_sem,
         note_keep,
@@ -242,7 +246,7 @@
         a_recv,
         b_recv,
         c_recv,
-    ) = refs[2 * count + 4 :]
+    ) = refs[:12]
     section, partner, across, wide, wide_at = all_places(halves)
     rank, team = wide // outer, wide % outer
     members = [None] + [{"wide": (rank + k) % TEAM * outer + team} for k in range(1, TEAM)]
@@ -268,6 +272,23 @@
         for m in range(2)
         for k in range(1, TEAM)
     ]
+    column_copies = []
+    for layer in range(2):
+        column_copies.append(
+            pltpu.make_async_copy(
+                columns[layer].at[rank], columns_out[layer].at[rank], note_keep.at[2 + layer]
+            )
+        )
+        column_copies += [
+            remote(
+                columns[layer].at[(rank + k) % TEAM],
+                columns_out[layer].at[rank],
+                note_send.at[2 + layer, k],
+                note_recv.at[2 + layer, k],
+                members[k],
+            )
+            for k in (4, 3, 5, 2, 6, 1, 7)
+        ]
     for copy in note_keeps + note_copies:
         copy.start()
 
@@ -326,6 +347,8 @@
         return carry
 
     lax.fori_loop(1, halves, pass_z, 0)
+    for copy in column_copies:
+        copy.start()
 
     def pass_a(j, carry):
         for n in range(count):
@@ -366,31 +389,46 @@
         return carry
 
     lax.fori_loop(1, halves, drain_z, 0)
-    for copy in note_keeps + note_copies:
+    work.run(gathereds, extra + refs[12:])
+    for copy in note_keeps + note_copies + column_copies:
         copy.wait()
 
 
-def spread(collective_id, wides, outer, blocks, notes):
+class Work:
+    def __init__(self, run=None, operands=(), outs=(), scratch=()):
+        self.body, self.operands, self.outs, self.scratch = run, operands, outs, scratch
+        self.inputs, self.outputs = len(operands), len(outs)
+
+    def run(self, gathereds, refs):
+        if self.body is not None:
+            self.body(gathereds, *refs)
+
+
+def spread(collective_id, wides, outer, blocks, notes, columns, work):
     count, halves = len(blocks), wides // 2
+    place = ANYWHERE if work.body is None else IN_VMEM
     return pl.pallas_call(
-        functools.partial(spread_kernel, count, halves, outer),
+        functools.partial(spread_kernel, count, halves, outer, work),
         out_shape=tuple(
             jax.ShapeDtypeStruct((SECTIONS, wides) + block.shape, block.dtype) for block in blocks
         )
-        + tuple(jax.ShapeDtypeStruct((TEAM,) + note.shape, note.dtype) for note in notes),
-        in_specs=[ANYWHERE] * (count + 2),
-        out_specs=(ANYWHERE,) * (count + 2),
-        scratch_shapes=[dma_sems(count), dma_sems(2), dma_sems(2, TEAM), dma_sems(2, TEAM)]
+        + tuple(jax.ShapeDtypeStruct((TEAM,) + note.shape, note.dtype) for note in notes)
+        + tuple(jax.ShapeDtypeStruct(item.shape, item.dtype) for item in columns)
+        + tuple(jax.ShapeDtypeStruct(shape, kind) for shape, kind in work.outs),
+        in_specs=[ANYWHERE] * (count + 4) + [IN_VMEM] * work.inputs,
+        out_specs=(place,) * count + (ANYWHERE,) * 4 + (IN_VMEM,) * work.outputs,
+        scratch_shapes=[dma_sems(count), dma_sems(4), dma_sems(4, TEAM), dma_sems(4, TEAM)]
         + [
             dma_sems(count, halves),
             dma_sems(count, halves),
             dma_sems(count, 2 * halves),
             dma_sems(count, 2),
         ]
-        * 2,
+        * 2
+        + list(work.scratch),
         compiler_params=settings(collective_id),
         name="spread",
-    )(*blocks, *notes)
+    )(*blocks, *notes, *columns, *work.operands)
 
 
 def collect_kernel(count, halves, *refs):
@@ -629,9 +667,24 @@
 
 
 def same_entry(count, slots):
-    row = lax.broadcasted_iota(jnp.int32, (count, count), 0)
-    column = lax.broadcasted_iota(jnp.int32, (count, count), 1)
-    return row // slots == column // slots
+    entry = lax.broadcasted_iota(jnp.int32, (count // slots, slots, count), 0)
+    column = lax.broadcasted_iota(jnp.int32, (count // slots, slots, count), 2)
+    return entry == column // slots
+
+
+def gathered_slots(products, mask):
+    return jnp.sum(jnp.where(mask, products.reshape(mask.shape), 0.0), axis=0)
+
+
+def spread_slots(values, mask):
+    spread = jnp.where(mask, values[None], 0.0)
+    return spread.reshape(mask.shape[0] * mask.shape[1], mask.shape[2])
+
+
+def slot_weights(query, key, mask, scale):
+    scores = gathered_slots(times_trans(key, query), mask) * scale
+    mass = jnp.exp(scores - jnp.max(scores, axis=0, keepdims=True))
+    return mass / jnp.sum(mass, axis=0, keepdims=True)
 
 
 def gelu(values):
@@ -677,8 +730,9 @@
             query, key, value = (
                 block[:, part * width + start : part * width + start + head] for part in range(3)
             )
-            weights = attend(query, key, mask, head ** (-0.5))
-            mixed.append(matmul(weights.astype(jnp.bfloat16), value))
+            weights = slot_weights(query, key, mask, head ** (-0.5))
+            weights = spread_slots(weights, mask).astype(jnp.bfloat16)
+            mixed.append(trans_times(weights, value))
         mixed_out[rows, :] = jnp.concatenate(mixed, axis=1).astype(jnp.bfloat16)
 
     for start in range(0, width, TILE):
@@ -707,24 +761,60 @@
         table[:, columns] = matmul(pooled_out[...], second[:, columns]).astype(jnp.bfloat16)
 
 
+class Rows:
+    def __init__(self, blocks):
+        self.blocks = blocks
+        sections, wides, rows, columns = blocks.shape
+        self.wides, self.rows, self.shape = wides, rows, (sections * wides * rows, columns)
+
+    def __getitem__(self, index):
+        rows, columns = index
+        if rows == slice(None):
+            values = self.blocks[:, :, :, columns]
+        else:
+            first = rows.start // self.rows
+            owners = pl.ds(first % self.wides, rows.size // self.rows)
+            values = self.blocks[first // self.wides, owners]
+        return values.reshape(-1, values.shape[-1])
+
+
+def hyper_outs(count, slots, width, feed, depth):
+    entries = count // slots
+    return [
+        ((entries, depth), jnp.bfloat16),
+        ((count, 3 * width), jnp.bfloat16),
+        ((count, width), jnp.bfloat16),
+        ((count, width), jnp.float32),
+        ((count, feed), jnp.float32),
+        ((entries, width), jnp.bfloat16),
+    ]
+
+
+def hyper_scratch(count, width):
+    return [pltpu.VMEM((count, width), jnp.bfloat16), pltpu.VMEM((count, width), jnp.float32)]
+
+
+def hyper_work(pieces, slots, feed, depth):
+    count, width = pieces.shape
+
+    def run(gathereds, pieces_ref, vectors, *refs):
+        first, second, third = (Rows(blocks) for blocks in gathereds)
+        turned = jnp.transpose(second[:, pl.ds(depth, LANES)].astype(jnp.float32))
+        vectors[...] = turned[: vectors.shape[0]]
+        hyper_kernel(slots, pieces_ref, first, second, third, vectors, *refs)
+
+    outs = [((8, width), jnp.float32)] + hyper_outs(count, slots, width, feed, depth)
+    return Work(run, (pieces,), outs, hyper_scratch(count, width))
+
+
 def hyper_forward(pieces, slots, params):
     count, width = pieces.shape
-    first, second, third, vectors = params
-    feed = third.shape[0]
-    depth = second.shape[1] - LANES
-    entries = count // slots
+    _, second, third, _ = params
     table, *stored = local(
         functools.partial(hyper_kernel, slots),
         (pieces, *params),
-        [
-            ((entries, depth), jnp.bfloat16),
-            ((count, 3 * width), jnp.bfloat16),
-            ((count, width), jnp.bfloat16),
-            ((count, width), jnp.float32),
-            ((count, feed), jnp.float32),
-            ((entries, width), jnp.bfloat16),
-        ],
-        [pltpu.VMEM((count, width), jnp.bfloat16), pltpu.VMEM((count, width), jnp.float32)],
+        hyper_outs(count, slots, width, third.shape[0], second.shape[1] - LANES),
+        hyper_scratch(count, width),
         "hyper",
     )
     return table, stored
@@ -809,15 +899,16 @@
                 block[:, part * width + start : part * width + start + head] for part in range(3)
             )
             outer = outer_block[:, start : start + head]
-            weights = attend(query, key, mask, scale)
-            weight_grad = times_trans(outer, value)
+            weights = slot_weights(query, key, mask, scale)
+            weight_grad = gathered_slots(times_trans(value, outer), mask)
             score_grad = weights * (
-                weight_grad - jnp.sum(weights * weight_grad, axis=1, keepdims=True)
+                weight_grad - jnp.sum(weights * weight_grad, axis=0, keepdims=True)
             )
-            score_grad = score_grad.astype(jnp.bfloat16)
-            grads[0].append(matmul(score_grad, key) * scale)
-            grads[1].append(trans_times(score_grad, query) * scale)
-            grads[2].append(trans_times(weights.astype(jnp.bfloat16), outer))
+            score_grad = spread_slots(score_grad, mask).astype(jnp.bfloat16)
+            weights = spread_slots(weights, mask).astype(jnp.bfloat16)
+            grads[0].append(trans_times(score_grad, key) * scale)
+            grads[1].append(matmul(score_grad, query) * scale)
+            grads[2].append(matmul(weights, outer))
         for part in range(3):
             heads_grad[rows, pl.ds(part * width, width)] = jnp.concatenate(
                 grads[part], axis=1
@@ -889,8 +980,8 @@
 
 
 def pack_kernel(plan, rows, *refs):
-    sources, targets = refs[:5], refs[5:7]
-    blocks, sem = refs[7:12], refs[12]
+    sources, maps, targets = refs[:5], refs[5:16], refs[16:23]
+    blocks, sem, square = refs[23:28], refs[28], refs[29]
     section = lax.axis_index("section")
     mine = pl.ds(pl.multiple_of(section * rows, rows), rows)
     copies = [
@@ -903,6 +994,26 @@
     for layer in range(2):
         for copy in copies[layer]:
             copy.start()
+    *heads, expand, embed, reduce, vectors, norms, feeds, tokens = maps
+    first, second, third, gains, notes = targets[2:]
+    width = heads[0].shape[1]
+    for n, item in enumerate(heads):
+        first[:, n * width : (n + 1) * width] = item[...].astype(jnp.bfloat16)
+    first[:, 4 * width :] = expand[...].astype(jnp.bfloat16)
+    depth = embed.shape[1]
+    second[:, :depth] = embed[...].astype(jnp.bfloat16)
+    square[...] = jnp.zeros_like(square)
+    square[: vectors.shape[0], : vectors.shape[1]] = vectors[...]
+    second[:, depth:] = jnp.transpose(square[...])[: second.shape[0]].astype(jnp.bfloat16)
+    third[...] = reduce[...].astype(jnp.bfloat16)
+    gains[...] = jnp.zeros_like(gains)
+    gains[0:2, :] = norms[...].astype(jnp.float32)
+    gains[2:4, :] = feeds[...].astype(jnp.float32)
+    notes[...] = jnp.zeros_like(notes)
+    for n in range(2):
+        for batch in range(MB):
+            own = pl.ds(n * MB + batch, 1)
+            notes[n : n + 1, batch * LEN : (batch + 1) * LEN] = tokens[own, :]
     for layer in range(2):
         for copy in copies[layer]:
             copy.wait()
@@ -920,13 +1031,16 @@
                     targets[layer][rank, :, start : start + part.shape[1]] = part
 
 
-def pack(weights):
+def pack(weights, maps, vectors, norms, tokens):
     rows = weights[0].shape[1] // SECTIONS
     plan, width = column_plan(weights[0].shape[2], weights[1].shape[2], weights[3].shape[2])
-    if rows % 16:
+    low = jnp.bfloat16
+    owned, hyper_width = maps[0].shape
+    feed, depth = maps[4].shape[1], maps[5].shape[1]
+    if rows % 16 or owned % 16:
         section = lax.axis_index("section")
         mine = [lax.dynamic_slice_in_dim(item, section * rows, rows, 1) for item in weights]
-        return tuple(
+        columns = tuple(
             jnp.stack(
                 [
                     jnp.concatenate(
@@ -937,16 +1051,58 @@
             )
             for layer in range(2)
         )
+        first = jnp.concatenate(maps[:5], axis=1).astype(low)
+        padded = jnp.pad(vectors.T, ((0, 0), (0, LANES - vectors.shape[0])))
+        second = jnp.concatenate([maps[5], padded], axis=1).astype(low)
+        gains = jnp.pad(jnp.concatenate(norms, axis=0).astype(jnp.float32), ((0, 4), (0, 0)))
+        notes = jnp.pad(tokens.reshape(2, -1), ((0, 6), (0, 0)))
+        return (*columns, first, second, maps[6].astype(low), gains, notes)
+    shapes = [((TEAM, rows, width), low)] * 2 + [
+        ((owned, 4 * hyper_width + feed), low),
+        ((owned, depth + LANES), low),
+        (maps[6].shape, low),
+        ((8, norms[0].shape[1]), jnp.float32),
+        ((8, MB * LEN), jnp.int32),
+    ]
     return pl.pallas_call(
         functools.partial(pack_kernel, plan, rows),
-        out_shape=(jax.ShapeDtypeStruct((TEAM, rows, width), jnp.bfloat16),) * 2,
-        in_specs=[ANYWHERE] * 5,
-        out_specs=(IN_VMEM,) * 2,
-        scratch_shapes=[pltpu.VMEM((2, rows, item.shape[2]), jnp.bfloat16) for item in weights]
-        + [dma_sems(2, 5)],
+        out_shape=tuple(jax.ShapeDtypeStruct(shape, kind) for shape, kind in shapes),
+        in_specs=[ANYWHERE] * 5 + [IN_VMEM] * 11,
+        out_specs=(IN_VMEM,) * 7,
+        scratch_shapes=[pltpu.VMEM((2, rows, item.shape[2]), low) for item in weights]
+        + [dma_sems(2, 5), pltpu.VMEM((LANES, LANES), jnp.float32)],
         compiler_params=pltpu.CompilerParams(vmem_limit_bytes=VMEM_LIMIT),
         name="pack",
-    )(*weights)
+    )(*weights, *maps, vectors, *norms, tokens)
+
+
+def deliver_kernel(embed, expand, reduce, front, rear, *refs):
+    outs, square = refs[:11], refs[11]
+    width = front.shape[1] // 2
+    square[...] = jnp.zeros_like(square)
+    square[: rear.shape[0], :] = rear[:, 2 * width :]
+    vectors = jnp.transpose(square[...])
+    for n in range(4):
+        outs[n][...] = vectors[n, : rear.shape[0]]
+    outs[4][...] = front[:, :width]
+    outs[5][...] = front[:, width:]
+    outs[6][...] = rear[:, :width]
+    outs[7][...] = rear[:, width : 2 * width]
+    outs[8][...] = expand[...]
+    outs[9][...] = reduce[...]
+    outs[10][...] = embed[...]
+
+
+def deliver(embed, expand, reduce, front, rear):
+    rows, width = front.shape[0], front.shape[1] // 2
+    shapes = [(rows,)] * 4 + [(rows, width)] * 4 + [expand.shape, reduce.shape, embed.shape]
+    return local(
+        deliver_kernel,
+        (embed, expand, reduce, front, rear),
+        [(shape, jnp.float32) for shape in shapes],
+        [pltpu.VMEM((LANES, LANES), jnp.float32)],
+        "deliver",
+    )
 
 
 ORDER = "grgrrgg"
@@ -964,7 +1120,6 @@
         for name, ref in refs.items():
             setattr(self, name, ref)
         self.section, self.partner, self.across = section_places()
-        self.beyond = (self.partner + 2) % SECTIONS
         wide = lax.axis_index("wide")
         self.rank, self.team = wide // self.outer, wide % self.outer
         self.line, self.column = self.rank // 2, self.rank % 2
@@ -983,75 +1138,47 @@
         return {"wide": (self.rank + step) % TEAM * self.outer + self.team}
 
     def greet(self):
-        sections = [{"section": place} for place in (self.partner, self.across, self.beyond)]
+        sections = [{"section": place} for place in (self.partner, self.across)]
         greet(sections + [self.ranked(k) for k in range(1, TEAM)])
 
-    def weight_copies(self):
-        heads, feed = pl.ds(0, self.q_width + LANES), pl.ds(self.q_width + LANES, 2 * self.share)
-        places = (self.section, self.across, self.partner, self.beyond)
-        self.head_loads = [[], []]
-        self.feed_loads = [[], []]
-        for n, (piece, place) in enumerate(zip(self.pieces, places)):
-            self.head_loads[0].append(
-                pltpu.make_async_copy(
-                    piece.at[:, :, heads], self.head_weight.at[0, :, place], self.load_sem.at[0, n]
-                )
+    def share_copy(self, layer, part, kind):
+        split = self.q_width + LANES
+        columns = pl.ds(split, 2 * self.share) if part else pl.ds(0, split)
+        weight = self.feed_weight if part else self.head_weight
+        source = self.own[layer].at[:, :, columns]
+        target = weight.at[layer, :, self.section]
+        if kind == "keep":
+            return pltpu.make_async_copy(source, target, self.load_sem.at[layer, part, 0])
+        if kind == "whole":
+            source = self.down_source if part else self.out_source
+            target = self.down_weight if part else self.out_weight
+            return pltpu.make_async_copy(
+                source.at[layer], target.at[layer], self.load_sem.at[layer, part, 1]
             )
-            self.feed_loads[0].append(
-                pltpu.make_async_copy(
-                    piece.at[:, :, feed], self.feed_weight.at[0, :, place], self.load_sem.at[1, n]
-                )
-            )
-        self.head_loads[1].append(
-            pltpu.make_async_copy(
-                self.own_two.at[:, :, heads],
-                self.head_weight.at[1, :, self.section],
-                self.load_sem.at[2, 0],
-            )
-        )
-        self.feed_loads[1].append(
-            pltpu.make_async_copy(
-                self.own_two.at[:, :, feed],
-                self.feed_weight.at[1, :, self.section],
-                self.load_sem.at[3, 0],
-            )
-        )
-        for n, place in enumerate((self.across, self.beyond, self.partner)):
-            peer = {"section": place}
-            self.head_loads[1].append(
-                remote(
-                    self.own_two.at[:, :, heads],
-                    self.head_weight.at[1, :, self.section],
-                    self.share_send.at[0, n],
-                    self.share_recv.at[0, n],
-                    peer,
-                )
-            )
-            self.feed_loads[1].append(
-                remote(
-                    self.own_two.at[:, :, feed],
-                    self.feed_weight.at[1, :, self.section],
-                    self.share_send.at[1, n],
-                    self.share_recv.at[1, n],
-                    peer,
-                )
-            )
-        for layer in range(2):
-            self.head_loads[layer].append(
-                pltpu.make_async_copy(
-                    self.out_source.at[layer], self.out_weight.at[layer], self.load_sem.at[4, layer]
-                )
-            )
-            self.feed_loads[layer].append(
-                pltpu.make_async_copy(
-                    self.down_source.at[layer],
-                    self.down_weight.at[layer],
-                    self.load_sem.at[5, layer],
-                )
-            )
-        for layer in range(2):
-            for copy in self.head_loads[layer] + self.feed_loads[layer]:
-                copy.start()
+        n = ("far", "near", "on").index(kind)
+        if kind == "on":
+            source = target = weight.at[layer, :, self.across]
+        return remote(
+            source,
+            target,
+            self.share_send.at[layer, part, n],
+            self.share_recv.at[layer, part, n],
+            {"section": self.across if kind == "far" else self.partner},
+        )
+
+    def share_start(self, layer):
+        for part in range(2):
+            for kind in ("far", "near", "keep", "whole"):
+                self.share_copy(layer, part, kind).start()
+
+    def share_on(self, layer, part):
+        self.share_copy(layer, part, "far").wait_recv()
+        self.share_copy(layer, part, "on").start()
+
+    def share_end(self, layer, part):
+        for kind in ("keep", "whole", "near", "on"):
+            self.share_copy(layer, part, kind).wait()
+        self.share_copy(layer, part, "far").wait_send()
 
     def send(self, half):
         self.sides = getattr(self, "sides", {})
@@ -1156,12 +1283,13 @@
             columns = pl.ds(pl.multiple_of(n * TILE, TILE), TILE)
             self.store_partial(half, columns, trans_times(hits, self.table[:, columns]))
 
+        if half == SECOND:
+            self.share_on(0, 0)
         yield
 
     def attention(self, layer, half):
         if half == FIRST:
-            for copy in self.head_loads[layer]:
-                copy.wait()
+            self.share_end(layer, 0)
         own = pl.ds(half * HALF, HALF)
         width = self.q_width + LANES
         projected = matmul(self.rows(half), self.head_weight[layer].reshape(self.depth, width))
@@ -1185,22 +1313,30 @@
             columns = pl.ds(pl.multiple_of(n * TILE, TILE), TILE)
             self.store_partial(half, columns, matmul(mixed, self.out_weight[layer, :, columns]))
 
+        if half == SECOND:
+            self.share_on(layer, 1)
+            if layer == 0:
+                self.share_start(1)
         yield
 
     def feed(self, layer, half):
         if half == FIRST:
-            for copy in self.feed_loads[layer]:
-                copy.wait()
+            self.share_end(layer, 1)
         own = pl.ds(half * HALF, HALF)
         edge, tail = self.edge, self.tail
-        for low, high in self.tiles(2 * self.share // LANES, 3):
+        def project(columns, width):
+            block = self.feed_weight[layer, :, :, :, columns].reshape(self.depth, width)
+            self.kept[layer, own, columns] = matmul(self.rows(half), block)
+
+        full, rest = 2 * self.share // TILE, 2 * self.share % TILE
+        for low, high in self.tiles(full, 3):
 
             @pl.loop(low, high)
             def _(n):
-                columns = pl.ds(pl.multiple_of(n * LANES, LANES), LANES)
-                block = self.feed_weight[layer, :, :, :, columns].reshape(self.depth, LANES)
-                self.kept[layer, own, columns] = matmul(self.rows(half), block)
-
+                project(pl.ds(pl.multiple_of(n * TILE, TILE), TILE), TILE)
+
+            if high == full and rest:
+                project(pl.ds(full * TILE, rest), rest)
             yield
 
         def activate(gate, up):
@@ -1220,6 +1356,8 @@
                 block = self.down_weight[layer, :, columns]
                 self.store_partial(half, columns, matmul(self.active[...], block))
 
+            if half == SECOND and layer == 0 and low:
+                self.share_on(1, 0)
             yield
 
     def head(self, half):
@@ -1406,12 +1544,12 @@
 
 def decode_kernel(shape, names, *refs):
     refs = dict(zip(names, refs))
-    refs["pieces"] = [refs.pop(name) for name in ("own_one", "y_one", "core_one", "beyond_one")]
+    refs["own"] = [refs.pop(name) for name in ("own_one", "own_two")]
     refs["gains"] = [refs["gain_rows"].at[pl.ds(n, 1)] for n in range(5)]
     this = Decoder(shape, refs)
     this.greet()
     this.moving = {}
-    this.weight_copies()
+    this.share_start(0)
     phases = [(this.inject, this.close_inject, 1)]
     for layer in range(2):
         phases.append((functools.partial(this.attention, layer), this.close_attention(layer), 1))
@@ -1470,7 +1608,7 @@
         back_tables=tables[1],
     )
     far_inputs = dict(
-        zip(("own_one", "y_one", "core_one", "beyond_one", "own_two"), weights),
+        zip(("own_one", "own_two"), weights),
         out_source=out_source,
         down_source=down_source,
     )
@@ -1499,9 +1637,9 @@
         middle=pltpu.VMEM((2, 2, EACH, depth), full),
         grad=pltpu.VMEM((2, EACH, depth), full),
         stats=pltpu.VMEM((2, TEAM, 8, HALF), full),
-        load_sem=dma_sems(6, 4),
-        share_send=dma_sems(2, 3),
-        share_recv=dma_sems(2, 3),
+        load_sem=dma_sems(2, 2, 2),
+        share_send=dma_sems(2, 2, 3),
+        share_recv=dma_sems(2, 2, 3),
         stats_send=dma_sems(2, TEAM),
         stats_recv=dma_sems(2, TEAM),
         keep_sem=dma_sems(2),
@@ -1537,47 +1675,48 @@
     def steps(self, n):
         return steps_of(n % 2 == 0, self.section, self.partner, self.across, self.wide)
 
-    def block(self, n, home, flip_b, flip_a, j):
+    def lines(self, n, home, flip_b, flip_a):
         (_, y_a, x_a), (_, y_b, x_b) = self.steps(n)
         flips_y = (y_a and flip_a) or (y_b and flip_b)
         flips_x = (x_a and flip_a) or (x_b and flip_b)
-        section, wide = owner_of(home, flips_y, flips_x, self.wide_at(j))
-        return self.partials[n].at[section * (2 * self.halves) + wide]
-
-    def core_copy(self, n, fb, fa, j):
-        slot = (fb * 2 + fa) * self.halves + j
+        section, wide = owner_of(home, flips_y, flips_x, self.wide)
+        return self.partials[n].at[section, :, wide % 2]
+
+    def line_block(self, n, j):
+        return self.partials[n].at[self.section, (self.wide // 2 + j) % self.halves, self.wide % 2]
+
+    def core_copy(self, n, fb, fa):
         return remote(
-            self.block(n, self.partner, fb, fa, j),
-            self.core_in[n].at[slot],
-            self.core_send.at[n, slot],
-            self.core_recv.at[n, slot],
+            self.lines(n, self.partner, fb, fa),
+            self.core_in[n].at[fb, fa],
+            self.core_send.at[n, fb, fa],
+            self.core_recv.at[n, fb, fa],
             {"section": self.partner},
         )
 
-    def b_copy(self, n, fa, j):
+    def b_copy(self, n, fa):
         _, (peer, _, _) = self.steps(n)
-        slot = fa * self.halves + j
         return remote(
-            self.block(n, self.section, 1, fa, j),
-            self.b_in[n].at[slot],
-            self.b_send.at[n, slot],
-            self.b_recv.at[n, slot],
+            self.lines(n, self.section, 1, fa),
+            self.b_in[n].at[fa],
+            self.b_send.at[n, fa],
+            self.b_recv.at[n, fa],
             peer,
         )
 
-    def a_copy(self, n, j):
+    def a_copy(self, n):
         (peer, _, _), _ = self.steps(n)
         return remote(
-            self.block(n, self.section, 0, 1, j),
-            self.a_in[n].at[j],
-            self.a_send.at[n, j],
-            self.a_recv.at[n, j],
+            self.lines(n, self.section, 0, 1),
+            self.a_in[n],
+            self.a_send.at[n],
+            self.a_recv.at[n],
             peer,
         )
 
     def z_copy(self, n, j):
         return remote(
-            self.block(n, self.section, 0, 0, j),
+            self.line_block(n, j),
             self.z_in[n].at[j],
             self.z_send.at[n, j],
             self.z_recv.at[n, j],
@@ -1587,69 +1726,45 @@
     def add(self, block, more):
         block[...] = (block[...].astype(jnp.float32) + more.astype(jnp.float32)).astype(jnp.bfloat16)
 
-    def over(self, first, body):
-        def step(j, carry):
-            body(j)
-            return carry
-
-        lax.fori_loop(first, self.halves, step, 0)
-
     def start(self, n):
         for fb, fa in self.groups:
-            self.over(0, lambda j: self.core_copy(n, fb, fa, j).start())
+            self.core_copy(n, fb, fa).start()
 
     def sum_core(self, n):
         for fb, fa in self.groups:
-
-            def body(j):
-                slot = (fb * 2 + fa) * self.halves + j
-                self.core_copy(n, fb, fa, j).wait_recv()
-                self.add(self.block(n, self.section, fb, fa, j), self.core_in[n][slot])
-                if fb:
-                    self.b_copy(n, fa, j).start()
-
-            self.over(0, body)
+            self.core_copy(n, fb, fa).wait_recv()
+            self.add(self.lines(n, self.section, fb, fa), self.core_in[n][fb, fa])
+            if fb:
+                self.b_copy(n, fa).start()
 
     def sum_b(self, n):
         for fa in (1, 0):
-
-            def body(j):
-                self.b_copy(n, fa, j).wait_recv()
-                block = self.block(n, self.section, 0, fa, j)
-                self.add(block, self.b_in[n][fa * self.halves + j])
-                if fa:
-                    self.a_copy(n, j).start()
-
-            self.over(0, body)
+            self.b_copy(n, fa).wait_recv()
+            self.add(self.lines(n, self.section, 0, fa), self.b_in[n][fa])
+            if fa:
+                self.a_copy(n).start()
 
     def sum_a(self, n):
-        def body(j):
-            self.a_copy(n, j).wait_recv()
-            self.add(self.block(n, self.section, 0, 0, j), self.a_in[n][j])
+        self.a_copy(n).wait_recv()
+        self.add(self.lines(n, self.section, 0, 0), self.a_in[n][...])
+        for j in range(1, self.halves):
             self.z_copy(n, j).start()
 
-        self.over(1, body)
-        self.a_copy(n, 0).wait_recv()
-        own = self.block(n, self.section, 0, 0, 0)[...]
-        self.sums[n][...] = own.astype(jnp.float32) + self.a_in[n][0].astype(jnp.float32)
-
     def sum_lines(self, n):
-        def body(j):
+        total = self.line_block(n, 0)[...].astype(jnp.float32)
+        for j in range(1, self.halves):
             self.z_copy(n, j).wait_recv()
-            self.sums[n][...] += self.z_in[n][j].astype(jnp.float32)
-
-        self.over(1, body)
+            total = total + self.z_in[n][j].astype(jnp.float32)
+        self.sums[n][...] = total
 
     def drain(self, n):
-        def body(j):
-            for fb, fa in self.groups:
-                self.core_copy(n, fb, fa, j).wait_send()
-            self.b_copy(n, 0, j).wait_send()
-            self.b_copy(n, 1, j).wait_send()
-            self.a_copy(n, j).wait_send()
-
-        self.over(0, body)
-        self.over(1, lambda j: self.z_copy(n, j).wait_send())
+        for fb, fa in self.groups:
+            self.core_copy(n, fb, fa).wait_send()
+        for fa in (0, 1):
+            self.b_copy(n, fa).wait_send()
+        self.a_copy(n).wait_send()
+        for j in range(1, self.halves):
+            self.z_copy(n, j).wait_send()
 
 
 EMBED, EXPAND, REDUCE, FRONT, REAR = range(5)
@@ -1671,8 +1786,8 @@
 
     def store(n, columns, values):
         block = this.partials[n]
-        block[:, :, columns] = values.astype(jnp.bfloat16).reshape(
-            block.shape[0], block.shape[1], values.shape[1]
+        block[:, :, :, :, columns] = values.astype(jnp.bfloat16).reshape(
+            block.shape[:4] + (values.shape[1],)
         )
 
     grad_low = this.table_grad[...].astype(jnp.bfloat16)
@@ -1699,9 +1814,11 @@
             erf = 0.5 * (1.0 + lax.erf(values * inv_root_two))
             active = (values * erf).astype(jnp.bfloat16)
             block = this.partials[REDUCE]
-            owners = TILE // block.shape[1]
+            owned = block.shape[3]
+            lines = TILE // (2 * owned)
+            at = n * lines
             turned = trans_times(active, outcome_low[...]).astype(jnp.bfloat16)
-            block[pl.ds(n * owners, owners)] = turned.reshape(owners, block.shape[1], width)
+            block[at // halves, pl.ds(at % halves, lines)] = turned.reshape(lines, 2, owned, width)
             active_grad = times_trans(outcome_low[...], third[tile, :])
             slope = erf + values * jnp.exp(-0.5 * values * values) * inv_root_tau
             low_grad = (active_grad * slope).astype(jnp.bfloat16)
@@ -1740,15 +1857,16 @@
                     for part in range(3)
                 )
                 outer = outer_block[:, start : start + head]
-                weights = attend(query, key, mask, scale)
-                weight_grad = times_trans(outer, value)
+                weights = slot_weights(query, key, mask, scale)
+                weight_grad = gathered_slots(times_trans(value, outer), mask)
                 score_grad = weights * (
-                    weight_grad - jnp.sum(weights * weight_grad, axis=1, keepdims=True)
+                    weight_grad - jnp.sum(weights * weight_grad, axis=0, keepdims=True)
                 )
-                score_grad = score_grad.astype(jnp.bfloat16)
-                grads[0].append(matmul(score_grad, key) * scale)
-                grads[1].append(trans_times(score_grad, query) * scale)
-                grads[2].append(trans_times(weights.astype(jnp.bfloat16), outer))
+                score_grad = spread_slots(score_grad, mask).astype(jnp.bfloat16)
+                weights = spread_slots(weights, mask).astype(jnp.bfloat16)
+                grads[0].append(trans_times(score_grad, key) * scale)
+                grads[1].append(matmul(score_grad, query) * scale)
+                grads[2].append(matmul(weights, outer))
             for part in range(3):
                 this.heads_grad[rows, pl.ds(part * width, width)] = jnp.concatenate(
                     grads[part], axis=1
@@ -1829,18 +1947,18 @@
         heads_grad=pltpu.VMEM((count, 3 * width), low),
         mixed_grad=pltpu.VMEM((count, width), low),
     )
-    for name, number in (
-        ("partials", devices),
-        ("core_in", 4 * halves),
-        ("b_in", 2 * halves),
-        ("a_in", halves),
-        ("z_in", halves),
+    for name, slots_of in (
+        ("partials", (SECTIONS, halves, 2)),
+        ("core_in", (2, 2, halves)),
+        ("b_in", (2, halves)),
+        ("a_in", (halves,)),
+        ("z_in", (halves,)),
     ):
         for n, shape in enumerate(shapes):
-            scratch[f"{name}{n}"] = pltpu.VMEM((number,) + shape, low)
-    for name, number in (("core", 4), ("b", 2), ("a", 1), ("z", 1)):
-        scratch[name + "_send"] = dma_sems(5, number * halves)
-        scratch[name + "_recv"] = dma_sems(5, number * halves)
+            scratch[f"{name}{n}"] = pltpu.VMEM(slots_of + shape, low)
+    for name, numbers in (("core", (2, 2)), ("b", (2,)), ("a", ()), ("z", (halves,))):
+        scratch[name + "_send"] = dma_sems(5, *numbers)
+        scratch[name + "_recv"] = dma_sems(5, *numbers)
     return pl.pallas_call(
         functools.partial(hyper_collect_kernel, slots, halves, (*inputs, *outputs, *scratch)),
         out_shape=tuple(outputs.values()),
@@ -1854,14 +1972,6 @@
 
 def team_groups(wides, outer):
     return [[rank * outer + team for team in range(outer)] for rank in range(wides // outer)]
-
-
-SWAP_Y = [(source, (source + 2) % SECTIONS) for source in range(SECTIONS)]
-SWAP_CORE = [(source, source + 1 - 2 * (source % 2)) for source in range(SECTIONS)]
-
-
-def together(*items):
-    return lax.optimization_barrier(items)
 
 
 def all_teams(pieces, outer, groups):
@@ -1912,53 +2022,6 @@
     model_width = embed_map.shape[1]
     total_tokens = wides * MB * LEN
 
-    rank_groups = [[rank * outer + team for rank in range(TEAM)] for team in range(outer)]
-
-    def to_ranks(block):
-        return lax.all_to_all(
-            block, "wide", 0, 0, axis_index_groups=rank_groups if outer > 1 else None, tiled=True
-        )
-
-    blocks = pack((query_weight, key_weight, value_weight, gate_weight, up_weight))
-    own_one = to_ranks(blocks[0])
-
-    vectors = jnp.stack([prenorm_gain, prenorm_bias, midnorm_gain, midnorm_bias], axis=1)
-    vectors = jnp.pad(vectors, ((0, 0), (0, LANES - 4)))
-    first = jnp.concatenate([query_map, key_map, value_map, output_map, expand_map], axis=1)
-    second = jnp.concatenate([embed_map, vectors], axis=1)
-    gains = jnp.concatenate([attention_gain, feed_gain], axis=0)
-    gains = jnp.pad(gains, ((0, 16 - gains.shape[0]), (0, 0)))
-    notes = jnp.concatenate([token_ids.reshape(1, -1), targets.reshape(1, -1)], axis=0)
-    notes = jnp.pad(notes, ((0, 6), (0, 0)))
-    first, second, third, gains, notes = spread(
-        1,
-        wides,
-        outer,
-        (first.astype(jnp.bfloat16), second.astype(jnp.bfloat16), reduce_map.astype(jnp.bfloat16)),
-        (gains, notes),
-    )
-    first, own_one, block = together(first, own_one, blocks[1])
-    own_two = to_ranks(block)
-    y_one = lax.ppermute(own_one, "section", SWAP_Y)
-    core_one = lax.ppermute(own_one, "section", SWAP_CORE)
-    first = first.reshape(hyper_width, -1)
-    second = second.reshape(hyper_width, -1)
-    third = third.reshape(hyper_feed, hyper_width)
-    vectors = second[:, model_width : model_width + 8].astype(jnp.float32).T
-    params = (first, second, third, vectors)
-    if outer > 1:
-        gains = lax.all_gather(gains, "wide", axis=1, axis_index_groups=groups)
-        gains = gains.reshape(-1, gains.shape[2], gains.shape[3])
-        output_weight, down_weight = (
-            lax.all_gather(item, "wide", axis=1, axis_index_groups=groups, tiled=True)
-            for item in (output_weight, down_weight)
-        )
-    gains = gains.astype(jnp.float32).transpose(1, 0, 2).reshape(-1, model_width)
-    final_scale = final_gain.astype(jnp.float32).reshape(1, model_width)
-    gains = jnp.concatenate([gains[:4], final_scale, gains[:3]], axis=0)
-    notes = lax.dynamic_slice_in_dim(notes, section_index * 2, 2, 0)
-    ids, wanted = notes[:, 0].reshape(-1), notes[:, 1].reshape(-1)
-
     entries, slot_count = slot_ids.shape
     group_hits = (
         group_ids[:, None] == jnp.arange(group_offsets.shape[0], dtype=jnp.int32)[None, :]
@@ -1966,9 +2029,44 @@
     row_start = jnp.sum(group_hits * group_offsets[None, :], axis=1)
     piece_rows = (row_start[:, None] + slot_ids).reshape(-1)
     pieces = jnp.take(piece_table, piece_rows, axis=0)
-    table_shard, hyper_stored = hyper_forward(pieces, slot_count, params)
-    table_shard, y_one = together(table_shard, y_one)
-    beyond_one = lax.ppermute(y_one, "section", SWAP_CORE)
+
+    *columns, first, second, third, gains, notes = pack(
+        (query_weight, key_weight, value_weight, gate_weight, up_weight),
+        (query_map, key_map, value_map, output_map, expand_map, embed_map, reduce_map),
+        jnp.stack([prenorm_gain, prenorm_bias, midnorm_gain, midnorm_bias]),
+        (attention_gain, feed_gain),
+        jnp.concatenate([token_ids, targets], axis=1).reshape(2 * MB, LEN),
+    )
+    blocks = (first, second, third)
+    whole_tiles = query_map.shape[0] % 16 == 0
+    work = hyper_work(pieces, slot_count, hyper_feed, model_width) if whole_tiles else Work()
+    first, second, third, gains, notes, own_one, own_two, *made = spread(
+        1, wides, outer, blocks, (gains, notes), columns, work
+    )
+    first = first.reshape(hyper_width, -1)
+    second = second.reshape(hyper_width, -1)
+    third = third.reshape(hyper_feed, hyper_width)
+    if whole_tiles:
+        vectors, table_shard, *hyper_stored = made
+        params = (first, second, third, vectors)
+    else:
+        vectors = second[:, model_width : model_width + 8].astype(jnp.float32).T
+        params = (first, second, third, vectors)
+        table_shard, hyper_stored = hyper_forward(pieces, slot_count, params)
+
+    if outer > 1:
+        gains = lax.all_gather(gains, "wide", axis=1, axis_index_groups=groups)
+        gains = gains.reshape(-1, gains.shape[2], gains.shape[3])
+        output_weight, down_weight = (
+            lax.all_gather(item, "wide", axis=1, axis_index_groups=groups, tiled=True)
+            for item in (output_weight, down_weight)
+        )
+    gains = gains.transpose(1, 0, 2).reshape(-1, model_width)
+    final_scale = final_gain.astype(jnp.float32).reshape(1, model_width)
+    gains = jnp.concatenate([gains[:4], final_scale, gains[:3]], axis=0)
+    notes = lax.dynamic_slice_in_dim(notes, section_index * 2, 2, 0)
+    ids, wanted = notes[:, 0].reshape(-1), notes[:, 1].reshape(-1)
+
     table_rows = section_gather(3, table_shard)
     if outer > 1:
         table_rows = lax.all_gather(table_rows, "wide", axis=1, axis_index_groups=groups)
@@ -1988,7 +2086,7 @@
         outer,
         4,
         total_tokens,
-        all_teams((own_one, y_one, core_one, beyond_one, own_two), outer, groups),
+        all_teams((own_one, own_two), outer, groups),
         output_weight,
         down_weight,
         gains,
@@ -2016,7 +2114,7 @@
         11, table_part.reshape(SECTIONS, entries, model_width), loss_block
     )
     mean_loss = loss_block[0, 0]
-    if hyper_width // (SECTIONS * wides) % 16 == 0:
+    if whole_tiles:
         grad_embed, grad_expand, grad_reduce, front, rear = hyper_collect(
             12, wides, pieces, slot_count, params, hyper_stored, table_grad
         )
@@ -2029,21 +2127,16 @@
         rear = jnp.concatenate(
             [first[:, 2 * hyper_width : 4 * hyper_width], second[:, model_width:]], axis=1
         )
-    vectors = rear[:, 2 * hyper_width : 2 * hyper_width + 4]
-    return (
-        mean_loss,
-        vectors[:, 0],
-        vectors[:, 1],
-        front[:, :hyper_width],
-        front[:, hyper_width:],
-        rear[:, :hyper_width],
-        rear[:, hyper_width : 2 * hyper_width],
-        vectors[:, 2],
-        vectors[:, 3],
-        grad_expand,
-        grad_reduce,
-        grad_embed,
-    )
+    if whole_tiles:
+        outs = deliver(grad_embed, grad_expand, grad_reduce, front, rear)
+    else:
+        vectors = rear[:, 2 * hyper_width : 2 * hyper_width + 4]
+        outs = [vectors[:, n] for n in range(4)]
+        outs += [front[:, :hyper_width], front[:, hyper_width:]]
+        outs += [rear[:, :hyper_width], rear[:, hyper_width : 2 * hyper_width]]
+        outs += [grad_expand, grad_reduce, grad_embed]
+    prescale, prebias, midscale, midshift, *maps = outs
+    return (mean_loss, prescale, prebias, *maps[:4], midscale, midshift, *maps[4:])
 
 
 def solution(mesh):

time: 595 us -> 577 us (0.970)
  starting transfers between devices: 19.4 us -> 0 us
  local copies, waits for them, and re-layouts: 21.7 us -> 11.6 us
  Pallas kernels: 540 us -> 547 us
    pallas_call x2, Pallas kernels: 91.7 us -> 123 us  [the longest x1 118 us: spread(): pl.pallas_call(functools.partial(spread_kernel, count, halves, outer, wor...]
    pallas_call x1, Pallas kernels: 28.4 us -> 1.92 us  [local(): pl.pallas_call(kernel, out_shape=tuple((jax.ShapeDtypeStruct(shape, kind)...]
    all_to_all x2 -> x0, starting transfers between devices: 17.3 us -> none  [to_ranks(): lax.all_to_all(block, 'wide', 0, 0, axis_index_groups=rank_groups if oute...]
  transfers between devices with their start and end apart: 5 -> 0, of which waited for: 0 -> 0; matrix products, arithmetic and copies ran while one was open for 2% -> 0% of each run, Pallas kernels for 21% -> 0%
where the time goes in v5:
time: 577 us; the launch traced here: 568 us
  Pallas kernels  547 us (95%)
  local copies, waits for them, and re-layouts  11.6 us (2%)
    pallas_call x1, Pallas kernels, decode(): pl.pallas_call(functools.partial(decode_kernel, (outer, tokens, share, q_...  321 us
    pallas_call x1, Pallas kernels, spread(): pl.pallas_call(functools.partial(spread_kernel, count, halves, outer, wor...  118 us
    pallas_call x1, Pallas kernels, hyper_collect(): pl.pallas_call(functools.partial(hyper_collect_kernel, slots, halves, (*i...  78.5 us
    pallas_call x1, Pallas kernels, section_sum(): pl.pallas_call(section_sum_kernel, out_shape=(jax.ShapeDtypeStruct(shape,...  12.3 us

profile of v5, /device:TPU:0, one launch (start us, length us, event | category | flops | bytes accessed | tf_op | source)
XLA Modules:
  0.0 567.6 jit_solution(658267081866770554)
XLA Ops:
  0.6 1.3 add_bitcast_fusion.refs_15_
  1.9 1.3 pad_maximum_fusion.2.refs_12_
  3.2 0.0 copy-start.4
  3.2 0.0 copy-start.5
  3.2 0.0 copy-start.3
  3.2 5.2 pack.1
  8.4 0.0 copy-done.4
  8.4 0.0 copy-done.5
  8.4 0.1 select_reduce_fusion
  8.5 0.0 copy-done.3
  8.5 0.1 copy.44
  8.6 0.1 reshape.156
  8.7 4.7 gather_fusion
  13.5 0.1 reshape.155
  13.6 0.9 broadcast_select_fusion.refs_7_.refs_1_
  14.5 0.0 copy-start.2
  14.5 117.7 %spread.1 = (bf16[4,8,16,4096]{3,2,1,0:T(8,128)(2,1)}, bf16[4,8,16,2176]{3,2,1,0:T(8,128)(2,1)}, bf16[4,8,64,512]{3,2,1,0:T(8,128)(2,1)}, f32[8,8,256]{2,1,0:T(8...) custom-call(bf16[16,4096]{1,0:T(8,128)(2,1)} %get-tuple-element.55.r, ...), custom_call_target="tpu_custom_call" | custom-call | tf_op jit(solution)/shard_map/spread/pallas_call | solution.py:410
  132.2 0.0 copy-start.1
  132.2 0.9 slice.30
  133.1 0.8 slice.31
  133.9 0.0 copy-done.2
  133.9 0.7 pad_maximum_fusion.refs_4_
  134.6 0.2 negate_select_fusion
  134.8 0.1 fusion.9
  134.9 0.1 fusion.6
  135.0 0.1 fusion.4
  135.1 0.1 fusion.5
  135.2 0.8 tile.8
  136.0 0.8 tile.20
  136.8 0.0 copy-done.1
  136.8 0.6 pad.12.refs_1_
  137.4 0.6 pad.13.refs_2_
  138.0 10.4 %section_gather.1 = bf16[4,64,2048]{2,1,0:T(8,128)(2,1)} custom-call(bf16[64,2048]{1,0:T(8,128)(2,1)} %get-tuple-element.63.block), custom_call_target="tpu_custom_call" | custom-call | tf_op jit(solution)/shard_map/section_gather/pallas_call | solution.py:137
  148.4 0.1 iota_add_fusion
  148.5 0.8 add.108.refs_0_
  149.3 320.6 %decode.1 = (bf16[2,8,16,2048]{3,2,1,0:T(8,128)(2,1)}, bf16[2,8,16,2048]{3,2,1,0:T(8,128)(2,1)}, bf16[256,256]{1,0:T(8,128)(2,1)}, f32[8,128]{1,0:T(8,128)}) custom-call(s32[256,1]{1,0:T(8,128)} %add.108.refs_0_, s32[8,128]{1,0:T(8,128)} %pad.12.refs_1_, s32[8,128]{1,0:T(8,128)} %pad.13.refs_2_, bf16[256,2048]{1,0:T(8,128)(2,1)} %bitcast.68, ...), custom_call_target="tpu_custom_call" | custom-call | tf_op jit(solution)/shard_map/decode/pallas_call | solution.py:1651
  469.9 0.0 copy-start
  469.9 1.8 fusion.12
  471.7 0.1 add.106
  471.8 0.0 copy-done
  471.8 1.5 fusion
  473.3 12.3 %section_sum.1 = (f32[64,2048]{1,0:T(8,128)}, f32[8,128]{1,0:T(8,128)}) custom-call(bf16[4,64,2048]{2,1,0:T(8,128)(2,1)} %bitcast.69, f32[8,128]{1,0:T(8,128)} %get-tuple-element.70.loss), custom_call_target="tpu_custom_call" | custom-call | tf_op jit(solution)/shard_map/section_sum/pallas_call | solution.py:191
  485.6 78.5 %hyper_collect.1 = (f32[16,2048]{1,0:T(8,128)}, f32[16,2048]{1,0:T(8,128)}, f32[64,512]{1,0:T(8,128)}, f32[16,1024]{1,0:T(8,128)}, f32[16,1152]{1,0:T(8,128)}) custom-call(f32[64,2048]{1,0:T(8,128)} %get-tuple-element.72.refs_0_, bf16[512,512]{1,0:T(8,128)(2,1)} %broadcast_select_fusion.refs_7_.refs_1_, bf16[512,4096]{1,0:T(8,128)(2,1)} %bitcast.67, ...), custom_call_target="tpu_custom_call" | custom-call | tf_op jit(solution)/shard_map/hyper_collect/pallas_call | solution.py:1962
  564.1 1.9 deliver.1
  566.0 1.2 slice.27
  (17 shorter events, 0.1 us)
Async XLA Ops:
  3.2 5.2 copy-start.4
  3.2 5.2 copy-start.5
  3.2 5.3 copy-start.3
  14.5 119.4 %copy-start.2 = (bf16[2048]{0:T(1024)(128)(2,1)S(1)}, bf16[2048]{0:T(1024)(128)(2,1)}, u32[]{:S(2)}) copy-start(bf16[2048]{0:T(1024)(128)(2,1)} %param.53) | copy-start | bytes 12292
  132.2 4.6 copy-start.1
  469.9 1.9 copy-start

commit v6 on v5

--- a/solution.py
+++ b/solution.py
@@ -230,9 +230,12 @@
     blocks, notes, columns = refs[:count], refs[count : count + 2], refs[count + 2 : count + 4]
     refs = refs[count + 4 :]
     extra, refs = refs[: work.inputs], refs[work.inputs :]
-    gathereds, notes_out, columns_out = refs[:count], refs[count : count + 2], refs[count + 2 : count + 4]
+    outs, notes_out, columns_out = refs[:count], refs[count : count + 2], refs[count + 2 : count + 4]
     refs = refs[count + 4 :]
     extra, refs = extra + refs[: work.outputs], refs[work.outputs :]
+    gathereds = outs
+    if work.body is not None:
+        gathereds, refs = refs[:count], refs[count:]
     (
         keep_sem,
         note_keep,
@@ -334,6 +337,7 @@
         return carry
 
     lax.fori_loop(1, halves, start_z, 0)
+    work.begin(extra + refs[12:])
     for n in range(count):
         keeps[n].wait()
         a_copy(n, 0).start()
@@ -389,15 +393,29 @@
         return carry
 
     lax.fori_loop(1, halves, drain_z, 0)
+    copies = []
+    if work.body is not None:
+        copies = [
+            pltpu.make_async_copy(gathereds[n], outs[n], keep_sem.at[n]) for n in range(count)
+        ]
+    for copy in copies:
+        copy.start()
     work.run(gathereds, extra + refs[12:])
+    for copy in copies:
+        copy.wait()
     for copy in note_keeps + note_copies + column_copies:
         copy.wait()
 
 
 class Work:
-    def __init__(self, run=None, operands=(), outs=(), scratch=()):
-        self.body, self.operands, self.outs, self.scratch = run, operands, outs, scratch
+    def __init__(self, early=None, body=None, operands=(), outs=(), scratch=()):
+        self.early, self.body = early, body
+        self.operands, self.outs, self.scratch = operands, outs, scratch
         self.inputs, self.outputs = len(operands), len(outs)
+
+    def begin(self, refs):
+        if self.early is not None:
+            self.early(*refs)
 
     def run(self, gathereds, refs):
         if self.body is not None:
@@ -406,7 +424,7 @@
 
 def spread(collective_id, wides, outer, blocks, notes, columns, work):
     count, halves = len(blocks), wides // 2
-    place = ANYWHERE if work.body is None else IN_VMEM
+    held = [] if work.body is None else blocks
     return pl.pallas_call(
         functools.partial(spread_kernel, count, halves, outer, work),
         out_shape=tuple(
@@ -414,10 +432,13 @@
         )
         + tuple(jax.ShapeDtypeStruct((TEAM,) + note.shape, note.dtype) for note in notes)
         + tuple(jax.ShapeDtypeStruct(item.shape, item.dtype) for item in columns)
-        + tuple(jax.ShapeDtypeStruct(shape, kind) for shape, kind in work.outs),
-        in_specs=[ANYWHERE] * (count + 4) + [IN_VMEM] * work.inputs,
-        out_specs=(place,) * count + (ANYWHERE,) * 4 + (IN_VMEM,) * work.outputs,
-        scratch_shapes=[dma_sems(count), dma_sems(4), dma_sems(4, TEAM), dma_sems(4, TEAM)]
+        + tuple(jax.ShapeDtypeStruct(shape, kind) for shape, kind, _ in work.outs),
+        in_specs=[ANYWHERE] * (count + 4) + [place for _, place in work.operands],
+        out_specs=(ANYWHERE,) * (count + 4) + tuple(place for _, _, place in work.outs),
+        scratch_shapes=[
+            pltpu.VMEM((SECTIONS, wides) + block.shape, block.dtype) for block in held
+        ]
+        + [dma_sems(count), dma_sems(4), dma_sems(4, TEAM), dma_sems(4, TEAM)]
         + [
             dma_sems(count, halves),
             dma_sems(count, halves),
@@ -428,7 +449,7 @@
         + list(work.scratch),
         compiler_params=settings(collective_id),
         name="spread",
-    )(*blocks, *notes, *columns, *work.operands)
+    )(*blocks, *notes, *columns, *(item for item, _ in work.operands))
 
 
 def collect_kernel(count, halves, *refs):
@@ -706,6 +727,7 @@
     pooled_out,
     entered,
     outcome,
+    done=lambda *names: None,
 ):
     width = pieces.shape[1]
     count, feed = pieces.shape[0], third.shape[0]
@@ -735,11 +757,13 @@
             mixed.append(trans_times(weights, value))
         mixed_out[rows, :] = jnp.concatenate(mixed, axis=1).astype(jnp.bfloat16)
 
+    done("heads", "mixed")
     for start in range(0, width, TILE):
         columns = pl.ds(start, TILE)
         middle_out[:, columns] = pieces[:, columns].astype(jnp.float32) + matmul(
             mixed_out[...], first[:, pl.ds(3 * width + start, TILE)]
         )
+    done("middle")
     normed, _ = center_norm(middle_out[...])
     entered[...] = (normed * vectors[2:3] + vectors[3:4]).astype(jnp.bfloat16)
     outcome[...] = middle_out[...]
@@ -752,6 +776,7 @@
         expanded_out[:, pl.ds(start, TILE)] = expanded
         outcome[...] += matmul(gelu(expanded).astype(jnp.bfloat16), third[pl.ds(start, TILE), :])
 
+    done("expanded")
     pooled = jnp.mean(outcome[...].reshape(count // slots, slots, width), axis=1)
     pooled_out[...] = pooled.astype(jnp.bfloat16)
 
@@ -794,17 +819,78 @@
     return [pltpu.VMEM((count, width), jnp.bfloat16), pltpu.VMEM((count, width), jnp.float32)]
 
 
-def hyper_work(pieces, slots, feed, depth):
-    count, width = pieces.shape
-
-    def run(gathereds, pieces_ref, vectors, *refs):
+def hyper_work(piece_rows, piece_table, slots, feed, depth):
+    count, width = piece_rows.shape[0], piece_table.shape[1]
+    table, heads, mixed, middle, expanded, pooled = hyper_outs(count, slots, width, feed, depth)
+    far = dict(heads=heads, mixed=mixed, middle=middle, expanded=expanded)
+
+    def unpack(refs):
+        rows, source, vectors, pieces, table_out, pooled_out, *refs = refs
+        outs, held = dict(zip(far, refs[:4])), dict(zip(far, refs[4:8]))
+        held_table, entered, outcome, sem = refs[8:]
+        return rows, source, vectors, pieces, table_out, pooled_out, outs, held, held_table, entered, outcome, sem
+
+    def early(*refs):
+        rows, source, _, pieces, *_, held_table, _, outcome, sem = unpack(refs)
+        load = pltpu.make_async_copy(source, held_table, sem.at[4])
+        load.start()
+        outcome[...] = jnp.zeros_like(outcome)
+        load.wait()
+
+        @pl.loop(0, held_table.shape[0] // TILE)
+        def _(n):
+            start = pl.multiple_of(n * TILE, TILE)
+            column = lax.broadcasted_iota(jnp.int32, (count, TILE), 1) + start
+            ones = jnp.where(rows[...] == column, 1.0, 0.0).astype(jnp.bfloat16)
+            outcome[...] += matmul(ones, held_table[pl.ds(start, TILE), :])
+
+        pieces[...] = outcome[...].astype(jnp.bfloat16)
+
+    def body(gathereds, *refs):
+        _, _, vectors, pieces, table_out, pooled_out, outs, held, _, entered, outcome, sem = unpack(refs)
         first, second, third = (Rows(blocks) for blocks in gathereds)
         turned = jnp.transpose(second[:, pl.ds(depth, LANES)].astype(jnp.float32))
         vectors[...] = turned[: vectors.shape[0]]
-        hyper_kernel(slots, pieces_ref, first, second, third, vectors, *refs)
-
-    outs = [((8, width), jnp.float32)] + hyper_outs(count, slots, width, feed, depth)
-    return Work(run, (pieces,), outs, hyper_scratch(count, width))
+        copies = {
+            name: pltpu.make_async_copy(held[name], outs[name], sem.at[n])
+            for n, name in enumerate(far)
+        }
+
+        def done(*names):
+            for name in names:
+                copies[name].start()
+
+        hyper_kernel(
+            slots,
+            pieces,
+            first,
+            second,
+            third,
+            vectors,
+            table_out,
+            held["heads"],
+            held["mixed"],
+            held["middle"],
+            held["expanded"],
+            pooled_out,
+            entered,
+            outcome,
+            done,
+        )
+        for name in far:
+            copies[name].wait()
+
+    near = [((8, width), jnp.float32), ((count, width), jnp.bfloat16), table, pooled]
+    return Work(
+        early,
+        body,
+        ((piece_rows, IN_VMEM), (piece_table, ANYWHERE)),
+        [(*item, IN_VMEM) for item in near] + [(*item, ANYWHERE) for item in far.values()],
+        [pltpu.VMEM(*item) for item in far.values()]
+        + [pltpu.VMEM(piece_table.shape, jnp.bfloat16)]
+        + hyper_scratch(count, width)
+        + [dma_sems(5)],
+    )
 
 
 def hyper_forward(pieces, slots, params):
@@ -1767,7 +1853,8 @@
             self.z_copy(n, j).wait_send()
 
 
-EMBED, EXPAND, REDUCE, FRONT, REAR = range(5)
+EMBED, REDUCE, EXPAND, FRONT, REAR = range(5)
+FAR = ("middle", "expanded", "third", "first", "mixed", "heads", "pieces")
 
 
 def hyper_collect_kernel(slots, halves, names, *refs):
@@ -1782,6 +1869,12 @@
     depth = this.table_grad.shape[1]
     head = width // HYPER_HEAD_COUNT
     scale = head ** (-0.5)
+    loads = {
+        name: pltpu.make_async_copy(getattr(this, "far_" + name), getattr(this, name), this.load_sem.at[n])
+        for n, name in enumerate(FAR)
+    }
+    for name in FAR:
+        loads[name].start()
     this.greet()
 
     def store(n, columns, values):
@@ -1799,10 +1892,31 @@
     outcome_grad = jnp.broadcast_to(pooled_grad[:, None, :], (count // slots, slots, width))
     outcome_grad = outcome_grad.reshape(count, width)
     outcome_low[...] = outcome_grad.astype(jnp.bfloat16)
+    loads["middle"].wait()
     normed, inverse = center_norm(this.middle[...])
     entered[...] = jnp.transpose(normed * vectors[2:3] + vectors[3:4]).astype(jnp.bfloat16)
     feed_grad[...] = jnp.zeros_like(feed_grad)
     this.sum_core(EMBED)
+
+    for name in FAR[1:]:
+        loads[name].wait()
+    tiles = feed // TILE
+
+    @pl.loop(0, tiles)
+    def _(n):
+        tile = pl.ds(pl.multiple_of(n * TILE, TILE), TILE)
+        values = this.expanded[:, tile]
+        erf = 0.5 * (1.0 + lax.erf(values * inv_root_two))
+        active = (values * erf).astype(jnp.bfloat16)
+        this.expanded[:, tile] = erf + values * jnp.exp(-0.5 * values * values) * inv_root_tau
+        block = this.partials[REDUCE]
+        owned = block.shape[3]
+        lines = TILE // (2 * owned)
+        at = n * lines
+        turned = trans_times(active, outcome_low[...]).astype(jnp.bfloat16)
+        block[at // halves, pl.ds(at % halves, lines)] = turned.reshape(lines, 2, owned, width)
+
+    this.start(REDUCE)
 
     def feed_tiles(low, high):
         @pl.loop(low, high)
@@ -1810,28 +1924,16 @@
             start = pl.multiple_of(n * TILE, TILE)
             tile = pl.ds(start, TILE)
             columns = pl.ds(pl.multiple_of(4 * width + start, TILE), TILE)
-            values = this.expanded[:, tile]
-            erf = 0.5 * (1.0 + lax.erf(values * inv_root_two))
-            active = (values * erf).astype(jnp.bfloat16)
-            block = this.partials[REDUCE]
-            owned = block.shape[3]
-            lines = TILE // (2 * owned)
-            at = n * lines
-            turned = trans_times(active, outcome_low[...]).astype(jnp.bfloat16)
-            block[at // halves, pl.ds(at % halves, lines)] = turned.reshape(lines, 2, owned, width)
             active_grad = times_trans(outcome_low[...], third[tile, :])
-            slope = erf + values * jnp.exp(-0.5 * values * values) * inv_root_tau
-            low_grad = (active_grad * slope).astype(jnp.bfloat16)
+            low_grad = (active_grad * this.expanded[:, tile]).astype(jnp.bfloat16)
             store(EXPAND, tile, matmul(entered[...], low_grad))
             feed_grad[...] += times_trans(low_grad, first[:, columns])
 
-    tiles = feed // TILE
     feed_tiles(0, tiles // 2)
+    this.sum_core(REDUCE)
     this.sum_b(EMBED)
     feed_tiles(tiles // 2, tiles)
     this.start(EXPAND)
-    this.start(REDUCE)
-    this.sum_a(EMBED)
 
     grad = feed_grad[...]
     scale_two = jnp.sum(grad * normed, axis=0, keepdims=True)
@@ -1843,6 +1945,7 @@
     this.mixed_grad[...] = times_trans(middle_low, first[:, out_columns]).astype(jnp.bfloat16)
     mask = same_entry(CHUNK, slots)
     this.sum_core(EXPAND)
+    this.sum_a(EMBED)
 
     def attention_chunks(low, high):
         @pl.loop(low, high)
@@ -1874,10 +1977,10 @@
 
     chunks = count // CHUNK
     attention_chunks(0, chunks // 2)
-    this.sum_core(REDUCE)
+    this.sum_b(REDUCE)
+    attention_chunks(chunks // 2, chunks)
     this.sum_b(EXPAND)
-    attention_chunks(chunks // 2, chunks)
-    this.sum_b(REDUCE)
+    this.sum_a(REDUCE)
 
     normed, _ = center_norm(this.pieces[...].astype(jnp.float32))
     entered[...] = jnp.transpose(normed * vectors[0:1] + vectors[1:2]).astype(jnp.bfloat16)
@@ -1890,8 +1993,6 @@
         feed_grad[...] += times_trans(low_grad, first[:, columns])
         if start + TILE == 2 * width:
             this.start(FRONT)
-            this.sum_a(EXPAND)
-            this.sum_a(REDUCE)
 
     grad = feed_grad[...]
     scale_one = jnp.sum(grad * normed, axis=0, keepdims=True)
@@ -1904,12 +2005,14 @@
     this.start(REAR)
     this.sum_core(FRONT)
     this.sum_core(REAR)
-    for n in (EMBED, EXPAND, REDUCE):
-        this.sum_lines(n)
+    this.sum_a(EXPAND)
+    this.sum_lines(EMBED)
     this.sum_b(FRONT)
     this.sum_b(REAR)
+    this.sum_lines(REDUCE)
     this.sum_a(FRONT)
     this.sum_a(REAR)
+    this.sum_lines(EXPAND)
     this.sum_lines(FRONT)
     this.sum_lines(REAR)
     for n in range(5):
@@ -1925,22 +2028,27 @@
     rows = width // devices
     shapes = [
         (rows, depth),
+        (feed // devices, width),
         (rows, feed),
-        (feed // devices, width),
         (rows, 2 * width),
         (rows, 2 * width + LANES),
     ]
-    inputs = dict(
-        table_grad=table_grad,
+    heads, mixed, middle, expanded, pooled = stored
+    inputs = dict(table_grad=table_grad, second=second, vectors=vectors, pooled=pooled)
+    far = dict(
+        middle=middle,
+        expanded=expanded,
+        third=third,
+        first=first,
+        mixed=mixed,
+        heads=heads,
         pieces=pieces,
-        first=first,
-        second=second,
-        third=third,
-        vectors=vectors,
     )
-    inputs.update(zip(("heads", "mixed", "middle", "expanded", "pooled"), stored))
+    inputs.update({"far_" + name: far[name] for name in FAR})
     outputs = {f"sums{n}": jax.ShapeDtypeStruct(shape, full) for n, shape in enumerate(shapes)}
-    scratch = dict(
+    scratch = {name: pltpu.VMEM(far[name].shape, far[name].dtype) for name in FAR}
+    scratch.update(
+        load_sem=dma_sems(len(FAR)),
         entered=pltpu.VMEM((width, count), low),
         outcome_low=pltpu.VMEM((count, width), low),
         feed_grad=pltpu.VMEM((count, width), full),
@@ -1962,7 +2070,7 @@
     return pl.pallas_call(
         functools.partial(hyper_collect_kernel, slots, halves, (*inputs, *outputs, *scratch)),
         out_shape=tuple(outputs.values()),
-        in_specs=[IN_VMEM] * len(inputs),
+        in_specs=[IN_VMEM] * (len(inputs) - len(FAR)) + [ANYWHERE] * len(FAR),
         out_specs=(IN_VMEM,) * len(outputs),
         scratch_shapes=list(scratch.values()),
         compiler_params=settings(collective_id),
@@ -2028,8 +2136,6 @@
     ).astype(jnp.int32)
     row_start = jnp.sum(group_hits * group_offsets[None, :], axis=1)
     piece_rows = (row_start[:, None] + slot_ids).reshape(-1)
-    pieces = jnp.take(piece_table, piece_rows, axis=0)
-
     *columns, first, second, third, gains, notes = pack(
         (query_weight, key_weight, value_weight, gate_weight, up_weight),
         (query_map, key_map, value_map, output_map, expand_map, embed_map, reduce_map),
@@ -2039,7 +2145,11 @@
     )
     blocks = (first, second, third)
     whole_tiles = query_map.shape[0] % 16 == 0
-    work = hyper_work(pieces, slot_count, hyper_feed, model_width) if whole_tiles else Work()
+    work = Work()
+    if whole_tiles:
+        work = hyper_work(
+            piece_rows.reshape(-1, 1), piece_table, slot_count, hyper_feed, model_width
+        )
     first, second, third, gains, notes, own_one, own_two, *made = spread(
         1, wides, outer, blocks, (gains, notes), columns, work
     )
@@ -2047,11 +2157,13 @@
     second = second.reshape(hyper_width, -1)
     third = third.reshape(hyper_feed, hyper_width)
     if whole_tiles:
-        vectors, table_shard, *hyper_stored = made
+        vectors, pieces, table_shard, pooled, *hyper_stored = made
+        hyper_stored = (*hyper_stored, pooled)
         params = (first, second, third, vectors)
     else:
         vectors = second[:, model_width : model_width + 8].astype(jnp.float32).T
         params = (first, second, third, vectors)
+        pieces = jnp.take(piece_table, piece_rows, axis=0)
         table_shard, hyper_stored = hyper_forward(pieces, slot_count, params)
 
     if outer > 1:
@@ -2115,7 +2227,7 @@
     )
     mean_loss = loss_block[0, 0]
     if whole_tiles:
-        grad_embed, grad_expand, grad_reduce, front, rear = hyper_collect(
+        grad_embed, grad_reduce, grad_expand, front, rear = hyper_collect(
             12, wides, pieces, slot_count, params, hyper_stored, table_grad
         )
     else:

time: 577 us -> 556 us (0.964)
  Pallas kernels: 547 us -> 533 us
    pallas_call x1, Pallas kernels: 78.5 us -> 68.7 us  [hyper_collect(): pl.pallas_call(functools.partial(hyper_collect_kernel, slots, halves, (*i...]
where the time goes in v6:
time: 556 us; the launch traced here: 549 us
  Pallas kernels  533 us (96%)
  local copies, waits for them, and re-layouts  7.51 us (1%)
    pallas_call x1, Pallas kernels, decode(): pl.pallas_call(functools.partial(decode_kernel, (outer, tokens, share, q_...  322 us
    pallas_call x1, Pallas kernels, spread(): pl.pallas_call(functools.partial(spread_kernel, count, halves, outer, wor...  113 us
    pallas_call x1, Pallas kernels, hyper_collect(): pl.pallas_call(functools.partial(hyper_collect_kernel, slots, halves, (*i...  68.7 us
    pallas_call x1, Pallas kernels, section_sum(): pl.pallas_call(section_sum_kernel, out_shape=(jax.ShapeDtypeStruct(shape,...  11.7 us

profile of v6, /device:TPU:0, one launch (start us, length us, event | category | flops | bytes accessed | tf_op | source)
XLA Modules:
  0.0 548.6 jit_solution(14323300867164971669)
XLA Ops:
  0.6 1.3 add_bitcast_fusion.refs_15_
  1.9 1.3 pad_maximum_fusion.2.refs_12_
  3.2 0.0 copy-start.4
  3.2 0.0 copy-start.5
  3.2 0.0 copy-start.3
  3.2 5.2 pack.1
  8.4 0.0 copy-done.4
  8.4 0.0 copy-done.5
  8.4 0.1 select_reduce_fusion
  8.5 0.0 copy-done.3
  8.5 0.1 copy.45
  8.6 0.8 reshape_reshape.9.refs_7_
  9.4 0.0 copy-start.2
  9.4 113.0 %spread.1 = (bf16[4,8,16,4096]{3,2,1,0:T(8,128)(2,1)}, bf16[4,8,16,2176]{3,2,1,0:T(8,128)(2,1)}, bf16[4,8,64,512]{3,2,1,0:T(8,128)(2,1)}, f32[8,8,256]{2,1,0:T(8...) custom-call(bf16[16,4096]{1,0:T(8,128)(2,1)} %get-tuple-element.56.r, ...), custom_call_target="tpu_custom_call" | custom-call | tf_op jit(solution)/shard_map/spread/pallas_call | solution.py:428
  122.4 0.0 copy-start.1
  122.4 0.9 slice.29
  123.3 0.8 slice.28
  124.1 0.0 copy-done.2
  124.1 0.7 pad_maximum_fusion.refs_4_
  124.8 0.2 negate_select_fusion
  125.1 0.1 fusion.9
  125.2 0.1 fusion.6
  125.2 0.1 fusion.4
  125.3 0.1 fusion.5
  125.5 0.8 tile.8
  126.3 0.8 tile.20
  127.0 0.0 copy-done.1
  127.1 0.6 pad.12.refs_1_
  127.7 0.6 pad.13.refs_2_
  128.3 10.4 %section_gather.1 = bf16[4,64,2048]{2,1,0:T(8,128)(2,1)} custom-call(bf16[64,2048]{1,0:T(8,128)(2,1)} %get-tuple-element.64.block), custom_call_target="tpu_custom_call" | custom-call | tf_op jit(solution)/shard_map/section_gather/pallas_call | solution.py:137
  138.7 0.1 iota_add_fusion
  138.7 0.8 add.83.refs_0_
  139.5 321.9 %decode.1 = (bf16[2,8,16,2048]{3,2,1,0:T(8,128)(2,1)}, bf16[2,8,16,2048]{3,2,1,0:T(8,128)(2,1)}, bf16[256,256]{1,0:T(8,128)(2,1)}, f32[8,128]{1,0:T(8,128)}) custom-call(s32[256,1]{1,0:T(8,128)} %add.83.refs_0_, s32[8,128]{1,0:T(8,128)} %pad.12.refs_1_, s32[8,128]{1,0:T(8,128)} %pad.13.refs_2_, bf16[256,2048]{1,0:T(8,128)(2,1)} %bitcast.67, ...), custom_call_target="tpu_custom_call" | custom-call | tf_op jit(solution)/shard_map/decode/pallas_call | solution.py:1737
  461.4 0.0 copy-start
  461.5 1.8 fusion.12
  463.3 0.1 add.81
  463.4 0.0 copy-done
  463.4 1.5 fusion
  464.8 11.7 %section_sum.1 = (f32[64,2048]{1,0:T(8,128)}, f32[8,128]{1,0:T(8,128)}) custom-call(bf16[4,64,2048]{2,1,0:T(8,128)(2,1)} %bitcast.68, f32[8,128]{1,0:T(8,128)} %get-tuple-element.71.loss), custom_call_target="tpu_custom_call" | custom-call | tf_op jit(solution)/shard_map/section_sum/pallas_call | solution.py:191
  476.6 68.7 %hyper_collect.1 = (f32[16,2048]{1,0:T(8,128)}, f32[64,512]{1,0:T(8,128)}, f32[16,2048]{1,0:T(8,128)}, f32[16,1024]{1,0:T(8,128)}, f32[16,1152]{1,0:T(8,128)}) custom-call(f32[64,2048]{1,0:T(8,128)} %get-tuple-element.73.refs_0_, bf16[512,2176]{1,0:T(8,128)(2,1)} %bitcast.69, f32[8,512]{1,0:T(8,128)} %get-tuple-element.75.refs_2_, ...), custom_call_target="tpu_custom_call" | custom-call | tf_op jit(solution)/shard_map/hyper_collect/pallas_call | solution.py:2070
  545.3 1.9 deliver.1
  547.2 1.2 slice.27
  (14 shorter events, 0.1 us)
Async XLA Ops:
  3.2 5.2 copy-start.4
  3.2 5.2 copy-start.5
  3.2 5.3 copy-start.3
  9.4 114.7 %copy-start.2 = (bf16[2048]{0:T(1024)(128)(2,1)S(1)}, bf16[2048]{0:T(1024)(128)(2,1)}, u32[]{:S(2)}) copy-start(bf16[2048]{0:T(1024)(128)(2,1)} %param.53) | copy-start | bytes 12292
  122.4 4.6 copy-start.1
  461.4 1.9 copy-start

commit v7 on v6

--- a/solution.py
+++ b/solution.py
@@ -638,7 +638,7 @@
 def causal_blocks(count, length):
     row = lax.broadcasted_iota(jnp.int32, (count, count), 0)
     column = lax.broadcasted_iota(jnp.int32, (count, count), 1)
-    return (row // length == column // length) & (column <= row)
+    return (row // length == column // length) & (row <= column)
 
 
 def turn(values, tables):
@@ -665,11 +665,9 @@
 
 
 def attend(queries, key, mask, scale):
-    scores = times_trans(queries, key) * scale
-    scores = jnp.where(mask, scores, -1e30)
-    peak = jnp.max(scores, axis=1, keepdims=True)
-    mass = jnp.exp(scores - peak)
-    return mass / jnp.sum(mass, axis=1, keepdims=True)
+    scores = jnp.where(mask, times_trans(key, queries) * scale, -1e30)
+    mass = jnp.exp(scores - jnp.max(scores, axis=0, keepdims=True))
+    return mass / jnp.sum(mass, axis=0, keepdims=True)
 
 
 def local(kernel, operands, outs, scratch, name):
@@ -1390,7 +1388,7 @@
         mixed = []
         for start in range(0, self.q_width, HEAD_DIM):
             weights = attend(queries[:, start : start + HEAD_DIM], key, mask, HEAD_DIM ** (-0.5))
-            mixed.append(matmul(weights.astype(jnp.bfloat16), value))
+            mixed.append(trans_times(weights.astype(jnp.bfloat16), value))
         mixed = jnp.concatenate(mixed, axis=1).astype(jnp.bfloat16)
         yield
 
@@ -1547,14 +1545,14 @@
             query = queries[:, start : start + HEAD_DIM]
             outer = mixed_grad[:, start : start + HEAD_DIM]
             weights = attend(query, key, mask, scale)
-            weight_grad = times_trans(outer, value)
+            weight_grad = times_trans(value, outer)
             score_grad = weights * (
-                weight_grad - jnp.sum(weights * weight_grad, axis=1, keepdims=True)
+                weight_grad - jnp.sum(weights * weight_grad, axis=0, keepdims=True)
             )
             score_grad = score_grad.astype(jnp.bfloat16)
-            query_grads.append(matmul(score_grad, key) * scale)
-            key_grad = key_grad + trans_times(score_grad, query) * scale
-            value_grad = value_grad + trans_times(weights.astype(jnp.bfloat16), outer)
+            query_grads.append(trans_times(score_grad, key) * scale)
+            key_grad = key_grad + matmul(score_grad, query) * scale
+            value_grad = value_grad + matmul(weights.astype(jnp.bfloat16), outer)
         query_grad = jnp.concatenate(query_grads, axis=1)
         query_grad = turn(query_grad, [self.back_tables[n] for n in range(3)])
         pair_grad = jnp.concatenate([key_grad, value_grad], axis=1)
@@ -2004,8 +2002,8 @@
     store(REAR, pl.ds(2 * width, LANES), jnp.transpose(summed))
     this.start(REAR)
     this.sum_core(FRONT)
+    this.sum_a(EXPAND)
     this.sum_core(REAR)
-    this.sum_a(EXPAND)
     this.sum_lines(EMBED)
     this.sum_b(FRONT)
     this.sum_b(REAR)

time: 556 us -> 558 us (level)
  no operation moved by 1% of the time
where the time goes in v7:
time: 558 us; the launch traced here: 549 us
  Pallas kernels  533 us (96%)
  local copies, waits for them, and re-layouts  7.51 us (1%)
    pallas_call x1, Pallas kernels, decode(): pl.pallas_call(functools.partial(decode_kernel, (outer, tokens, share, q_...  321 us
    pallas_call x1, Pallas kernels, spread(): pl.pallas_call(functools.partial(spread_kernel, count, halves, outer, wor...  113 us
    pallas_call x1, Pallas kernels, hyper_collect(): pl.pallas_call(functools.partial(hyper_collect_kernel, slots, halves, (*i...  70.5 us
    pallas_call x1, Pallas kernels, section_sum(): pl.pallas_call(section_sum_kernel, out_shape=(jax.ShapeDtypeStruct(shape,...  11.7 us

profile of v7, /device:TPU:0, one launch (start us, length us, event | category | flops | bytes accessed | tf_op | source)
XLA Modules:
  0.0 549.3 jit_solution(5147598512335730751)
XLA Ops:
  0.6 1.3 add_bitcast_fusion.refs_15_
  1.9 1.3 pad_maximum_fusion.2.refs_12_
  3.2 0.0 copy-start.4
  3.2 0.0 copy-start.5
  3.2 0.0 copy-start.3
  3.2 5.2 pack.1
  8.4 0.0 copy-done.4
  8.4 0.0 copy-done.5
  8.4 0.1 select_reduce_fusion
  8.5 0.0 copy-done.3
  8.5 0.1 copy.45
  8.6 0.8 reshape_reshape.9.refs_7_
  9.4 0.0 copy-start.2
  9.4 113.0 %spread.1 = (bf16[4,8,16,4096]{3,2,1,0:T(8,128)(2,1)}, bf16[4,8,16,2176]{3,2,1,0:T(8,128)(2,1)}, bf16[4,8,64,512]{3,2,1,0:T(8,128)(2,1)}, f32[8,8,256]{2,1,0:T(8...) custom-call(bf16[16,4096]{1,0:T(8,128)(2,1)} %get-tuple-element.56.r, ...), custom_call_target="tpu_custom_call" | custom-call | tf_op jit(solution)/shard_map/spread/pallas_call | solution.py:428
  122.4 0.0 copy-start.1
  122.4 0.9 slice.29
  123.3 0.8 slice.28
  124.1 0.0 copy-done.2
  124.1 0.7 pad_maximum_fusion.refs_4_
  124.8 0.2 negate_select_fusion
  125.1 0.1 fusion.9
  125.2 0.1 fusion.6
  125.2 0.1 fusion.4
  125.3 0.1 fusion.5
  125.5 0.8 tile.8
  126.3 0.8 tile.20
  127.0 0.0 copy-done.1
  127.1 0.6 pad.12.refs_1_
  127.7 0.6 pad.13.refs_2_
  128.3 10.4 %section_gather.1 = bf16[4,64,2048]{2,1,0:T(8,128)(2,1)} custom-call(bf16[64,2048]{1,0:T(8,128)(2,1)} %get-tuple-element.64.block), custom_call_target="tpu_custom_call" | custom-call | tf_op jit(solution)/shard_map/section_gather/pallas_call | solution.py:137
  138.7 0.1 iota_add_fusion
  138.7 0.8 add.83.refs_0_
  139.5 320.6 %decode.1 = (bf16[2,8,16,2048]{3,2,1,0:T(8,128)(2,1)}, bf16[2,8,16,2048]{3,2,1,0:T(8,128)(2,1)}, bf16[256,256]{1,0:T(8,128)(2,1)}, f32[8,128]{1,0:T(8,128)}) custom-call(s32[256,1]{1,0:T(8,128)} %add.83.refs_0_, s32[8,128]{1,0:T(8,128)} %pad.12.refs_1_, s32[8,128]{1,0:T(8,128)} %pad.13.refs_2_, bf16[256,2048]{1,0:T(8,128)(2,1)} %bitcast.67, ...), custom_call_target="tpu_custom_call" | custom-call | tf_op jit(solution)/shard_map/decode/pallas_call | solution.py:1735
  460.1 0.0 copy-start
  460.1 1.8 fusion.12
  462.0 0.1 add.81
  462.0 0.0 copy-done
  462.0 1.5 fusion
  463.5 11.7 %section_sum.1 = (f32[64,2048]{1,0:T(8,128)}, f32[8,128]{1,0:T(8,128)}) custom-call(bf16[4,64,2048]{2,1,0:T(8,128)(2,1)} %bitcast.68, f32[8,128]{1,0:T(8,128)} %get-tuple-element.71.loss), custom_call_target="tpu_custom_call" | custom-call | tf_op jit(solution)/shard_map/section_sum/pallas_call | solution.py:191
  475.3 70.5 %hyper_collect.1 = (f32[16,2048]{1,0:T(8,128)}, f32[64,512]{1,0:T(8,128)}, f32[16,2048]{1,0:T(8,128)}, f32[16,1024]{1,0:T(8,128)}, f32[16,1152]{1,0:T(8,128)}) custom-call(f32[64,2048]{1,0:T(8,128)} %get-tuple-element.73.refs_0_, bf16[512,2176]{1,0:T(8,128)(2,1)} %bitcast.69, f32[8,512]{1,0:T(8,128)} %get-tuple-element.75.refs_2_, ...), custom_call_target="tpu_custom_call" | custom-call | tf_op jit(solution)/shard_map/hyper_collect/pallas_call | solution.py:2068
  545.8 1.9 deliver.1
  547.7 1.2 slice.27
  (14 shorter events, 0.1 us)
Async XLA Ops:
  3.2 5.2 copy-start.4
  3.2 5.2 copy-start.5
  3.2 5.3 copy-start.3
  9.4 114.7 %copy-start.2 = (bf16[2048]{0:T(1024)(128)(2,1)S(1)}, bf16[2048]{0:T(1024)(128)(2,1)}, u32[]{:S(2)}) copy-start(bf16[2048]{0:T(1024)(128)(2,1)} %param.53) | copy-start | bytes 12292
  122.4 4.6 copy-start.1
  460.1 1.9 copy-start
